TPU v7x, 256 devices: a whole 4x4x8 slice. The times are simulated.
256 devices in a mesh: axial: 16 (over z, core), azim: 16 (over y, x).
Axes of the slice: x: 4, y: 4, z: 8, core: 2. Of those that a mesh axis runs over, the one named last changes fastest.
Arguments:
- stored: bfloat16 [4, 16, 16, 16, 2, 8, 2048], P(None, 'axial', 'azim'), may hold values from -4 to 4, as said below
- holder: int32 [4, 16, 16], replicated, may hold values from 0 to 31, as said below
- seed_temp: float32 [64, 1024, 128], P('axial', 'azim'), may hold values from -6 to 6
- seed_disloc: float32 [64, 1024, 128], P('axial', 'azim'), may hold values from -6 to 6
- decay_length: float32 [1024, 128], P('azim'), may hold values from 12 to 256
- face_radius: int32 [64, 1024], P('axial', 'azim'), may hold values from 64 to 127
- kernel: float32 [17], replicated, may hold values from 0.1 to 1
Outputs:
- adj_temp: float32 [64, 1024, 128], P('axial', 'azim')
- adj_disloc: float32 [64, 1024, 128], P('axial', 'azim')
- heater_grad: float32 [64, 1024], P('axial', 'azim')
Inputs may be any that keep to these rules, and one draw needn't show every extreme that they name: holder[k, o, j] = 2 p + c says that piece j of the checkpoint of axial index o for step k is in slot c of axial peer p; every slot holds at most one piece; per owner and step, about a quarter of the peers hold 2 pieces and some hold none. `stored`: slots that hold no piece are zero.
All inputs are finite; a program needn't handle non-finite values.
Results may differ from a plain program's by a relative error of at most 0.0003.
Values may be sent and summed in bfloat16 or wider, within the bound.
No kernel may reach another device: no remote copies, remote signals or barrier semaphores. Data moves between devices by JAX's collectives and lax.ppermute only.
A program may use at most 64 MiB of HBM per device.

v0:
```python
import jax
import jax.numpy as jnp
from jax import lax
from jax.sharding import PartitionSpec as P


def padded_2(cells, sides, width, closed):
    for axis, dim in sides:
        count = lax.axis_size(axis)
        ends = count if closed else count - 1
        head = lax.slice_in_dim(cells, 0, width, axis=dim)
        tail = lax.slice_in_dim(cells, cells.shape[dim] - width, cells.shape[dim], axis=dim)
        cells = jnp.concatenate(
            [
                lax.ppermute(tail, axis, [(i, (i + 1) % count) for i in range(ends)]),
                cells,
                lax.ppermute(head, axis, [((i + 1) % count, i) for i in range(ends)]),
            ],
            axis=dim,
        )
    return cells


def carried_in(shard, axis, combine, identity):
    devices, position = (lax.axis_size(axis), lax.axis_index(axis))
    everything = jax.tree.map(lambda part: lax.all_gather(part, axis), shard)
    start = jax.tree.map(
        lambda part, zero: jnp.broadcast_to(jnp.asarray(zero, part.dtype), part.shape),
        shard,
        identity,
    )

    def lap(k, before):
        at = devices - 1 - k
        reached = at > position
        new = combine(before, jax.tree.map(lambda part: part[at], everything))
        return jax.tree.map(lambda a, b: jnp.where(reached, a, b), new, before)

    return lax.fori_loop(0, devices, lap, start)


def laplace(field):
    axial_pad = padded_2(field, (("axial", 0),), 1, False)
    sector_pad = padded_2(field, (("azim", 1),), 1, True)
    radial_pad = jnp.pad(field, ((0, 0), (0, 0), (1, 1)))
    total = axial_pad[2:] + axial_pad[:-2]
    total = total + sector_pad[:, 2:] + sector_pad[:, :-2]
    total = total + radial_pad[:, :, 2:] + radial_pad[:, :, :-2]
    return total - 6.0 * field


def compose(earlier, later):
    return (earlier[0] * later[0], later[0] * earlier[1] + later[1])


def glide_chain(adj_disloc, decay):
    layers = adj_disloc.shape[0]
    carry = jnp.zeros_like(decay)
    power = jnp.ones_like(decay)
    partial_list = [None] * layers
    power_list = [None] * layers
    for layer in reversed(range(layers)):
        partial_list[layer] = carry
        power_list[layer] = power
        carry = decay * carry + (1.0 - decay) * adj_disloc[layer]
        power = power * decay
    identity = (jnp.ones_like(decay), jnp.zeros_like(decay))
    _, incoming = carried_in((power, carry), "axial", compose, identity)
    return jnp.stack(partial_list) + jnp.stack(power_list) * incoming


def local(stored, holder, seed_temp, seed_disloc, decay_length, face_radius, kernel):
    axial_index = lax.axis_index("axial")
    steps, peers, slots = (stored.shape[0], stored.shape[3], stored.shape[4])
    layers, azimuths, radials = seed_temp.shape
    band = (kernel.shape[0] - 1) // 2
    decay = jnp.exp(-1.0 / decay_length)
    radial = lax.broadcasted_iota(jnp.int32, (layers, azimuths, radials), 2)
    face_mask = (radial == face_radius[:, :, None]).astype(jnp.float32)
    adj_temp, adj_disloc = (seed_temp, seed_disloc)
    flux = jnp.zeros((layers, azimuths), jnp.float32)
    for step in reversed(range(steps)):
        received = lax.all_to_all(
            stored[step, 0, 0], "axial", split_axis=0, concat_axis=0, tiled=True
        )
        flat = received.reshape(peers * slots, 8, received.shape[-1])
        wanted = lax.dynamic_index_in_dim(holder[step], axial_index, 0, keepdims=False)
        pieces = jnp.take(flat, wanted, axis=0)
        state = (
            jnp.transpose(pieces, (1, 0, 2))
            .reshape(8, layers, azimuths, radials)
            .astype(jnp.float32)
        )
        theta, rho = (state[0], state[7])
        flux = flux + jnp.sum(adj_temp * face_mask, axis=2)
        stress = jnp.sqrt(1.0 + jnp.sum(state[1:7] * state[1:7], axis=0) / 6.0)
        slope = jnp.tanh(theta)
        rate = stress * jnp.exp(0.5 * slope)
        chain = glide_chain(adj_disloc, decay)
        new_temp = (
            adj_temp
            + 0.15 * laplace(adj_temp)
            + 0.2 * rho * rate * 0.5 * (1.0 - slope * slope) * adj_disloc
        )
        new_disloc = -0.3 * adj_temp + (1.0 + 0.2 * rate) * adj_disloc + chain
        adj_temp, adj_disloc = (new_temp, new_disloc)
    padded = padded_2(flux, (("azim", 1),), band, True)
    heater_grad = jnp.zeros_like(flux)
    for offset in range(2 * band + 1):
        heater_grad = heater_grad + kernel[offset] * padded[:, offset : offset + azimuths]
    return (adj_temp, adj_disloc, heater_grad)


def solution(mesh):
    in_specs = (
        P(None, "axial", "azim", None, None, None, None),
        P(),
        P("axial", "azim", None),
        P("axial", "azim", None),
        P("azim", None),
        P("axial", "azim"),
        P(),
    )
    out_specs = (P("axial", "azim", None), P("axial", "azim", None), P("axial", "azim"))
    return jax.shard_map(local, mesh=mesh, in_specs=in_specs, out_specs=out_specs, check_vma=False)
```

profile of v0, /device:TPU:1, one launch (start us, length us, event | category | flops | bytes accessed | tf_op | source)
XLA Modules:
  0.0 278.6 jit_solution(11857009038543982973)
XLA Ops:
  0.7 4.5 %slice_bitcast_fusion = (bf16[16,2,8,2048]{3,2,1,0:T(8,128)(2,1)}, bf16[16,2,8,2048]{3,2,1,0:T(8,128)(2,1)}, bf16[16,2,8,2048]{3,2,1,0:T(8,128)(2,1)}, bf16[16,2,8,2048]{3,2,1,0:T(8,128)(2,1)}) fusion(bf16[4,1,1,16,2,8,2048]{6,5,4,3,2,1,0:T(8,128)(2,1)} %param.17), kind=kLoop, calls=%fused_computation.28 | loop fusion | bytes 8388608 | tf_op jit(solution)/shard_map/squeeze | solution.py:84
  5.2 10.0 %all-to-all-start = ((bf16[16,2,8,2048]{3,2,1,0:T(8,128)(2,1)}), bf16[16,2,8,2048]{3,2,1,0:T(8,128)(2,1)S(1)}, u32[]{:S(2)}, u32[]{:S(2)}) async-start(bf16[16,2,8,2048]{3,2,1,0:T(8,128)(2,1)} %get-tuple-element.668), calls=%async_computation | async-start | bytes 2097152 | tf_op jit(solution)/shard_map/all_to_all | solution.py:83
  17.8 3.6 %collective-permute-start.1 = (f32[1,64,128]{2,1,0:T(8,128)}, f32[1,64,128]{2,1,0:T(8,128)}, u32[]{:S(2)}, u32[]{:S(2)}) collective-permute-start(f32[1,64,128]{2,1,0:T(8,128)} %get-tuple-element.711), channel_id=1, source_target_pairs={{0,16},{16,32},{32,48},{48,64},{64,80},{80,96},{96,112},{112,128},... | collective-permute-start | bytes 98312 | tf_op jit(solution)/shard_map/ppermute | solution.py:15
  22.0 4.9 %collective-permute-start.2 = (f32[4,1,128]{2,1,0:T(1,128)}, f32[4,1,128]{2,1,0:T(1,128)}, u32[]{:S(2)}, u32[]{:S(2)}) collective-permute-start(f32[4,1,128]{2,1,0:T(1,128)} %get-tuple-element.712), channel_id=1, source_target_pairs={{1,0},{2,1},{3,2},{4,3},{5,4},{6,5},{7,6},{8,7},{9,8},{10,9},{11,1... | collective-permute-start | bytes 6152 | tf_op jit(solution)/shard_map/ppermute | solution.py:17
  30.2 24.0 %all-gather = f32[1024,128]{1,0:T(8,128)S(1)} all-gather(f32[64,128]{1,0:T(8,128)S(1)} %get-tuple-element.721), channel_id=2, replica_groups=mesh['axial'=16,'azim'=16] {'axial'}, dimensions={0}, use_global_device_ids=true | all-gather | bytes 557056 | tf_op jit(solution)/shard_map/all_gather | solution.py:26
  54.2 15.9 %all-gather.1 = f32[1024,128]{1,0:T(8,128)S(1)} all-gather(f32[64,128]{1,0:T(8,128)S(1)} %get-tuple-element.697), channel_id=3, replica_groups=mesh['axial'=16,'azim'=16] {'axial'}, dimensions={0}, use_global_device_ids=true | all-gather | bytes 557056 | tf_op jit(solution)/shard_map/all_gather | solution.py:26
  70.1 6.1 %all-to-all-start.1 = ((bf16[16,2,8,2048]{3,2,1,0:T(8,128)(2,1)}), bf16[16,2,8,2048]{3,2,1,0:T(8,128)(2,1)S(1)}, u32[]{:S(2)}, u32[]{:S(2)}) async-start(bf16[16,2,8,2048]{3,2,1,0:T(8,128)(2,1)} %get-tuple-element.667), calls=%async_computation.1 | async-start | bytes 2097152 | tf_op jit(solution)/shard_map/all_to_all | solution.py:83
  77.6 26.6 %all-to-all-done.1 = bf16[16,2,8,2048]{3,2,1,0:T(8,128)(2,1)S(1)} async-done(((bf16[16,2,8,2048]{3,2,1,0:T(8,128)(2,1)}), bf16[16,2,8,2048]{3,2,1,0:T(8,128)(2,1)S(1)}, u32[]{:S(2)}, u32[]{:S(2)}) %all-to-all-start.1) | async-done | bytes 1048608 | tf_op jit(solution)/shard_map/all_to_all | solution.py:83
  104.2 4.2 %all-to-all-start.2 = ((bf16[16,2,8,2048]{3,2,1,0:T(8,128)(2,1)}), bf16[16,2,8,2048]{3,2,1,0:T(8,128)(2,1)}, u32[]{:S(2)}, u32[]{:S(2)}) async-start(bf16[16,2,8,2048]{3,2,1,0:T(8,128)(2,1)} %get-tuple-element.669), calls=%async_computation.2 | async-start | bytes 2097152 | tf_op jit(solution)/shard_map/all_to_all | solution.py:83
  113.3 22.5 %all-to-all-done.2 = bf16[16,2,8,2048]{3,2,1,0:T(8,128)(2,1)} async-done(((bf16[16,2,8,2048]{3,2,1,0:T(8,128)(2,1)}), bf16[16,2,8,2048]{3,2,1,0:T(8,128)(2,1)}, u32[]{:S(2)}, u32[]{:S(2)}) %all-to-all-start.2) | async-done | bytes 1048608 | tf_op jit(solution)/shard_map/all_to_all | solution.py:83
  135.7 4.2 %all-to-all-start.3 = ((bf16[16,2,8,2048]{3,2,1,0:T(8,128)(2,1)}), bf16[16,2,8,2048]{3,2,1,0:T(8,128)(2,1)}, u32[]{:S(2)}, u32[]{:S(2)}) async-start(bf16[16,2,8,2048]{3,2,1,0:T(8,128)(2,1)} %get-tuple-element.666), calls=%async_computation.3 | async-start | bytes 2097152 | tf_op jit(solution)/shard_map/all_to_all | solution.py:83
  150.3 17.0 %all-to-all-done.3 = bf16[16,2,8,2048]{3,2,1,0:T(8,128)(2,1)} async-done(((bf16[16,2,8,2048]{3,2,1,0:T(8,128)(2,1)}), bf16[16,2,8,2048]{3,2,1,0:T(8,128)(2,1)}, u32[]{:S(2)}, u32[]{:S(2)}) %all-to-all-start.3) | async-done | bytes 1048608 | tf_op jit(solution)/shard_map/all_to_all | solution.py:83
  172.0 3.6 %collective-permute-start.5 = (f32[1,64,128]{2,1,0:T(8,128)}, f32[1,64,128]{2,1,0:T(8,128)}, u32[]{:S(2)}, u32[]{:S(2)}) collective-permute-start(f32[1,64,128]{2,1,0:T(8,128)} %get-tuple-element.707), channel_id=1, source_target_pairs={{0,16},{16,32},{32,48},{48,64},{64,80},{80,96},{96,112},{112,128},... | collective-permute-start | bytes 98312 | tf_op jit(solution)/shard_map/ppermute | solution.py:15
  175.6 5.0 %collective-permute-start.6 = (f32[4,1,128]{2,1,0:T(1,128)}, f32[4,1,128]{2,1,0:T(1,128)S(1)}, u32[]{:S(2)}, u32[]{:S(2)}) collective-permute-start(f32[4,1,128]{2,1,0:T(1,128)} %get-tuple-element.708), channel_id=1, source_target_pairs={{1,0},{2,1},{3,2},{4,3},{5,4},{6,5},{7,6},{8,7},{9,8},{10,9},{11,1... | collective-permute-start | bytes 6152 | tf_op jit(solution)/shard_map/ppermute | solution.py:17
  181.6 5.0 %collective-permute-done.7 = f32[4,1,128]{2,1,0:T(1,128)S(1)} collective-permute-done((f32[4,1,128]{2,1,0:T(1,128)}, f32[4,1,128]{2,1,0:T(1,128)S(1)}, u32[]{:S(2)}, u32[]{:S(2)}) %collective-permute-start.7) | collective-permute-done | bytes 2080 | tf_op jit(solution)/shard_map/ppermute | solution.py:15
  187.8 17.2 %all-gather.2 = f32[1024,128]{1,0:T(8,128)S(1)} all-gather(f32[64,128]{1,0:T(8,128)S(1)} %get-tuple-element.693), channel_id=4, replica_groups=mesh['axial'=16,'azim'=16] {'axial'}, dimensions={0}, use_global_device_ids=true | all-gather | bytes 557056 | tf_op jit(solution)/shard_map/all_gather | solution.py:26
  207.1 3.5 %collective-permute-start.9 = (f32[1,64,128]{2,1,0:T(8,128)S(1)}, f32[1,64,128]{2,1,0:T(8,128)S(1)}, u32[]{:S(2)}, u32[]{:S(2)}) collective-permute-start(f32[1,64,128]{2,1,0:T(8,128)S(1)} %get-tuple-element.703), channel_id=1, source_target_pairs={{0,16},{16,32},{32,48},{48,64},{64,80},{80,96},{96,112},{112,128},... | collective-permute-start | bytes 98312 | tf_op jit(solution)/shard_map/ppermute | solution.py:15
  213.1 3.6 %collective-permute-done.11 = f32[4,1,128]{2,1,0:T(1,128)S(1)} collective-permute-done((f32[4,1,128]{2,1,0:T(1,128)S(1)}, f32[4,1,128]{2,1,0:T(1,128)S(1)}, u32[]{:S(2)}, u32[]{:S(2)}) %collective-permute-start.11) | collective-permute-done | bytes 2080 | tf_op jit(solution)/shard_map/ppermute | solution.py:15
  218.2 4.8 %collective-permute-start.17 = (f32[4,8]{1,0:T(4,128)S(1)}, f32[4,8]{1,0:T(4,128)S(1)}, u32[]{:S(2)}, u32[]{:S(2)}) collective-permute-start(f32[4,8]{1,0:T(4,128)S(1)} %get-tuple-element.725), channel_id=1, source_target_pairs={{1,0},{2,1},{3,2},{4,3},{5,4},{6,5},{7,6},{8,7},{9,8},{10,9},{11,1... | collective-permute-start | bytes 392 | tf_op jit(solution)/shard_map/ppermute | solution.py:17
  223.0 17.5 %all-gather.3 = f32[1024,128]{1,0:T(8,128)S(1)} all-gather(f32[64,128]{1,0:T(8,128)S(1)} %get-tuple-element.689), channel_id=5, replica_groups=mesh['axial'=16,'azim'=16] {'axial'}, dimensions={0}, use_global_device_ids=true | all-gather | bytes 557056 | tf_op jit(solution)/shard_map/all_gather | solution.py:26
  241.3 2.1 collective-permute-start.12
  243.4 3.5 %collective-permute-start.13 = (f32[1,64,128]{2,1,0:T(8,128)S(1)}, f32[1,64,128]{2,1,0:T(8,128)S(1)}, u32[]{:S(2)}, u32[]{:S(2)}) collective-permute-start(f32[1,64,128]{2,1,0:T(8,128)S(1)} %get-tuple-element.699), channel_id=1, source_target_pairs={{0,16},{16,32},{32,48},{48,64},{64,80},{80,96},{96,112},{112,128},... | collective-permute-start | bytes 98312 | tf_op jit(solution)/shard_map/ppermute | solution.py:15
  248.5 11.3 %multiply_add_fusion = f32[4,64]{1,0:T(4,128)} fusion(f32[4,72]{1,0:T(4,128)S(1)} %get-tuple-element.723, f32[4,64]{1,0:T(4,128)S(1)} %add_add_fusion, f32[4,72]{1,0:T(4,128)S(1)} %get-tuple-element.722, f32[]{:T(128)} %bitcast.80, f32[]{:T(128)} %bitcast.79, f32[]{:T(128)} %bitcast.78, f32[]{:T(128)} %bitcast.77, f32[]{:T(128)} %bitcast.76, f32[]{:T(128)} %bitcast.75, ...), kind=kLoop, calls=%fused_computation.193 | loop fusion | flops 8448 | bytes 18500 | tf_op jit(solution)/shard_map/add | solution.py:110
  260.7 16.4 %all-gather.4 = f32[1024,128]{1,0:T(8,128)S(1)} all-gather(f32[64,128]{1,0:T(8,128)S(1)} %get-tuple-element.682), channel_id=6, replica_groups=mesh['axial'=16,'azim'=16] {'axial'}, dimensions={0}, use_global_device_ids=true | all-gather | bytes 557056 | tf_op jit(solution)/shard_map/all_gather | solution.py:26
  (191 shorter events, 41.1 us)
Async XLA Ops:
  5.2 64.9 %all-to-all-start = ((bf16[16,2,8,2048]{3,2,1,0:T(8,128)(2,1)}), bf16[16,2,8,2048]{3,2,1,0:T(8,128)(2,1)S(1)}, u32[]{:S(2)}, u32[]{:S(2)}) async-start(bf16[16,2,8,2048]{3,2,1,0:T(8,128)(2,1)} %get-tuple-element.668), calls=%async_computation | async-start | bytes 2097152 | tf_op jit(solution)/shard_map/all_to_all | solution.py:83
  15.8 129.8 %collective-permute-start = (f32[1,64,128]{2,1,0:T(8,128)}, f32[1,64,128]{2,1,0:T(8,128)}, u32[]{:S(2)}, u32[]{:S(2)}) collective-permute-start(f32[1,64,128]{2,1,0:T(8,128)} %get-tuple-element.710), channel_id=1, source_target_pairs={{16,0},{32,16},{48,32},{64,48},{80,64},{96,80},{112,96},{128,112},... | collective-permute-start | bytes 98312 | tf_op jit(solution)/shard_map/ppermute | solution.py:17
  17.8 127.8 %collective-permute-start.1 = (f32[1,64,128]{2,1,0:T(8,128)}, f32[1,64,128]{2,1,0:T(8,128)}, u32[]{:S(2)}, u32[]{:S(2)}) collective-permute-start(f32[1,64,128]{2,1,0:T(8,128)} %get-tuple-element.711), channel_id=1, source_target_pairs={{0,16},{16,32},{32,48},{48,64},{64,80},{80,96},{96,112},{112,128},... | collective-permute-start | bytes 98312 | tf_op jit(solution)/shard_map/ppermute | solution.py:15
  22.0 123.6 %collective-permute-start.2 = (f32[4,1,128]{2,1,0:T(1,128)}, f32[4,1,128]{2,1,0:T(1,128)}, u32[]{:S(2)}, u32[]{:S(2)}) collective-permute-start(f32[4,1,128]{2,1,0:T(1,128)} %get-tuple-element.712), channel_id=1, source_target_pairs={{1,0},{2,1},{3,2},{4,3},{5,4},{6,5},{7,6},{8,7},{9,8},{10,9},{11,1... | collective-permute-start | bytes 6152 | tf_op jit(solution)/shard_map/ppermute | solution.py:17
  26.9 118.7 %collective-permute-start.3 = (f32[4,1,128]{2,1,0:T(1,128)}, f32[4,1,128]{2,1,0:T(1,128)}, u32[]{:S(2)}, u32[]{:S(2)}) collective-permute-start(f32[4,1,128]{2,1,0:T(1,128)} %get-tuple-element.713), channel_id=1, source_target_pairs={{0,1},{1,2},{2,3},{3,4},{4,5},{5,6},{6,7},{7,8},{8,9},{9,10},{10,1... | collective-permute-start | bytes 6152 | tf_op jit(solution)/shard_map/ppermute | solution.py:15
  70.1 34.1 %all-to-all-start.1 = ((bf16[16,2,8,2048]{3,2,1,0:T(8,128)(2,1)}), bf16[16,2,8,2048]{3,2,1,0:T(8,128)(2,1)S(1)}, u32[]{:S(2)}, u32[]{:S(2)}) async-start(bf16[16,2,8,2048]{3,2,1,0:T(8,128)(2,1)} %get-tuple-element.667), calls=%async_computation.1 | async-start | bytes 2097152 | tf_op jit(solution)/shard_map/all_to_all | solution.py:83
  104.2 31.6 %all-to-all-start.2 = ((bf16[16,2,8,2048]{3,2,1,0:T(8,128)(2,1)}), bf16[16,2,8,2048]{3,2,1,0:T(8,128)(2,1)}, u32[]{:S(2)}, u32[]{:S(2)}) async-start(bf16[16,2,8,2048]{3,2,1,0:T(8,128)(2,1)} %get-tuple-element.669), calls=%async_computation.2 | async-start | bytes 2097152 | tf_op jit(solution)/shard_map/all_to_all | solution.py:83
  135.7 31.6 %all-to-all-start.3 = ((bf16[16,2,8,2048]{3,2,1,0:T(8,128)(2,1)}), bf16[16,2,8,2048]{3,2,1,0:T(8,128)(2,1)}, u32[]{:S(2)}, u32[]{:S(2)}) async-start(bf16[16,2,8,2048]{3,2,1,0:T(8,128)(2,1)} %get-tuple-element.666), calls=%async_computation.3 | async-start | bytes 2097152 | tf_op jit(solution)/shard_map/all_to_all | solution.py:83
  169.1 47.6 %copy-start.5 = (f32[1,64,128]{2,1,0:T(8,128)S(1)}, f32[1,64,128]{2,1,0:T(8,128)}, u32[]{:S(2)}) copy-start(f32[1,64,128]{2,1,0:T(8,128)} %get-tuple-element.718) | copy-start | bytes 98308
  169.1 47.6 %copy-start.6 = (f32[1,64,128]{2,1,0:T(8,128)S(1)}, f32[1,64,128]{2,1,0:T(8,128)}, u32[]{:S(2)}) copy-start(f32[1,64,128]{2,1,0:T(8,128)} %get-tuple-element.719) | copy-start | bytes 98308
  170.1 16.6 %collective-permute-start.4 = (f32[1,64,128]{2,1,0:T(8,128)}, f32[1,64,128]{2,1,0:T(8,128)}, u32[]{:S(2)}, u32[]{:S(2)}) collective-permute-start(f32[1,64,128]{2,1,0:T(8,128)} %get-tuple-element.706), channel_id=1, source_target_pairs={{16,0},{32,16},{48,32},{64,48},{80,64},{96,80},{112,96},{128,112},... | collective-permute-start | bytes 98312 | tf_op jit(solution)/shard_map/ppermute | solution.py:17
  172.0 14.6 %collective-permute-start.5 = (f32[1,64,128]{2,1,0:T(8,128)}, f32[1,64,128]{2,1,0:T(8,128)}, u32[]{:S(2)}, u32[]{:S(2)}) collective-permute-start(f32[1,64,128]{2,1,0:T(8,128)} %get-tuple-element.707), channel_id=1, source_target_pairs={{0,16},{16,32},{32,48},{48,64},{64,80},{80,96},{96,112},{112,128},... | collective-permute-start | bytes 98312 | tf_op jit(solution)/shard_map/ppermute | solution.py:15
  175.6 6.0 %collective-permute-start.6 = (f32[4,1,128]{2,1,0:T(1,128)}, f32[4,1,128]{2,1,0:T(1,128)S(1)}, u32[]{:S(2)}, u32[]{:S(2)}) collective-permute-start(f32[4,1,128]{2,1,0:T(1,128)} %get-tuple-element.708), channel_id=1, source_target_pairs={{1,0},{2,1},{3,2},{4,3},{5,4},{6,5},{7,6},{8,7},{9,8},{10,9},{11,1... | collective-permute-start | bytes 6152 | tf_op jit(solution)/shard_map/ppermute | solution.py:17
  180.6 6.0 %collective-permute-start.7 = (f32[4,1,128]{2,1,0:T(1,128)}, f32[4,1,128]{2,1,0:T(1,128)S(1)}, u32[]{:S(2)}, u32[]{:S(2)}) collective-permute-start(f32[4,1,128]{2,1,0:T(1,128)} %get-tuple-element.709), channel_id=1, source_target_pairs={{0,1},{1,2},{2,3},{3,4},{4,5},{5,6},{6,7},{7,8},{8,9},{9,10},{10,1... | collective-permute-start | bytes 6152 | tf_op jit(solution)/shard_map/ppermute | solution.py:15
  205.0 11.7 %collective-permute-start.8 = (f32[1,64,128]{2,1,0:T(8,128)S(1)}, f32[1,64,128]{2,1,0:T(8,128)S(1)}, u32[]{:S(2)}, u32[]{:S(2)}) collective-permute-start(f32[1,64,128]{2,1,0:T(8,128)S(1)} %get-tuple-element.702), channel_id=1, source_target_pairs={{16,0},{32,16},{48,32},{64,48},{80,64},{96,80},{112,96},{128,112},... | collective-permute-start | bytes 98312 | tf_op jit(solution)/shard_map/ppermute | solution.py:17
  207.1 9.6 %collective-permute-start.9 = (f32[1,64,128]{2,1,0:T(8,128)S(1)}, f32[1,64,128]{2,1,0:T(8,128)S(1)}, u32[]{:S(2)}, u32[]{:S(2)}) collective-permute-start(f32[1,64,128]{2,1,0:T(8,128)S(1)} %get-tuple-element.703), channel_id=1, source_target_pairs={{0,16},{16,32},{32,48},{48,64},{64,80},{80,96},{96,112},{112,128},... | collective-permute-start | bytes 98312 | tf_op jit(solution)/shard_map/ppermute | solution.py:15
  210.6 2.5 collective-permute-start.10
  210.7 6.0 %collective-permute-start.11 = (f32[4,1,128]{2,1,0:T(1,128)S(1)}, f32[4,1,128]{2,1,0:T(1,128)S(1)}, u32[]{:S(2)}, u32[]{:S(2)}) collective-permute-start(f32[4,1,128]{2,1,0:T(1,128)S(1)} %get-tuple-element.705), channel_id=1, source_target_pairs={{0,1},{1,2},{2,3},{3,4},{4,5},{5,6},{6,7},{7,8},{8,9},{9,10},{10,1... | collective-permute-start | bytes 6152 | tf_op jit(solution)/shard_map/ppermute | solution.py:15
  218.2 28.8 %collective-permute-start.16 = (f32[4,8]{1,0:T(4,128)S(1)}, f32[4,8]{1,0:T(4,128)S(1)}, u32[]{:S(2)}, u32[]{:S(2)}) collective-permute-start(f32[4,8]{1,0:T(4,128)S(1)} %get-tuple-element.724), channel_id=1, source_target_pairs={{0,1},{1,2},{2,3},{3,4},{4,5},{5,6},{6,7},{7,8},{8,9},{9,10},{10,1... | collective-permute-start | bytes 392 | tf_op jit(solution)/shard_map/ppermute | solution.py:15
  218.2 30.2 %collective-permute-start.17 = (f32[4,8]{1,0:T(4,128)S(1)}, f32[4,8]{1,0:T(4,128)S(1)}, u32[]{:S(2)}, u32[]{:S(2)}) collective-permute-start(f32[4,8]{1,0:T(4,128)S(1)} %get-tuple-element.725), channel_id=1, source_target_pairs={{1,0},{2,1},{3,2},{4,3},{5,4},{6,5},{7,6},{8,7},{9,8},{10,9},{11,1... | collective-permute-start | bytes 392 | tf_op jit(solution)/shard_map/ppermute | solution.py:17
  241.3 18.5 %collective-permute-start.12 = (f32[1,64,128]{2,1,0:T(8,128)S(1)}, f32[1,64,128]{2,1,0:T(8,128)S(1)}, u32[]{:S(2)}, u32[]{:S(2)}) collective-permute-start(f32[1,64,128]{2,1,0:T(8,128)S(1)} %get-tuple-element.698), channel_id=1, source_target_pairs={{16,0},{32,16},{48,32},{64,48},{80,64},{96,80},{112,96},{128,112},... | collective-permute-start | bytes 98312 | tf_op jit(solution)/shard_map/ppermute | solution.py:17
  243.4 16.4 %collective-permute-start.13 = (f32[1,64,128]{2,1,0:T(8,128)S(1)}, f32[1,64,128]{2,1,0:T(8,128)S(1)}, u32[]{:S(2)}, u32[]{:S(2)}) collective-permute-start(f32[1,64,128]{2,1,0:T(8,128)S(1)} %get-tuple-element.699), channel_id=1, source_target_pairs={{0,16},{16,32},{32,48},{48,64},{64,80},{80,96},{96,112},{112,128},... | collective-permute-start | bytes 98312 | tf_op jit(solution)/shard_map/ppermute | solution.py:15
  246.9 12.9 %collective-permute-start.14 = (f32[4,1,128]{2,1,0:T(1,128)S(1)}, f32[4,1,128]{2,1,0:T(1,128)S(1)}, u32[]{:S(2)}, u32[]{:S(2)}) collective-permute-start(f32[4,1,128]{2,1,0:T(1,128)S(1)} %get-tuple-element.700), channel_id=1, source_target_pairs={{1,0},{2,1},{3,2},{4,3},{5,4},{6,5},{7,6},{8,7},{9,8},{10,9},{11,1... | collective-permute-start | bytes 6152 | tf_op jit(solution)/shard_map/ppermute | solution.py:17
  247.0 12.8 %collective-permute-start.15 = (f32[4,1,128]{2,1,0:T(1,128)S(1)}, f32[4,1,128]{2,1,0:T(1,128)S(1)}, u32[]{:S(2)}, u32[]{:S(2)}) collective-permute-start(f32[4,1,128]{2,1,0:T(1,128)S(1)} %get-tuple-element.701), channel_id=1, source_target_pairs={{0,1},{1,2},{2,3},{3,4},{4,5},{5,6},{6,7},{7,8},{8,9},{9,10},{10,1... | collective-permute-start | bytes 6152 | tf_op jit(solution)/shard_map/ppermute | solution.py:15
  (16 other events, 503.3 us)
where the time goes:
time: 280 us; the launch traced here: 279 us
  blocking collectives  91 us (32%)
  waiting for transfers between devices  75.6 us (27%)
  starting transfers between devices  64.6 us (23%)
  other arithmetic  29.3 us (10%)
  local copies, waits for them, and re-layouts  14.6 us (5%)
    all_gather x5, blocking collectives, carried_in(): everything = jax.tree.map(lambda part: lax.all_gather(part, axis), shard)  91 us
    all_to_all x4, waiting for transfers between devices, local(): lax.all_to_all(stored[step, 0, 0], 'axial', split_axis=0, concat_axis=0,...  66.1 us
    all_to_all x4, starting transfers between devices, local(): lax.all_to_all(stored[step, 0, 0], 'axial', split_axis=0, concat_axis=0,...  24.6 us
    ppermute x9, starting transfers between devices, padded_2(): lax.ppermute(head, axis, [((i + 1) % count, i) for i in range(ends)])  22.9 us
    ppermute x9, starting transfers between devices, padded_2(): lax.ppermute(tail, axis, [(i, (i + 1) % count) for i in range(ends)])  17.1 us
    add x1, other arithmetic, local(): heater_grad + kernel[offset] * padded[:, offset:offset + azimuths]  11.3 us
    ppermute x9, waiting for transfers between devices, padded_2(): lax.ppermute(tail, axis, [(i, (i + 1) % count) for i in range(ends)])  8.63 us
  transfers between devices with their start and end apart: 22, of which 7 were waited for; matrix products, arithmetic and copies ran while one was open for 12% of the time, Pallas kernels for 0%

commit v1 on v0

v1 whole, which is shorter than its diff:
```python
import functools

import jax
import jax.numpy as jnp
from jax import lax
from jax.experimental import pallas as pl
from jax.experimental.pallas import tpu as pltpu
from jax.sharding import PartitionSpec as P

ROWS = 16
LANES = 128
RATE_MID = 3.7
RATE_SCALE = 10500.0
COEF_SCALE = 1374.0
COEF_BASE = 23.0
VMEM_LIMIT = 48 * 1024 * 1024


def encode_body(stored_ref, out_ref, mixed):
    slots = stored_ref.shape[1]
    cap = out_ref.shape[2]
    for slot in range(slots):
        for row in range(ROWS):
            mixed[slot, 8 * row : 8 * row + 8, :] = stored_ref[
                0, slot, :, LANES * row : LANES * (row + 1)
            ].astype(jnp.float32)
    for slot in range(slots):

        def part(index):
            return mixed[slot, pl.ds(index, ROWS, stride=8), :]

        squares = part(1) * part(1)
        for index in range(2, 7):
            squares = squares + part(index) * part(index)
        slope = jnp.tanh(part(0))
        rate = jnp.sqrt(1.0 + squares / 6.0) * jnp.exp(0.5 * slope)
        coef = 0.1 * part(7) * rate * (1.0 - slope * slope)
        size = jnp.log2(jnp.maximum(jnp.abs(coef), 2.0 ** -(COEF_BASE + 1.0)))
        size = jnp.maximum(jnp.round((size + COEF_BASE) * COEF_SCALE), 0.0)
        coef_code = jnp.where(coef < 0.0, -size, size)
        rate_code = jnp.round((rate - RATE_MID) * RATE_SCALE)
        out_ref[slot // cap, 0, slot % cap, 0] = rate_code.astype(jnp.int32).astype(jnp.int16)
        out_ref[slot // cap, 0, slot % cap, 1] = coef_code.astype(jnp.int32).astype(jnp.int16)


def encode(stored, first, count):
    steps, _, _, owners, cap, comps, cells = stored.shape
    flat = stored.reshape(steps, owners * cap, comps, cells)
    chunk = 4
    return pl.pallas_call(
        encode_body,
        grid=(count, owners // chunk),
        in_specs=[
            pl.BlockSpec((1, chunk * cap, comps, cells), lambda k, c: (first - k, c, 0, 0))
        ],
        out_specs=pl.BlockSpec(
            (chunk, 1, cap, 2, ROWS, LANES), lambda k, c: (c, k, 0, 0, 0, 0)
        ),
        out_shape=jax.ShapeDtypeStruct((owners, count, cap, 2, ROWS, LANES), jnp.int16),
        scratch_shapes=[pltpu.VMEM((chunk * cap, 8 * ROWS, LANES), jnp.float32)],
        compiler_params=pltpu.CompilerParams(vmem_limit_bytes=VMEM_LIMIT),
    )(flat)


def decoded(info_ref, rec_ref, step, place, layer, field):
    pieces = []
    for quarter in range(4):
        held = info_ref[16 * step + 4 * layer + quarter]
        code = rec_ref[held // 2, place, held % 2, field].astype(jnp.int32).astype(jnp.float32)
        if field == 0:
            pieces.append(code * (1.0 / RATE_SCALE) + RATE_MID)
        else:
            size = jnp.exp2(jnp.abs(code) * (1.0 / COEF_SCALE) - COEF_BASE)
            pieces.append(jnp.where(code > 0.0, size, jnp.where(code < 0.0, -size, 0.0)))
    return jnp.concatenate(pieces, axis=0)


def laplace(field, low, high, left, right):
    layers = len(field)
    azimuths, radials = field[0].shape
    row = lax.broadcasted_iota(jnp.int32, (azimuths, radials), 0)
    lane = lax.broadcasted_iota(jnp.int32, (azimuths, radials), 1)
    out = []
    for layer in range(layers):
        x = field[layer]
        below = low if layer == 0 else field[layer - 1]
        above = high if layer == layers - 1 else field[layer + 1]
        before = jnp.where(row == 0, left[layer : layer + 1, :], pltpu.roll(x, 1, axis=0))
        after = jnp.where(
            row == azimuths - 1, right[layer : layer + 1, :], pltpu.roll(x, azimuths - 1, axis=0)
        )
        inner = jnp.where(lane == 0, 0.0, pltpu.roll(x, 1, axis=1))
        outer = jnp.where(lane == radials - 1, 0.0, pltpu.roll(x, radials - 1, axis=1))
        out.append(((below + above) + (before + after)) + (inner + outer) - 6.0 * x)
    return out


def chain(field, decay, carry):
    layers = len(field)
    out = [None] * layers
    for layer in reversed(range(layers)):
        out[layer] = carry
        carry = decay * carry + (1.0 - decay) * field[layer]
    return out, carry


def put_edges(field, low_ref, high_ref, left_ref, right_ref):
    layers = len(field)
    azimuths = field[0].shape[0]
    low_ref[...] = field[0]
    high_ref[...] = field[-1]
    for layer in range(layers):
        left_ref[layer : layer + 1, :] = field[layer][0:1, :]
        right_ref[layer : layer + 1, :] = field[layer][azimuths - 1 : azimuths, :]


def summary_body(lr_ref, length_ref, out_ref):
    decay = jnp.exp(-1.0 / length_ref[...])
    field = [lr_ref[layer] for layer in range(lr_ref.shape[0])]
    _, out_ref[...] = chain(field, decay, jnp.zeros_like(decay))


def first_body(
    info_ref, rec_ref, lt_ref, lr_ref, low_ref, high_ref, left_ref, right_ref, length_ref,
    sums_ref, new_lt_ref, new_lr_ref, out_ref, low_out, high_out, left_out, right_out,
):
    layers = lt_ref.shape[0]
    me = info_ref[64]
    peers = sums_ref.shape[0]
    decay = jnp.exp(-1.0 / length_ref[...])
    power = decay * decay
    power = power * power
    carry = lax.fori_loop(
        0,
        peers - 1 - me,
        lambda k, value: power * value + sums_ref[peers - 1 - k],
        jnp.zeros_like(decay),
    )
    lt = [lt_ref[layer] for layer in range(layers)]
    lr = [lr_ref[layer] for layer in range(layers)]
    spread = laplace(lt, low_ref[...], high_ref[...], left_ref[...], right_ref[...])
    new_lt = [
        lt[l] + 0.15 * spread[l] + decoded(info_ref, rec_ref, 3, 0, l, 1) * lr[l]
        for l in range(layers)
    ]
    put_edges(new_lt, low_out, high_out, left_out, right_out)
    climbs, _ = chain(lr, decay, carry)
    new_lr = [
        -0.3 * lt[l] + (1.0 + 0.2 * decoded(info_ref, rec_ref, 3, 0, l, 0)) * lr[l] + climbs[l]
        for l in range(layers)
    ]
    climbs, total = chain(new_lr, decay, jnp.zeros_like(decay))
    out_ref[0] = total
    later = [
        -0.3 * new_lt[l]
        + (1.0 + 0.2 * decoded(info_ref, rec_ref, 2, 1, l, 0)) * new_lr[l]
        + climbs[l]
        for l in range(layers)
    ]
    _, out_ref[1] = chain(later, decay, jnp.zeros_like(decay))
    for l in range(layers):
        new_lt_ref[l] = new_lt[l]
        new_lr_ref[l] = new_lr[l]


def second_body(
    info_ref, rec_ref, next_ref, lt_ref, lr_ref, low_ref, high_ref, left_ref, right_ref,
    length_ref, sums_ref, new_lt_ref, mid_lr_ref, new_lr_ref, out_ref, low_out, high_out,
    left_out, right_out,
):
    layers = lt_ref.shape[0]
    me = info_ref[64]
    peers = sums_ref.shape[0]
    decay = jnp.exp(-1.0 / length_ref[...])
    power = decay * decay
    cross = 4.0 * (1.0 - decay) * power * decay
    power = power * power

    def climb(k, values):
        one, two = values
        at = peers - 1 - k
        return (
            power * one + sums_ref[at, 0],
            power * two + (sums_ref[at, 1] + cross * one),
        )

    zero = jnp.zeros_like(decay)
    one, two = lax.fori_loop(0, peers - 1 - me, climb, (zero, zero))
    lt = [lt_ref[layer] for layer in range(layers)]
    lr = [lr_ref[layer] for layer in range(layers)]
    spread = laplace(lt, low_ref[...], high_ref[...], left_ref[...], right_ref[...])
    new_lt = [
        lt[l] + 0.15 * spread[l] + decoded(info_ref, rec_ref, 2, 1, l, 1) * lr[l]
        for l in range(layers)
    ]
    put_edges(new_lt, low_out, high_out, left_out, right_out)
    climbs, _ = chain(lr, decay, one)
    mid_lr = [
        -0.3 * lt[l] + (1.0 + 0.2 * decoded(info_ref, rec_ref, 2, 1, l, 0)) * lr[l] + climbs[l]
        for l in range(layers)
    ]
    climbs, _ = chain(mid_lr, decay, two)
    new_lr = [
        -0.3 * new_lt[l]
        + (1.0 + 0.2 * decoded(info_ref, next_ref, 1, 0, l, 0)) * mid_lr[l]
        + climbs[l]
        for l in range(layers)
    ]
    _, total = chain(new_lr, decay, zero)
    for peer in range(peers):
        out_ref[peer] = total
    for l in range(layers):
        new_lt_ref[l] = new_lt[l]
        mid_lr_ref[l] = mid_lr[l]
        new_lr_ref[l] = new_lr[l]


def third_body(
    info_ref, next_ref, lt_ref, lr_ref, low_ref, high_ref, left_ref, right_ref, old_ref,
    older_ref, face_ref, new_lt_ref, flux_ref, low_out, high_out, left_out, right_out,
):
    layers = lt_ref.shape[0]
    lt = [lt_ref[layer] for layer in range(layers)]
    spread = laplace(lt, low_ref[...], high_ref[...], left_ref[...], right_ref[...])
    new_lt = [
        lt[l] + 0.15 * spread[l] + decoded(info_ref, next_ref, 1, 0, l, 1) * lr_ref[l]
        for l in range(layers)
    ]
    put_edges(new_lt, low_out, high_out, left_out, right_out)
    for l in range(layers):
        new_lt_ref[l] = new_lt[l]
    lane = lax.broadcasted_iota(jnp.int32, lt[0].shape, 1)
    for l in range(layers):
        total = (older_ref[l] + old_ref[l]) + (lt[l] + new_lt[l])
        kept = jnp.where(lane == face_ref[l], total, 0.0)
        flux_ref[l] = jnp.sum(kept, axis=1, keepdims=True)


def last_body(
    info_ref, next_ref, lt_ref, lr_ref, low_ref, high_ref, left_ref, right_ref, length_ref,
    sums_ref, new_lt_ref, new_lr_ref,
):
    layers = lt_ref.shape[0]
    me = info_ref[64]
    peers = sums_ref.shape[0]
    decay = jnp.exp(-1.0 / length_ref[...])
    power = decay * decay
    power = power * power
    carry = lax.fori_loop(
        0,
        peers - 1 - me,
        lambda k, value: power * value + sums_ref[peers - 1 - k],
        jnp.zeros_like(decay),
    )
    lt = [lt_ref[layer] for layer in range(layers)]
    lr = [lr_ref[layer] for layer in range(layers)]
    spread = laplace(lt, low_ref[...], high_ref[...], left_ref[...], right_ref[...])
    climbs, _ = chain(lr, decay, carry)
    for l in range(layers):
        new_lt_ref[l] = (
            lt[l] + 0.15 * spread[l] + decoded(info_ref, next_ref, 0, 1, l, 1) * lr[l]
        )
        new_lr_ref[l] = (
            -0.3 * lt[l]
            + (1.0 + 0.2 * decoded(info_ref, next_ref, 0, 1, l, 0)) * lr[l]
            + climbs[l]
        )


def run(body, info, args, shapes):
    smem = pl.BlockSpec(memory_space=pltpu.SMEM)
    vmem = pl.BlockSpec(memory_space=pltpu.VMEM)
    return pl.pallas_call(
        body,
        in_specs=([smem] if info is not None else []) + [vmem] * len(args),
        out_specs=[vmem] * len(shapes),
        out_shape=[jax.ShapeDtypeStruct(shape, jnp.float32) for shape in shapes],
        compiler_params=pltpu.CompilerParams(vmem_limit_bytes=VMEM_LIMIT),
    )(*(() if info is None else (info,)), *args)


def exchanged(low, high, left, right):
    axial, azim = lax.axis_size("axial"), lax.axis_size("azim")
    up = [(i, i + 1) for i in range(axial - 1)]
    down = [(i + 1, i) for i in range(axial - 1)]
    ahead = [(i, (i + 1) % azim) for i in range(azim)]
    back = [((i + 1) % azim, i) for i in range(azim)]
    return (
        lax.ppermute(high, "axial", up),
        lax.ppermute(low, "axial", down),
        lax.ppermute(right, "azim", ahead),
        lax.ppermute(left, "azim", back),
    )


def local(stored, holder, seed_temp, seed_disloc, decay_length, face_radius, kernel):
    layers, azimuths, radials = seed_temp.shape
    peers = stored.shape[3]
    me = lax.axis_index("axial")
    wanted = lax.dynamic_index_in_dim(holder, me, 1, keepdims=False).reshape(-1)
    info = jnp.concatenate([wanted, jnp.full((16,), me, jnp.int32)])
    plane = (azimuths, radials)
    side = (layers, radials)
    block = (layers, azimuths, radials)
    edges = [plane, plane, side, side]

    early = encode(stored, 3, 2)
    early = lax.all_to_all(early, "axial", 0, 0, tiled=True)
    late = encode(stored, 1, 2)

    (total,) = run(summary_body, None, (seed_disloc, decay_length), [plane])
    sums = lax.all_gather(total, "axial")
    halo = exchanged(
        seed_temp[0], seed_temp[layers - 1], seed_temp[:, 0], seed_temp[:, azimuths - 1]
    )
    lt1, lr1, pair, *rim = run(
        first_body,
        info,
        (early, seed_temp, seed_disloc, *halo, decay_length, sums),
        [block, block, (2, *plane), *edges],
    )
    late, pair, rim = lax.optimization_barrier((late, pair, rim))
    late = lax.all_to_all(late, "axial", 0, 0, tiled=True)
    halo = exchanged(*rim)
    sums = lax.all_gather(pair, "axial")
    lt2, lr2, lr3, spread, *rim = run(
        second_body,
        info,
        (early, late, lt1, lr1, *halo, decay_length, sums),
        [block, block, block, (peers, *plane), *edges],
    )
    halo = exchanged(*rim)
    sums = lax.all_to_all(spread, "axial", 0, 0, tiled=True)
    lt3, flux, *rim = run(
        third_body,
        info,
        (late, lt2, lr2, *halo, lt1, seed_temp, face_radius[:, :, None]),
        [block, (layers, azimuths, 1), *edges],
    )
    halo = exchanged(*rim)
    flux = flux[:, :, 0]
    band = (kernel.shape[0] - 1) // 2
    azim = lax.axis_size("azim")
    before = lax.ppermute(
        flux[:, azimuths - band :], "azim", [(i, (i + 1) % azim) for i in range(azim)]
    )
    after = lax.ppermute(
        flux[:, :band], "azim", [((i + 1) % azim, i) for i in range(azim)]
    )
    adj_temp, adj_disloc = run(
        last_body, info, (late, lt3, lr3, *halo, decay_length, sums), [block, block]
    )
    padded = jnp.concatenate([before, flux, after], axis=1)
    heater_grad = jnp.zeros_like(flux)
    for offset in range(2 * band + 1):
        heater_grad = heater_grad + kernel[offset] * padded[:, offset : offset + azimuths]
    return (adj_temp, adj_disloc, heater_grad)


def solution(mesh):
    in_specs = (
        P(None, "axial", "azim", None, None, None, None),
        P(),
        P("axial", "azim", None),
        P("axial", "azim", None),
        P("azim", None),
        P("axial", "azim"),
        P(),
    )
    out_specs = (P("axial", "azim", None), P("axial", "azim", None), P("axial", "azim"))
    return jax.shard_map(local, mesh=mesh, in_specs=in_specs, out_specs=out_specs, check_vma=False)
```

time: 280 us -> 157 us (0.56)
  blocking collectives: 91 us -> 19.1 us
  waiting for transfers between devices: 75.6 us -> 25.9 us
  other arithmetic: 29.3 us -> 11.4 us
  between operations: 1.26 us -> 14.2 us
  Pallas kernels: 0 us -> 12.8 us
  local copies, waits for them, and re-layouts: 14.6 us -> 6.65 us
    all_gather x5 -> x1, blocking collectives: 91 us -> 19.1 us  [local(): sums = lax.all_gather(total, 'axial')]
    all_to_all x4 -> x3, waiting for transfers between devices: 66.1 us -> 2.78 us  [the longest x1 2.78 us: local(): late = lax.all_to_all(late, 'axial', 0, 0, tiled=True)]
    all_gather x0 -> x1, waiting for transfers between devices: none -> 13.4 us  [local(): sums = lax.all_gather(pair, 'axial')]
    pallas_call x0 -> x7, Pallas kernels: none -> 12.8 us  [the longest x2 6.75 us: encode(): pl.pallas_call(encode_body, grid=(count, owners // chunk), in_specs=[pl.B...]
    gather x4 -> x0, local copies, waits for them, and re-layouts: 5.56 us -> none  [local(): pieces = jnp.take(flat, wanted, axis=0)]
    unnamed x36 -> x18, local copies, waits for them, and re-layouts: 0.08 us -> 5.63 us
    ppermute x18, starting transfers between devices: 40 us -> 45.1 us  [the longest x4 17.6 us: exchanged(): lax.ppermute(left, 'azim', back)]
    squeeze x1, local copies, waits for them, and re-layouts: 4.52 us -> 0.01 us  [local(): seed_temp[0]]
  transfers between devices with their start and end apart: 22 -> 22, of which waited for: 7 -> 7; matrix products, arithmetic and copies ran while one was open for 12% -> 8% of each run, Pallas kernels for 0% -> 3%
where the time goes in v1:
time: 157 us; the launch traced here: 156 us
  starting transfers between devices  65.7 us (42%)
  waiting for transfers between devices  25.9 us (16%)
  blocking collectives  19.1 us (12%)
  between operations  14.2 us (9%)
  Pallas kernels  12.8 us (8%)
  other arithmetic  11.4 us (7%)
  local copies, waits for them, and re-layouts  6.65 us (4%)
    all_gather x1, blocking collectives, local(): sums = lax.all_gather(total, 'axial')  19.1 us
    ppermute x4, starting transfers between devices, exchanged(): lax.ppermute(left, 'azim', back)  17.6 us
    all_gather x1, waiting for transfers between devices, local(): sums = lax.all_gather(pair, 'axial')  13.4 us
    ppermute x4, starting transfers between devices, exchanged(): lax.ppermute(high, 'axial', up)  12.9 us
    add x1, other arithmetic, local(): heater_grad + kernel[offset] * padded[:, offset:offset + azimuths]  11.3 us
    all_to_all x1, starting transfers between devices, local(): early = lax.all_to_all(early, 'axial', 0, 0, tiled=True)  9.98 us
    ppermute x4, starting transfers between devices, exchanged(): lax.ppermute(low, 'axial', down)  7.8 us
    ppermute x4, waiting for transfers between devices, exchanged(): lax.ppermute(low, 'axial', down)  7.12 us
  transfers between devices with their start and end apart: 22, of which 7 were waited for; matrix products, arithmetic and copies ran while one was open for 8% of the time, Pallas kernels for 3%

profile of v1, /device:TPU:1, one launch (start us, length us, event | category | flops | bytes accessed | tf_op | source)
XLA Modules:
  0.0 155.8 jit_solution(14343278972164314553)
XLA Ops:
  7.2 2.2 %copy-done.1 = bf16[4,1,1,16,2,8,2048]{6,5,4,3,2,1,0:T(8,128)(2,1)S(1)} copy-done((bf16[4,1,1,16,2,8,2048]{6,5,4,3,2,1,0:T(8,128)(2,1)S(1)}, bf16[4,1,1,16,2,8,2048]{6,5,4,3,2,1,0:T(8,128)(2,1)}, u32[]{:S(2)}) %copy-start.1) | copy-done | bytes 4194328
  9.4 3.4 %shard_map.95 = s16[16,2,2,2,16,128]{5,4,3,2,1,0:T(8,128)(2,1)} custom-call(bf16[4,32,8,2048]{3,2,1,0:T(8,128)(2,1)S(1)} %bitcast.31), custom_call_target="tpu_custom_call" | custom-call | tf_op jit(solution)/shard_map/pallas_call | solution.py:50
  12.8 10.0 %all-to-all-start = ((s16[16,2,2,2,16,128]{5,4,3,2,1,0:T(8,128)(2,1)}), s16[16,2,2,2,16,128]{5,4,3,2,1,0:T(8,128)(2,1)S(1)}, u32[]{:S(2)}, u32[]{:S(2)}) async-start(s16[16,2,2,2,16,128]{5,4,3,2,1,0:T(8,128)(2,1)} %shard_map.95), calls=%async_computation | async-start | bytes 1048576 | tf_op jit(solution)/shard_map/all_to_all | solution.py:308
  22.8 3.5 %collective-permute-start = (f32[64,128]{1,0:T(8,128)S(1)}, f32[64,128]{1,0:T(8,128)S(1)}, u32[]{:S(2)}, u32[]{:S(2)}) collective-permute-start(f32[64,128]{1,0:T(8,128)S(1)} %get-tuple-element.64), channel_id=1, source_target_pairs={{0,16},{16,32},{32,48},{48,64},{64,80},{80,96},{96,112},{112,128},... | collective-permute-start | bytes 98312 | tf_op jit(solution)/shard_map/ppermute | solution.py:289
  26.4 1.9 %collective-permute-start.1 = (f32[64,128]{1,0:T(8,128)S(1)}, f32[64,128]{1,0:T(8,128)S(1)}, u32[]{:S(2)}, u32[]{:S(2)}) collective-permute-start(f32[64,128]{1,0:T(8,128)S(1)} %get-tuple-element.63), channel_id=1, source_target_pairs={{16,0},{32,16},{48,32},{64,48},{80,64},{96,80},{112,96},{128,112},... | collective-permute-start | bytes 98312 | tf_op jit(solution)/shard_map/ppermute | solution.py:290
  29.6 3.8 %collective-permute-start.3 = (f32[4,128]{1,0:T(4,128)S(1)}, f32[4,128]{1,0:T(4,128)S(1)}, u32[]{:S(2)}, u32[]{:S(2)}) collective-permute-start(f32[4,128]{1,0:T(4,128)S(1)} %bitcast.36), channel_id=1, source_target_pairs={{1,0},{2,1},{3,2},{4,3},{5,4},{6,5},{7,6},{8,7},{9,8},{10,9},{11,1... | collective-permute-start | bytes 6152 | tf_op jit(solution)/shard_map/ppermute | solution.py:292
  33.5 19.1 %all-gather = f32[1024,128]{1,0:T(8,128)S(1)} all-gather(f32[64,128]{1,0:T(8,128)S(1)} %shard_map.96), channel_id=2, replica_groups=mesh['axial'=16,'azim'=16] {'axial'}, dimensions={0}, use_global_device_ids=true | all-gather | bytes 557056 | tf_op jit(solution)/shard_map/all_gather | solution.py:312
  52.5 2.2 %copy-done.2 = bf16[4,1,1,16,2,8,2048]{6,5,4,3,2,1,0:T(8,128)(2,1)S(1)} copy-done((bf16[4,1,1,16,2,8,2048]{6,5,4,3,2,1,0:T(8,128)(2,1)S(1)}, bf16[4,1,1,16,2,8,2048]{6,5,4,3,2,1,0:T(8,128)(2,1)}, u32[]{:S(2)}) %copy-start.2) | copy-done | bytes 4194328
  54.7 3.4 %shard_map.94 = s16[16,2,2,2,16,128]{5,4,3,2,1,0:T(8,128)(2,1)} custom-call(bf16[4,32,8,2048]{3,2,1,0:T(8,128)(2,1)S(1)} %bitcast.32), custom_call_target="tpu_custom_call" | custom-call | tf_op jit(solution)/shard_map/pallas_call | solution.py:50
  59.8 5.9 %all-to-all-start.1 = ((s16[16,2,2,2,16,128]{5,4,3,2,1,0:T(8,128)(2,1)}), s16[16,2,2,2,16,128]{5,4,3,2,1,0:T(8,128)(2,1)S(1)}, u32[]{:S(2)}, u32[]{:S(2)}) async-start(s16[16,2,2,2,16,128]{5,4,3,2,1,0:T(8,128)(2,1)} %shard_map.94), calls=%async_computation.1 | async-start | bytes 1048576 | tf_op jit(solution)/shard_map/all_to_all | solution.py:323
  65.7 3.5 %collective-permute-start.4 = (f32[64,128]{1,0:T(8,128)S(1)}, f32[64,128]{1,0:T(8,128)S(1)}, u32[]{:S(2)}, u32[]{:S(2)}) collective-permute-start(f32[64,128]{1,0:T(8,128)S(1)} %get-tuple-element.40), channel_id=1, source_target_pairs={{0,16},{16,32},{32,48},{48,64},{64,80},{80,96},{96,112},{112,128},... | collective-permute-start | bytes 98312 | tf_op jit(solution)/shard_map/ppermute | solution.py:289
  71.3 4.8 %collective-permute-start.7 = (f32[4,128]{1,0:T(4,128)S(1)}, f32[4,128]{1,0:T(4,128)S(1)}, u32[]{:S(2)}, u32[]{:S(2)}) collective-permute-start(f32[4,128]{1,0:T(4,128)S(1)} %get-tuple-element.43), channel_id=1, source_target_pairs={{1,0},{2,1},{3,2},{4,3},{5,4},{6,5},{7,6},{8,7},{9,8},{10,9},{11,1... | collective-permute-start | bytes 6152 | tf_op jit(solution)/shard_map/ppermute | solution.py:292
  78.1 4.3 %collective-permute-done.5.high_ref = f32[64,128]{1,0:T(8,128)S(1)} collective-permute-done((f32[64,128]{1,0:T(8,128)S(1)}, f32[64,128]{1,0:T(8,128)S(1)}, u32[]{:S(2)}, u32[]{:S(2)}) %collective-permute-start.5) | collective-permute-done | bytes 32800 | tf_op jit(solution)/shard_map/ppermute | solution.py:290
  82.4 2.8 %all-to-all-done.1.next_ref = s16[16,2,2,2,16,128]{5,4,3,2,1,0:T(8,128)(2,1)S(1)} async-done(((s16[16,2,2,2,16,128]{5,4,3,2,1,0:T(8,128)(2,1)}), s16[16,2,2,2,16,128]{5,4,3,2,1,0:T(8,128)(2,1)S(1)}, u32[]{:S(2)}, u32[]{:S(2)}) %all-to-all-start.1) | async-done | bytes 524320 | tf_op jit(solution)/shard_map/all_to_all | solution.py:323
  85.1 13.4 %all-gather.4.cloned.1.call-done = f32[32,64,128]{2,1,0:T(8,128)} async-done(((f32[2,64,128]{2,1,0:T(8,128)}), f32[32,64,128]{2,1,0:T(8,128)}) %all-gather.4.cloned.1.call-update) | async-done | bytes 1048592 | tf_op jit(solution)/shard_map/all_gather | solution.py:325
  101.6 4.7 %all-to-all-start.2 = ((f32[16,64,128]{2,1,0:T(8,128)}), f32[16,64,128]{2,1,0:T(8,128)S(1)}, u32[]{:S(2)}, u32[]{:S(2)}) async-start(f32[16,64,128]{2,1,0:T(8,128)} %get-tuple-element.57), calls=%async_computation.2 | async-start | bytes 1048576 | tf_op jit(solution)/shard_map/all_to_all | solution.py:333
  106.3 3.5 %collective-permute-start.8 = (f32[64,128]{1,0:T(8,128)S(1)}, f32[64,128]{1,0:T(8,128)S(1)}, u32[]{:S(2)}, u32[]{:S(2)}) collective-permute-start(f32[64,128]{1,0:T(8,128)S(1)} %get-tuple-element.47), channel_id=1, source_target_pairs={{0,16},{16,32},{32,48},{48,64},{64,80},{80,96},{96,112},{112,128},... | collective-permute-start | bytes 98312 | tf_op jit(solution)/shard_map/ppermute | solution.py:289
  112.4 4.2 %collective-permute-start.11 = (f32[4,128]{1,0:T(4,128)S(1)}, f32[4,128]{1,0:T(4,128)S(1)}, u32[]{:S(2)}, u32[]{:S(2)}) collective-permute-start(f32[4,128]{1,0:T(4,128)S(1)} %get-tuple-element.50), channel_id=1, source_target_pairs={{1,0},{2,1},{3,2},{4,3},{5,4},{6,5},{7,6},{8,7},{9,8},{10,9},{11,1... | collective-permute-start | bytes 6152 | tf_op jit(solution)/shard_map/ppermute | solution.py:292
  117.9 2.9 %collective-permute-done.9.high_ref = f32[64,128]{1,0:T(8,128)S(1)} collective-permute-done((f32[64,128]{1,0:T(8,128)S(1)}, f32[64,128]{1,0:T(8,128)S(1)}, u32[]{:S(2)}, u32[]{:S(2)}) %collective-permute-start.9) | collective-permute-done | bytes 32800 | tf_op jit(solution)/shard_map/ppermute | solution.py:290
  122.6 4.2 %collective-permute-start.17 = (f32[4,8]{1,0:T(4,128)S(1)}, f32[4,8]{1,0:T(4,128)S(1)}, u32[]{:S(2)}, u32[]{:S(2)}) collective-permute-start(f32[4,8]{1,0:T(4,128)S(1)} %get-tuple-element.68), channel_id=1, source_target_pairs={{1,0},{2,1},{3,2},{4,3},{5,4},{6,5},{7,6},{8,7},{9,8},{10,9},{11,1... | collective-permute-start | bytes 392 | tf_op jit(solution)/shard_map/ppermute | solution.py:347
  126.8 2.3 %collective-permute-start.12 = (f32[64,128]{1,0:T(8,128)S(1)}, f32[64,128]{1,0:T(8,128)S(1)}, u32[]{:S(2)}, u32[]{:S(2)}) collective-permute-start(f32[64,128]{1,0:T(8,128)S(1)} %get-tuple-element.53), channel_id=1, source_target_pairs={{0,16},{16,32},{32,48},{48,64},{64,80},{80,96},{96,112},{112,128},... | collective-permute-start | bytes 98312 | tf_op jit(solution)/shard_map/ppermute | solution.py:289
  129.1 2.0 %collective-permute-start.13 = (f32[64,128]{1,0:T(8,128)S(1)}, f32[64,128]{1,0:T(8,128)S(1)}, u32[]{:S(2)}, u32[]{:S(2)}) collective-permute-start(f32[64,128]{1,0:T(8,128)S(1)} %get-tuple-element.54), channel_id=1, source_target_pairs={{16,0},{32,16},{48,32},{64,48},{80,64},{96,80},{112,96},{128,112},... | collective-permute-start | bytes 98312 | tf_op jit(solution)/shard_map/ppermute | solution.py:290
  131.3 4.8 %collective-permute-start.15 = (f32[4,128]{1,0:T(4,128)S(1)}, f32[4,128]{1,0:T(4,128)S(1)}, u32[]{:S(2)}, u32[]{:S(2)}) collective-permute-start(f32[4,128]{1,0:T(4,128)S(1)} %get-tuple-element.56), channel_id=1, source_target_pairs={{1,0},{2,1},{3,2},{4,3},{5,4},{6,5},{7,6},{8,7},{9,8},{10,9},{11,1... | collective-permute-start | bytes 6152 | tf_op jit(solution)/shard_map/ppermute | solution.py:292
  136.1 11.3 %multiply_add_fusion = f32[4,64]{1,0:T(4,128)} fusion(f32[4,72]{1,0:T(4,128)S(1)} %get-tuple-element.66, f32[4,64]{1,0:T(4,128)S(1)} %reduce.1, f32[4,72]{1,0:T(4,128)S(1)} %get-tuple-element.65, f32[]{:T(128)} %bitcast.24, f32[]{:T(128)} %bitcast.23, f32[]{:T(128)} %bitcast.22, f32[]{:T(128)} %bitcast.21, f32[]{:T(128)} %bitcast.20, f32[]{:T(128)} %bitcast.19, ...), kind=kLoop, calls=%fused_computation.4 | loop fusion | flops 8448 | bytes 18500 | tf_op jit(solution)/shard_map/add | solution.py:356
  (58 shorter events, 17.6 us)
Async XLA Ops:
  12.8 45.4 %all-to-all-start = ((s16[16,2,2,2,16,128]{5,4,3,2,1,0:T(8,128)(2,1)}), s16[16,2,2,2,16,128]{5,4,3,2,1,0:T(8,128)(2,1)S(1)}, u32[]{:S(2)}, u32[]{:S(2)}) async-start(s16[16,2,2,2,16,128]{5,4,3,2,1,0:T(8,128)(2,1)} %shard_map.95), calls=%async_computation | async-start | bytes 1048576 | tf_op jit(solution)/shard_map/all_to_all | solution.py:308
  22.8 75.8 %all-gather.4.cloned.1.call-start = ((), (), s32[]{:S(2)}) async-start(), calls=%async_computation.3 | async-start | bytes 1114112 | tf_op jit(solution)/shard_map/all_gather | solution.py:325
  22.8 35.4 %collective-permute-start = (f32[64,128]{1,0:T(8,128)S(1)}, f32[64,128]{1,0:T(8,128)S(1)}, u32[]{:S(2)}, u32[]{:S(2)}) collective-permute-start(f32[64,128]{1,0:T(8,128)S(1)} %get-tuple-element.64), channel_id=1, source_target_pairs={{0,16},{16,32},{32,48},{48,64},{64,80},{80,96},{96,112},{112,128},... | collective-permute-start | bytes 98312 | tf_op jit(solution)/shard_map/ppermute | solution.py:289
  26.4 31.8 %collective-permute-start.1 = (f32[64,128]{1,0:T(8,128)S(1)}, f32[64,128]{1,0:T(8,128)S(1)}, u32[]{:S(2)}, u32[]{:S(2)}) collective-permute-start(f32[64,128]{1,0:T(8,128)S(1)} %get-tuple-element.63), channel_id=1, source_target_pairs={{16,0},{32,16},{48,32},{64,48},{80,64},{96,80},{112,96},{128,112},... | collective-permute-start | bytes 98312 | tf_op jit(solution)/shard_map/ppermute | solution.py:290
  28.3 29.9 %collective-permute-start.2 = (f32[4,128]{1,0:T(4,128)S(1)}, f32[4,128]{1,0:T(4,128)S(1)}, u32[]{:S(2)}, u32[]{:S(2)}) collective-permute-start(f32[4,128]{1,0:T(4,128)S(1)} %bitcast.37), channel_id=1, source_target_pairs={{0,1},{1,2},{2,3},{3,4},{4,5},{5,6},{6,7},{7,8},{8,9},{9,10},{10,1... | collective-permute-start | bytes 6152 | tf_op jit(solution)/shard_map/ppermute | solution.py:291
  29.6 28.6 %collective-permute-start.3 = (f32[4,128]{1,0:T(4,128)S(1)}, f32[4,128]{1,0:T(4,128)S(1)}, u32[]{:S(2)}, u32[]{:S(2)}) collective-permute-start(f32[4,128]{1,0:T(4,128)S(1)} %bitcast.36), channel_id=1, source_target_pairs={{1,0},{2,1},{3,2},{4,3},{5,4},{6,5},{7,6},{8,7},{9,8},{10,9},{11,1... | collective-permute-start | bytes 6152 | tf_op jit(solution)/shard_map/ppermute | solution.py:292
  58.1 58.6 %copy-start.7 = (f32[17]{0:T(128)S(1)}, f32[17]{0:T(128)}, u32[]{:S(2)}) copy-start(f32[17]{0:T(128)} %param.13) | copy-start | bytes 208
  58.1 59.3 %copy-start.8 = (s32[4,64]{1,0:T(4,128)S(1)}, s32[4,64]{1,0:T(4,128)}, u32[]{:S(2)}) copy-start(s32[4,64]{1,0:T(4,128)} %param.12) | copy-start | bytes 3076
  59.8 25.3 %all-to-all-start.1 = ((s16[16,2,2,2,16,128]{5,4,3,2,1,0:T(8,128)(2,1)}), s16[16,2,2,2,16,128]{5,4,3,2,1,0:T(8,128)(2,1)S(1)}, u32[]{:S(2)}, u32[]{:S(2)}) async-start(s16[16,2,2,2,16,128]{5,4,3,2,1,0:T(8,128)(2,1)} %shard_map.94), calls=%async_computation.1 | async-start | bytes 1048576 | tf_op jit(solution)/shard_map/all_to_all | solution.py:323
  65.7 12.4 %collective-permute-start.4 = (f32[64,128]{1,0:T(8,128)S(1)}, f32[64,128]{1,0:T(8,128)S(1)}, u32[]{:S(2)}, u32[]{:S(2)}) collective-permute-start(f32[64,128]{1,0:T(8,128)S(1)} %get-tuple-element.40), channel_id=1, source_target_pairs={{0,16},{16,32},{32,48},{48,64},{64,80},{80,96},{96,112},{112,128},... | collective-permute-start | bytes 98312 | tf_op jit(solution)/shard_map/ppermute | solution.py:289
  69.2 13.1 %collective-permute-start.5 = (f32[64,128]{1,0:T(8,128)S(1)}, f32[64,128]{1,0:T(8,128)S(1)}, u32[]{:S(2)}, u32[]{:S(2)}) collective-permute-start(f32[64,128]{1,0:T(8,128)S(1)} %get-tuple-element.41), channel_id=1, source_target_pairs={{16,0},{32,16},{48,32},{64,48},{80,64},{96,80},{112,96},{128,112},... | collective-permute-start | bytes 98312 | tf_op jit(solution)/shard_map/ppermute | solution.py:290
  71.2 6.1 %collective-permute-start.6 = (f32[4,128]{1,0:T(4,128)S(1)}, f32[4,128]{1,0:T(4,128)S(1)}, u32[]{:S(2)}, u32[]{:S(2)}) collective-permute-start(f32[4,128]{1,0:T(4,128)S(1)} %get-tuple-element.42), channel_id=1, source_target_pairs={{0,1},{1,2},{2,3},{3,4},{4,5},{5,6},{6,7},{7,8},{8,9},{9,10},{10,1... | collective-permute-start | bytes 6152 | tf_op jit(solution)/shard_map/ppermute | solution.py:291
  71.3 6.0 %collective-permute-start.7 = (f32[4,128]{1,0:T(4,128)S(1)}, f32[4,128]{1,0:T(4,128)S(1)}, u32[]{:S(2)}, u32[]{:S(2)}) collective-permute-start(f32[4,128]{1,0:T(4,128)S(1)} %get-tuple-element.43), channel_id=1, source_target_pairs={{1,0},{2,1},{3,2},{4,3},{5,4},{6,5},{7,6},{8,7},{9,8},{10,9},{11,1... | collective-permute-start | bytes 6152 | tf_op jit(solution)/shard_map/ppermute | solution.py:292
  101.6 45.8 %all-to-all-start.2 = ((f32[16,64,128]{2,1,0:T(8,128)}), f32[16,64,128]{2,1,0:T(8,128)S(1)}, u32[]{:S(2)}, u32[]{:S(2)}) async-start(f32[16,64,128]{2,1,0:T(8,128)} %get-tuple-element.57), calls=%async_computation.2 | async-start | bytes 1048576 | tf_op jit(solution)/shard_map/all_to_all | solution.py:333
  106.3 11.6 %collective-permute-start.8 = (f32[64,128]{1,0:T(8,128)S(1)}, f32[64,128]{1,0:T(8,128)S(1)}, u32[]{:S(2)}, u32[]{:S(2)}) collective-permute-start(f32[64,128]{1,0:T(8,128)S(1)} %get-tuple-element.47), channel_id=1, source_target_pairs={{0,16},{16,32},{32,48},{48,64},{64,80},{80,96},{96,112},{112,128},... | collective-permute-start | bytes 98312 | tf_op jit(solution)/shard_map/ppermute | solution.py:289
  109.8 10.9 %collective-permute-start.9 = (f32[64,128]{1,0:T(8,128)S(1)}, f32[64,128]{1,0:T(8,128)S(1)}, u32[]{:S(2)}, u32[]{:S(2)}) collective-permute-start(f32[64,128]{1,0:T(8,128)S(1)} %get-tuple-element.48), channel_id=1, source_target_pairs={{16,0},{32,16},{48,32},{64,48},{80,64},{96,80},{112,96},{128,112},... | collective-permute-start | bytes 98312 | tf_op jit(solution)/shard_map/ppermute | solution.py:290
  111.8 6.1 %collective-permute-start.10 = (f32[4,128]{1,0:T(4,128)S(1)}, f32[4,128]{1,0:T(4,128)S(1)}, u32[]{:S(2)}, u32[]{:S(2)}) collective-permute-start(f32[4,128]{1,0:T(4,128)S(1)} %get-tuple-element.49), channel_id=1, source_target_pairs={{0,1},{1,2},{2,3},{3,4},{4,5},{5,6},{6,7},{7,8},{8,9},{9,10},{10,1... | collective-permute-start | bytes 6152 | tf_op jit(solution)/shard_map/ppermute | solution.py:291
  112.4 5.5 %collective-permute-start.11 = (f32[4,128]{1,0:T(4,128)S(1)}, f32[4,128]{1,0:T(4,128)S(1)}, u32[]{:S(2)}, u32[]{:S(2)}) collective-permute-start(f32[4,128]{1,0:T(4,128)S(1)} %get-tuple-element.50), channel_id=1, source_target_pairs={{1,0},{2,1},{3,2},{4,3},{5,4},{6,5},{7,6},{8,7},{9,8},{10,9},{11,1... | collective-permute-start | bytes 6152 | tf_op jit(solution)/shard_map/ppermute | solution.py:292
  122.0 9.2 %collective-permute-start.16 = (f32[4,8]{1,0:T(4,128)S(1)}, f32[4,8]{1,0:T(4,128)S(1)}, u32[]{:S(2)}, u32[]{:S(2)}) collective-permute-start(f32[4,8]{1,0:T(4,128)S(1)} %get-tuple-element.67), channel_id=1, source_target_pairs={{0,1},{1,2},{2,3},{3,4},{4,5},{5,6},{6,7},{7,8},{8,9},{9,10},{10,1... | collective-permute-start | bytes 392 | tf_op jit(solution)/shard_map/ppermute | solution.py:344
  122.6 13.4 %collective-permute-start.17 = (f32[4,8]{1,0:T(4,128)S(1)}, f32[4,8]{1,0:T(4,128)S(1)}, u32[]{:S(2)}, u32[]{:S(2)}) collective-permute-start(f32[4,8]{1,0:T(4,128)S(1)} %get-tuple-element.68), channel_id=1, source_target_pairs={{1,0},{2,1},{3,2},{4,3},{5,4},{6,5},{7,6},{8,7},{9,8},{10,9},{11,1... | collective-permute-start | bytes 392 | tf_op jit(solution)/shard_map/ppermute | solution.py:347
  126.8 20.5 %collective-permute-start.12 = (f32[64,128]{1,0:T(8,128)S(1)}, f32[64,128]{1,0:T(8,128)S(1)}, u32[]{:S(2)}, u32[]{:S(2)}) collective-permute-start(f32[64,128]{1,0:T(8,128)S(1)} %get-tuple-element.53), channel_id=1, source_target_pairs={{0,16},{16,32},{32,48},{48,64},{64,80},{80,96},{96,112},{112,128},... | collective-permute-start | bytes 98312 | tf_op jit(solution)/shard_map/ppermute | solution.py:289
  129.1 18.3 %collective-permute-start.13 = (f32[64,128]{1,0:T(8,128)S(1)}, f32[64,128]{1,0:T(8,128)S(1)}, u32[]{:S(2)}, u32[]{:S(2)}) collective-permute-start(f32[64,128]{1,0:T(8,128)S(1)} %get-tuple-element.54), channel_id=1, source_target_pairs={{16,0},{32,16},{48,32},{64,48},{80,64},{96,80},{112,96},{128,112},... | collective-permute-start | bytes 98312 | tf_op jit(solution)/shard_map/ppermute | solution.py:290
  131.2 16.2 %collective-permute-start.14 = (f32[4,128]{1,0:T(4,128)S(1)}, f32[4,128]{1,0:T(4,128)S(1)}, u32[]{:S(2)}, u32[]{:S(2)}) collective-permute-start(f32[4,128]{1,0:T(4,128)S(1)} %get-tuple-element.55), channel_id=1, source_target_pairs={{0,1},{1,2},{2,3},{3,4},{4,5},{5,6},{6,7},{7,8},{8,9},{9,10},{10,1... | collective-permute-start | bytes 6152 | tf_op jit(solution)/shard_map/ppermute | solution.py:291
  131.3 16.1 %collective-permute-start.15 = (f32[4,128]{1,0:T(4,128)S(1)}, f32[4,128]{1,0:T(4,128)S(1)}, u32[]{:S(2)}, u32[]{:S(2)}) collective-permute-start(f32[4,128]{1,0:T(4,128)S(1)} %get-tuple-element.56), channel_id=1, source_target_pairs={{1,0},{2,1},{3,2},{4,3},{5,4},{6,5},{7,6},{8,7},{9,8},{10,9},{11,1... | collective-permute-start | bytes 6152 | tf_op jit(solution)/shard_map/ppermute | solution.py:292
  (7 other events, 118.0 us)
Sparse Core Ops, SparseCore 0:
  59.9 38.6 all-gather.3

commit v2 on v1

v2 whole, which is shorter than its diff:
```python
import jax
import jax.numpy as jnp
from jax import lax
from jax.experimental import pallas as pl
from jax.experimental.pallas import tpu as pltpu
from jax.sharding import PartitionSpec as P

ROWS = 16
LANES = 128
RATE_MID = 3.7
RATE_SCALE = 10500.0
COEF_SCALE = 1374.0
COEF_BASE = 23.0
ENCODE_VMEM = 60 * 1024 * 1024
STEP_VMEM = 16 * 1024 * 1024


def encode_body(stored_ref, out_ref):
    slots = stored_ref.shape[1]
    cap = out_ref.shape[2]
    rows = 8 * ROWS
    row = lax.broadcasted_iota(jnp.int32, (rows, rows), 0)
    column = lax.broadcasted_iota(jnp.int32, (rows, rows), 1)
    picked = (row % ROWS) * 8 + row // ROWS == column
    order = jnp.where(picked, 1.0, 0.0).astype(jnp.bfloat16)
    for slot in range(slots):
        mixed = stored_ref[0, slot].astype(jnp.float32)
        mixed = jnp.concatenate(
            [mixed[:, LANES * r : LANES * (r + 1)] for r in range(ROWS)], axis=0
        ).astype(jnp.bfloat16)
        parts = jnp.dot(order, mixed, preferred_element_type=jnp.float32)

        def part(index):
            return parts[ROWS * index : ROWS * (index + 1), :]

        squares = part(1) * part(1)
        for index in range(2, 7):
            squares = squares + part(index) * part(index)
        slope = jnp.tanh(part(0))
        rate = jnp.sqrt(1.0 + squares * (1.0 / 6.0)) * jnp.exp(0.5 * slope)
        coef = 0.1 * part(7) * rate * (1.0 - slope * slope)
        size = jnp.log2(jnp.maximum(jnp.abs(coef), 2.0 ** -(COEF_BASE + 1.0)))
        size = jnp.maximum(jnp.round((size + COEF_BASE) * COEF_SCALE), 0.0)
        coef_code = jnp.where(coef < 0.0, -size, size)
        rate_code = jnp.round((rate - RATE_MID) * RATE_SCALE)
        out_ref[slot // cap, 0, slot % cap, 0] = rate_code.astype(jnp.int32).astype(jnp.int16)
        out_ref[slot // cap, 0, slot % cap, 1] = coef_code.astype(jnp.int32).astype(jnp.int16)


def encode(stored):
    steps, _, _, owners, cap, comps, cells = stored.shape
    flat = stored.reshape(steps, owners * cap, comps, cells)
    chunk = 8
    return pl.pallas_call(
        encode_body,
        grid=(steps, owners // chunk),
        in_specs=[pl.BlockSpec((1, chunk * cap, comps, cells), lambda k, c: (k, c, 0, 0))],
        out_specs=pl.BlockSpec(
            (chunk, 1, cap, 2, ROWS, LANES), lambda k, c: (c, k, 0, 0, 0, 0)
        ),
        out_shape=jax.ShapeDtypeStruct((owners, steps, cap, 2, ROWS, LANES), jnp.int16),
        compiler_params=pltpu.CompilerParams(vmem_limit_bytes=ENCODE_VMEM),
    )(flat)


def decoded(info_ref, rec_ref, step, layer, field):
    pieces = []
    for quarter in range(4):
        held = info_ref[16 * step + 4 * layer + quarter]
        code = rec_ref[held // 2, step, held % 2, field].astype(jnp.int32).astype(jnp.float32)
        if field == 0:
            pieces.append(code * (1.0 / RATE_SCALE) + RATE_MID)
        else:
            size = jnp.exp2(jnp.abs(code) * (1.0 / COEF_SCALE) - COEF_BASE)
            pieces.append(jnp.where(code > 0.0, size, jnp.where(code < 0.0, -size, 0.0)))
    return jnp.concatenate(pieces, axis=0)


def laplace(info_ref, field, low_ref, high_ref, left_ref, right_ref):
    layers = len(field)
    low = jnp.where(info_ref[64] == 0, 0.0, low_ref[...])
    high = jnp.where(info_ref[64] == info_ref[65] - 1, 0.0, high_ref[...])
    left, right = left_ref[...], right_ref[...]
    azimuths, radials = field[0].shape
    row = lax.broadcasted_iota(jnp.int32, (azimuths, radials), 0)
    lane = lax.broadcasted_iota(jnp.int32, (azimuths, radials), 1)
    out = []
    for layer in range(layers):
        x = field[layer]
        below = low if layer == 0 else field[layer - 1]
        above = high if layer == layers - 1 else field[layer + 1]
        before = jnp.where(row == 0, left[layer : layer + 1, :], pltpu.roll(x, 1, axis=0))
        after = jnp.where(
            row == azimuths - 1, right[layer : layer + 1, :], pltpu.roll(x, azimuths - 1, axis=0)
        )
        inner = jnp.where(lane == 0, 0.0, pltpu.roll(x, 1, axis=1))
        outer = jnp.where(lane == radials - 1, 0.0, pltpu.roll(x, radials - 1, axis=1))
        out.append(((below + above) + (before + after)) + (inner + outer) - 6.0 * x)
    return out


def chain(field, decay, carry):
    layers = len(field)
    out = [None] * layers
    for layer in reversed(range(layers)):
        out[layer] = carry
        carry = decay * carry + (1.0 - decay) * field[layer]
    return out, carry


def put_edges(field, low_ref, high_ref, left_ref, right_ref):
    layers = len(field)
    azimuths = field[0].shape[0]
    low_ref[...] = field[0]
    high_ref[...] = field[-1]
    for layer in range(layers):
        left_ref[layer : layer + 1, :] = field[layer][0:1, :]
        right_ref[layer : layer + 1, :] = field[layer][azimuths - 1 : azimuths, :]


def powers(length):
    decay = jnp.exp(-1.0 / length)
    cube = decay * decay * decay
    return decay, decay * cube, 4.0 * (1.0 - decay) * cube


def applied(carry, here, fall, cross):
    out = [sums + fall * value for value, sums in zip(carry, here)]
    if len(carry) > 1:
        out[1] = out[1] + cross * carry[0]
        out[2] = out[2] + cross * carry[1] + here[3] * carry[0]
    return tuple(out)


def halves(info_ref, values, scratch, keep_ref, give_ref):
    mine = info_ref[64] % 2
    half = scratch.shape[1] // 2
    for index, value in enumerate(values):
        scratch[index] = value
    for index in range(len(values)):
        keep_ref[index] = scratch[index, pl.ds(half * mine, half), :]
        give_ref[index] = scratch[index, pl.ds(half * (1 - mine), half), :]


def restored(info_ref, mine_ref, got_ref, scratch):
    mine = info_ref[64] % 2
    half = scratch.shape[1] // 2
    count = scratch.shape[0]
    for index in range(count):
        scratch[index, pl.ds(half * mine, half), :] = mine_ref[index]
        scratch[index, pl.ds(half * (1 - mine), half), :] = got_ref[index]
    return [scratch[index] for index in range(count)]


def half_powers(info_ref, length_ref):
    half = length_ref.shape[0] // 2
    return powers(length_ref[pl.ds(half * (info_ref[64] % 2), half), :])


def cores(info_ref, keep_ref, got_ref):
    upper_here = info_ref[64] % 2 == 1
    own = [keep_ref[index] for index in range(keep_ref.shape[0])]
    other = [got_ref[index] for index in range(got_ref.shape[0])]
    upper = [jnp.where(upper_here, a, b) for a, b in zip(own, other)]
    lower = [jnp.where(upper_here, b, a) for a, b in zip(own, other)]
    return upper, lower


def chip_body(info_ref, keep_ref, got_ref, length_ref, out_ref):
    _, fall, cross = half_powers(info_ref, length_ref)
    upper, lower = cores(info_ref, keep_ref, got_ref)
    count = 3 if len(upper) > 1 else 1
    total = list(applied(upper[:count], lower, fall, cross))
    if count > 1:
        total.append(fall * (lower[3] + upper[3]) + cross * cross)
    for chip in range(out_ref.shape[0]):
        for index, value in enumerate(total):
            out_ref[chip, index] = value


def carry_body(info_ref, keep_ref, got_ref, sums_ref, length_ref, mine_ref, other_ref):
    _, fall, cross = half_powers(info_ref, length_ref)
    chips, fields = sums_ref.shape[:2]
    count = mine_ref.shape[0]

    def climb(k, total):
        at = chips - 1 - k
        here = [sums_ref[at, index] for index in range(fields)]
        return applied(total, here, fall * fall, 2.0 * fall * cross)

    zero = jnp.zeros_like(fall)
    total = lax.fori_loop(0, chips - 1 - info_ref[64] // 2, climb, (zero,) * count)
    upper, _ = cores(info_ref, keep_ref, got_ref)
    below = applied(total, upper, fall, cross)
    upper_here = info_ref[64] % 2 == 1
    for index in range(count):
        mine_ref[index] = jnp.where(upper_here, total[index], below[index])
        other_ref[index] = jnp.where(upper_here, below[index], total[index])


def first_body(
    info_ref, rec_ref, lt_ref, lr_ref, low_ref, high_ref, left_ref, right_ref, length_ref,
    new_lt_ref, keep_ref, give_ref, low_out, high_out, left_out, right_out, scratch,
):
    layers = lt_ref.shape[0]
    decay, _, _ = powers(length_ref[...])
    nothing = jnp.zeros_like(decay)
    lt = [lt_ref[layer] for layer in range(layers)]
    lr = [lr_ref[layer] for layer in range(layers)]
    climbs, now = chain(lr, decay, nothing)
    new_lr = [
        -0.3 * lt[l] + (1.0 + 0.2 * decoded(info_ref, rec_ref, 3, l, 0)) * lr[l] + climbs[l]
        for l in range(layers)
    ]
    spread = laplace(info_ref, lt, low_ref, high_ref, left_ref, right_ref)
    new_lt = [
        lt[l] + 0.15 * spread[l] + decoded(info_ref, rec_ref, 3, l, 1) * lr[l]
        for l in range(layers)
    ]
    put_edges(new_lt, low_out, high_out, left_out, right_out)
    gain = [1.0 + 0.2 * decoded(info_ref, rec_ref, 2, l, 0) for l in range(layers)]
    climbs, soon = chain(new_lr, decay, nothing)
    after = [-0.3 * new_lt[l] + gain[l] * new_lr[l] + climbs[l] for l in range(layers)]
    _, later = chain(after, decay, nothing)
    shares = [None] * layers
    power = jnp.ones_like(decay)
    for layer in reversed(range(layers)):
        shares[layer] = power
        power = decay * power
    climbs, _ = chain(shares, decay, nothing)
    after = [gain[l] * shares[l] + climbs[l] for l in range(layers)]
    _, weight = chain(after, decay, nothing)
    halves(info_ref, (now, soon, later, weight), scratch, keep_ref, give_ref)
    for l in range(layers):
        new_lt_ref[l] = new_lt[l]


def second_body(
    info_ref, rec_ref, seed_ref, lr_ref, lt_ref, low_ref, high_ref, left_ref, right_ref,
    length_ref, mine_ref, got_ref, new_lt_ref, mid_lr_ref, new_lr_ref, keep_ref, give_ref,
    low_out, high_out, left_out, right_out, carried, scratch,
):
    layers = lt_ref.shape[0]
    decay, _, _ = powers(length_ref[...])
    zero, one, two = restored(info_ref, mine_ref, got_ref, carried)
    lt = [lt_ref[layer] for layer in range(layers)]
    lr = [lr_ref[layer] for layer in range(layers)]
    climbs, _ = chain(lr, decay, zero)
    lr = [
        -0.3 * seed_ref[l]
        + (1.0 + 0.2 * decoded(info_ref, rec_ref, 3, l, 0)) * lr[l]
        + climbs[l]
        for l in range(layers)
    ]
    spread = laplace(info_ref, lt, low_ref, high_ref, left_ref, right_ref)
    new_lt = [
        lt[l] + 0.15 * spread[l] + decoded(info_ref, rec_ref, 2, l, 1) * lr[l]
        for l in range(layers)
    ]
    put_edges(new_lt, low_out, high_out, left_out, right_out)
    climbs, _ = chain(lr, decay, one)
    lr = [
        -0.3 * lt[l] + (1.0 + 0.2 * decoded(info_ref, rec_ref, 2, l, 0)) * lr[l] + climbs[l]
        for l in range(layers)
    ]
    climbs, _ = chain(lr, decay, two)
    new_lr = [
        -0.3 * new_lt[l]
        + (1.0 + 0.2 * decoded(info_ref, rec_ref, 1, l, 0)) * lr[l]
        + climbs[l]
        for l in range(layers)
    ]
    _, total = chain(new_lr, decay, jnp.zeros_like(decay))
    halves(info_ref, (total,), scratch, keep_ref, give_ref)
    for l in range(layers):
        new_lt_ref[l] = new_lt[l]
        mid_lr_ref[l] = lr[l]
        new_lr_ref[l] = new_lr[l]


def third_body(
    info_ref, rec_ref, seed_ref, one_ref, lt_ref, lr_ref, low_ref, high_ref, left_ref,
    right_ref, face_ref, new_lt_ref, flux_ref, low_out, high_out, left_out, right_out,
):
    layers, azimuths, radials = lt_ref.shape
    lt = [lt_ref[layer] for layer in range(layers)]
    spread = laplace(info_ref, lt, low_ref, high_ref, left_ref, right_ref)
    new_lt = [
        lt[l] + 0.15 * spread[l] + decoded(info_ref, rec_ref, 1, l, 1) * lr_ref[l]
        for l in range(layers)
    ]
    put_edges(new_lt, low_out, high_out, left_out, right_out)
    for l in range(layers):
        new_lt_ref[l] = new_lt[l]
    lane = lax.broadcasted_iota(jnp.int32, (azimuths, radials), 1)
    ones = jnp.ones((8, radials), jnp.float32)
    for l in range(layers):
        kept = jnp.where(
            lane == face_ref[l], (seed_ref[l] + one_ref[l]) + (lt[l] + new_lt[l]), 0.0
        )
        row = lax.dot_general(
            ones,
            kept,
            (((1,), (1,)), ((), ())),
            precision=lax.Precision.HIGHEST,
            preferred_element_type=jnp.float32,
        )[0:1, :]
        twice = jnp.concatenate([row, row], axis=1)
        flux_ref[l : l + 1, :] = twice
        left_out[layers + l : layers + l + 1, :] = twice
        right_out[layers + l : layers + l + 1, :] = twice


def last_body(
    info_ref, weight_ref, rec_ref, lt_ref, lr_ref, low_ref, high_ref, left_ref, right_ref,
    length_ref, mine_ref, got_ref, flux_ref, new_lt_ref, new_lr_ref, heat_ref, scratch,
):
    layers, azimuths, radials = lt_ref.shape
    band = weight_ref.shape[0] // 2
    decay, _, _ = powers(length_ref[...])
    (three,) = restored(info_ref, mine_ref, got_ref, scratch)
    lt = [lt_ref[layer] for layer in range(layers)]
    lr = [lr_ref[layer] for layer in range(layers)]
    spread = laplace(info_ref, lt, low_ref, high_ref, left_ref, right_ref)
    climbs, _ = chain(lr, decay, three)
    for l in range(layers):
        new_lt_ref[l] = lt[l] + 0.15 * spread[l] + decoded(info_ref, rec_ref, 0, l, 1) * lr[l]
        new_lr_ref[l] = (
            -0.3 * lt[l]
            + (1.0 + 0.2 * decoded(info_ref, rec_ref, 0, l, 0)) * lr[l]
            + climbs[l]
        )
    lane = lax.broadcasted_iota(jnp.int32, (layers, radials), 1)
    ring = jnp.where(
        lane < azimuths,
        flux_ref[...],
        jnp.where(
            lane < azimuths + band,
            right_ref[layers : 2 * layers, :],
            left_ref[layers : 2 * layers, :],
        ),
    )
    heat = jnp.zeros_like(ring)
    for offset in range(-band, band + 1):
        heat = heat + weight_ref[offset + band] * pltpu.roll(ring, (-offset) % radials, axis=1)
    heat_ref[...] = heat[:, :azimuths]


def run(body, scalars, args, shapes, scratch=()):
    smem = pl.BlockSpec(memory_space=pltpu.SMEM)
    vmem = pl.BlockSpec(memory_space=pltpu.VMEM)
    return pl.pallas_call(
        body,
        in_specs=[smem] * len(scalars) + [vmem] * len(args),
        out_specs=[vmem] * len(shapes),
        out_shape=[jax.ShapeDtypeStruct(shape, jnp.float32) for shape in shapes],
        scratch_shapes=[pltpu.VMEM(shape, jnp.float32) for shape in scratch],
        compiler_params=pltpu.CompilerParams(vmem_limit_bytes=STEP_VMEM),
    )(*scalars, *args)


def turned(value, axis, shift):
    count = lax.axis_size(axis)
    return lax.ppermute(value, axis, [(i, (i + shift) % count) for i in range(count)])


def exchanged(low, high, left, right):
    return (
        turned(high, "axial", 1),
        turned(low, "axial", -1),
        turned(right, "azim", 1),
        turned(left, "azim", -1),
    )


def swapped(value):
    return lax.ppermute(value, "axial", [(i, i ^ 1) for i in range(lax.axis_size("axial"))])


def carries(info, keep, give, length, count, rim):
    got = swapped(give)
    axial = lax.axis_size("axial")
    (total,) = run(chip_body, (info,), (keep, got, length), [(axial // 2, *keep.shape)])
    groups = [list(range(core, axial, 2)) for core in range(2)]
    sums = lax.all_to_all(total, "axial", 0, 0, tiled=True, axis_index_groups=groups)
    halo = exchanged(*rim)
    sums, halo = lax.optimization_barrier((sums, halo))
    shape = (count, *keep.shape[1:])
    mine, other = run(carry_body, (info,), (keep, got, sums, length), [shape, shape])
    return (mine, swapped(other)), halo


def local(stored, holder, seed_temp, seed_disloc, decay_length, face_radius, kernel):
    layers, azimuths, radials = seed_temp.shape
    axial, me = lax.axis_size("axial"), lax.axis_index("axial")
    wanted = lax.dynamic_index_in_dim(holder, me, 1, keepdims=False).reshape(-1)
    info = jnp.concatenate([wanted, jnp.stack([me, axial]).astype(jnp.int32)])
    plane = (azimuths, radials)
    side = (layers, radials)
    wide = (2 * layers, radials)
    block = (layers, azimuths, radials)
    first = (4, azimuths // 2, radials)
    single = (1, azimuths // 2, radials)
    edges = [plane, plane, side, side]

    pieces = lax.all_to_all(encode(stored), "axial", 0, 0, tiled=True)
    halo = exchanged(
        seed_temp[0], seed_temp[layers - 1], seed_temp[:, 0], seed_temp[:, azimuths - 1]
    )
    lt1, keep, give, *rim = run(
        first_body,
        (info,),
        (pieces, seed_temp, seed_disloc, *halo, decay_length),
        [block, first, first, *edges],
        [(4, *plane)],
    )
    carry, halo = carries(info, keep, give, decay_length, 3, rim)
    lt2, lr2, lr3, keep, give, *rim = run(
        second_body,
        (info,),
        (pieces, seed_temp, seed_disloc, lt1, *halo, decay_length, *carry),
        [block, block, block, single, single, *edges],
        [(3, *plane), (1, *plane)],
    )
    carry, halo = carries(info, keep, give, decay_length, 1, rim)
    lt3, flux, *rim = run(
        third_body,
        (info,),
        (pieces, seed_temp, lt1, lt2, lr2, *halo, face_radius[:, :, None]),
        [block, side, plane, plane, wide, wide],
    )
    halo = exchanged(*rim)
    return tuple(
        run(
            last_body,
            (info, kernel),
            (pieces, lt3, lr3, *halo, decay_length, *carry, flux),
            [block, block, (layers, azimuths)],
            [(1, *plane)],
        )
    )


def solution(mesh):
    in_specs = (
        P(None, "axial", "azim", None, None, None, None),
        P(),
        P("axial", "azim", None),
        P("axial", "azim", None),
        P("azim", None),
        P("axial", "azim"),
        P(),
    )
    out_specs = (P("axial", "azim", None), P("axial", "azim", None), P("axial", "azim"))
    return jax.shard_map(local, mesh=mesh, in_specs=in_specs, out_specs=out_specs, check_vma=False)
```

time: 157 us -> 103 us (0.66)
  blocking collectives: 19.1 us -> 0 us
  starting transfers between devices: 65.7 us -> 48.7 us
  between operations: 14.2 us -> 0.78 us
  waiting for transfers between devices: 25.9 us -> 37.3 us
  other arithmetic: 11.4 us -> 0.08 us
  local copies, waits for them, and re-layouts: 6.65 us -> 0.27 us
  Pallas kernels: 12.8 us -> 15.5 us
    ppermute x18 -> x20, waiting for transfers between devices: 9.67 us -> 30.7 us  [the longest x16 27.7 us: turned(): lax.ppermute(value, axis, [(i, (i + shift) % count) for i in range(count)])]
    all_gather x1 -> x0, blocking collectives: 19.1 us -> none  [local(): sums = lax.all_gather(total, 'axial')]
    ppermute x18 -> x20, starting transfers between devices: 45.1 us -> 31.7 us  [the longest x16 27.7 us: turned(): lax.ppermute(value, axis, [(i, (i + shift) % count) for i in range(count)])]
    all_gather x1 -> x0, waiting for transfers between devices: 13.4 us -> none  [local(): sums = lax.all_gather(pair, 'axial')]
    add x1 -> x0, other arithmetic: 11.3 us -> none  [local(): heater_grad + kernel[offset] * padded[:, offset:offset + azimuths]]
    unnamed x18 -> x12, local copies, waits for them, and re-layouts: 5.63 us -> 0.03 us
    all_to_all x3, waiting for transfers between devices: 2.78 us -> 6.57 us  [the longest x2 4.34 us: carries(): lax.all_to_all(total, 'axial', 0, 0, tiled=True, axis_index_groups=groups)]
    all_to_all x3, starting transfers between devices: 20.5 us -> 17 us  [the longest x1 10.1 us: local(): pieces = lax.all_to_all(encode(stored), 'axial', 0, 0, tiled=True)]
  transfers between devices with their start and end apart: 22 -> 23, of which waited for: 7 -> 14; matrix products, arithmetic and copies ran while one was open for 8% -> 0% of each run, Pallas kernels for 3% -> 1%
where the time goes in v2:
time: 103 us
  starting transfers between devices  48.7 us (47%)
  waiting for transfers between devices  37.3 us (36%)
  Pallas kernels  15.5 us (15%)
    ppermute x16, waiting for transfers between devices, turned(): lax.ppermute(value, axis, [(i, (i + shift) % count) for i in range(count)])  27.7 us
    ppermute x16, starting transfers between devices, turned(): lax.ppermute(value, axis, [(i, (i + shift) % count) for i in range(count)])  27.7 us
    all_to_all x1, starting transfers between devices, local(): pieces = lax.all_to_all(encode(stored), 'axial', 0, 0, tiled=True)  10.1 us
    pallas_call x8, Pallas kernels, run(): pl.pallas_call(body, in_specs=[smem] * len(scalars) + [vmem] * len(args),...  8.21 us
    pallas_call x1, Pallas kernels, encode(): pl.pallas_call(encode_body, grid=(steps, owners // chunk), in_specs=[pl.B...  7.32 us
    all_to_all x2, starting transfers between devices, carries(): lax.all_to_all(total, 'axial', 0, 0, tiled=True, axis_index_groups=groups)  6.86 us
    all_to_all x2, waiting for transfers between devices, carries(): lax.all_to_all(total, 'axial', 0, 0, tiled=True, axis_index_groups=groups)  4.34 us
    ppermute x4, starting transfers between devices, swapped(): lax.ppermute(value, 'axial', [(i, i ^ 1) for i in range(lax.axis_size('ax...  3.95 us
  transfers between devices with their start and end apart: 23, of which 14 were waited for; matrix products, arithmetic and copies ran while one was open for 0% of the time, Pallas kernels for 1%

profile of v2, /device:TPU:1, one launch (start us, length us, event | category | flops | bytes accessed | tf_op | source)
XLA Modules:
  0.0 102.6 jit_solution(6103057996518607599)
XLA Ops:
  0.7 7.3 %shard_map.94 = s16[16,4,2,2,16,128]{5,4,3,2,1,0:T(8,128)(2,1)} custom-call(bf16[4,32,8,2048]{3,2,1,0:T(8,128)(2,1)} %bitcast.13), custom_call_target="tpu_custom_call" | custom-call | tf_op jit(solution)/shard_map/pallas_call | solution.py:54
  8.0 10.1 %all-to-all-start = ((s16[16,4,2,2,16,128]{5,4,3,2,1,0:T(8,128)(2,1)}), s16[16,4,2,2,16,128]{5,4,3,2,1,0:T(8,128)(2,1)S(1)}, u32[]{:S(2)}, u32[]{:S(2)}) async-start(s16[16,4,2,2,16,128]{5,4,3,2,1,0:T(8,128)(2,1)} %shard_map.94), calls=%async_computation | async-start | bytes 2097152 | tf_op jit(solution)/shard_map/all_to_all | solution.py:406
  18.2 1.6 %collective-permute-start = (f32[64,128]{1,0:T(8,128)S(1)}, f32[64,128]{1,0:T(8,128)S(1)}, u32[]{:S(2)}, u32[]{:S(2)}) collective-permute-start(f32[64,128]{1,0:T(8,128)S(1)} %get-tuple-element.78), channel_id=1, source_target_pairs={{0,16},{16,32},{32,48},{48,64},{64,80},{80,96},{96,112},{112,128},... | collective-permute-start | bytes 98312 | tf_op jit(solution)/shard_map/ppermute | solution.py:364
  19.8 1.3 %collective-permute-start.2 = (f32[4,128]{1,0:T(4,128)S(1)}, f32[4,128]{1,0:T(4,128)S(1)}, u32[]{:S(2)}, u32[]{:S(2)}) collective-permute-start(f32[4,128]{1,0:T(4,128)S(1)} %bitcast.16), channel_id=1, source_target_pairs={{0,1},{1,2},{2,3},{3,4},{4,5},{5,6},{6,7},{7,8},{8,9},{9,10},{10,1... | collective-permute-start | bytes 6152 | tf_op jit(solution)/shard_map/ppermute | solution.py:364
  21.1 3.8 %collective-permute-start.3 = (f32[4,128]{1,0:T(4,128)S(1)}, f32[4,128]{1,0:T(4,128)S(1)}, u32[]{:S(2)}, u32[]{:S(2)}) collective-permute-start(f32[4,128]{1,0:T(4,128)S(1)} %bitcast.15), channel_id=1, source_target_pairs={{0,15},{1,0},{2,1},{3,2},{4,3},{5,4},{6,5},{7,6},{8,7},{9,8},{10,9... | collective-permute-start | bytes 6152 | tf_op jit(solution)/shard_map/ppermute | solution.py:364
  25.8 15.5 %collective-permute-done.low_ref = f32[64,128]{1,0:T(8,128)S(1)} collective-permute-done((f32[64,128]{1,0:T(8,128)S(1)}, f32[64,128]{1,0:T(8,128)S(1)}, u32[]{:S(2)}, u32[]{:S(2)}) %collective-permute-start) | collective-permute-done | bytes 32800 | tf_op jit(solution)/shard_map/ppermute | solution.py:364
  41.3 2.5 %collective-permute-done.1.high_ref = f32[64,128]{1,0:T(8,128)S(1)} collective-permute-done((f32[64,128]{1,0:T(8,128)S(1)}, f32[64,128]{1,0:T(8,128)S(1)}, u32[]{:S(2)}, u32[]{:S(2)}) %collective-permute-start.1) | collective-permute-done | bytes 32800 | tf_op jit(solution)/shard_map/ppermute | solution.py:364
  43.8 2.2 %all-to-all-done.rec_ref = s16[16,4,2,2,16,128]{5,4,3,2,1,0:T(8,128)(2,1)S(1)} async-done(((s16[16,4,2,2,16,128]{5,4,3,2,1,0:T(8,128)(2,1)}), s16[16,4,2,2,16,128]{5,4,3,2,1,0:T(8,128)(2,1)S(1)}, u32[]{:S(2)}, u32[]{:S(2)}) %all-to-all-start) | async-done | bytes 1048608 | tf_op jit(solution)/shard_map/all_to_all | solution.py:406
  47.0 1.2 %collective-permute-done.4.got_ref = f32[4,32,128]{2,1,0:T(8,128)S(1)} collective-permute-done((f32[4,32,128]{2,1,0:T(8,128)S(1)}, f32[4,32,128]{2,1,0:T(8,128)S(1)}, u32[]{:S(2)}, u32[]{:S(2)}) %collective-permute-start.4) | collective-permute-done | bytes 65568 | tf_op jit(solution)/shard_map/ppermute | solution.py:377
  48.3 1.4 %shard_map.96 = f32[8,4,32,128]{3,2,1,0:T(8,128)} custom-call(s32[66]{0:T(128)S(1)} %pad_add_fusion.info_ref, f32[4,32,128]{2,1,0:T(8,128)S(1)} %get-tuple-element.40.keep_ref, f32[4,32,128]{2,1,0:T(8,128)S(1)} %collective-permute-done.4.got_ref, f32[64,128]{1,0:T(8,128)S(1)} %copy-done.2), custom_call_target="tpu_custom_call" | custom-call | tf_op jit(solution)/shard_map/pallas_call | solution.py:352
  49.7 3.5 %all-to-all-start.1 = ((f32[8,4,32,128]{3,2,1,0:T(8,128)}), f32[8,4,32,128]{3,2,1,0:T(8,128)S(1)}, u32[]{:S(2)}, u32[]{:S(2)}) async-start(f32[8,4,32,128]{3,2,1,0:T(8,128)} %shard_map.96), calls=%async_computation.1 | async-start | bytes 1048576 | tf_op jit(solution)/shard_map/all_to_all | solution.py:385
  53.2 2.0 %collective-permute-start.5 = (f32[64,128]{1,0:T(8,128)S(1)}, f32[64,128]{1,0:T(8,128)S(1)}, u32[]{:S(2)}, u32[]{:S(2)}) collective-permute-start(f32[64,128]{1,0:T(8,128)S(1)} %get-tuple-element.42), channel_id=1, source_target_pairs={{0,16},{16,32},{32,48},{48,64},{64,80},{80,96},{96,112},{112,128},... | collective-permute-start | bytes 98312 | tf_op jit(solution)/shard_map/ppermute | solution.py:364
  56.4 3.7 %collective-permute-start.8 = (f32[4,128]{1,0:T(4,128)S(1)}, f32[4,128]{1,0:T(4,128)S(1)}, u32[]{:S(2)}, u32[]{:S(2)}) collective-permute-start(f32[4,128]{1,0:T(4,128)S(1)} %get-tuple-element.45), channel_id=1, source_target_pairs={{0,15},{1,0},{2,1},{3,2},{4,3},{5,4},{6,5},{7,6},{8,7},{9,8},{10,9... | collective-permute-start | bytes 6152 | tf_op jit(solution)/shard_map/ppermute | solution.py:364
  61.2 2.4 %collective-permute-done.5.low_ref = f32[64,128]{1,0:T(8,128)S(1)} collective-permute-done((f32[64,128]{1,0:T(8,128)S(1)}, f32[64,128]{1,0:T(8,128)S(1)}, u32[]{:S(2)}, u32[]{:S(2)}) %collective-permute-start.5) | collective-permute-done | bytes 32800 | tf_op jit(solution)/shard_map/ppermute | solution.py:364
  63.6 3.6 %collective-permute-done.6.high_ref = f32[64,128]{1,0:T(8,128)S(1)} collective-permute-done((f32[64,128]{1,0:T(8,128)S(1)}, f32[64,128]{1,0:T(8,128)S(1)}, u32[]{:S(2)}, u32[]{:S(2)}) %collective-permute-start.6) | collective-permute-done | bytes 32800 | tf_op jit(solution)/shard_map/ppermute | solution.py:364
  67.3 3.8 %all-to-all-done.1.sums_ref = f32[8,4,32,128]{3,2,1,0:T(8,128)S(1)} async-done(((f32[8,4,32,128]{3,2,1,0:T(8,128)}), f32[8,4,32,128]{3,2,1,0:T(8,128)S(1)}, u32[]{:S(2)}, u32[]{:S(2)}) %all-to-all-start.1) | async-done | bytes 524320 | tf_op jit(solution)/shard_map/all_to_all | solution.py:385
  75.5 1.2 %shard_map.99 = f32[8,1,32,128]{3,2,1,0:T(8,128)} custom-call(s32[66]{0:T(128)S(1)} %pad_add_fusion.info_ref, f32[1,32,128]{2,1,0:T(8,128)S(1)} %get-tuple-element.55.keep_ref, f32[1,32,128]{2,1,0:T(8,128)S(1)} %collective-permute-done.10.got_ref, f32[64,128]{1,0:T(8,128)S(1)} %copy-done.2), custom_call_target="tpu_custom_call" | custom-call | tf_op jit(solution)/shard_map/pallas_call | solution.py:352
  76.7 3.4 %all-to-all-start.2 = ((f32[8,1,32,128]{3,2,1,0:T(8,128)}), f32[8,1,32,128]{3,2,1,0:T(8,128)S(1)}, u32[]{:S(2)}, u32[]{:S(2)}) async-start(f32[8,1,32,128]{3,2,1,0:T(8,128)} %shard_map.99), calls=%async_computation.2 | async-start | bytes 262144 | tf_op jit(solution)/shard_map/all_to_all | solution.py:385
  80.1 1.9 %collective-permute-start.11 = (f32[64,128]{1,0:T(8,128)S(1)}, f32[64,128]{1,0:T(8,128)S(1)}, u32[]{:S(2)}, u32[]{:S(2)}) collective-permute-start(f32[64,128]{1,0:T(8,128)S(1)} %get-tuple-element.57), channel_id=1, source_target_pairs={{0,16},{16,32},{32,48},{48,64},{64,80},{80,96},{96,112},{112,128},... | collective-permute-start | bytes 98312 | tf_op jit(solution)/shard_map/ppermute | solution.py:364
  83.2 3.7 %collective-permute-start.14 = (f32[4,128]{1,0:T(4,128)S(1)}, f32[4,128]{1,0:T(4,128)S(1)}, u32[]{:S(2)}, u32[]{:S(2)}) collective-permute-start(f32[4,128]{1,0:T(4,128)S(1)} %get-tuple-element.60), channel_id=1, source_target_pairs={{0,15},{1,0},{2,1},{3,2},{4,3},{5,4},{6,5},{7,6},{8,7},{9,8},{10,9... | collective-permute-start | bytes 6152 | tf_op jit(solution)/shard_map/ppermute | solution.py:364
  89.5 2.2 %collective-permute-start.15 = (f32[64,128]{1,0:T(8,128)S(1)}, f32[64,128]{1,0:T(8,128)S(1)}, u32[]{:S(2)}, u32[]{:S(2)}) collective-permute-start(f32[64,128]{1,0:T(8,128)S(1)} %get-tuple-element.67), channel_id=1, source_target_pairs={{0,16},{16,32},{32,48},{48,64},{64,80},{80,96},{96,112},{112,128},... | collective-permute-start | bytes 98312 | tf_op jit(solution)/shard_map/ppermute | solution.py:364
  92.3 2.8 %collective-permute-start.19 = (f32[1,32,128]{2,1,0:T(8,128)S(1)}, f32[1,32,128]{2,1,0:T(8,128)S(1)}, u32[]{:S(2)}, u32[]{:S(2)}) collective-permute-start(f32[1,32,128]{2,1,0:T(8,128)S(1)} %get-tuple-element.73), channel_id=1, source_target_pairs={{0,16},{16,0},{32,48},{48,32},{64,80},{80,64},{96,112},{112,96},{1... | collective-permute-start | bytes 49160 | tf_op jit(solution)/shard_map/ppermute | solution.py:377
  96.3 3.8 %collective-permute-start.18 = (f32[8,128]{1,0:T(8,128)S(1)}, f32[8,128]{1,0:T(8,128)S(1)}, u32[]{:S(2)}, u32[]{:S(2)}) collective-permute-start(f32[8,128]{1,0:T(8,128)S(1)} %get-tuple-element.70), channel_id=1, source_target_pairs={{0,15},{1,0},{2,1},{3,2},{4,3},{5,4},{6,5},{7,6},{8,7},{9,8},{10,9... | collective-permute-start | bytes 12296 | tf_op jit(solution)/shard_map/ppermute | solution.py:364
  101.1 1.5 %shard_map.102 = (f32[4,64,128]{2,1,0:T(8,128)}, f32[4,64,128]{2,1,0:T(8,128)}, f32[4,64]{1,0:T(4,128)}) custom-call(s32[66]{0:T(128)S(1)} %pad_add_fusion.info_ref, f32[17]{0:T(128)S(1)} %copy-done.4, s16[16,4,2,2,16,128]{5,4,3,2,1,0:T(8,128)(2,1)S(1)} %all-to-all-done.rec_ref, f32[4,64,128]{2,1,0:T(8,128)S(1)} %get-tuple-element.65.lt_ref, ...), custom_call_target="tpu_custom_call" | custom-call | tf_op jit(solution)/shard_map/pallas_call | solution.py:352
  (49 shorter events, 15.2 us)
Async XLA Ops:
  8.0 38.1 %all-to-all-start = ((s16[16,4,2,2,16,128]{5,4,3,2,1,0:T(8,128)(2,1)}), s16[16,4,2,2,16,128]{5,4,3,2,1,0:T(8,128)(2,1)S(1)}, u32[]{:S(2)}, u32[]{:S(2)}) async-start(s16[16,4,2,2,16,128]{5,4,3,2,1,0:T(8,128)(2,1)} %shard_map.94), calls=%async_computation | async-start | bytes 2097152 | tf_op jit(solution)/shard_map/all_to_all | solution.py:406
  18.1 83.0 %copy-start.4 = (f32[17]{0:T(128)S(1)}, f32[17]{0:T(128)}, u32[]{:S(2)}) copy-start(f32[17]{0:T(128)} %weight_ref.1) | copy-start | bytes 208
  18.2 23.2 %collective-permute-start = (f32[64,128]{1,0:T(8,128)S(1)}, f32[64,128]{1,0:T(8,128)S(1)}, u32[]{:S(2)}, u32[]{:S(2)}) collective-permute-start(f32[64,128]{1,0:T(8,128)S(1)} %get-tuple-element.78), channel_id=1, source_target_pairs={{0,16},{16,32},{32,48},{48,64},{64,80},{80,96},{96,112},{112,128},... | collective-permute-start | bytes 98312 | tf_op jit(solution)/shard_map/ppermute | solution.py:364
  19.8 24.0 %collective-permute-start.1 = (f32[64,128]{1,0:T(8,128)S(1)}, f32[64,128]{1,0:T(8,128)S(1)}, u32[]{:S(2)}, u32[]{:S(2)}) collective-permute-start(f32[64,128]{1,0:T(8,128)S(1)} %get-tuple-element.77), channel_id=1, source_target_pairs={{0,240},{16,0},{32,16},{48,32},{64,48},{80,64},{96,80},{112,96},{1... | collective-permute-start | bytes 98312 | tf_op jit(solution)/shard_map/ppermute | solution.py:364
  19.8 6.0 %collective-permute-start.2 = (f32[4,128]{1,0:T(4,128)S(1)}, f32[4,128]{1,0:T(4,128)S(1)}, u32[]{:S(2)}, u32[]{:S(2)}) collective-permute-start(f32[4,128]{1,0:T(4,128)S(1)} %bitcast.16), channel_id=1, source_target_pairs={{0,1},{1,2},{2,3},{3,4},{4,5},{5,6},{6,7},{7,8},{8,9},{9,10},{10,1... | collective-permute-start | bytes 6152 | tf_op jit(solution)/shard_map/ppermute | solution.py:364
  21.1 4.7 %collective-permute-start.3 = (f32[4,128]{1,0:T(4,128)S(1)}, f32[4,128]{1,0:T(4,128)S(1)}, u32[]{:S(2)}, u32[]{:S(2)}) collective-permute-start(f32[4,128]{1,0:T(4,128)S(1)} %bitcast.15), channel_id=1, source_target_pairs={{0,15},{1,0},{2,1},{3,2},{4,3},{5,4},{6,5},{7,6},{8,7},{9,8},{10,9... | collective-permute-start | bytes 6152 | tf_op jit(solution)/shard_map/ppermute | solution.py:364
  46.9 1.3 %collective-permute-start.4 = (f32[4,32,128]{2,1,0:T(8,128)S(1)}, f32[4,32,128]{2,1,0:T(8,128)S(1)}, u32[]{:S(2)}, u32[]{:S(2)}) collective-permute-start(f32[4,32,128]{2,1,0:T(8,128)S(1)} %get-tuple-element.41), channel_id=1, source_target_pairs={{0,16},{16,0},{32,48},{48,32},{64,80},{80,64},{96,112},{112,96},{1... | collective-permute-start | bytes 196616 | tf_op jit(solution)/shard_map/ppermute | solution.py:377
  49.7 21.4 %all-to-all-start.1 = ((f32[8,4,32,128]{3,2,1,0:T(8,128)}), f32[8,4,32,128]{3,2,1,0:T(8,128)S(1)}, u32[]{:S(2)}, u32[]{:S(2)}) async-start(f32[8,4,32,128]{3,2,1,0:T(8,128)} %shard_map.96), calls=%async_computation.1 | async-start | bytes 1048576 | tf_op jit(solution)/shard_map/all_to_all | solution.py:385
  53.2 10.5 %collective-permute-start.5 = (f32[64,128]{1,0:T(8,128)S(1)}, f32[64,128]{1,0:T(8,128)S(1)}, u32[]{:S(2)}, u32[]{:S(2)}) collective-permute-start(f32[64,128]{1,0:T(8,128)S(1)} %get-tuple-element.42), channel_id=1, source_target_pairs={{0,16},{16,32},{32,48},{48,64},{64,80},{80,96},{96,112},{112,128},... | collective-permute-start | bytes 98312 | tf_op jit(solution)/shard_map/ppermute | solution.py:364
  55.2 12.1 %collective-permute-start.6 = (f32[64,128]{1,0:T(8,128)S(1)}, f32[64,128]{1,0:T(8,128)S(1)}, u32[]{:S(2)}, u32[]{:S(2)}) collective-permute-start(f32[64,128]{1,0:T(8,128)S(1)} %get-tuple-element.43), channel_id=1, source_target_pairs={{0,240},{16,0},{32,16},{48,32},{64,48},{80,64},{96,80},{112,96},{1... | collective-permute-start | bytes 98312 | tf_op jit(solution)/shard_map/ppermute | solution.py:364
  55.2 6.0 %collective-permute-start.7 = (f32[4,128]{1,0:T(4,128)S(1)}, f32[4,128]{1,0:T(4,128)S(1)}, u32[]{:S(2)}, u32[]{:S(2)}) collective-permute-start(f32[4,128]{1,0:T(4,128)S(1)} %get-tuple-element.44), channel_id=1, source_target_pairs={{0,1},{1,2},{2,3},{3,4},{4,5},{5,6},{6,7},{7,8},{8,9},{9,10},{10,1... | collective-permute-start | bytes 6152 | tf_op jit(solution)/shard_map/ppermute | solution.py:364
  56.4 4.8 %collective-permute-start.8 = (f32[4,128]{1,0:T(4,128)S(1)}, f32[4,128]{1,0:T(4,128)S(1)}, u32[]{:S(2)}, u32[]{:S(2)}) collective-permute-start(f32[4,128]{1,0:T(4,128)S(1)} %get-tuple-element.45), channel_id=1, source_target_pairs={{0,15},{1,0},{2,1},{3,2},{4,3},{5,4},{6,5},{7,6},{8,7},{9,8},{10,9... | collective-permute-start | bytes 6152 | tf_op jit(solution)/shard_map/ppermute | solution.py:364
  71.7 1.5 %collective-permute-start.9 = (f32[3,32,128]{2,1,0:T(8,128)S(1)}, f32[3,32,128]{2,1,0:T(8,128)S(1)}, u32[]{:S(2)}, u32[]{:S(2)}) collective-permute-start(f32[3,32,128]{2,1,0:T(8,128)S(1)} %get-tuple-element.52), channel_id=1, source_target_pairs={{0,16},{16,0},{32,48},{48,32},{64,80},{80,64},{96,112},{112,96},{1... | collective-permute-start | bytes 147464 | tf_op jit(solution)/shard_map/ppermute | solution.py:377
  74.2 1.3 %collective-permute-start.10 = (f32[1,32,128]{2,1,0:T(8,128)S(1)}, f32[1,32,128]{2,1,0:T(8,128)S(1)}, u32[]{:S(2)}, u32[]{:S(2)}) collective-permute-start(f32[1,32,128]{2,1,0:T(8,128)S(1)} %get-tuple-element.56), channel_id=1, source_target_pairs={{0,16},{16,0},{32,48},{48,32},{64,80},{80,64},{96,112},{112,96},{1... | collective-permute-start | bytes 49160 | tf_op jit(solution)/shard_map/ppermute | solution.py:377
  76.7 11.7 %all-to-all-start.2 = ((f32[8,1,32,128]{3,2,1,0:T(8,128)}), f32[8,1,32,128]{3,2,1,0:T(8,128)S(1)}, u32[]{:S(2)}, u32[]{:S(2)}) async-start(f32[8,1,32,128]{3,2,1,0:T(8,128)} %shard_map.99), calls=%async_computation.2 | async-start | bytes 262144 | tf_op jit(solution)/shard_map/all_to_all | solution.py:385
  80.1 7.8 %collective-permute-start.11 = (f32[64,128]{1,0:T(8,128)S(1)}, f32[64,128]{1,0:T(8,128)S(1)}, u32[]{:S(2)}, u32[]{:S(2)}) collective-permute-start(f32[64,128]{1,0:T(8,128)S(1)} %get-tuple-element.57), channel_id=1, source_target_pairs={{0,16},{16,32},{32,48},{48,64},{64,80},{80,96},{96,112},{112,128},... | collective-permute-start | bytes 98312 | tf_op jit(solution)/shard_map/ppermute | solution.py:364
  82.0 5.9 %collective-permute-start.12 = (f32[64,128]{1,0:T(8,128)S(1)}, f32[64,128]{1,0:T(8,128)S(1)}, u32[]{:S(2)}, u32[]{:S(2)}) collective-permute-start(f32[64,128]{1,0:T(8,128)S(1)} %get-tuple-element.58), channel_id=1, source_target_pairs={{0,240},{16,0},{32,16},{48,32},{64,48},{80,64},{96,80},{112,96},{1... | collective-permute-start | bytes 98312 | tf_op jit(solution)/shard_map/ppermute | solution.py:364
  82.0 5.9 %collective-permute-start.13 = (f32[4,128]{1,0:T(4,128)S(1)}, f32[4,128]{1,0:T(4,128)S(1)}, u32[]{:S(2)}, u32[]{:S(2)}) collective-permute-start(f32[4,128]{1,0:T(4,128)S(1)} %get-tuple-element.59), channel_id=1, source_target_pairs={{0,1},{1,2},{2,3},{3,4},{4,5},{5,6},{6,7},{7,8},{8,9},{9,10},{10,1... | collective-permute-start | bytes 6152 | tf_op jit(solution)/shard_map/ppermute | solution.py:364
  83.2 4.7 %collective-permute-start.14 = (f32[4,128]{1,0:T(4,128)S(1)}, f32[4,128]{1,0:T(4,128)S(1)}, u32[]{:S(2)}, u32[]{:S(2)}) collective-permute-start(f32[4,128]{1,0:T(4,128)S(1)} %get-tuple-element.60), channel_id=1, source_target_pairs={{0,15},{1,0},{2,1},{3,2},{4,3},{5,4},{6,5},{7,6},{8,7},{9,8},{10,9... | collective-permute-start | bytes 6152 | tf_op jit(solution)/shard_map/ppermute | solution.py:364
  89.5 11.6 %collective-permute-start.15 = (f32[64,128]{1,0:T(8,128)S(1)}, f32[64,128]{1,0:T(8,128)S(1)}, u32[]{:S(2)}, u32[]{:S(2)}) collective-permute-start(f32[64,128]{1,0:T(8,128)S(1)} %get-tuple-element.67), channel_id=1, source_target_pairs={{0,16},{16,32},{32,48},{48,64},{64,80},{80,96},{96,112},{112,128},... | collective-permute-start | bytes 98312 | tf_op jit(solution)/shard_map/ppermute | solution.py:364
  91.7 9.4 %collective-permute-start.16 = (f32[64,128]{1,0:T(8,128)S(1)}, f32[64,128]{1,0:T(8,128)S(1)}, u32[]{:S(2)}, u32[]{:S(2)}) collective-permute-start(f32[64,128]{1,0:T(8,128)S(1)} %get-tuple-element.68), channel_id=1, source_target_pairs={{0,240},{16,0},{32,16},{48,32},{64,48},{80,64},{96,80},{112,96},{1... | collective-permute-start | bytes 98312 | tf_op jit(solution)/shard_map/ppermute | solution.py:364
  92.3 8.8 %collective-permute-start.19 = (f32[1,32,128]{2,1,0:T(8,128)S(1)}, f32[1,32,128]{2,1,0:T(8,128)S(1)}, u32[]{:S(2)}, u32[]{:S(2)}) collective-permute-start(f32[1,32,128]{2,1,0:T(8,128)S(1)} %get-tuple-element.73), channel_id=1, source_target_pairs={{0,16},{16,0},{32,48},{48,32},{64,80},{80,64},{96,112},{112,96},{1... | collective-permute-start | bytes 49160 | tf_op jit(solution)/shard_map/ppermute | solution.py:377
  95.1 6.0 %collective-permute-start.17 = (f32[8,128]{1,0:T(8,128)S(1)}, f32[8,128]{1,0:T(8,128)S(1)}, u32[]{:S(2)}, u32[]{:S(2)}) collective-permute-start(f32[8,128]{1,0:T(8,128)S(1)} %get-tuple-element.69), channel_id=1, source_target_pairs={{0,1},{1,2},{2,3},{3,4},{4,5},{5,6},{6,7},{7,8},{8,9},{9,10},{10,1... | collective-permute-start | bytes 12296 | tf_op jit(solution)/shard_map/ppermute | solution.py:364
  96.3 4.8 %collective-permute-start.18 = (f32[8,128]{1,0:T(8,128)S(1)}, f32[8,128]{1,0:T(8,128)S(1)}, u32[]{:S(2)}, u32[]{:S(2)}) collective-permute-start(f32[8,128]{1,0:T(8,128)S(1)} %get-tuple-element.70), channel_id=1, source_target_pairs={{0,15},{1,0},{2,1},{3,2},{4,3},{5,4},{6,5},{7,6},{8,7},{9,8},{10,9... | collective-permute-start | bytes 12296 | tf_op jit(solution)/shard_map/ppermute | solution.py:364
  (5 other events, 211.4 us)

commit v3 on v2

v3 whole, which is shorter than its diff:
```python
import jax
import jax.numpy as jnp
from jax import lax
from jax.experimental import pallas as pl
from jax.experimental.pallas import tpu as pltpu
from jax.sharding import PartitionSpec as P

ROWS = 16
LANES = 128
RATE_MID = 3.7
RATE_SCALE = 10500.0
COEF_SCALE = 1374.0
COEF_BASE = 23.0
SEED_SCALE = 1023.0
SEED_BASE = 31.0
ENCODE_VMEM = 60 * 1024 * 1024
STEP_VMEM = 16 * 1024 * 1024


def squeezed(value, base, scale):
    size = jnp.log2(jnp.maximum(jnp.abs(value), 2.0**-base))
    size = size * scale + (base * scale + 0.5)
    return jnp.where(value < 0.0, -size, size).astype(jnp.int32).astype(jnp.int16)


def spread_out(code, base, scale):
    code = code.astype(jnp.int32).astype(jnp.float32)
    size = jnp.exp2(jnp.abs(code) * (1.0 / scale) - base)
    return jnp.where(code > 0.0, size, jnp.where(code < 0.0, -size, 0.0))


def encode_body(
    stored_ref, seed_ref, length_ref, out_ref, pieces, seed, length, codes, in_sems, more_sems,
    out_sems,
):
    steps, slots = stored_ref.shape[:2]
    owners = out_ref.shape[0]
    cap = slots // owners
    rows = 8 * ROWS
    first = [
        pltpu.make_async_copy(seed_ref, seed, more_sems.at[0]),
        pltpu.make_async_copy(length_ref, length, more_sems.at[1]),
    ]
    arrivals = [
        pltpu.make_async_copy(stored_ref.at[step], pieces.at[step], in_sems.at[step])
        for step in range(steps)
    ]
    for copy in first + arrivals:
        copy.start()
    row = lax.broadcasted_iota(jnp.int32, (rows, rows), 0)
    column = lax.broadcasted_iota(jnp.int32, (rows, rows), 1)
    picked = (row % ROWS) * 8 + row // ROWS == column
    order = jnp.where(picked, 1.0, 0.0).astype(jnp.bfloat16)
    for copy in first:
        copy.wait()
    decay, _, _ = powers(length[...])
    field = [seed[layer] for layer in range(seed.shape[0])]
    _, total = chain(field, decay, jnp.zeros_like(decay))
    total = squeezed(total, SEED_BASE, SEED_SCALE)
    per = 2 * cap
    half = total.shape[0] // 2
    for owner in range(owners):
        for block in range(half // ROWS):
            top = half * (owner % 2) + ROWS * block
            codes[owner, steps * per + block] = total[top : top + ROWS, :]

    def mixed(step, slot):
        cells = pieces[step, slot].astype(jnp.float32)
        return jnp.concatenate(
            [cells[:, LANES * r : LANES * (r + 1)] for r in range(ROWS)], axis=0
        ).astype(jnp.bfloat16)

    departures = []

    def depart(start, count):
        copy = pltpu.make_async_copy(
            codes.at[:, pl.ds(start, count)],
            out_ref.at[:, pl.ds(start, count)],
            out_sems.at[len(departures)],
        )
        copy.start()
        departures.append(copy)

    depart(steps * per, half // ROWS)
    for step in range(steps):
        arrivals[step].wait()
        for slot in range(0, slots, cap):
            both = jnp.concatenate([mixed(step, slot + c) for c in range(cap)], axis=1)
            parts = jnp.dot(order, both, preferred_element_type=jnp.float32)

            def part(index):
                return parts[ROWS * index : ROWS * (index + 1), :]

            squares = part(1) * part(1)
            for index in range(2, 7):
                squares = squares + part(index) * part(index)
            slope = jnp.tanh(part(0))
            total = 1.0 + squares * (1.0 / 6.0)
            rate = total * lax.rsqrt(total) * jnp.exp(0.5 * slope)
            coef = (0.1 * part(7)) * rate * (1.0 - slope * slope)
            coef_code = squeezed(coef, COEF_BASE, COEF_SCALE)
            rate_code = jnp.round((rate - RATE_MID) * RATE_SCALE)
            rate_code = rate_code.astype(jnp.int32).astype(jnp.int16)
            for c in range(cap):
                lanes = slice(LANES * c, LANES * (c + 1))
                codes[slot // cap, per * step + 2 * c] = rate_code[:, lanes]
                codes[slot // cap, per * step + 2 * c + 1] = coef_code[:, lanes]
        depart(per * step, per)
    for copy in departures:
        copy.wait()


def encode(stored, seed, length):
    steps, _, _, owners, cap, comps, cells = stored.shape
    flat = stored.reshape(steps, owners * cap, comps, cells)
    shape = (owners, steps * cap * 2 + seed.shape[1] // (2 * ROWS), ROWS, LANES)
    return pl.pallas_call(
        encode_body,
        in_specs=[pl.BlockSpec(memory_space=pl.ANY)] * 3,
        out_specs=pl.BlockSpec(memory_space=pl.ANY),
        out_shape=jax.ShapeDtypeStruct(shape, jnp.int16),
        scratch_shapes=[
            pltpu.VMEM(flat.shape, jnp.bfloat16),
            pltpu.VMEM(seed.shape, jnp.float32),
            pltpu.VMEM(length.shape, jnp.float32),
            pltpu.VMEM(shape, jnp.int16),
            pltpu.SemaphoreType.DMA((steps,)),
            pltpu.SemaphoreType.DMA((2,)),
            pltpu.SemaphoreType.DMA((steps + 1,)),
        ],
        compiler_params=pltpu.CompilerParams(vmem_limit_bytes=ENCODE_VMEM),
    )(flat, seed, length)


def decoded(info_ref, rec_ref, step, layer, field):
    pieces = []
    for quarter in range(4):
        held = info_ref[16 * step + 4 * layer + quarter]
        code = rec_ref[held // 2, 4 * step + 2 * (held % 2) + field]
        if field == 0:
            code = code.astype(jnp.int32).astype(jnp.float32)
            pieces.append(code * (1.0 / RATE_SCALE) + RATE_MID)
        else:
            pieces.append(spread_out(code, COEF_BASE, COEF_SCALE))
    return jnp.concatenate(pieces, axis=0)


def halos(info_ref, low_ref, high_ref, left_ref, right_ref):
    low = jnp.where(info_ref[64] == 0, 0.0, low_ref[...])
    high = jnp.where(info_ref[64] == info_ref[65] - 1, 0.0, high_ref[...])
    return low, high, left_ref[...], right_ref[...]


def radial(x):
    lane = lax.broadcasted_iota(jnp.int32, x.shape, 1)
    inner = jnp.where(lane == 0, 0.0, pltpu.roll(x, 1, axis=1))
    outer = jnp.where(lane == x.shape[1] - 1, 0.0, pltpu.roll(x, x.shape[1] - 1, axis=1))
    return inner + outer


def laplace(field, low, high, left=None, right=None):
    layers = len(field)
    azimuths = field[0].shape[0]
    row = lax.broadcasted_iota(jnp.int32, field[0].shape, 0)
    out = []
    for layer in range(layers):
        x = field[layer]
        below = low if layer == 0 else field[layer - 1]
        above = high if layer == layers - 1 else field[layer + 1]
        first = 0.0 if left is None else left[layer : layer + 1, :]
        last = 0.0 if right is None else right[layer : layer + 1, :]
        before = jnp.where(row == 0, first, pltpu.roll(x, 1, axis=0))
        after = jnp.where(row == azimuths - 1, last, pltpu.roll(x, azimuths - 1, axis=0))
        out.append(((below + above) + (before + after)) + radial(x) - 6.0 * x)
    return out


def chain(field, decay, carry):
    layers = len(field)
    out = [None] * layers
    for layer in reversed(range(layers)):
        out[layer] = carry
        carry = decay * carry + (1.0 - decay) * field[layer]
    return out, carry


def put_edges(field, low_ref, high_ref, left_ref, right_ref):
    layers = len(field)
    azimuths = field[0].shape[0]
    low_ref[...] = field[0]
    high_ref[...] = field[-1]
    for layer in range(layers):
        left_ref[layer : layer + 1, :] = field[layer][0:1, :]
        right_ref[layer : layer + 1, :] = field[layer][azimuths - 1 : azimuths, :]


def powers(length):
    decay = jnp.exp(-1.0 / length)
    cube = decay * decay * decay
    return decay, decay * cube, 4.0 * (1.0 - decay) * cube


def half_powers(info_ref, length_ref):
    half = length_ref.shape[0] // 2
    return powers(length_ref[pl.ds(half * (info_ref[64] % 2), half), :])


def halves(info_ref, values, scratch, keep_ref, give_ref):
    mine = info_ref[64] % 2
    half = scratch.shape[1] // 2
    for index, value in enumerate(values):
        scratch[index] = value
    for index in range(len(values)):
        keep_ref[index] = scratch[index, pl.ds(half * mine, half), :]
        give_ref[index] = scratch[index, pl.ds(half * (1 - mine), half), :]


def restored(info_ref, mine_ref, got_ref, scratch):
    mine = info_ref[64] % 2
    half = scratch.shape[1] // 2
    count = scratch.shape[0]
    for index in range(count):
        scratch[index, pl.ds(half * mine, half), :] = mine_ref[index]
        scratch[index, pl.ds(half * (1 - mine), half), :] = got_ref[index]
    return [scratch[index] for index in range(count)]


def cores(info_ref, keep_ref, got_ref):
    upper_here = info_ref[64] % 2 == 1
    own = [keep_ref[index] for index in range(keep_ref.shape[0])]
    other = [got_ref[index] for index in range(got_ref.shape[0])]
    upper = [jnp.where(upper_here, a, b) for a, b in zip(own, other)]
    lower = [jnp.where(upper_here, b, a) for a, b in zip(own, other)]
    return upper, lower


def share_out(info_ref, upper, lower, mine_ref, other_ref):
    upper_here = info_ref[64] % 2 == 1
    for index, (a, b) in enumerate(zip(upper, lower)):
        mine_ref[index] = jnp.where(upper_here, a, b)
        other_ref[index] = jnp.where(upper_here, b, a)


def applied(carry, here, fall, cross):
    out = [sums + fall * value for value, sums in zip(carry, here)]
    if len(carry) > 1:
        out[1] = out[1] + cross * carry[0]
    return tuple(out)


def climbed(info_ref, sums_ref, fall, cross):
    chips, count = sums_ref.shape[:2]

    def climb(k, total):
        here = [sums_ref[chips - 1 - k, index] for index in range(count)]
        return applied(total, here, fall * fall, 2.0 * fall * cross)

    zero = jnp.zeros_like(fall)
    return lax.fori_loop(0, chips - 1 - info_ref[64] // 2, climb, (zero,) * count)


def answered(gain, share, decay):
    climbs, _ = chain(share, decay, jnp.zeros_like(decay))
    return [g * s + c for g, s, c in zip(gain, share, climbs)]


def seed_carry_body(info_ref, rec_ref, length_ref, mine_ref, other_ref):
    _, fall, _ = half_powers(info_ref, length_ref)
    peers, blocks = rec_ref.shape[:2]
    count = fall.shape[0] // ROWS

    def total_of(peer):
        code = [rec_ref[peer, blocks - count + block] for block in range(count)]
        return jnp.concatenate(
            [spread_out(part, SEED_BASE, SEED_SCALE) for part in code], axis=0
        )

    upper = info_ref[64] // 2 * 2 + 1
    above = lax.fori_loop(
        0,
        peers - 1 - upper,
        lambda k, value: fall * value + total_of(peers - 1 - k),
        jnp.zeros_like(fall),
    )
    below = fall * above + total_of(upper)
    share_out(info_ref, (above,), (below,), mine_ref, other_ref)


def first_body(
    info_ref, rec_ref, lt_ref, lr_ref, low_ref, high_ref, left_ref, right_ref, length_ref,
    mine_ref, got_ref, new_lt_ref, new_lr_ref, source_ref, up_ref, down_ref, keep_ref, give_ref,
    carried, scratch,
):
    layers = lt_ref.shape[0]
    decay, _, _ = powers(length_ref[...])
    (zero,) = restored(info_ref, mine_ref, got_ref, carried)
    lt = [lt_ref[layer] for layer in range(layers)]
    lr = [lr_ref[layer] for layer in range(layers)]
    spread = laplace(lt, *halos(info_ref, low_ref, high_ref, left_ref, right_ref))
    new_lt = [
        lt[l] + 0.15 * spread[l] + decoded(info_ref, rec_ref, 3, l, 1) * lr[l]
        for l in range(layers)
    ]
    climbs, _ = chain(lr, decay, zero)
    lr = [
        -0.3 * lt[l] + (1.0 + 0.2 * decoded(info_ref, rec_ref, 3, l, 0)) * lr[l] + climbs[l]
        for l in range(layers)
    ]
    source = [decoded(info_ref, rec_ref, 2, l, 1) * lr[l] for l in range(layers)]
    up_ref[0], up_ref[1], up_ref[2] = new_lt[-2], new_lt[-1], source[-1]
    down_ref[0], down_ref[1], down_ref[2] = new_lt[0], new_lt[1], source[0]
    nothing = jnp.zeros_like(decay)
    _, now = chain(lr, decay, nothing)
    gain = [1.0 + 0.2 * decoded(info_ref, rec_ref, 2, l, 0) for l in range(layers)]
    after = [a - 0.3 * new_lt[l] for l, a in enumerate(answered(gain, lr, decay))]
    _, later = chain(after, decay, nothing)
    halves(info_ref, (now, later), scratch, keep_ref, give_ref)
    for l in range(layers):
        new_lt_ref[l] = new_lt[l]
        new_lr_ref[l] = lr[l]
        source_ref[l] = source[l]


def pair_chip_body(info_ref, keep_ref, got_ref, length_ref, out_ref):
    _, fall, cross = half_powers(info_ref, length_ref)
    upper, lower = cores(info_ref, keep_ref, got_ref)
    total = applied(upper, lower, fall, cross)
    for chip in range(out_ref.shape[0]):
        for index, value in enumerate(total):
            out_ref[chip, index] = value


def reach_body(
    info_ref, lt_ref, source_ref, low_ref, high_ref, new_lt_ref, left_out, right_out,
):
    layers, azimuths, _ = lt_ref.shape
    bottom = info_ref[64] == 0
    top = info_ref[64] == info_ref[65] - 1
    low = [jnp.where(bottom, 0.0, low_ref[index]) for index in range(3)]
    high = [jnp.where(top, 0.0, high_ref[index]) for index in range(3)]
    lt = [low[1], *[lt_ref[l] for l in range(layers)], high[0]]
    source = [low[2], *[source_ref[l] for l in range(layers)], high[2]]
    spread = laplace(lt, low[0], high[1])
    new_lt = [lt[l] + 0.15 * spread[l] + source[l] for l in range(layers + 2)]
    new_lt[0] = jnp.where(bottom, 0.0, new_lt[0])
    new_lt[-1] = jnp.where(top, 0.0, new_lt[-1])
    sides = ((left_out, 0, 1), (right_out, azimuths - 1, azimuths - 2))
    for out, edge, inside in sides:
        for l in range(layers + 2):
            out[l : l + 1, :] = lt[l][edge : edge + 1, :]
        out[layers + 2 : layers + 4, :] = jnp.zeros_like(out[layers + 2 : layers + 4, :])
        for l in range(layers):
            out[8 + l : 9 + l, :] = lt[l + 1][inside : inside + 1, :]
            out[12 + l : 13 + l, :] = source[l + 1][edge : edge + 1, :]
    for l in range(layers + 2):
        new_lt_ref[l] = new_lt[l]


def beyond(there, here):
    middle = there[1:5]
    total = (there[0:4] + there[2:6]) + (there[8:12] + here[1:5]) + radial(middle)
    return middle + 0.15 * (total - 6.0 * middle) + there[12:16]


def second_body(
    info_ref, rec_ref, old_lt_ref, lr_ref, lt_ref, own_left_ref, own_right_ref, left_ref,
    right_ref, length_ref, new_lt_ref, sides_ref, keep_ref, give_ref, scratch,
):
    layers, azimuths, radials = lr_ref.shape
    decay, _, _ = powers(length_ref[...])
    nothing = jnp.zeros_like(decay)
    left, right = left_ref[...], right_ref[...]
    sides_ref[0:layers, :] = beyond(left, own_left_ref[...])
    sides_ref[layers : 2 * layers, :] = beyond(right, own_right_ref[...])
    row = lax.broadcasted_iota(jnp.int32, (azimuths, radials), 0)
    new_lt = []
    for l in range(layers + 2):
        missing = jnp.where(
            row == 0,
            left[l : l + 1, :],
            jnp.where(row == azimuths - 1, right[l : l + 1, :], 0.0),
        )
        new_lt.append(lt_ref[l] + 0.15 * missing)
        new_lt_ref[l] = new_lt[l]
    new_lt = new_lt[1:-1]
    one = [1.0 + 0.2 * decoded(info_ref, rec_ref, 2, l, 0) for l in range(layers)]
    two = [1.0 + 0.2 * decoded(info_ref, rec_ref, 1, l, 0) for l in range(layers)]
    lr = [lr_ref[layer] for layer in range(layers)]
    lr = [a - 0.3 * old_lt_ref[l] for l, a in enumerate(answered(one, lr, decay))]
    lr = [a - 0.3 * new_lt[l] for l, a in enumerate(answered(two, lr, decay))]
    _, later = chain(lr, decay, nothing)
    share = [None] * layers
    power = jnp.ones_like(decay)
    for layer in reversed(range(layers)):
        share[layer] = power
        power = decay * power
    _, weight = chain(answered(two, share, decay), decay, nothing)
    halves(info_ref, (later, weight), scratch, keep_ref, give_ref)


def pair_carry_body(
    info_ref, keep_ref, got_ref, more_ref, more_got_ref, sums_ref, length_ref,
    mine_ref, other_ref, out_ref,
):
    _, fall, cross = half_powers(info_ref, length_ref)
    above = climbed(info_ref, sums_ref, fall, cross)
    upper, _ = cores(info_ref, keep_ref, got_ref)
    below = applied(above, upper, fall, cross)
    share_out(info_ref, above, below, mine_ref, other_ref)
    upper, lower = cores(info_ref, more_ref, more_got_ref)
    upper = upper[0] + upper[1] * above[0] + cross * above[1]
    lower = lower[0] + lower[1] * below[0] + cross * below[1]
    total = lower + fall * upper
    for peer in range(out_ref.shape[0]):
        out_ref[peer] = jnp.where(info_ref[64] // 2 == peer // 2, upper, total)


def third_body(
    info_ref, rec_ref, seed_ref, one_ref, lt_ref, lr_ref, sides_ref, length_ref, face_ref,
    mine_ref, got_ref, new_lt_ref, new_lr_ref, flux_ref, low_out, high_out, left_out, right_out,
    scratch,
):
    layers, azimuths, radials = lr_ref.shape
    decay, _, _ = powers(length_ref[...])
    one, two = restored(info_ref, mine_ref, got_ref, scratch)
    before = [one_ref[layer] for layer in range(layers)]
    lt = [lt_ref[layer + 1] for layer in range(layers)]
    lr = [lr_ref[layer] for layer in range(layers)]
    climbs, _ = chain(lr, decay, one)
    lr = [
        -0.3 * before[l]
        + (1.0 + 0.2 * decoded(info_ref, rec_ref, 2, l, 0)) * lr[l]
        + climbs[l]
        for l in range(layers)
    ]
    sides = sides_ref[...]
    spread = laplace(lt, lt_ref[0], lt_ref[layers + 1], sides[:layers], sides[layers:])
    new_lt = [
        lt[l] + 0.15 * spread[l] + decoded(info_ref, rec_ref, 1, l, 1) * lr[l]
        for l in range(layers)
    ]
    put_edges(new_lt, low_out, high_out, left_out, right_out)
    climbs, _ = chain(lr, decay, two)
    for l in range(layers):
        new_lt_ref[l] = new_lt[l]
        new_lr_ref[l] = (
            -0.3 * lt[l] + (1.0 + 0.2 * decoded(info_ref, rec_ref, 1, l, 0)) * lr[l] + climbs[l]
        )
    lane = lax.broadcasted_iota(jnp.int32, (azimuths, radials), 1)
    ones = jnp.ones((8, radials), jnp.float32)
    for l in range(layers):
        kept = jnp.where(
            lane == face_ref[l], (seed_ref[l] + before[l]) + (lt[l] + new_lt[l]), 0.0
        )
        row = lax.dot_general(
            ones,
            kept,
            (((1,), (1,)), ((), ())),
            precision=lax.Precision.HIGHEST,
            preferred_element_type=jnp.float32,
        )[0:1, :]
        twice = jnp.concatenate([row, row], axis=1)
        flux_ref[l : l + 1, :] = twice
        left_out[layers + l : layers + l + 1, :] = twice
        right_out[layers + l : layers + l + 1, :] = twice


def last_body(
    info_ref, weight_ref, rec_ref, lt_ref, lr_ref, low_ref, high_ref, left_ref, right_ref,
    length_ref, sums_ref, flux_ref, new_lt_ref, new_lr_ref, heat_ref,
):
    layers, azimuths, radials = lt_ref.shape
    band = weight_ref.shape[0] // 2
    decay, fall, _ = powers(length_ref[...])
    chips = sums_ref.shape[0] // 2
    here = info_ref[64] // 2

    def total_of(chip):
        return jnp.concatenate([sums_ref[2 * chip], sums_ref[2 * chip + 1]], axis=0)

    above = lax.fori_loop(
        0,
        chips - 1 - here,
        lambda k, value: fall * fall * value + total_of(chips - 1 - k),
        jnp.zeros_like(fall),
    )
    three = jnp.where(info_ref[64] % 2 == 1, above, fall * above + total_of(here))
    lt = [lt_ref[layer] for layer in range(layers)]
    lr = [lr_ref[layer] for layer in range(layers)]
    spread = laplace(lt, *halos(info_ref, low_ref, high_ref, left_ref, right_ref))
    climbs, _ = chain(lr, decay, three)
    for l in range(layers):
        new_lt_ref[l] = lt[l] + 0.15 * spread[l] + decoded(info_ref, rec_ref, 0, l, 1) * lr[l]
        new_lr_ref[l] = (
            -0.3 * lt[l]
            + (1.0 + 0.2 * decoded(info_ref, rec_ref, 0, l, 0)) * lr[l]
            + climbs[l]
        )
    lane = lax.broadcasted_iota(jnp.int32, (layers, radials), 1)
    ring = jnp.where(
        lane < azimuths,
        flux_ref[...],
        jnp.where(
            lane < azimuths + band,
            right_ref[layers : 2 * layers, :],
            left_ref[layers : 2 * layers, :],
        ),
    )
    heat = jnp.zeros_like(ring)
    for offset in range(-band, band + 1):
        heat = heat + weight_ref[offset + band] * pltpu.roll(ring, (-offset) % radials, axis=1)
    heat_ref[...] = heat[:, :azimuths]


def run(body, scalars, args, shapes, scratch=()):
    smem = pl.BlockSpec(memory_space=pltpu.SMEM)
    vmem = pl.BlockSpec(memory_space=pltpu.VMEM)
    return pl.pallas_call(
        body,
        in_specs=[smem] * len(scalars) + [vmem] * len(args),
        out_specs=[vmem] * len(shapes),
        out_shape=[jax.ShapeDtypeStruct(shape, jnp.float32) for shape in shapes],
        scratch_shapes=[pltpu.VMEM(shape, jnp.float32) for shape in scratch],
        compiler_params=pltpu.CompilerParams(vmem_limit_bytes=STEP_VMEM),
    )(*scalars, *args)


def turned(value, axis, shift):
    count = lax.axis_size(axis)
    return lax.ppermute(value, axis, [(i, (i + shift) % count) for i in range(count)])


def exchanged(low, high, left, right):
    return (
        turned(high, "axial", 1),
        turned(low, "axial", -1),
        turned(right, "azim", 1),
        turned(left, "azim", -1),
    )


def swapped(value):
    return lax.ppermute(value, "axial", [(i, i ^ 1) for i in range(lax.axis_size("axial"))])


def between_chips(value):
    axial = lax.axis_size("axial")
    groups = [list(range(core, axial, 2)) for core in range(2)]
    return lax.all_to_all(value, "axial", 0, 0, tiled=True, axis_index_groups=groups)


def local(stored, holder, seed_temp, seed_disloc, decay_length, face_radius, kernel):
    layers, azimuths, radials = seed_temp.shape
    axial, me = lax.axis_size("axial"), lax.axis_index("axial")
    wanted = lax.dynamic_index_in_dim(holder, me, 1, keepdims=False).reshape(-1)
    info = jnp.concatenate([wanted, jnp.stack([me, axial]).astype(jnp.int32)])
    plane = (azimuths, radials)
    side = (layers, radials)
    wide = (2 * layers, radials)
    block = (layers, azimuths, radials)

    def half(count):
        return (count, azimuths // 2, radials)

    def copies(count):
        return (axial // 2, *half(count))

    codes = encode(stored, seed_disloc, decay_length)
    pieces = lax.all_to_all(codes, "axial", 0, 0, tiled=True)
    halo = exchanged(
        seed_temp[0], seed_temp[layers - 1], seed_temp[:, 0], seed_temp[:, azimuths - 1]
    )
    pieces, *halo = lax.optimization_barrier((pieces, *halo))
    mine, other = run(seed_carry_body, (info,), (pieces, decay_length), [half(1)] * 2)
    lt1, lr1, source, up, down, keep, give = run(
        first_body,
        (info,),
        (pieces, seed_temp, seed_disloc, *halo, decay_length, mine, swapped(other)),
        [block, block, block, (3, *plane), (3, *plane), half(2), half(2)],
        [(1, *plane), (2, *plane)],
    )
    got = swapped(give)
    low, high = turned(up, "axial", 1), turned(down, "axial", -1)
    got, low, high = lax.optimization_barrier((got, low, high))
    (total,) = run(pair_chip_body, (info,), (keep, got, decay_length), [copies(2)])
    sums = between_chips(total)
    lt2, left, right = run(
        reach_body,
        (info,),
        (lt1, source, low, high),
        [(layers + 2, *plane), (16, radials), (16, radials)],
    )
    before, after = turned(right, "azim", 1), turned(left, "azim", -1)
    lt2, sides, more, give = run(
        second_body,
        (info,),
        (pieces, lt1, lr1, lt2, left, right, before, after, decay_length),
        [(layers + 2, *plane), wide, half(2), half(2)],
        [(2, *plane)],
    )
    more_got = swapped(give)
    sums, more_got = lax.optimization_barrier((sums, more_got))
    mine, other, total = run(
        pair_carry_body,
        (info,),
        (keep, got, more, more_got, sums, decay_length),
        [half(2), half(2), (axial, *half(1)[1:])],
    )
    sums = lax.all_to_all(total, "axial", 0, 0, tiled=True)
    lt3, lr3, flux, *rim = run(
        third_body,
        (info,),
        (
            pieces, seed_temp, lt1, lt2, lr1, sides, decay_length, face_radius[:, :, None],
            mine, swapped(other),
        ),
        [block, block, side, plane, plane, wide, wide],
        [(2, *plane)],
    )
    halo = exchanged(*rim)
    return tuple(
        run(
            last_body,
            (info, kernel),
            (pieces, lt3, lr3, *halo, decay_length, sums, flux),
            [block, block, (layers, azimuths)],
        )
    )


def solution(mesh):
    in_specs = (
        P(None, "axial", "azim", None, None, None, None),
        P(),
        P("axial", "azim", None),
        P("axial", "azim", None),
        P("azim", None),
        P("axial", "azim"),
        P(),
    )
    out_specs = (P("axial", "azim", None), P("axial", "azim", None), P("axial", "azim"))
    return jax.shard_map(local, mesh=mesh, in_specs=in_specs, out_specs=out_specs, check_vma=False)
```

time: 103 us -> 91.8 us (0.89)
  starting transfers between devices: 48.7 us -> 42.5 us
  waiting for transfers between devices: 37.3 us -> 34.6 us
  Pallas kernels: 15.5 us -> 13.3 us
    ppermute x16 -> x12, starting transfers between devices: 27.7 us -> 19.1 us  [turned(): lax.ppermute(value, axis, [(i, (i + shift) % count) for i in range(count)])]
    ppermute x16 -> x12, waiting for transfers between devices: 27.7 us -> 24 us  [turned(): lax.ppermute(value, axis, [(i, (i + shift) % count) for i in range(count)])]
    all_to_all x3, starting transfers between devices: 17 us -> 19.6 us  [the longest x1 10.1 us: local(): pieces = lax.all_to_all(codes, 'axial', 0, 0, tiled=True)]
    pallas_call x1, Pallas kernels: 7.32 us -> 4.73 us  [encode(): pl.pallas_call(encode_body, in_specs=[pl.BlockSpec(memory_space=pl.ANY)]...]
  transfers between devices with their start and end apart: 23 -> 19, of which waited for: 14 -> 13; matrix products, arithmetic and copies ran while one was open for 0% -> 0% of each run, Pallas kernels for 1% -> 3%
where the time goes in v3:
time: 91.8 us; the launch traced here: 91.5 us
  starting transfers between devices  42.5 us (46%)
  waiting for transfers between devices  34.6 us (38%)
  Pallas kernels  13.3 us (14%)
    ppermute x12, waiting for transfers between devices, turned(): lax.ppermute(value, axis, [(i, (i + shift) % count) for i in range(count)])  24 us
    ppermute x12, starting transfers between devices, turned(): lax.ppermute(value, axis, [(i, (i + shift) % count) for i in range(count)])  19.1 us
    all_to_all x1, starting transfers between devices, local(): pieces = lax.all_to_all(codes, 'axial', 0, 0, tiled=True)  10.1 us
    pallas_call x8, Pallas kernels, run(): pl.pallas_call(body, in_specs=[smem] * len(scalars) + [vmem] * len(args),...  8.55 us
    all_to_all x1, starting transfers between devices, between_chips(): lax.all_to_all(value, 'axial', 0, 0, tiled=True, axis_index_groups=groups)  4.9 us
    pallas_call x1, Pallas kernels, encode(): pl.pallas_call(encode_body, in_specs=[pl.BlockSpec(memory_space=pl.ANY)]...  4.73 us
    all_to_all x1, starting transfers between devices, local(): sums = lax.all_to_all(total, 'axial', 0, 0, tiled=True)  4.63 us
    ppermute x4, waiting for transfers between devices, swapped(): lax.ppermute(value, 'axial', [(i, i ^ 1) for i in range(lax.axis_size('ax...  3.87 us
  transfers between devices with their start and end apart: 19, of which 13 were waited for; matrix products, arithmetic and copies ran while one was open for 0% of the time, Pallas kernels for 3%

profile of v3, /device:TPU:1, one launch (start us, length us, event | category | flops | bytes accessed | tf_op | source)
XLA Modules:
  0.0 91.5 jit_solution(5466961558471464120)
XLA Ops:
  0.6 4.7 %shard_map.94 = s16[16,18,16,128]{3,2,1,0:T(8,128)(2,1)} custom-call(bf16[4,32,8,2048]{3,2,1,0:T(8,128)(2,1)} %bitcast.13, f32[4,64,128]{2,1,0:T(8,128)} %lr_ref.1, f32[64,128]{1,0:T(8,128)} %length_ref.15), custom_call_target="tpu_custom_call" | custom-call | tf_op jit(solution)/shard_map/pallas_call | solution.py:117
  5.4 10.1 %all-to-all-start = ((s16[16,18,16,128]{3,2,1,0:T(8,128)(2,1)}), s16[16,18,16,128]{3,2,1,0:T(8,128)(2,1)S(1)}, u32[]{:S(2)}, u32[]{:S(2)}) async-start(s16[16,18,16,128]{3,2,1,0:T(8,128)(2,1)} %shard_map.94), calls=%async_computation | async-start | bytes 2359296 | tf_op jit(solution)/shard_map/all_to_all | solution.py:569
  15.6 1.6 %collective-permute-start = (f32[64,128]{1,0:T(8,128)S(1)}, f32[64,128]{1,0:T(8,128)S(1)}, u32[]{:S(2)}, u32[]{:S(2)}) collective-permute-start(f32[64,128]{1,0:T(8,128)S(1)} %get-tuple-element.78), channel_id=1, source_target_pairs={{0,16},{16,32},{32,48},{48,64},{64,80},{80,96},{96,112},{112,128},... | collective-permute-start | bytes 98312 | tf_op jit(solution)/shard_map/ppermute | solution.py:530
  17.2 1.3 %collective-permute-start.2 = (f32[4,128]{1,0:T(4,128)S(1)}, f32[4,128]{1,0:T(4,128)S(1)}, u32[]{:S(2)}, u32[]{:S(2)}) collective-permute-start(f32[4,128]{1,0:T(4,128)S(1)} %bitcast.16), channel_id=1, source_target_pairs={{0,1},{1,2},{2,3},{3,4},{4,5},{5,6},{6,7},{7,8},{8,9},{9,10},{10,1... | collective-permute-start | bytes 6152 | tf_op jit(solution)/shard_map/ppermute | solution.py:530
  18.5 3.8 %collective-permute-start.3 = (f32[4,128]{1,0:T(4,128)S(1)}, f32[4,128]{1,0:T(4,128)S(1)}, u32[]{:S(2)}, u32[]{:S(2)}) collective-permute-start(f32[4,128]{1,0:T(4,128)S(1)} %bitcast.15), channel_id=1, source_target_pairs={{0,15},{1,0},{2,1},{3,2},{4,3},{5,4},{6,5},{7,6},{8,7},{9,8},{10,9... | collective-permute-start | bytes 6152 | tf_op jit(solution)/shard_map/ppermute | solution.py:530
  23.2 18.3 %collective-permute-done.low_ref = f32[64,128]{1,0:T(8,128)S(1)} collective-permute-done((f32[64,128]{1,0:T(8,128)S(1)}, f32[64,128]{1,0:T(8,128)S(1)}, u32[]{:S(2)}, u32[]{:S(2)}) %collective-permute-start) | collective-permute-done | bytes 32800 | tf_op jit(solution)/shard_map/ppermute | solution.py:530
  41.5 2.5 %collective-permute-done.1.high_ref = f32[64,128]{1,0:T(8,128)S(1)} collective-permute-done((f32[64,128]{1,0:T(8,128)S(1)}, f32[64,128]{1,0:T(8,128)S(1)}, u32[]{:S(2)}, u32[]{:S(2)}) %collective-permute-start.1) | collective-permute-done | bytes 32800 | tf_op jit(solution)/shard_map/ppermute | solution.py:530
  44.0 2.1 %all-to-all-done.rec_ref = s16[16,18,16,128]{3,2,1,0:T(8,128)(2,1)S(1)} async-done(((s16[16,18,16,128]{3,2,1,0:T(8,128)(2,1)}), s16[16,18,16,128]{3,2,1,0:T(8,128)(2,1)S(1)}, u32[]{:S(2)}, u32[]{:S(2)}) %all-to-all-start) | async-done | bytes 1179680 | tf_op jit(solution)/shard_map/all_to_all | solution.py:569
  47.0 1.2 %collective-permute-done.4.got_ref = f32[1,32,128]{2,1,0:T(8,128)S(1)} collective-permute-done((f32[1,32,128]{2,1,0:T(8,128)S(1)}, f32[1,32,128]{2,1,0:T(8,128)S(1)}, u32[]{:S(2)}, u32[]{:S(2)}) %collective-permute-start.4) | collective-permute-done | bytes 16416 | tf_op jit(solution)/shard_map/ppermute | solution.py:543
  49.6 2.6 %collective-permute-start.5 = (f32[2,32,128]{2,1,0:T(8,128)S(1)}, f32[2,32,128]{2,1,0:T(8,128)S(1)}, u32[]{:S(2)}, u32[]{:S(2)}) collective-permute-start(f32[2,32,128]{2,1,0:T(8,128)S(1)} %get-tuple-element.49), channel_id=1, source_target_pairs={{0,16},{16,0},{32,48},{48,32},{64,80},{80,64},{96,112},{112,96},{1... | collective-permute-start | bytes 98312 | tf_op jit(solution)/shard_map/ppermute | solution.py:543
  53.5 1.3 %shard_map.99 = f32[8,2,32,128]{3,2,1,0:T(8,128)} custom-call(s32[66]{0:T(128)S(1)} %pad_add_fusion.info_ref, f32[2,32,128]{2,1,0:T(8,128)S(1)} %get-tuple-element.59.keep_ref, f32[2,32,128]{2,1,0:T(8,128)S(1)} %collective-permute-done.5.got_ref, f32[64,128]{1,0:T(8,128)S(1)} %copy-done.1), custom_call_target="tpu_custom_call" | custom-call | tf_op jit(solution)/shard_map/pallas_call | solution.py:518
  54.7 4.9 %all-to-all-start.1 = ((f32[8,2,32,128]{3,2,1,0:T(8,128)}), f32[8,2,32,128]{3,2,1,0:T(8,128)S(1)}, u32[]{:S(2)}, u32[]{:S(2)}) async-start(f32[8,2,32,128]{3,2,1,0:T(8,128)} %shard_map.99), calls=%async_computation.1 | async-start | bytes 524288 | tf_op jit(solution)/shard_map/all_to_all | solution.py:549
  60.4 1.3 %collective-permute-start.8 = (f32[16,128]{1,0:T(8,128)S(1)}, f32[16,128]{1,0:T(8,128)S(1)}, u32[]{:S(2)}, u32[]{:S(2)}) collective-permute-start(f32[16,128]{1,0:T(8,128)S(1)} %get-tuple-element.56.own_right_ref), channel_id=1, source_target_pairs={{0,1},{1,2},{2,3},{3,4},{4,5},{5,6},{6,7},{7,8},{8,9},{9,10},{10,1... | collective-permute-start | bytes 24584 | tf_op jit(solution)/shard_map/ppermute | solution.py:530
  61.7 3.8 %collective-permute-start.9 = (f32[16,128]{1,0:T(8,128)S(1)}, f32[16,128]{1,0:T(8,128)S(1)}, u32[]{:S(2)}, u32[]{:S(2)}) collective-permute-start(f32[16,128]{1,0:T(8,128)S(1)} %get-tuple-element.55.own_left_ref), channel_id=1, source_target_pairs={{0,15},{1,0},{2,1},{3,2},{4,3},{5,4},{6,5},{7,6},{8,7},{9,8},{10,9... | collective-permute-start | bytes 24584 | tf_op jit(solution)/shard_map/ppermute | solution.py:530
  65.5 1.1 %collective-permute-done.8.left_ref = f32[16,128]{1,0:T(8,128)S(1)} collective-permute-done((f32[16,128]{1,0:T(8,128)S(1)}, f32[16,128]{1,0:T(8,128)S(1)}, u32[]{:S(2)}, u32[]{:S(2)}) %collective-permute-start.8) | collective-permute-done | bytes 8224 | tf_op jit(solution)/shard_map/ppermute | solution.py:530
  69.1 2.9 %all-to-all-done.1.sums_ref = f32[8,2,32,128]{3,2,1,0:T(8,128)S(1)} async-done(((f32[8,2,32,128]{3,2,1,0:T(8,128)}), f32[8,2,32,128]{3,2,1,0:T(8,128)S(1)}, u32[]{:S(2)}, u32[]{:S(2)}) %all-to-all-start.1) | async-done | bytes 262176 | tf_op jit(solution)/shard_map/all_to_all | solution.py:549
  72.0 1.3 %shard_map.100 = (f32[2,32,128]{2,1,0:T(8,128)S(1)}, f32[2,32,128]{2,1,0:T(8,128)S(1)}, f32[16,32,128]{2,1,0:T(8,128)}) custom-call(s32[66]{0:T(128)S(1)} %pad_add_fusion.info_ref, f32[2,32,128]{2,1,0:T(8,128)S(1)} %get-tuple-element.59.keep_ref, f32[2,32,128]{2,1,0:T(8,128)S(1)} %collective-permute-done.5.got_ref, ...), custom_call_target="tpu_custom_call" | custom-call | tf_op jit(solution)/shard_map/pallas_call | solution.py:518
  73.4 4.6 %all-to-all-start.2 = ((f32[16,32,128]{2,1,0:T(8,128)}), f32[16,32,128]{2,1,0:T(8,128)S(1)}, u32[]{:S(2)}, u32[]{:S(2)}) async-start(f32[16,32,128]{2,1,0:T(8,128)} %get-tuple-element.73), calls=%async_computation.2 | async-start | bytes 524288 | tf_op jit(solution)/shard_map/all_to_all | solution.py:609
  79.3 1.1 %shard_map.101 = (f32[4,64,128]{2,1,0:T(8,128)S(1)}, f32[4,64,128]{2,1,0:T(8,128)S(1)}, f32[4,128]{1,0:T(4,128)S(1)}, f32[64,128]{1,0:T(8,128)S(1)}, f32[64,128]...) custom-call(s32[66]{0:T(128)S(1)} %pad_add_fusion.info_ref, ...), custom_call_target="tpu_custom_call" | custom-call | tf_op jit(solution)/shard_map/pallas_call | solution.py:518
  80.5 1.7 %collective-permute-start.12 = (f32[64,128]{1,0:T(8,128)S(1)}, f32[64,128]{1,0:T(8,128)S(1)}, u32[]{:S(2)}, u32[]{:S(2)}) collective-permute-start(f32[64,128]{1,0:T(8,128)S(1)} %get-tuple-element.69), channel_id=1, source_target_pairs={{0,16},{16,32},{32,48},{48,64},{64,80},{80,96},{96,112},{112,128},... | collective-permute-start | bytes 98312 | tf_op jit(solution)/shard_map/ppermute | solution.py:530
  82.4 4.7 %collective-permute-start.15 = (f32[8,128]{1,0:T(8,128)S(1)}, f32[8,128]{1,0:T(8,128)S(1)}, u32[]{:S(2)}, u32[]{:S(2)}) collective-permute-start(f32[8,128]{1,0:T(8,128)S(1)} %get-tuple-element.72), channel_id=1, source_target_pairs={{0,15},{1,0},{2,1},{3,2},{4,3},{5,4},{6,5},{7,6},{8,7},{9,8},{10,9... | collective-permute-start | bytes 12296 | tf_op jit(solution)/shard_map/ppermute | solution.py:530
  87.2 1.0 %collective-permute-done.14.left_ref = f32[8,128]{1,0:T(8,128)S(1)} collective-permute-done((f32[8,128]{1,0:T(8,128)S(1)}, f32[8,128]{1,0:T(8,128)S(1)}, u32[]{:S(2)}, u32[]{:S(2)}) %collective-permute-start.14) | collective-permute-done | bytes 4128 | tf_op jit(solution)/shard_map/ppermute | solution.py:530
  88.2 1.8 %all-to-all-done.2.sums_ref = f32[16,32,128]{2,1,0:T(8,128)S(1)} async-done(((f32[16,32,128]{2,1,0:T(8,128)}), f32[16,32,128]{2,1,0:T(8,128)S(1)}, u32[]{:S(2)}, u32[]{:S(2)}) %all-to-all-start.2) | async-done | bytes 262176 | tf_op jit(solution)/shard_map/all_to_all | solution.py:609
  90.0 1.5 %shard_map.102 = (f32[4,64,128]{2,1,0:T(8,128)}, f32[4,64,128]{2,1,0:T(8,128)}, f32[4,64]{1,0:T(4,128)}) custom-call(s32[66]{0:T(128)S(1)} %pad_add_fusion.info_ref, f32[17]{0:T(128)S(1)} %copy-done.4, s16[16,18,16,128]{3,2,1,0:T(8,128)(2,1)S(1)} %all-to-all-done.rec_ref, f32[4,64,128]{2,1,0:T(8,128)S(1)} %get-tuple-element.67.lt_ref, ...), custom_call_target="tpu_custom_call" | custom-call | tf_op jit(solution)/shard_map/pallas_call | solution.py:518
  (41 shorter events, 9.4 us)
Async XLA Ops:
  0.6 21.7 %copy-start = (s32[4,16,16]{2,1,0:T(8,128)S(1)}, s32[4,16,16]{2,1,0:T(8,128)}, u32[]{:S(2)}) copy-start(s32[4,16,16]{2,1,0:T(8,128)} %param.8) | copy-start | bytes 12292
  5.4 40.7 %copy-start.1 = (f32[64,128]{1,0:T(8,128)S(1)}, f32[64,128]{1,0:T(8,128)}, u32[]{:S(2)}) copy-start(f32[64,128]{1,0:T(8,128)} %length_ref.15) | copy-start | bytes 98308
  5.4 40.7 %all-to-all-start = ((s16[16,18,16,128]{3,2,1,0:T(8,128)(2,1)}), s16[16,18,16,128]{3,2,1,0:T(8,128)(2,1)S(1)}, u32[]{:S(2)}, u32[]{:S(2)}) async-start(s16[16,18,16,128]{3,2,1,0:T(8,128)(2,1)} %shard_map.94), calls=%async_computation | async-start | bytes 2359296 | tf_op jit(solution)/shard_map/all_to_all | solution.py:569
  15.5 32.7 %copy-start.3 = (f32[4,64,128]{2,1,0:T(8,128)S(1)}, f32[4,64,128]{2,1,0:T(8,128)}, u32[]{:S(2)}) copy-start(f32[4,64,128]{2,1,0:T(8,128)} %lr_ref.1) | copy-start | bytes 393220
  15.6 26.0 %collective-permute-start = (f32[64,128]{1,0:T(8,128)S(1)}, f32[64,128]{1,0:T(8,128)S(1)}, u32[]{:S(2)}, u32[]{:S(2)}) collective-permute-start(f32[64,128]{1,0:T(8,128)S(1)} %get-tuple-element.78), channel_id=1, source_target_pairs={{0,16},{16,32},{32,48},{48,64},{64,80},{80,96},{96,112},{112,128},... | collective-permute-start | bytes 98312 | tf_op jit(solution)/shard_map/ppermute | solution.py:530
  17.2 26.8 %collective-permute-start.1 = (f32[64,128]{1,0:T(8,128)S(1)}, f32[64,128]{1,0:T(8,128)S(1)}, u32[]{:S(2)}, u32[]{:S(2)}) collective-permute-start(f32[64,128]{1,0:T(8,128)S(1)} %get-tuple-element.77), channel_id=1, source_target_pairs={{0,240},{16,0},{32,16},{48,32},{64,48},{80,64},{96,80},{112,96},{1... | collective-permute-start | bytes 98312 | tf_op jit(solution)/shard_map/ppermute | solution.py:530
  17.2 6.0 %collective-permute-start.2 = (f32[4,128]{1,0:T(4,128)S(1)}, f32[4,128]{1,0:T(4,128)S(1)}, u32[]{:S(2)}, u32[]{:S(2)}) collective-permute-start(f32[4,128]{1,0:T(4,128)S(1)} %bitcast.16), channel_id=1, source_target_pairs={{0,1},{1,2},{2,3},{3,4},{4,5},{5,6},{6,7},{7,8},{8,9},{9,10},{10,1... | collective-permute-start | bytes 6152 | tf_op jit(solution)/shard_map/ppermute | solution.py:530
  18.5 4.7 %collective-permute-start.3 = (f32[4,128]{1,0:T(4,128)S(1)}, f32[4,128]{1,0:T(4,128)S(1)}, u32[]{:S(2)}, u32[]{:S(2)}) collective-permute-start(f32[4,128]{1,0:T(4,128)S(1)} %bitcast.15), channel_id=1, source_target_pairs={{0,15},{1,0},{2,1},{3,2},{4,3},{5,4},{6,5},{7,6},{8,7},{9,8},{10,9... | collective-permute-start | bytes 6152 | tf_op jit(solution)/shard_map/ppermute | solution.py:530
  46.9 1.3 %collective-permute-start.4 = (f32[1,32,128]{2,1,0:T(8,128)S(1)}, f32[1,32,128]{2,1,0:T(8,128)S(1)}, u32[]{:S(2)}, u32[]{:S(2)}) collective-permute-start(f32[1,32,128]{2,1,0:T(8,128)S(1)} %get-tuple-element.45), channel_id=1, source_target_pairs={{0,16},{16,0},{32,48},{48,32},{64,80},{80,64},{96,112},{112,96},{1... | collective-permute-start | bytes 49160 | tf_op jit(solution)/shard_map/ppermute | solution.py:543
  49.1 4.0 %collective-permute-start.6 = (f32[3,64,128]{2,1,0:T(8,128)S(1)}, f32[3,64,128]{2,1,0:T(8,128)S(1)}, u32[]{:S(2)}, u32[]{:S(2)}) collective-permute-start(f32[3,64,128]{2,1,0:T(8,128)S(1)} %get-tuple-element.50), channel_id=1, source_target_pairs={{0,16},{16,32},{32,48},{48,64},{64,80},{80,96},{96,112},{112,128},... | collective-permute-start | bytes 294920 | tf_op jit(solution)/shard_map/ppermute | solution.py:530
  49.1 4.3 %collective-permute-start.7 = (f32[3,64,128]{2,1,0:T(8,128)S(1)}, f32[3,64,128]{2,1,0:T(8,128)S(1)}, u32[]{:S(2)}, u32[]{:S(2)}) collective-permute-start(f32[3,64,128]{2,1,0:T(8,128)S(1)} %get-tuple-element.51), channel_id=1, source_target_pairs={{0,240},{16,0},{32,16},{48,32},{64,48},{80,64},{96,80},{112,96},{1... | collective-permute-start | bytes 294920 | tf_op jit(solution)/shard_map/ppermute | solution.py:530
  49.6 3.5 %collective-permute-start.5 = (f32[2,32,128]{2,1,0:T(8,128)S(1)}, f32[2,32,128]{2,1,0:T(8,128)S(1)}, u32[]{:S(2)}, u32[]{:S(2)}) collective-permute-start(f32[2,32,128]{2,1,0:T(8,128)S(1)} %get-tuple-element.49), channel_id=1, source_target_pairs={{0,16},{16,0},{32,48},{48,32},{64,80},{80,64},{96,112},{112,96},{1... | collective-permute-start | bytes 98312 | tf_op jit(solution)/shard_map/ppermute | solution.py:543
  54.7 17.3 %all-to-all-start.1 = ((f32[8,2,32,128]{3,2,1,0:T(8,128)}), f32[8,2,32,128]{3,2,1,0:T(8,128)S(1)}, u32[]{:S(2)}, u32[]{:S(2)}) async-start(f32[8,2,32,128]{3,2,1,0:T(8,128)} %shard_map.99), calls=%async_computation.1 | async-start | bytes 524288 | tf_op jit(solution)/shard_map/all_to_all | solution.py:549
  60.4 6.2 %collective-permute-start.8 = (f32[16,128]{1,0:T(8,128)S(1)}, f32[16,128]{1,0:T(8,128)S(1)}, u32[]{:S(2)}, u32[]{:S(2)}) collective-permute-start(f32[16,128]{1,0:T(8,128)S(1)} %get-tuple-element.56.own_right_ref), channel_id=1, source_target_pairs={{0,1},{1,2},{2,3},{3,4},{4,5},{5,6},{6,7},{7,8},{8,9},{9,10},{10,1... | collective-permute-start | bytes 24584 | tf_op jit(solution)/shard_map/ppermute | solution.py:530
  61.7 4.9 %collective-permute-start.9 = (f32[16,128]{1,0:T(8,128)S(1)}, f32[16,128]{1,0:T(8,128)S(1)}, u32[]{:S(2)}, u32[]{:S(2)}) collective-permute-start(f32[16,128]{1,0:T(8,128)S(1)} %get-tuple-element.55.own_left_ref), channel_id=1, source_target_pairs={{0,15},{1,0},{2,1},{3,2},{4,3},{5,4},{6,5},{7,6},{8,7},{9,8},{10,9... | collective-permute-start | bytes 24584 | tf_op jit(solution)/shard_map/ppermute | solution.py:530
  66.6 11.6 %copy-start.5 = (s32[4,64]{1,0:T(4,128)S(1)}, s32[4,64]{1,0:T(4,128)}, u32[]{:S(2)}) copy-start(s32[4,64]{1,0:T(4,128)} %param.12) | copy-start | bytes 3076
  67.4 1.7 %collective-permute-start.10 = (f32[2,32,128]{2,1,0:T(8,128)S(1)}, f32[2,32,128]{2,1,0:T(8,128)S(1)}, u32[]{:S(2)}, u32[]{:S(2)}) collective-permute-start(f32[2,32,128]{2,1,0:T(8,128)S(1)} %get-tuple-element.62), channel_id=1, source_target_pairs={{0,16},{16,0},{32,48},{48,32},{64,80},{80,64},{96,112},{112,96},{1... | collective-permute-start | bytes 98312 | tf_op jit(solution)/shard_map/ppermute | solution.py:543
  73.4 16.6 %all-to-all-start.2 = ((f32[16,32,128]{2,1,0:T(8,128)}), f32[16,32,128]{2,1,0:T(8,128)S(1)}, u32[]{:S(2)}, u32[]{:S(2)}) async-start(f32[16,32,128]{2,1,0:T(8,128)} %get-tuple-element.73), calls=%async_computation.2 | async-start | bytes 524288 | tf_op jit(solution)/shard_map/all_to_all | solution.py:609
  78.0 12.0 %copy-start.4 = (f32[17]{0:T(128)S(1)}, f32[17]{0:T(128)}, u32[]{:S(2)}) copy-start(f32[17]{0:T(128)} %weight_ref.1) | copy-start | bytes 208
  78.0 1.3 %collective-permute-start.11 = (f32[2,32,128]{2,1,0:T(8,128)S(1)}, f32[2,32,128]{2,1,0:T(8,128)S(1)}, u32[]{:S(2)}, u32[]{:S(2)}) collective-permute-start(f32[2,32,128]{2,1,0:T(8,128)S(1)} %get-tuple-element.66), channel_id=1, source_target_pairs={{0,16},{16,0},{32,48},{48,32},{64,80},{80,64},{96,112},{112,96},{1... | collective-permute-start | bytes 98312 | tf_op jit(solution)/shard_map/ppermute | solution.py:543
  80.5 7.7 %collective-permute-start.12 = (f32[64,128]{1,0:T(8,128)S(1)}, f32[64,128]{1,0:T(8,128)S(1)}, u32[]{:S(2)}, u32[]{:S(2)}) collective-permute-start(f32[64,128]{1,0:T(8,128)S(1)} %get-tuple-element.69), channel_id=1, source_target_pairs={{0,16},{16,32},{32,48},{48,64},{64,80},{80,96},{96,112},{112,128},... | collective-permute-start | bytes 98312 | tf_op jit(solution)/shard_map/ppermute | solution.py:530
  82.1 6.1 %collective-permute-start.13 = (f32[64,128]{1,0:T(8,128)S(1)}, f32[64,128]{1,0:T(8,128)S(1)}, u32[]{:S(2)}, u32[]{:S(2)}) collective-permute-start(f32[64,128]{1,0:T(8,128)S(1)} %get-tuple-element.70), channel_id=1, source_target_pairs={{0,240},{16,0},{32,16},{48,32},{64,48},{80,64},{96,80},{112,96},{1... | collective-permute-start | bytes 98312 | tf_op jit(solution)/shard_map/ppermute | solution.py:530
  82.1 6.1 %collective-permute-start.14 = (f32[8,128]{1,0:T(8,128)S(1)}, f32[8,128]{1,0:T(8,128)S(1)}, u32[]{:S(2)}, u32[]{:S(2)}) collective-permute-start(f32[8,128]{1,0:T(8,128)S(1)} %get-tuple-element.71), channel_id=1, source_target_pairs={{0,1},{1,2},{2,3},{3,4},{4,5},{5,6},{6,7},{7,8},{8,9},{9,10},{10,1... | collective-permute-start | bytes 12296 | tf_op jit(solution)/shard_map/ppermute | solution.py:530
  82.4 5.7 %collective-permute-start.15 = (f32[8,128]{1,0:T(8,128)S(1)}, f32[8,128]{1,0:T(8,128)S(1)}, u32[]{:S(2)}, u32[]{:S(2)}) collective-permute-start(f32[8,128]{1,0:T(8,128)S(1)} %get-tuple-element.72), channel_id=1, source_target_pairs={{0,15},{1,0},{2,1},{3,2},{4,3},{5,4},{6,5},{7,6},{8,7},{9,8},{10,9... | collective-permute-start | bytes 12296 | tf_op jit(solution)/shard_map/ppermute | solution.py:530
  (1 other events, 10.2 us)

commit v4 on v3

--- a/solution.py
+++ b/solution.py
@@ -13,14 +13,21 @@
 COEF_BASE = 23.0
 SEED_SCALE = 1023.0
 SEED_BASE = 31.0
+SUM_SCALE = 728.0
+SUM_BASE = 36.0
 ENCODE_VMEM = 60 * 1024 * 1024
 STEP_VMEM = 16 * 1024 * 1024
+SPAN_FLOPS = 1_000_000_000
+SPAN_BYTES = 3_000_000
+CHIP_SPAN = 50
+REACH_SPAN = 100
+THIRD_SPAN = 100
 
 
 def squeezed(value, base, scale):
     size = jnp.log2(jnp.maximum(jnp.abs(value), 2.0**-base))
     size = size * scale + (base * scale + 0.5)
-    return jnp.where(value < 0.0, -size, size).astype(jnp.int32).astype(jnp.int16)
+    return jnp.where(value < 0.0, -size, size).astype(jnp.int32)
 
 
 def spread_out(code, base, scale):
@@ -56,7 +63,7 @@
     decay, _, _ = powers(length[...])
     field = [seed[layer] for layer in range(seed.shape[0])]
     _, total = chain(field, decay, jnp.zeros_like(decay))
-    total = squeezed(total, SEED_BASE, SEED_SCALE)
+    total = squeezed(total, SEED_BASE, SEED_SCALE).astype(jnp.int16)
     per = 2 * cap
     half = total.shape[0] // 2
     for owner in range(owners):
@@ -98,7 +105,7 @@
             total = 1.0 + squares * (1.0 / 6.0)
             rate = total * lax.rsqrt(total) * jnp.exp(0.5 * slope)
             coef = (0.1 * part(7)) * rate * (1.0 - slope * slope)
-            coef_code = squeezed(coef, COEF_BASE, COEF_SCALE)
+            coef_code = squeezed(coef, COEF_BASE, COEF_SCALE).astype(jnp.int16)
             rate_code = jnp.round((rate - RATE_MID) * RATE_SCALE)
             rate_code = rate_code.astype(jnp.int32).astype(jnp.int16)
             for c in range(cap):
@@ -228,7 +235,7 @@
 def cores(info_ref, keep_ref, got_ref):
     upper_here = info_ref[64] % 2 == 1
     own = [keep_ref[index] for index in range(keep_ref.shape[0])]
-    other = [got_ref[index] for index in range(got_ref.shape[0])]
+    other = [got_ref[index] for index in range(len(own))]
     upper = [jnp.where(upper_here, a, b) for a, b in zip(own, other)]
     lower = [jnp.where(upper_here, b, a) for a, b in zip(own, other)]
     return upper, lower
@@ -248,11 +255,24 @@
     return tuple(out)
 
 
+def put_sum(out_ref, at, start, code):
+    code = code.astype(jnp.int16)
+    for block in range(code.shape[0] // ROWS):
+        out_ref[at, start + block] = code[ROWS * block : ROWS * (block + 1), :]
+
+
+def got_sum(sums_ref, at, start, count):
+    code = [sums_ref[at, start + block] for block in range(count)]
+    return jnp.concatenate([spread_out(part, SUM_BASE, SUM_SCALE) for part in code], axis=0)
+
+
 def climbed(info_ref, sums_ref, fall, cross):
-    chips, count = sums_ref.shape[:2]
+    chips, blocks = sums_ref.shape[:2]
+    per = fall.shape[0] // ROWS
+    count = blocks // per
 
     def climb(k, total):
-        here = [sums_ref[chips - 1 - k, index] for index in range(count)]
+        here = [got_sum(sums_ref, chips - 1 - k, per * index, per) for index in range(count)]
         return applied(total, here, fall * fall, 2.0 * fall * cross)
 
     zero = jnp.zeros_like(fall)
@@ -288,7 +308,7 @@
 
 def first_body(
     info_ref, rec_ref, lt_ref, lr_ref, low_ref, high_ref, left_ref, right_ref, length_ref,
-    mine_ref, got_ref, new_lt_ref, new_lr_ref, source_ref, up_ref, down_ref, keep_ref, give_ref,
+    mine_ref, got_ref, new_lt_ref, new_lr_ref, source_ref, far_ref, keep_ref, give_ref,
     carried, scratch,
 ):
     layers = lt_ref.shape[0]
@@ -307,8 +327,14 @@
         for l in range(layers)
     ]
     source = [decoded(info_ref, rec_ref, 2, l, 1) * lr[l] for l in range(layers)]
-    up_ref[0], up_ref[1], up_ref[2] = new_lt[-2], new_lt[-1], source[-1]
-    down_ref[0], down_ref[1], down_ref[2] = new_lt[0], new_lt[1], source[0]
+    half = decay.shape[0] // 2
+    up, down = (new_lt[-2], new_lt[-1], source[-1]), (new_lt[0], new_lt[1], source[0])
+    upper_here = info_ref[64] % 2 == 1
+    for index in range(3):
+        far_ref[index] = jnp.where(upper_here, up[index], down[index])
+        near = jnp.where(upper_here, down[index], up[index])
+        give_ref[2 + 2 * index] = near[:half]
+        give_ref[3 + 2 * index] = near[half:]
     nothing = jnp.zeros_like(decay)
     _, now = chain(lr, decay, nothing)
     gain = [1.0 + 0.2 * decoded(info_ref, rec_ref, 2, l, 0) for l in range(layers)]
@@ -325,19 +351,26 @@
     _, fall, cross = half_powers(info_ref, length_ref)
     upper, lower = cores(info_ref, keep_ref, got_ref)
     total = applied(upper, lower, fall, cross)
+    total = [squeezed(value, SUM_BASE, SUM_SCALE) for value in total]
+    per = fall.shape[0] // ROWS
     for chip in range(out_ref.shape[0]):
         for index, value in enumerate(total):
-            out_ref[chip, index] = value
+            put_sum(out_ref, chip, per * index, value)
 
 
 def reach_body(
-    info_ref, lt_ref, source_ref, low_ref, high_ref, new_lt_ref, left_out, right_out,
+    info_ref, lt_ref, source_ref, near_ref, far_ref, new_lt_ref, left_out, right_out,
 ):
     layers, azimuths, _ = lt_ref.shape
     bottom = info_ref[64] == 0
     top = info_ref[64] == info_ref[65] - 1
-    low = [jnp.where(bottom, 0.0, low_ref[index]) for index in range(3)]
-    high = [jnp.where(top, 0.0, high_ref[index]) for index in range(3)]
+    upper_here = info_ref[64] % 2 == 1
+    low, high = [], []
+    for index in range(3):
+        near = jnp.concatenate([near_ref[2 + 2 * index], near_ref[3 + 2 * index]], axis=0)
+        far = jnp.where(jnp.logical_or(bottom, top), 0.0, far_ref[index])
+        low.append(jnp.where(upper_here, near, far))
+        high.append(jnp.where(upper_here, far, near))
     lt = [low[1], *[lt_ref[l] for l in range(layers)], high[0]]
     source = [low[2], *[source_ref[l] for l in range(layers)], high[2]]
     spread = laplace(lt, low[0], high[1])
@@ -410,14 +443,15 @@
     upper, lower = cores(info_ref, more_ref, more_got_ref)
     upper = upper[0] + upper[1] * above[0] + cross * above[1]
     lower = lower[0] + lower[1] * below[0] + cross * below[1]
-    total = lower + fall * upper
+    total = squeezed(lower + fall * upper, SUM_BASE, SUM_SCALE)
+    upper = squeezed(upper, SUM_BASE, SUM_SCALE)
     for peer in range(out_ref.shape[0]):
-        out_ref[peer] = jnp.where(info_ref[64] // 2 == peer // 2, upper, total)
+        put_sum(out_ref, peer, 0, jnp.where(info_ref[64] // 2 == peer // 2, upper, total))
 
 
 def third_body(
     info_ref, rec_ref, seed_ref, one_ref, lt_ref, lr_ref, sides_ref, length_ref, face_ref,
-    mine_ref, got_ref, new_lt_ref, new_lr_ref, flux_ref, low_out, high_out, left_out, right_out,
+    mine_ref, got_ref, new_lt_ref, new_lr_ref, flux_ref, near_out, far_out, left_out, right_out,
     scratch,
 ):
     layers, azimuths, radials = lr_ref.shape
@@ -439,7 +473,12 @@
         lt[l] + 0.15 * spread[l] + decoded(info_ref, rec_ref, 1, l, 1) * lr[l]
         for l in range(layers)
     ]
-    put_edges(new_lt, low_out, high_out, left_out, right_out)
+    upper_here = info_ref[64] % 2 == 1
+    near_out[...] = jnp.where(upper_here, new_lt[0], new_lt[-1])
+    far_out[...] = jnp.where(upper_here, new_lt[-1], new_lt[0])
+    for l in range(layers):
+        left_out[l : l + 1, :] = new_lt[l][0:1, :]
+        right_out[l : l + 1, :] = new_lt[l][azimuths - 1 : azimuths, :]
     climbs, _ = chain(lr, decay, two)
     for l in range(layers):
         new_lt_ref[l] = new_lt[l]
@@ -466,7 +505,7 @@
 
 
 def last_body(
-    info_ref, weight_ref, rec_ref, lt_ref, lr_ref, low_ref, high_ref, left_ref, right_ref,
+    info_ref, weight_ref, rec_ref, lt_ref, lr_ref, near_ref, far_ref, left_ref, right_ref,
     length_ref, sums_ref, flux_ref, new_lt_ref, new_lr_ref, heat_ref,
 ):
     layers, azimuths, radials = lt_ref.shape
@@ -475,8 +514,12 @@
     chips = sums_ref.shape[0] // 2
     here = info_ref[64] // 2
 
+    per = sums_ref.shape[1]
+
     def total_of(chip):
-        return jnp.concatenate([sums_ref[2 * chip], sums_ref[2 * chip + 1]], axis=0)
+        return jnp.concatenate(
+            [got_sum(sums_ref, 2 * chip + core, 0, per) for core in range(2)], axis=0
+        )
 
     above = lax.fori_loop(
         0,
@@ -487,7 +530,11 @@
     three = jnp.where(info_ref[64] % 2 == 1, above, fall * above + total_of(here))
     lt = [lt_ref[layer] for layer in range(layers)]
     lr = [lr_ref[layer] for layer in range(layers)]
-    spread = laplace(lt, *halos(info_ref, low_ref, high_ref, left_ref, right_ref))
+    end = jnp.logical_or(info_ref[64] == 0, info_ref[64] == info_ref[65] - 1)
+    near, far = near_ref[...], jnp.where(end, 0.0, far_ref[...])
+    upper_here = info_ref[64] % 2 == 1
+    low, high = jnp.where(upper_here, near, far), jnp.where(upper_here, far, near)
+    spread = laplace(lt, low, high, left_ref[...], right_ref[...])
     climbs, _ = chain(lr, decay, three)
     for l in range(layers):
         new_lt_ref[l] = lt[l] + 0.15 * spread[l] + decoded(info_ref, rec_ref, 0, l, 1) * lr[l]
@@ -512,16 +559,22 @@
     heat_ref[...] = heat[:, :azimuths]
 
 
-def run(body, scalars, args, shapes, scratch=()):
+def run(body, scalars, args, shapes, scratch=(), span=1):
     smem = pl.BlockSpec(memory_space=pltpu.SMEM)
     vmem = pl.BlockSpec(memory_space=pltpu.VMEM)
     return pl.pallas_call(
         body,
         in_specs=[smem] * len(scalars) + [vmem] * len(args),
         out_specs=[vmem] * len(shapes),
-        out_shape=[jax.ShapeDtypeStruct(shape, jnp.float32) for shape in shapes],
+        out_shape=[
+            jax.ShapeDtypeStruct(shape, jnp.int16 if len(shape) == 4 else jnp.float32)
+            for shape in shapes
+        ],
         scratch_shapes=[pltpu.VMEM(shape, jnp.float32) for shape in scratch],
         compiler_params=pltpu.CompilerParams(vmem_limit_bytes=STEP_VMEM),
+        cost_estimate=pl.CostEstimate(
+            flops=span * SPAN_FLOPS, bytes_accessed=span * SPAN_BYTES, transcendentals=0
+        ),
     )(*scalars, *args)
 
 
@@ -541,6 +594,13 @@
 
 def swapped(value):
     return lax.ppermute(value, "axial", [(i, i ^ 1) for i in range(lax.axis_size("axial"))])
+
+
+def crossed(value):
+    axial = lax.axis_size("axial")
+    return lax.ppermute(
+        value, "axial", [(i, (i - 1 + 2 * (i % 2)) % axial) for i in range(axial)]
+    )
 
 
 def between_chips(value):
@@ -562,8 +622,8 @@
     def half(count):
         return (count, azimuths // 2, radials)
 
-    def copies(count):
-        return (axial // 2, *half(count))
+    def copies(peers, count):
+        return (peers, count * azimuths // (2 * ROWS), ROWS, radials)
 
     codes = encode(stored, seed_disloc, decay_length)
     pieces = lax.all_to_all(codes, "axial", 0, 0, tiled=True)
@@ -572,23 +632,25 @@
     )
     pieces, *halo = lax.optimization_barrier((pieces, *halo))
     mine, other = run(seed_carry_body, (info,), (pieces, decay_length), [half(1)] * 2)
-    lt1, lr1, source, up, down, keep, give = run(
+    lt1, lr1, source, far, keep, give = run(
         first_body,
         (info,),
         (pieces, seed_temp, seed_disloc, *halo, decay_length, mine, swapped(other)),
-        [block, block, block, (3, *plane), (3, *plane), half(2), half(2)],
+        [block, block, block, (3, *plane), half(2), half(8)],
         [(1, *plane), (2, *plane)],
     )
     got = swapped(give)
-    low, high = turned(up, "axial", 1), turned(down, "axial", -1)
-    got, low, high = lax.optimization_barrier((got, low, high))
-    (total,) = run(pair_chip_body, (info,), (keep, got, decay_length), [copies(2)])
+    far = crossed(far)
+    (total,) = run(
+        pair_chip_body, (info,), (keep, got, decay_length), [copies(axial // 2, 2)], span=CHIP_SPAN
+    )
     sums = between_chips(total)
     lt2, left, right = run(
         reach_body,
         (info,),
-        (lt1, source, low, high),
+        (lt1, source, got, far),
         [(layers + 2, *plane), (16, radials), (16, radials)],
+        span=REACH_SPAN,
     )
     before, after = turned(right, "azim", 1), turned(left, "azim", -1)
     lt2, sides, more, give = run(
@@ -604,10 +666,10 @@
         pair_carry_body,
         (info,),
         (keep, got, more, more_got, sums, decay_length),
-        [half(2), half(2), (axial, *half(1)[1:])],
+        [half(2), half(2), copies(axial, 1)],
     )
     sums = lax.all_to_all(total, "axial", 0, 0, tiled=True)
-    lt3, lr3, flux, *rim = run(
+    lt3, lr3, flux, near, far, left, right = run(
         third_body,
         (info,),
         (
@@ -616,8 +678,14 @@
         ),
         [block, block, side, plane, plane, wide, wide],
         [(2, *plane)],
-    )
-    halo = exchanged(*rim)
+        span=THIRD_SPAN,
+    )
+    halo = (
+        swapped(near),
+        crossed(far),
+        turned(right, "azim", 1),
+        turned(left, "azim", -1),
+    )
     return tuple(
         run(
             last_body,

time: 91.8 us -> 87.6 us (0.954)
  waiting for transfers between devices: 34.6 us -> 29.1 us
    all_to_all x1, waiting for transfers between devices: 2.92 us -> 0.01 us  [between_chips(): lax.all_to_all(value, 'axial', 0, 0, tiled=True, axis_index_groups=groups)]
    all_to_all x1, starting transfers between devices: 4.63 us -> 7.3 us  [local(): sums = lax.all_to_all(total, 'axial', 0, 0, tiled=True)]
    ppermute x12 -> x8, starting transfers between devices: 19.1 us -> 16.9 us  [turned(): lax.ppermute(value, axis, [(i, (i + shift) % count) for i in range(count)])]
    ppermute x0 -> x2, starting transfers between devices: none -> 1.68 us  [crossed(): lax.ppermute(value, 'axial', [(i, (i - 1 + 2 * (i % 2)) % axial) for i in...]
    all_to_all x1, waiting for transfers between devices: 1.78 us -> 0.3 us  [local(): sums = lax.all_to_all(total, 'axial', 0, 0, tiled=True)]
    all_to_all x1, starting transfers between devices: 4.9 us -> 3.47 us  [between_chips(): lax.all_to_all(value, 'axial', 0, 0, tiled=True, axis_index_groups=groups)]
    ppermute x4 -> x5, waiting for transfers between devices: 3.87 us -> 3.21 us  [swapped(): lax.ppermute(value, 'axial', [(i, i ^ 1) for i in range(lax.axis_size('ax...]
    ppermute x12 -> x8, waiting for transfers between devices: 24 us -> 23.5 us  [turned(): lax.ppermute(value, axis, [(i, (i + shift) % count) for i in range(count)])]
  transfers between devices with their start and end apart: 19 -> 18, of which waited for: 13 -> 10; matrix products, arithmetic and copies ran while one was open for 0% -> 0% of each run, Pallas kernels for 3% -> 5%
where the time goes in v4:
time: 87.6 us; the launch traced here: 86.5 us
  starting transfers between devices  42.9 us (49%)
  waiting for transfers between devices  29.1 us (33%)
  Pallas kernels  13.5 us (15%)
    ppermute x8, waiting for transfers between devices, turned(): lax.ppermute(value, axis, [(i, (i + shift) % count) for i in range(count)])  23.5 us
    ppermute x8, starting transfers between devices, turned(): lax.ppermute(value, axis, [(i, (i + shift) % count) for i in range(count)])  16.9 us
    all_to_all x1, starting transfers between devices, local(): pieces = lax.all_to_all(codes, 'axial', 0, 0, tiled=True)  10.1 us
    pallas_call x8, Pallas kernels, run(): pl.pallas_call(body, in_specs=[smem] * len(scalars) + [vmem] * len(args),...  8.75 us
    all_to_all x1, starting transfers between devices, local(): sums = lax.all_to_all(total, 'axial', 0, 0, tiled=True)  7.3 us
    pallas_call x1, Pallas kernels, encode(): pl.pallas_call(encode_body, in_specs=[pl.BlockSpec(memory_space=pl.ANY)]...  4.73 us
    all_to_all x1, starting transfers between devices, between_chips(): lax.all_to_all(value, 'axial', 0, 0, tiled=True, axis_index_groups=groups)  3.47 us
    ppermute x5, starting transfers between devices, swapped(): lax.ppermute(value, 'axial', [(i, i ^ 1) for i in range(lax.axis_size('ax...  3.37 us
  transfers between devices with their start and end apart: 18, of which 10 were waited for; matrix products, arithmetic and copies ran while one was open for 0% of the time, Pallas kernels for 5%

profile of v4, /device:TPU:1, one launch (start us, length us, event | category | flops | bytes accessed | tf_op | source)
XLA Modules:
  0.0 86.5 jit_solution(15998704736538887949)
XLA Ops:
  0.6 4.7 %shard_map.94 = s16[16,18,16,128]{3,2,1,0:T(8,128)(2,1)} custom-call(bf16[4,32,8,2048]{3,2,1,0:T(8,128)(2,1)} %bitcast.13, f32[4,64,128]{2,1,0:T(8,128)} %lr_ref.1, f32[64,128]{1,0:T(8,128)} %length_ref.15), custom_call_target="tpu_custom_call" | custom-call | tf_op jit(solution)/shard_map/pallas_call | solution.py:124
  5.4 10.1 %all-to-all-start = ((s16[16,18,16,128]{3,2,1,0:T(8,128)(2,1)}), s16[16,18,16,128]{3,2,1,0:T(8,128)(2,1)S(1)}, u32[]{:S(2)}, u32[]{:S(2)}) async-start(s16[16,18,16,128]{3,2,1,0:T(8,128)(2,1)} %shard_map.94), calls=%async_computation | async-start | bytes 2359296 | tf_op jit(solution)/shard_map/all_to_all | solution.py:629
  15.6 1.6 %collective-permute-start = (f32[64,128]{1,0:T(8,128)S(1)}, f32[64,128]{1,0:T(8,128)S(1)}, u32[]{:S(2)}, u32[]{:S(2)}) collective-permute-start(f32[64,128]{1,0:T(8,128)S(1)} %get-tuple-element.70), channel_id=1, source_target_pairs={{0,16},{16,32},{32,48},{48,64},{64,80},{80,96},{96,112},{112,128},... | collective-permute-start | bytes 98312 | tf_op jit(solution)/shard_map/ppermute | solution.py:583
  17.2 1.3 %collective-permute-start.2 = (f32[4,128]{1,0:T(4,128)S(1)}, f32[4,128]{1,0:T(4,128)S(1)}, u32[]{:S(2)}, u32[]{:S(2)}) collective-permute-start(f32[4,128]{1,0:T(4,128)S(1)} %bitcast.16), channel_id=1, source_target_pairs={{0,1},{1,2},{2,3},{3,4},{4,5},{5,6},{6,7},{7,8},{8,9},{9,10},{10,1... | collective-permute-start | bytes 6152 | tf_op jit(solution)/shard_map/ppermute | solution.py:583
  18.5 3.8 %collective-permute-start.3 = (f32[4,128]{1,0:T(4,128)S(1)}, f32[4,128]{1,0:T(4,128)S(1)}, u32[]{:S(2)}, u32[]{:S(2)}) collective-permute-start(f32[4,128]{1,0:T(4,128)S(1)} %bitcast.15), channel_id=1, source_target_pairs={{0,15},{1,0},{2,1},{3,2},{4,3},{5,4},{6,5},{7,6},{8,7},{9,8},{10,9... | collective-permute-start | bytes 6152 | tf_op jit(solution)/shard_map/ppermute | solution.py:583
  23.2 18.3 %collective-permute-done.low_ref = f32[64,128]{1,0:T(8,128)S(1)} collective-permute-done((f32[64,128]{1,0:T(8,128)S(1)}, f32[64,128]{1,0:T(8,128)S(1)}, u32[]{:S(2)}, u32[]{:S(2)}) %collective-permute-start) | collective-permute-done | bytes 32800 | tf_op jit(solution)/shard_map/ppermute | solution.py:583
  41.5 2.5 %collective-permute-done.1.high_ref = f32[64,128]{1,0:T(8,128)S(1)} collective-permute-done((f32[64,128]{1,0:T(8,128)S(1)}, f32[64,128]{1,0:T(8,128)S(1)}, u32[]{:S(2)}, u32[]{:S(2)}) %collective-permute-start.1) | collective-permute-done | bytes 32800 | tf_op jit(solution)/shard_map/ppermute | solution.py:583
  44.0 2.1 %all-to-all-done.rec_ref = s16[16,18,16,128]{3,2,1,0:T(8,128)(2,1)S(1)} async-done(((s16[16,18,16,128]{3,2,1,0:T(8,128)(2,1)}), s16[16,18,16,128]{3,2,1,0:T(8,128)(2,1)S(1)}, u32[]{:S(2)}, u32[]{:S(2)}) %all-to-all-start) | async-done | bytes 1179680 | tf_op jit(solution)/shard_map/all_to_all | solution.py:629
  47.0 1.2 %collective-permute-done.4.got_ref = f32[1,32,128]{2,1,0:T(8,128)S(1)} collective-permute-done((f32[1,32,128]{2,1,0:T(8,128)S(1)}, f32[1,32,128]{2,1,0:T(8,128)S(1)}, u32[]{:S(2)}, u32[]{:S(2)}) %collective-permute-start.4) | collective-permute-done | bytes 16416 | tf_op jit(solution)/shard_map/ppermute | solution.py:596
  48.2 0.9 %shard_map.96 = (f32[4,64,128]{2,1,0:T(8,128)S(1)}, f32[4,64,128]{2,1,0:T(8,128)S(1)}, f32[4,64,128]{2,1,0:T(8,128)S(1)}, f32[3,64,128]{2,1,0:T(8,128)S(1)}, f32...) custom-call(s32[66]{0:T(128)S(1)} %pad_add_fusion.info_ref, s16[16,18,16,128]{3,2,1,0:T(8,128)(2,1)S(1)} %all-to-all-done.rec_ref, ...), custom_call_target="tpu_custom_call" | custom-call | flops 1000000000 | bytes 3000000 | tf_op jit(solution)/shard_map/pallas_call | solution.py:565
  49.4 1.2 %collective-permute-done.5.near_ref.got_ref = f32[8,32,128]{2,1,0:T(8,128)S(1)} collective-permute-done((f32[8,32,128]{2,1,0:T(8,128)S(1)}, f32[8,32,128]{2,1,0:T(8,128)S(1)}, u32[]{:S(2)}, u32[]{:S(2)}) %collective-permute-start.5) | collective-permute-done | bytes 131104 | tf_op jit(solution)/shard_map/ppermute | solution.py:596
  50.5 1.3 %shard_map.99 = s16[8,4,16,128]{3,2,1,0:T(8,128)(2,1)} custom-call(s32[66]{0:T(128)S(1)} %pad_add_fusion.info_ref, f32[2,32,128]{2,1,0:T(8,128)S(1)} %get-tuple-element.52.keep_ref, f32[8,32,128]{2,1,0:T(8,128)S(1)} %collective-permute-done.5.near_ref.got_ref, f32[64,128]{1,0:T(8,128)S(1)} %copy-done.4), custom_call_target="tpu_custom_call" | custom-call | flops 49999998976 | bytes 150000000 | tf_op jit(solution)/shard_map/pallas_call | solution.py:565
  51.8 3.5 %all-to-all-start.1 = ((s16[8,4,16,128]{3,2,1,0:T(8,128)(2,1)}), s16[8,4,16,128]{3,2,1,0:T(8,128)(2,1)S(1)}, u32[]{:S(2)}, u32[]{:S(2)}) async-start(s16[8,4,16,128]{3,2,1,0:T(8,128)(2,1)} %shard_map.99), calls=%async_computation.1 | async-start | bytes 262144 | tf_op jit(solution)/shard_map/all_to_all | solution.py:609
  56.0 1.3 %collective-permute-start.7 = (f32[16,128]{1,0:T(8,128)S(1)}, f32[16,128]{1,0:T(8,128)S(1)}, u32[]{:S(2)}, u32[]{:S(2)}) collective-permute-start(f32[16,128]{1,0:T(8,128)S(1)} %get-tuple-element.49.own_right_ref), channel_id=1, source_target_pairs={{0,1},{1,2},{2,3},{3,4},{4,5},{5,6},{6,7},{7,8},{8,9},{9,10},{10,1... | collective-permute-start | bytes 24584 | tf_op jit(solution)/shard_map/ppermute | solution.py:583
  57.3 3.8 %collective-permute-start.8 = (f32[16,128]{1,0:T(8,128)S(1)}, f32[16,128]{1,0:T(8,128)S(1)}, u32[]{:S(2)}, u32[]{:S(2)}) collective-permute-start(f32[16,128]{1,0:T(8,128)S(1)} %get-tuple-element.48.own_left_ref), channel_id=1, source_target_pairs={{0,15},{1,0},{2,1},{3,2},{4,3},{5,4},{6,5},{7,6},{8,7},{9,8},{10,9... | collective-permute-start | bytes 24584 | tf_op jit(solution)/shard_map/ppermute | solution.py:583
  61.1 0.9 %collective-permute-done.7.left_ref = f32[16,128]{1,0:T(8,128)S(1)} collective-permute-done((f32[16,128]{1,0:T(8,128)S(1)}, f32[16,128]{1,0:T(8,128)S(1)}, u32[]{:S(2)}, u32[]{:S(2)}) %collective-permute-start.7) | collective-permute-done | bytes 8224 | tf_op jit(solution)/shard_map/ppermute | solution.py:583
  62.9 2.5 %collective-permute-start.9 = (f32[2,32,128]{2,1,0:T(8,128)S(1)}, f32[2,32,128]{2,1,0:T(8,128)S(1)}, u32[]{:S(2)}, u32[]{:S(2)}) collective-permute-start(f32[2,32,128]{2,1,0:T(8,128)S(1)} %get-tuple-element.54), channel_id=1, source_target_pairs={{0,16},{16,0},{32,48},{48,32},{64,80},{80,64},{96,112},{112,96},{1... | collective-permute-start | bytes 98312 | tf_op jit(solution)/shard_map/ppermute | solution.py:596
  66.3 1.4 %shard_map.100 = (f32[2,32,128]{2,1,0:T(8,128)S(1)}, f32[2,32,128]{2,1,0:T(8,128)S(1)}, s16[16,2,16,128]{3,2,1,0:T(8,128)(2,1)}) custom-call(s32[66]{0:T(128)S(1)} %pad_add_fusion.info_ref, f32[2,32,128]{2,1,0:T(8,128)S(1)} %get-tuple-element.52.keep_ref, f32[8,32,128]{2,1,0:T(8,128)S(1)} %collective-permute-done.5.near_ref.got_ref, ...), custom_call_target="tpu_custom_call" | custom-call | flops 1000000000 | bytes 3000000 | tf_op jit(solution)/shard_map/pallas_call | solution.py:565
  68.2 7.3 %all-to-all-start.2 = ((s16[16,2,16,128]{3,2,1,0:T(8,128)(2,1)}), s16[16,2,16,128]{3,2,1,0:T(8,128)(2,1)S(1)}, u32[]{:S(2)}, u32[]{:S(2)}) async-start(s16[16,2,16,128]{3,2,1,0:T(8,128)(2,1)} %get-tuple-element.65), calls=%async_computation.2 | async-start | bytes 262144 | tf_op jit(solution)/shard_map/all_to_all | solution.py:671
  75.5 1.1 %shard_map.101 = (f32[4,64,128]{2,1,0:T(8,128)S(1)}, f32[4,64,128]{2,1,0:T(8,128)S(1)}, f32[4,128]{1,0:T(4,128)S(1)}, f32[64,128]{1,0:T(8,128)S(1)}, f32[64,128]...) custom-call(s32[66]{0:T(128)S(1)} %pad_add_fusion.info_ref, ...), custom_call_target="tpu_custom_call" | custom-call | flops 99999997952 | bytes 300000000 | tf_op jit(solution)/shard_map/pallas_call | solution.py:565
  76.8 1.7 %collective-permute-start.12 = (f32[64,128]{1,0:T(8,128)S(1)}, f32[64,128]{1,0:T(8,128)S(1)}, u32[]{:S(2)}, u32[]{:S(2)}) collective-permute-start(f32[64,128]{1,0:T(8,128)S(1)} %get-tuple-element.62), channel_id=1, source_target_pairs={{0,240},{16,32},{32,16},{48,64},{64,48},{80,96},{96,80},{112,128},... | collective-permute-start | bytes 98312 | tf_op jit(solution)/shard_map/ppermute | solution.py:601
  78.5 5.1 %collective-permute-start.14 = (f32[8,128]{1,0:T(8,128)S(1)}, f32[8,128]{1,0:T(8,128)S(1)}, u32[]{:S(2)}, u32[]{:S(2)}) collective-permute-start(f32[8,128]{1,0:T(8,128)S(1)} %get-tuple-element.64), channel_id=1, source_target_pairs={{0,15},{1,0},{2,1},{3,2},{4,3},{5,4},{6,5},{7,6},{8,7},{9,8},{10,9... | collective-permute-start | bytes 12296 | tf_op jit(solution)/shard_map/ppermute | solution.py:583
  83.6 1.0 %collective-permute-done.13.left_ref = f32[8,128]{1,0:T(8,128)S(1)} collective-permute-done((f32[8,128]{1,0:T(8,128)S(1)}, f32[8,128]{1,0:T(8,128)S(1)}, u32[]{:S(2)}, u32[]{:S(2)}) %collective-permute-start.13) | collective-permute-done | bytes 4128 | tf_op jit(solution)/shard_map/ppermute | solution.py:583
  84.9 1.6 %shard_map.102 = (f32[4,64,128]{2,1,0:T(8,128)}, f32[4,64,128]{2,1,0:T(8,128)}, f32[4,64]{1,0:T(4,128)}) custom-call(s32[66]{0:T(128)S(1)} %pad_add_fusion.info_ref, f32[17]{0:T(128)S(1)} %copy-done.5, s16[16,18,16,128]{3,2,1,0:T(8,128)(2,1)S(1)} %all-to-all-done.rec_ref, f32[4,64,128]{2,1,0:T(8,128)S(1)} %get-tuple-element.59.lt_ref, ...), custom_call_target="tpu_custom_call" | custom-call | flops 1000000000 | bytes 3000000 | tf_op jit(solution)/shard_map/pallas_call | solution.py:565
  (41 shorter events, 5.5 us)
Async XLA Ops:
  0.6 21.7 %copy-start = (s32[4,16,16]{2,1,0:T(8,128)S(1)}, s32[4,16,16]{2,1,0:T(8,128)}, u32[]{:S(2)}) copy-start(s32[4,16,16]{2,1,0:T(8,128)} %param.8) | copy-start | bytes 12292
  5.4 10.2 %copy-start.2 = (f32[4,64,128]{2,1,0:T(8,128)S(1)}, f32[4,64,128]{2,1,0:T(8,128)}, u32[]{:S(2)}) copy-start(f32[4,64,128]{2,1,0:T(8,128)} %seed_ref.3) | copy-start | bytes 393220
  5.4 40.7 %copy-start.4 = (f32[64,128]{1,0:T(8,128)S(1)}, f32[64,128]{1,0:T(8,128)}, u32[]{:S(2)}) copy-start(f32[64,128]{1,0:T(8,128)} %length_ref.15) | copy-start | bytes 98308
  5.4 40.7 %all-to-all-start = ((s16[16,18,16,128]{3,2,1,0:T(8,128)(2,1)}), s16[16,18,16,128]{3,2,1,0:T(8,128)(2,1)S(1)}, u32[]{:S(2)}, u32[]{:S(2)}) async-start(s16[16,18,16,128]{3,2,1,0:T(8,128)(2,1)} %shard_map.94), calls=%async_computation | async-start | bytes 2359296 | tf_op jit(solution)/shard_map/all_to_all | solution.py:629
  15.6 26.0 %collective-permute-start = (f32[64,128]{1,0:T(8,128)S(1)}, f32[64,128]{1,0:T(8,128)S(1)}, u32[]{:S(2)}, u32[]{:S(2)}) collective-permute-start(f32[64,128]{1,0:T(8,128)S(1)} %get-tuple-element.70), channel_id=1, source_target_pairs={{0,16},{16,32},{32,48},{48,64},{64,80},{80,96},{96,112},{112,128},... | collective-permute-start | bytes 98312 | tf_op jit(solution)/shard_map/ppermute | solution.py:583
  17.2 26.8 %collective-permute-start.1 = (f32[64,128]{1,0:T(8,128)S(1)}, f32[64,128]{1,0:T(8,128)S(1)}, u32[]{:S(2)}, u32[]{:S(2)}) collective-permute-start(f32[64,128]{1,0:T(8,128)S(1)} %get-tuple-element.69), channel_id=1, source_target_pairs={{0,240},{16,0},{32,16},{48,32},{64,48},{80,64},{96,80},{112,96},{1... | collective-permute-start | bytes 98312 | tf_op jit(solution)/shard_map/ppermute | solution.py:583
  17.2 6.0 %collective-permute-start.2 = (f32[4,128]{1,0:T(4,128)S(1)}, f32[4,128]{1,0:T(4,128)S(1)}, u32[]{:S(2)}, u32[]{:S(2)}) collective-permute-start(f32[4,128]{1,0:T(4,128)S(1)} %bitcast.16), channel_id=1, source_target_pairs={{0,1},{1,2},{2,3},{3,4},{4,5},{5,6},{6,7},{7,8},{8,9},{9,10},{10,1... | collective-permute-start | bytes 6152 | tf_op jit(solution)/shard_map/ppermute | solution.py:583
  18.5 4.7 %collective-permute-start.3 = (f32[4,128]{1,0:T(4,128)S(1)}, f32[4,128]{1,0:T(4,128)S(1)}, u32[]{:S(2)}, u32[]{:S(2)}) collective-permute-start(f32[4,128]{1,0:T(4,128)S(1)} %bitcast.15), channel_id=1, source_target_pairs={{0,15},{1,0},{2,1},{3,2},{4,3},{5,4},{6,5},{7,6},{8,7},{9,8},{10,9... | collective-permute-start | bytes 6152 | tf_op jit(solution)/shard_map/ppermute | solution.py:583
  22.5 25.7 %copy-start.1 = (f32[4,64,128]{2,1,0:T(8,128)S(1)}, f32[4,64,128]{2,1,0:T(8,128)}, u32[]{:S(2)}) copy-start(f32[4,64,128]{2,1,0:T(8,128)} %lr_ref.1) | copy-start | bytes 393220
  46.9 1.3 %collective-permute-start.4 = (f32[1,32,128]{2,1,0:T(8,128)S(1)}, f32[1,32,128]{2,1,0:T(8,128)S(1)}, u32[]{:S(2)}, u32[]{:S(2)}) collective-permute-start(f32[1,32,128]{2,1,0:T(8,128)S(1)} %get-tuple-element.41), channel_id=1, source_target_pairs={{0,16},{16,0},{32,48},{48,32},{64,80},{80,64},{96,112},{112,96},{1... | collective-permute-start | bytes 49160 | tf_op jit(solution)/shard_map/ppermute | solution.py:596
  49.1 1.4 %collective-permute-start.5 = (f32[8,32,128]{2,1,0:T(8,128)S(1)}, f32[8,32,128]{2,1,0:T(8,128)S(1)}, u32[]{:S(2)}, u32[]{:S(2)}) collective-permute-start(f32[8,32,128]{2,1,0:T(8,128)S(1)} %get-tuple-element.45), channel_id=1, source_target_pairs={{0,16},{16,0},{32,48},{48,32},{64,80},{80,64},{96,112},{112,96},{1... | collective-permute-start | bytes 393224 | tf_op jit(solution)/shard_map/ppermute | solution.py:596
  49.4 5.9 %collective-permute-start.6 = (f32[3,64,128]{2,1,0:T(8,128)S(1)}, f32[3,64,128]{2,1,0:T(8,128)S(1)}, u32[]{:S(2)}, u32[]{:S(2)}) collective-permute-start(f32[3,64,128]{2,1,0:T(8,128)S(1)} %get-tuple-element.46), channel_id=1, source_target_pairs={{0,240},{16,32},{32,16},{48,64},{64,48},{80,96},{96,80},{112,128},... | collective-permute-start | bytes 294920 | tf_op jit(solution)/shard_map/ppermute | solution.py:601
  51.8 14.5 %all-to-all-start.1 = ((s16[8,4,16,128]{3,2,1,0:T(8,128)(2,1)}), s16[8,4,16,128]{3,2,1,0:T(8,128)(2,1)S(1)}, u32[]{:S(2)}, u32[]{:S(2)}) async-start(s16[8,4,16,128]{3,2,1,0:T(8,128)(2,1)} %shard_map.99), calls=%async_computation.1 | async-start | bytes 262144 | tf_op jit(solution)/shard_map/all_to_all | solution.py:609
  56.0 6.0 %collective-permute-start.7 = (f32[16,128]{1,0:T(8,128)S(1)}, f32[16,128]{1,0:T(8,128)S(1)}, u32[]{:S(2)}, u32[]{:S(2)}) collective-permute-start(f32[16,128]{1,0:T(8,128)S(1)} %get-tuple-element.49.own_right_ref), channel_id=1, source_target_pairs={{0,1},{1,2},{2,3},{3,4},{4,5},{5,6},{6,7},{7,8},{8,9},{9,10},{10,1... | collective-permute-start | bytes 24584 | tf_op jit(solution)/shard_map/ppermute | solution.py:583
  57.3 4.8 %collective-permute-start.8 = (f32[16,128]{1,0:T(8,128)S(1)}, f32[16,128]{1,0:T(8,128)S(1)}, u32[]{:S(2)}, u32[]{:S(2)}) collective-permute-start(f32[16,128]{1,0:T(8,128)S(1)} %get-tuple-element.48.own_left_ref), channel_id=1, source_target_pairs={{0,15},{1,0},{2,1},{3,2},{4,3},{5,4},{6,5},{7,6},{8,7},{9,8},{10,9... | collective-permute-start | bytes 24584 | tf_op jit(solution)/shard_map/ppermute | solution.py:583
  62.9 3.4 %collective-permute-start.9 = (f32[2,32,128]{2,1,0:T(8,128)S(1)}, f32[2,32,128]{2,1,0:T(8,128)S(1)}, u32[]{:S(2)}, u32[]{:S(2)}) collective-permute-start(f32[2,32,128]{2,1,0:T(8,128)S(1)} %get-tuple-element.54), channel_id=1, source_target_pairs={{0,16},{16,0},{32,48},{48,32},{64,80},{80,64},{96,112},{112,96},{1... | collective-permute-start | bytes 98312 | tf_op jit(solution)/shard_map/ppermute | solution.py:596
  66.3 9.2 %copy-start.3 = (f32[4,64,128]{2,1,0:T(8,128)S(1)}, f32[4,64,128]{2,1,0:T(8,128)}, u32[]{:S(2)}) copy-start(f32[4,64,128]{2,1,0:T(8,128)} %seed_ref.3) | copy-start | bytes 393220
  67.7 7.8 %collective-permute-start.10 = (f32[2,32,128]{2,1,0:T(8,128)S(1)}, f32[2,32,128]{2,1,0:T(8,128)S(1)}, u32[]{:S(2)}, u32[]{:S(2)}) collective-permute-start(f32[2,32,128]{2,1,0:T(8,128)S(1)} %get-tuple-element.58), channel_id=1, source_target_pairs={{0,16},{16,0},{32,48},{48,32},{64,80},{80,64},{96,112},{112,96},{1... | collective-permute-start | bytes 98312 | tf_op jit(solution)/shard_map/ppermute | solution.py:596
  68.2 16.7 %all-to-all-start.2 = ((s16[16,2,16,128]{3,2,1,0:T(8,128)(2,1)}), s16[16,2,16,128]{3,2,1,0:T(8,128)(2,1)S(1)}, u32[]{:S(2)}, u32[]{:S(2)}) async-start(s16[16,2,16,128]{3,2,1,0:T(8,128)(2,1)} %get-tuple-element.65), calls=%async_computation.2 | async-start | bytes 262144 | tf_op jit(solution)/shard_map/all_to_all | solution.py:671
  75.5 9.3 %copy-start.5 = (f32[17]{0:T(128)S(1)}, f32[17]{0:T(128)}, u32[]{:S(2)}) copy-start(f32[17]{0:T(128)} %weight_ref.1) | copy-start | bytes 208
  76.7 7.9 %collective-permute-start.11 = (f32[64,128]{1,0:T(8,128)S(1)}, f32[64,128]{1,0:T(8,128)S(1)}, u32[]{:S(2)}, u32[]{:S(2)}) collective-permute-start(f32[64,128]{1,0:T(8,128)S(1)} %get-tuple-element.61), channel_id=1, source_target_pairs={{0,16},{16,0},{32,48},{48,32},{64,80},{80,64},{96,112},{112,96},{1... | collective-permute-start | bytes 98312 | tf_op jit(solution)/shard_map/ppermute | solution.py:596
  76.8 7.7 %collective-permute-start.12 = (f32[64,128]{1,0:T(8,128)S(1)}, f32[64,128]{1,0:T(8,128)S(1)}, u32[]{:S(2)}, u32[]{:S(2)}) collective-permute-start(f32[64,128]{1,0:T(8,128)S(1)} %get-tuple-element.62), channel_id=1, source_target_pairs={{0,240},{16,32},{32,16},{48,64},{64,48},{80,96},{96,80},{112,128},... | collective-permute-start | bytes 98312 | tf_op jit(solution)/shard_map/ppermute | solution.py:601
  78.5 6.1 %collective-permute-start.13 = (f32[8,128]{1,0:T(8,128)S(1)}, f32[8,128]{1,0:T(8,128)S(1)}, u32[]{:S(2)}, u32[]{:S(2)}) collective-permute-start(f32[8,128]{1,0:T(8,128)S(1)} %get-tuple-element.63), channel_id=1, source_target_pairs={{0,1},{1,2},{2,3},{3,4},{4,5},{5,6},{6,7},{7,8},{8,9},{9,10},{10,1... | collective-permute-start | bytes 12296 | tf_op jit(solution)/shard_map/ppermute | solution.py:583
  78.5 6.1 %collective-permute-start.14 = (f32[8,128]{1,0:T(8,128)S(1)}, f32[8,128]{1,0:T(8,128)S(1)}, u32[]{:S(2)}, u32[]{:S(2)}) collective-permute-start(f32[8,128]{1,0:T(8,128)S(1)} %get-tuple-element.64), channel_id=1, source_target_pairs={{0,15},{1,0},{2,1},{3,2},{4,3},{5,4},{6,5},{7,6},{8,7},{9,8},{10,9... | collective-permute-start | bytes 12296 | tf_op jit(solution)/shard_map/ppermute | solution.py:583
  (1 other events, 1.8 us)

commit v5 on v4

--- a/solution.py
+++ b/solution.py
@@ -48,11 +48,17 @@
         pltpu.make_async_copy(seed_ref, seed, more_sems.at[0]),
         pltpu.make_async_copy(length_ref, length, more_sems.at[1]),
     ]
-    arrivals = [
-        pltpu.make_async_copy(stored_ref.at[step], pieces.at[step], in_sems.at[step])
-        for step in range(steps)
-    ]
-    for copy in first + arrivals:
+    half_way = steps // 2
+    cuts = [*range(half_way), half_way, steps]
+    arrivals = {
+        start: pltpu.make_async_copy(
+            stored_ref.at[pl.ds(start, end - start)],
+            pieces.at[pl.ds(start, end - start)],
+            in_sems.at[start],
+        )
+        for start, end in zip(cuts[:-1], cuts[1:])
+    }
+    for copy in [*first, *arrivals.values()]:
         copy.start()
     row = lax.broadcasted_iota(jnp.int32, (rows, rows), 0)
     column = lax.broadcasted_iota(jnp.int32, (rows, rows), 1)
@@ -88,9 +94,9 @@
         copy.start()
         departures.append(copy)
 
-    depart(steps * per, half // ROWS)
     for step in range(steps):
-        arrivals[step].wait()
+        if step in arrivals:
+            arrivals[step].wait()
         for slot in range(0, slots, cap):
             both = jnp.concatenate([mixed(step, slot + c) for c in range(cap)], axis=1)
             parts = jnp.dot(order, both, preferred_element_type=jnp.float32)
@@ -112,7 +118,9 @@
                 lanes = slice(LANES * c, LANES * (c + 1))
                 codes[slot // cap, per * step + 2 * c] = rate_code[:, lanes]
                 codes[slot // cap, per * step + 2 * c + 1] = coef_code[:, lanes]
-        depart(per * step, per)
+        if step + 1 == half_way:
+            depart(0, per * half_way)
+    depart(per * half_way, out_ref.shape[1] - per * half_way)
     for copy in departures:
         copy.wait()
 
@@ -270,13 +278,13 @@
     chips, blocks = sums_ref.shape[:2]
     per = fall.shape[0] // ROWS
     count = blocks // per
-
-    def climb(k, total):
-        here = [got_sum(sums_ref, chips - 1 - k, per * index, per) for index in range(count)]
-        return applied(total, here, fall * fall, 2.0 * fall * cross)
-
-    zero = jnp.zeros_like(fall)
-    return lax.fori_loop(0, chips - 1 - info_ref[64] // 2, climb, (zero,) * count)
+    total = (jnp.zeros_like(fall),) * count
+    for chip in reversed(range(1, chips)):
+        here = [got_sum(sums_ref, chip, per * index, per) for index in range(count)]
+        new = applied(total, here, fall * fall, 2.0 * fall * cross)
+        inside = chip > info_ref[64] // 2
+        total = tuple(jnp.where(inside, a, b) for a, b in zip(new, total))
+    return total
 
 
 def answered(gain, share, decay):
@@ -296,12 +304,9 @@
         )
 
     upper = info_ref[64] // 2 * 2 + 1
-    above = lax.fori_loop(
-        0,
-        peers - 1 - upper,
-        lambda k, value: fall * value + total_of(peers - 1 - k),
-        jnp.zeros_like(fall),
-    )
+    above = jnp.zeros_like(fall)
+    for peer in reversed(range(2, peers)):
+        above = jnp.where(peer > upper, fall * above + total_of(peer), above)
     below = fall * above + total_of(upper)
     share_out(info_ref, (above,), (below,), mine_ref, other_ref)
 
@@ -335,6 +340,9 @@
         near = jnp.where(upper_here, down[index], up[index])
         give_ref[2 + 2 * index] = near[:half]
         give_ref[3 + 2 * index] = near[half:]
+    for l in range(layers):
+        give_ref[8, l : l + 1, :] = new_lt[l][0:1, :]
+        give_ref[8, layers + l : layers + l + 1, :] = new_lt[l][2 * half - 1 : 2 * half, :]
     nothing = jnp.zeros_like(decay)
     _, now = chain(lr, decay, nothing)
     gain = [1.0 + 0.2 * decoded(info_ref, rec_ref, 2, l, 0) for l in range(layers)]
@@ -359,7 +367,8 @@
 
 
 def reach_body(
-    info_ref, lt_ref, source_ref, near_ref, far_ref, new_lt_ref, left_out, right_out,
+    info_ref, rec_ref, lt_ref, lr_ref, source_ref, near_ref, far_ref, length_ref,
+    new_lt_ref, left_out, right_out, keep_ref, give_ref, scratch,
 ):
     layers, azimuths, _ = lt_ref.shape
     bottom = info_ref[64] == 0
@@ -377,49 +386,25 @@
     new_lt = [lt[l] + 0.15 * spread[l] + source[l] for l in range(layers + 2)]
     new_lt[0] = jnp.where(bottom, 0.0, new_lt[0])
     new_lt[-1] = jnp.where(top, 0.0, new_lt[-1])
-    sides = ((left_out, 0, 1), (right_out, azimuths - 1, azimuths - 2))
-    for out, edge, inside in sides:
+    sides = ((left_out, 0, 1, 0), (right_out, azimuths - 1, azimuths - 2, layers))
+    for out, edge, inside, other in sides:
         for l in range(layers + 2):
             out[l : l + 1, :] = lt[l][edge : edge + 1, :]
         out[layers + 2 : layers + 4, :] = jnp.zeros_like(out[layers + 2 : layers + 4, :])
         for l in range(layers):
             out[8 + l : 9 + l, :] = lt[l + 1][inside : inside + 1, :]
             out[12 + l : 13 + l, :] = source[l + 1][edge : edge + 1, :]
+        out[16:20, :] = near_ref[8, other : other + layers, :]
+        out[20:24, :] = jnp.zeros_like(out[20:24, :])
     for l in range(layers + 2):
         new_lt_ref[l] = new_lt[l]
-
-
-def beyond(there, here):
-    middle = there[1:5]
-    total = (there[0:4] + there[2:6]) + (there[8:12] + here[1:5]) + radial(middle)
-    return middle + 0.15 * (total - 6.0 * middle) + there[12:16]
-
-
-def second_body(
-    info_ref, rec_ref, old_lt_ref, lr_ref, lt_ref, own_left_ref, own_right_ref, left_ref,
-    right_ref, length_ref, new_lt_ref, sides_ref, keep_ref, give_ref, scratch,
-):
-    layers, azimuths, radials = lr_ref.shape
+    new_lt = new_lt[1:-1]
     decay, _, _ = powers(length_ref[...])
     nothing = jnp.zeros_like(decay)
-    left, right = left_ref[...], right_ref[...]
-    sides_ref[0:layers, :] = beyond(left, own_left_ref[...])
-    sides_ref[layers : 2 * layers, :] = beyond(right, own_right_ref[...])
-    row = lax.broadcasted_iota(jnp.int32, (azimuths, radials), 0)
-    new_lt = []
-    for l in range(layers + 2):
-        missing = jnp.where(
-            row == 0,
-            left[l : l + 1, :],
-            jnp.where(row == azimuths - 1, right[l : l + 1, :], 0.0),
-        )
-        new_lt.append(lt_ref[l] + 0.15 * missing)
-        new_lt_ref[l] = new_lt[l]
-    new_lt = new_lt[1:-1]
     one = [1.0 + 0.2 * decoded(info_ref, rec_ref, 2, l, 0) for l in range(layers)]
     two = [1.0 + 0.2 * decoded(info_ref, rec_ref, 1, l, 0) for l in range(layers)]
     lr = [lr_ref[layer] for layer in range(layers)]
-    lr = [a - 0.3 * old_lt_ref[l] for l, a in enumerate(answered(one, lr, decay))]
+    lr = [a - 0.3 * lt_ref[l] for l, a in enumerate(answered(one, lr, decay))]
     lr = [a - 0.3 * new_lt[l] for l, a in enumerate(answered(two, lr, decay))]
     _, later = chain(lr, decay, nothing)
     share = [None] * layers
@@ -431,9 +416,15 @@
     halves(info_ref, (later, weight), scratch, keep_ref, give_ref)
 
 
+def beyond(there, here):
+    middle = there[1:5]
+    total = (there[0:4] + there[2:6]) + (there[8:12] + here[1:5]) + radial(middle)
+    return middle + 0.15 * (total - 6.0 * middle) + there[12:16]
+
+
 def pair_carry_body(
-    info_ref, keep_ref, got_ref, more_ref, more_got_ref, sums_ref, length_ref,
-    mine_ref, other_ref, out_ref,
+    info_ref, keep_ref, got_ref, more_ref, more_got_ref, sums_ref, left_ref, right_ref,
+    length_ref, mine_ref, other_ref, out_ref,
 ):
     _, fall, cross = half_powers(info_ref, length_ref)
     above = climbed(info_ref, sums_ref, fall, cross)
@@ -443,6 +434,20 @@
     upper, lower = cores(info_ref, more_ref, more_got_ref)
     upper = upper[0] + upper[1] * above[0] + cross * above[1]
     lower = lower[0] + lower[1] * below[0] + cross * below[1]
+    upper_here = info_ref[64] % 2 == 1
+    end = length_ref.shape[0] - 1
+    beside = jnp.where(upper_here, right_ref[...], left_ref[...])
+    decay, _, _ = powers(jnp.where(upper_here, length_ref[end:, :], length_ref[0:1, :]))
+    row = lax.broadcasted_iota(jnp.int32, fall.shape, 0)
+    edge = row == jnp.where(upper_here, fall.shape[0] - 1, 0)
+    weight = (-0.3 * 0.15) * (1.0 - decay)
+    own, other = jnp.zeros_like(decay), jnp.zeros_like(decay)
+    for layer in range(4):
+        own = own + weight * beside[1 + layer : 2 + layer, :]
+        other = other + weight * beside[16 + layer : 17 + layer, :]
+        weight = weight * decay
+    upper = upper + jnp.where(edge, jnp.where(upper_here, own, other), 0.0)
+    lower = lower + jnp.where(edge, jnp.where(upper_here, other, own), 0.0)
     total = squeezed(lower + fall * upper, SUM_BASE, SUM_SCALE)
     upper = squeezed(upper, SUM_BASE, SUM_SCALE)
     for peer in range(out_ref.shape[0]):
@@ -450,7 +455,8 @@
 
 
 def third_body(
-    info_ref, rec_ref, seed_ref, one_ref, lt_ref, lr_ref, sides_ref, length_ref, face_ref,
+    info_ref, rec_ref, seed_ref, one_ref, lt_ref, lr_ref, own_left_ref, own_right_ref,
+    left_ref, right_ref, length_ref, face_ref,
     mine_ref, got_ref, new_lt_ref, new_lr_ref, flux_ref, near_out, far_out, left_out, right_out,
     scratch,
 ):
@@ -458,7 +464,17 @@
     decay, _, _ = powers(length_ref[...])
     one, two = restored(info_ref, mine_ref, got_ref, scratch)
     before = [one_ref[layer] for layer in range(layers)]
-    lt = [lt_ref[layer + 1] for layer in range(layers)]
+    left, right = left_ref[...], right_ref[...]
+    row = lax.broadcasted_iota(jnp.int32, (azimuths, radials), 0)
+    full = []
+    for l in range(layers + 2):
+        missing = jnp.where(
+            row == 0,
+            left[l : l + 1, :],
+            jnp.where(row == azimuths - 1, right[l : l + 1, :], 0.0),
+        )
+        full.append(lt_ref[l] + 0.15 * missing)
+    lt = full[1:-1]
     lr = [lr_ref[layer] for layer in range(layers)]
     climbs, _ = chain(lr, decay, one)
     lr = [
@@ -467,8 +483,13 @@
         + climbs[l]
         for l in range(layers)
     ]
-    sides = sides_ref[...]
-    spread = laplace(lt, lt_ref[0], lt_ref[layers + 1], sides[:layers], sides[layers:])
+    spread = laplace(
+        lt,
+        full[0],
+        full[-1],
+        beyond(left, own_left_ref[...]),
+        beyond(right, own_right_ref[...]),
+    )
     new_lt = [
         lt[l] + 0.15 * spread[l] + decoded(info_ref, rec_ref, 1, l, 1) * lr[l]
         for l in range(layers)
@@ -491,14 +512,14 @@
         kept = jnp.where(
             lane == face_ref[l], (seed_ref[l] + before[l]) + (lt[l] + new_lt[l]), 0.0
         )
-        row = lax.dot_general(
+        line = lax.dot_general(
             ones,
             kept,
             (((1,), (1,)), ((), ())),
             precision=lax.Precision.HIGHEST,
             preferred_element_type=jnp.float32,
         )[0:1, :]
-        twice = jnp.concatenate([row, row], axis=1)
+        twice = jnp.concatenate([line, line], axis=1)
         flux_ref[l : l + 1, :] = twice
         left_out[layers + l : layers + l + 1, :] = twice
         right_out[layers + l : layers + l + 1, :] = twice
@@ -521,12 +542,9 @@
             [got_sum(sums_ref, 2 * chip + core, 0, per) for core in range(2)], axis=0
         )
 
-    above = lax.fori_loop(
-        0,
-        chips - 1 - here,
-        lambda k, value: fall * fall * value + total_of(chips - 1 - k),
-        jnp.zeros_like(fall),
-    )
+    above = jnp.zeros_like(fall)
+    for chip in reversed(range(1, chips)):
+        above = jnp.where(chip > here, fall * fall * above + total_of(chip), above)
     three = jnp.where(info_ref[64] % 2 == 1, above, fall * above + total_of(here))
     lt = [lt_ref[layer] for layer in range(layers)]
     lr = [lr_ref[layer] for layer in range(layers)]
@@ -636,7 +654,7 @@
         first_body,
         (info,),
         (pieces, seed_temp, seed_disloc, *halo, decay_length, mine, swapped(other)),
-        [block, block, block, (3, *plane), half(2), half(8)],
+        [block, block, block, (3, *plane), half(2), half(9)],
         [(1, *plane), (2, *plane)],
     )
     got = swapped(give)
@@ -645,27 +663,21 @@
         pair_chip_body, (info,), (keep, got, decay_length), [copies(axial // 2, 2)], span=CHIP_SPAN
     )
     sums = between_chips(total)
-    lt2, left, right = run(
+    lt2, left, right, more, give = run(
         reach_body,
         (info,),
-        (lt1, source, got, far),
-        [(layers + 2, *plane), (16, radials), (16, radials)],
+        (pieces, lt1, lr1, source, got, far, decay_length),
+        [(layers + 2, *plane), (24, radials), (24, radials), half(2), half(2)],
+        [(2, *plane)],
         span=REACH_SPAN,
     )
-    before, after = turned(right, "azim", 1), turned(left, "azim", -1)
-    lt2, sides, more, give = run(
-        second_body,
-        (info,),
-        (pieces, lt1, lr1, lt2, left, right, before, after, decay_length),
-        [(layers + 2, *plane), wide, half(2), half(2)],
-        [(2, *plane)],
-    )
     more_got = swapped(give)
-    sums, more_got = lax.optimization_barrier((sums, more_got))
+    sides = (turned(right, "azim", 1), turned(left, "azim", -1))
+    sums, *sides = lax.optimization_barrier((sums, *sides))
     mine, other, total = run(
         pair_carry_body,
         (info,),
-        (keep, got, more, more_got, sums, decay_length),
+        (keep, got, more, more_got, sums, *sides, decay_length),
         [half(2), half(2), copies(axial, 1)],
     )
     sums = lax.all_to_all(total, "axial", 0, 0, tiled=True)
@@ -673,8 +685,8 @@
         third_body,
         (info,),
         (
-            pieces, seed_temp, lt1, lt2, lr1, sides, decay_length, face_radius[:, :, None],
-            mine, swapped(other),
+            pieces, seed_temp, lt1, lt2, lr1, left, right, *sides, decay_length,
+            face_radius[:, :, None], mine, swapped(other),
         ),
         [block, block, side, plane, plane, wide, wide],
         [(2, *plane)],

time: 87.6 us -> 85.5 us (0.976)
  Pallas kernels: 13.5 us -> 12.3 us
    all_to_all x1, starting transfers between devices: 7.3 us -> 6.37 us  [local(): sums = lax.all_to_all(total, 'axial', 0, 0, tiled=True)]
    pallas_call x8 -> x7, Pallas kernels: 8.75 us -> 7.84 us  [run(): pl.pallas_call(body, in_specs=[smem] * len(scalars) + [vmem] * len(args),...]
  transfers between devices with their start and end apart: 18 -> 18, of which waited for: 10 -> 9; matrix products, arithmetic and copies ran while one was open for 0% -> 0% of each run, Pallas kernels for 5% -> 4%
where the time goes in v5:
time: 85.5 us; the launch traced here: 84.3 us
  starting transfers between devices  42.5 us (50%)
  waiting for transfers between devices  28.4 us (33%)
  Pallas kernels  12.3 us (14%)
    ppermute x8, waiting for transfers between devices, turned(): lax.ppermute(value, axis, [(i, (i + shift) % count) for i in range(count)])  23.6 us
    ppermute x8, starting transfers between devices, turned(): lax.ppermute(value, axis, [(i, (i + shift) % count) for i in range(count)])  16.7 us
    all_to_all x1, starting transfers between devices, local(): pieces = lax.all_to_all(codes, 'axial', 0, 0, tiled=True)  10.1 us
    pallas_call x7, Pallas kernels, run(): pl.pallas_call(body, in_specs=[smem] * len(scalars) + [vmem] * len(args),...  7.84 us
    all_to_all x1, starting transfers between devices, local(): sums = lax.all_to_all(total, 'axial', 0, 0, tiled=True)  6.37 us
    pallas_call x1, Pallas kernels, encode(): pl.pallas_call(encode_body, in_specs=[pl.BlockSpec(memory_space=pl.ANY)]...  4.43 us
    ppermute x5, starting transfers between devices, swapped(): lax.ppermute(value, 'axial', [(i, i ^ 1) for i in range(lax.axis_size('ax...  4 us
    all_to_all x1, starting transfers between devices, between_chips(): lax.all_to_all(value, 'axial', 0, 0, tiled=True, axis_index_groups=groups)  3.62 us
  transfers between devices with their start and end apart: 18, of which 9 were waited for; matrix products, arithmetic and copies ran while one was open for 0% of the time, Pallas kernels for 4%

profile of v5, /device:TPU:1, one launch (start us, length us, event | category | flops | bytes accessed | tf_op | source)
XLA Modules:
  0.0 84.3 jit_solution(14057221913678165179)
XLA Ops:
  0.6 4.4 %shard_map.94 = s16[16,18,16,128]{3,2,1,0:T(8,128)(2,1)} custom-call(bf16[4,32,8,2048]{3,2,1,0:T(8,128)(2,1)} %bitcast.13, f32[4,64,128]{2,1,0:T(8,128)} %lr_ref.1, f32[64,128]{1,0:T(8,128)} %length_ref.15), custom_call_target="tpu_custom_call" | custom-call | tf_op jit(solution)/shard_map/pallas_call | solution.py:132
  5.1 10.1 %all-to-all-start = ((s16[16,18,16,128]{3,2,1,0:T(8,128)(2,1)}), s16[16,18,16,128]{3,2,1,0:T(8,128)(2,1)S(1)}, u32[]{:S(2)}, u32[]{:S(2)}) async-start(s16[16,18,16,128]{3,2,1,0:T(8,128)(2,1)} %shard_map.94), calls=%async_computation | async-start | bytes 2359296 | tf_op jit(solution)/shard_map/all_to_all | solution.py:647
  15.3 1.6 %collective-permute-start = (f32[64,128]{1,0:T(8,128)S(1)}, f32[64,128]{1,0:T(8,128)S(1)}, u32[]{:S(2)}, u32[]{:S(2)}) collective-permute-start(f32[64,128]{1,0:T(8,128)S(1)} %get-tuple-element.68), channel_id=1, source_target_pairs={{0,16},{16,32},{32,48},{48,64},{64,80},{80,96},{96,112},{112,128},... | collective-permute-start | bytes 98312 | tf_op jit(solution)/shard_map/ppermute | solution.py:601
  16.9 1.3 %collective-permute-start.2 = (f32[4,128]{1,0:T(4,128)S(1)}, f32[4,128]{1,0:T(4,128)S(1)}, u32[]{:S(2)}, u32[]{:S(2)}) collective-permute-start(f32[4,128]{1,0:T(4,128)S(1)} %bitcast.16), channel_id=1, source_target_pairs={{0,1},{1,2},{2,3},{3,4},{4,5},{5,6},{6,7},{7,8},{8,9},{9,10},{10,1... | collective-permute-start | bytes 6152 | tf_op jit(solution)/shard_map/ppermute | solution.py:601
  18.2 3.8 %collective-permute-start.3 = (f32[4,128]{1,0:T(4,128)S(1)}, f32[4,128]{1,0:T(4,128)S(1)}, u32[]{:S(2)}, u32[]{:S(2)}) collective-permute-start(f32[4,128]{1,0:T(4,128)S(1)} %bitcast.15), channel_id=1, source_target_pairs={{0,15},{1,0},{2,1},{3,2},{4,3},{5,4},{6,5},{7,6},{8,7},{9,8},{10,9... | collective-permute-start | bytes 6152 | tf_op jit(solution)/shard_map/ppermute | solution.py:601
  22.9 18.3 %collective-permute-done.low_ref = f32[64,128]{1,0:T(8,128)S(1)} collective-permute-done((f32[64,128]{1,0:T(8,128)S(1)}, f32[64,128]{1,0:T(8,128)S(1)}, u32[]{:S(2)}, u32[]{:S(2)}) %collective-permute-start) | collective-permute-done | bytes 32800 | tf_op jit(solution)/shard_map/ppermute | solution.py:601
  41.2 2.5 %collective-permute-done.1.high_ref = f32[64,128]{1,0:T(8,128)S(1)} collective-permute-done((f32[64,128]{1,0:T(8,128)S(1)}, f32[64,128]{1,0:T(8,128)S(1)}, u32[]{:S(2)}, u32[]{:S(2)}) %collective-permute-start.1) | collective-permute-done | bytes 32800 | tf_op jit(solution)/shard_map/ppermute | solution.py:601
  43.7 2.1 %all-to-all-done.rec_ref = s16[16,18,16,128]{3,2,1,0:T(8,128)(2,1)S(1)} async-done(((s16[16,18,16,128]{3,2,1,0:T(8,128)(2,1)}), s16[16,18,16,128]{3,2,1,0:T(8,128)(2,1)S(1)}, u32[]{:S(2)}, u32[]{:S(2)}) %all-to-all-start) | async-done | bytes 1179680 | tf_op jit(solution)/shard_map/all_to_all | solution.py:647
  46.6 1.2 %collective-permute-done.4.got_ref = f32[1,32,128]{2,1,0:T(8,128)S(1)} collective-permute-done((f32[1,32,128]{2,1,0:T(8,128)S(1)}, f32[1,32,128]{2,1,0:T(8,128)S(1)}, u32[]{:S(2)}, u32[]{:S(2)}) %collective-permute-start.4) | collective-permute-done | bytes 16416 | tf_op jit(solution)/shard_map/ppermute | solution.py:614
  48.9 1.2 %collective-permute-done.5.near_ref.got_ref = f32[9,32,128]{2,1,0:T(8,128)S(1)} collective-permute-done((f32[9,32,128]{2,1,0:T(8,128)S(1)}, f32[9,32,128]{2,1,0:T(8,128)S(1)}, u32[]{:S(2)}, u32[]{:S(2)}) %collective-permute-start.5) | collective-permute-done | bytes 147488 | tf_op jit(solution)/shard_map/ppermute | solution.py:614
  50.1 1.3 %shard_map.98 = s16[8,4,16,128]{3,2,1,0:T(8,128)(2,1)} custom-call(s32[66]{0:T(128)S(1)} %pad_add_fusion.info_ref, f32[2,32,128]{2,1,0:T(8,128)S(1)} %get-tuple-element.49.keep_ref, f32[9,32,128]{2,1,0:T(8,128)S(1)} %collective-permute-done.5.near_ref.got_ref, f32[64,128]{1,0:T(8,128)S(1)} %copy-done.4), custom_call_target="tpu_custom_call" | custom-call | flops 49999998976 | bytes 150000000 | tf_op jit(solution)/shard_map/pallas_call | solution.py:583
  51.4 3.6 %all-to-all-start.1 = ((s16[8,4,16,128]{3,2,1,0:T(8,128)(2,1)}), s16[8,4,16,128]{3,2,1,0:T(8,128)(2,1)S(1)}, u32[]{:S(2)}, u32[]{:S(2)}) async-start(s16[8,4,16,128]{3,2,1,0:T(8,128)(2,1)} %shard_map.98), calls=%async_computation.1 | async-start | bytes 262144 | tf_op jit(solution)/shard_map/all_to_all | solution.py:627
  55.9 1.5 %collective-permute-start.9 = (f32[2,32,128]{2,1,0:T(8,128)S(1)}, f32[2,32,128]{2,1,0:T(8,128)S(1)}, u32[]{:S(2)}, u32[]{:S(2)}) collective-permute-start(f32[2,32,128]{2,1,0:T(8,128)S(1)} %get-tuple-element.53), channel_id=1, source_target_pairs={{0,16},{16,0},{32,48},{48,32},{64,80},{80,64},{96,112},{112,96},{1... | collective-permute-start | bytes 98312 | tf_op jit(solution)/shard_map/ppermute | solution.py:614
  57.4 1.2 %collective-permute-start.7 = (f32[24,128]{1,0:T(8,128)S(1)}, f32[24,128]{1,0:T(8,128)S(1)}, u32[]{:S(2)}, u32[]{:S(2)}) collective-permute-start(f32[24,128]{1,0:T(8,128)S(1)} %get-tuple-element.48.own_right_ref), channel_id=1, source_target_pairs={{0,1},{1,2},{2,3},{3,4},{4,5},{5,6},{6,7},{7,8},{8,9},{9,10},{10,1... | collective-permute-start | bytes 36872 | tf_op jit(solution)/shard_map/ppermute | solution.py:601
  58.6 3.7 %collective-permute-start.8 = (f32[24,128]{1,0:T(8,128)S(1)}, f32[24,128]{1,0:T(8,128)S(1)}, u32[]{:S(2)}, u32[]{:S(2)}) collective-permute-start(f32[24,128]{1,0:T(8,128)S(1)} %get-tuple-element.47.own_left_ref), channel_id=1, source_target_pairs={{0,15},{1,0},{2,1},{3,2},{4,3},{5,4},{6,5},{7,6},{8,7},{9,8},{10,9... | collective-permute-start | bytes 36872 | tf_op jit(solution)/shard_map/ppermute | solution.py:601
  62.3 1.1 %collective-permute-done.7.left_ref = f32[24,128]{1,0:T(8,128)S(1)} collective-permute-done((f32[24,128]{1,0:T(8,128)S(1)}, f32[24,128]{1,0:T(8,128)S(1)}, u32[]{:S(2)}, u32[]{:S(2)}) %collective-permute-start.7) | collective-permute-done | bytes 12320 | tf_op jit(solution)/shard_map/ppermute | solution.py:601
  63.4 1.4 %shard_map.99 = (f32[2,32,128]{2,1,0:T(8,128)S(1)}, f32[2,32,128]{2,1,0:T(8,128)S(1)}, s16[16,2,16,128]{3,2,1,0:T(8,128)(2,1)}) custom-call(s32[66]{0:T(128)S(1)} %pad_add_fusion.info_ref, f32[2,32,128]{2,1,0:T(8,128)S(1)} %get-tuple-element.49.keep_ref, f32[9,32,128]{2,1,0:T(8,128)S(1)} %collective-permute-done.5.near_ref.got_ref, ...), custom_call_target="tpu_custom_call" | custom-call | flops 1000000000 | bytes 3000000 | tf_op jit(solution)/shard_map/pallas_call | solution.py:583
  64.8 2.1 %collective-permute-start.10 = (f32[2,32,128]{2,1,0:T(8,128)S(1)}, f32[2,32,128]{2,1,0:T(8,128)S(1)}, u32[]{:S(2)}, u32[]{:S(2)}) collective-permute-start(f32[2,32,128]{2,1,0:T(8,128)S(1)} %get-tuple-element.56), channel_id=1, source_target_pairs={{0,16},{16,0},{32,48},{48,32},{64,80},{80,64},{96,112},{112,96},{1... | collective-permute-start | bytes 98312 | tf_op jit(solution)/shard_map/ppermute | solution.py:614
  67.0 6.4 %all-to-all-start.2 = ((s16[16,2,16,128]{3,2,1,0:T(8,128)(2,1)}), s16[16,2,16,128]{3,2,1,0:T(8,128)(2,1)S(1)}, u32[]{:S(2)}, u32[]{:S(2)}) async-start(s16[16,2,16,128]{3,2,1,0:T(8,128)(2,1)} %get-tuple-element.63), calls=%async_computation.2 | async-start | bytes 262144 | tf_op jit(solution)/shard_map/all_to_all | solution.py:683
  73.4 1.2 %shard_map.100 = (f32[4,64,128]{2,1,0:T(8,128)S(1)}, f32[4,64,128]{2,1,0:T(8,128)S(1)}, f32[4,128]{1,0:T(4,128)S(1)}, f32[64,128]{1,0:T(8,128)S(1)}, f32[64,128]...) custom-call(s32[66]{0:T(128)S(1)} %pad_add_fusion.info_ref, ...), custom_call_target="tpu_custom_call" | custom-call | flops 99999997952 | bytes 300000000 | tf_op jit(solution)/shard_map/pallas_call | solution.py:583
  74.7 1.7 %collective-permute-start.12 = (f32[64,128]{1,0:T(8,128)S(1)}, f32[64,128]{1,0:T(8,128)S(1)}, u32[]{:S(2)}, u32[]{:S(2)}) collective-permute-start(f32[64,128]{1,0:T(8,128)S(1)} %get-tuple-element.60), channel_id=1, source_target_pairs={{0,240},{16,32},{32,16},{48,64},{64,48},{80,96},{96,80},{112,128},... | collective-permute-start | bytes 98312 | tf_op jit(solution)/shard_map/ppermute | solution.py:619
  76.3 5.1 %collective-permute-start.14 = (f32[8,128]{1,0:T(8,128)S(1)}, f32[8,128]{1,0:T(8,128)S(1)}, u32[]{:S(2)}, u32[]{:S(2)}) collective-permute-start(f32[8,128]{1,0:T(8,128)S(1)} %get-tuple-element.62), channel_id=1, source_target_pairs={{0,15},{1,0},{2,1},{3,2},{4,3},{5,4},{6,5},{7,6},{8,7},{9,8},{10,9... | collective-permute-start | bytes 12296 | tf_op jit(solution)/shard_map/ppermute | solution.py:601
  81.4 1.0 %collective-permute-done.13.left_ref = f32[8,128]{1,0:T(8,128)S(1)} collective-permute-done((f32[8,128]{1,0:T(8,128)S(1)}, f32[8,128]{1,0:T(8,128)S(1)}, u32[]{:S(2)}, u32[]{:S(2)}) %collective-permute-start.13) | collective-permute-done | bytes 4128 | tf_op jit(solution)/shard_map/ppermute | solution.py:601
  82.7 1.6 %shard_map.101 = (f32[4,64,128]{2,1,0:T(8,128)}, f32[4,64,128]{2,1,0:T(8,128)}, f32[4,64]{1,0:T(4,128)}) custom-call(s32[66]{0:T(128)S(1)} %pad_add_fusion.info_ref, f32[17]{0:T(128)S(1)} %copy-done.5, s16[16,18,16,128]{3,2,1,0:T(8,128)(2,1)S(1)} %all-to-all-done.rec_ref, f32[4,64,128]{2,1,0:T(8,128)S(1)} %get-tuple-element.57.lt_ref, ...), custom_call_target="tpu_custom_call" | custom-call | flops 1000000000 | bytes 3000000 | tf_op jit(solution)/shard_map/pallas_call | solution.py:583
  (40 shorter events, 4.3 us)
Async XLA Ops:
  0.6 21.4 %copy-start = (s32[4,16,16]{2,1,0:T(8,128)S(1)}, s32[4,16,16]{2,1,0:T(8,128)}, u32[]{:S(2)}) copy-start(s32[4,16,16]{2,1,0:T(8,128)} %param.8) | copy-start | bytes 12292
  5.1 10.2 %copy-start.2 = (f32[4,64,128]{2,1,0:T(8,128)S(1)}, f32[4,64,128]{2,1,0:T(8,128)}, u32[]{:S(2)}) copy-start(f32[4,64,128]{2,1,0:T(8,128)} %seed_ref.3) | copy-start | bytes 393220
  5.1 40.7 %copy-start.4 = (f32[64,128]{1,0:T(8,128)S(1)}, f32[64,128]{1,0:T(8,128)}, u32[]{:S(2)}) copy-start(f32[64,128]{1,0:T(8,128)} %length_ref.15) | copy-start | bytes 98308
  5.1 40.7 %all-to-all-start = ((s16[16,18,16,128]{3,2,1,0:T(8,128)(2,1)}), s16[16,18,16,128]{3,2,1,0:T(8,128)(2,1)S(1)}, u32[]{:S(2)}, u32[]{:S(2)}) async-start(s16[16,18,16,128]{3,2,1,0:T(8,128)(2,1)} %shard_map.94), calls=%async_computation | async-start | bytes 2359296 | tf_op jit(solution)/shard_map/all_to_all | solution.py:647
  15.3 26.0 %collective-permute-start = (f32[64,128]{1,0:T(8,128)S(1)}, f32[64,128]{1,0:T(8,128)S(1)}, u32[]{:S(2)}, u32[]{:S(2)}) collective-permute-start(f32[64,128]{1,0:T(8,128)S(1)} %get-tuple-element.68), channel_id=1, source_target_pairs={{0,16},{16,32},{32,48},{48,64},{64,80},{80,96},{96,112},{112,128},... | collective-permute-start | bytes 98312 | tf_op jit(solution)/shard_map/ppermute | solution.py:601
  16.9 26.8 %collective-permute-start.1 = (f32[64,128]{1,0:T(8,128)S(1)}, f32[64,128]{1,0:T(8,128)S(1)}, u32[]{:S(2)}, u32[]{:S(2)}) collective-permute-start(f32[64,128]{1,0:T(8,128)S(1)} %get-tuple-element.67), channel_id=1, source_target_pairs={{0,240},{16,0},{32,16},{48,32},{64,48},{80,64},{96,80},{112,96},{1... | collective-permute-start | bytes 98312 | tf_op jit(solution)/shard_map/ppermute | solution.py:601
  16.9 6.0 %collective-permute-start.2 = (f32[4,128]{1,0:T(4,128)S(1)}, f32[4,128]{1,0:T(4,128)S(1)}, u32[]{:S(2)}, u32[]{:S(2)}) collective-permute-start(f32[4,128]{1,0:T(4,128)S(1)} %bitcast.16), channel_id=1, source_target_pairs={{0,1},{1,2},{2,3},{3,4},{4,5},{5,6},{6,7},{7,8},{8,9},{9,10},{10,1... | collective-permute-start | bytes 6152 | tf_op jit(solution)/shard_map/ppermute | solution.py:601
  18.2 4.7 %collective-permute-start.3 = (f32[4,128]{1,0:T(4,128)S(1)}, f32[4,128]{1,0:T(4,128)S(1)}, u32[]{:S(2)}, u32[]{:S(2)}) collective-permute-start(f32[4,128]{1,0:T(4,128)S(1)} %bitcast.15), channel_id=1, source_target_pairs={{0,15},{1,0},{2,1},{3,2},{4,3},{5,4},{6,5},{7,6},{8,7},{9,8},{10,9... | collective-permute-start | bytes 6152 | tf_op jit(solution)/shard_map/ppermute | solution.py:601
  22.2 25.6 %copy-start.1 = (f32[4,64,128]{2,1,0:T(8,128)S(1)}, f32[4,64,128]{2,1,0:T(8,128)}, u32[]{:S(2)}) copy-start(f32[4,64,128]{2,1,0:T(8,128)} %lr_ref.1) | copy-start | bytes 393220
  46.5 1.3 %collective-permute-start.4 = (f32[1,32,128]{2,1,0:T(8,128)S(1)}, f32[1,32,128]{2,1,0:T(8,128)S(1)}, u32[]{:S(2)}, u32[]{:S(2)}) collective-permute-start(f32[1,32,128]{2,1,0:T(8,128)S(1)} %get-tuple-element.40), channel_id=1, source_target_pairs={{0,16},{16,0},{32,48},{48,32},{64,80},{80,64},{96,112},{112,96},{1... | collective-permute-start | bytes 49160 | tf_op jit(solution)/shard_map/ppermute | solution.py:614
  48.7 1.5 %collective-permute-start.5 = (f32[9,32,128]{2,1,0:T(8,128)S(1)}, f32[9,32,128]{2,1,0:T(8,128)S(1)}, u32[]{:S(2)}, u32[]{:S(2)}) collective-permute-start(f32[9,32,128]{2,1,0:T(8,128)S(1)} %get-tuple-element.44), channel_id=1, source_target_pairs={{0,16},{16,0},{32,48},{48,32},{64,80},{80,64},{96,112},{112,96},{1... | collective-permute-start | bytes 442376 | tf_op jit(solution)/shard_map/ppermute | solution.py:614
  48.9 6.1 %collective-permute-start.6 = (f32[3,64,128]{2,1,0:T(8,128)S(1)}, f32[3,64,128]{2,1,0:T(8,128)S(1)}, u32[]{:S(2)}, u32[]{:S(2)}) collective-permute-start(f32[3,64,128]{2,1,0:T(8,128)S(1)} %get-tuple-element.45), channel_id=1, source_target_pairs={{0,240},{16,32},{32,16},{48,64},{64,48},{80,96},{96,80},{112,128},... | collective-permute-start | bytes 294920 | tf_op jit(solution)/shard_map/ppermute | solution.py:619
  51.4 12.0 %all-to-all-start.1 = ((s16[8,4,16,128]{3,2,1,0:T(8,128)(2,1)}), s16[8,4,16,128]{3,2,1,0:T(8,128)(2,1)S(1)}, u32[]{:S(2)}, u32[]{:S(2)}) async-start(s16[8,4,16,128]{3,2,1,0:T(8,128)(2,1)} %shard_map.98), calls=%async_computation.1 | async-start | bytes 262144 | tf_op jit(solution)/shard_map/all_to_all | solution.py:627
  55.9 7.5 %collective-permute-start.9 = (f32[2,32,128]{2,1,0:T(8,128)S(1)}, f32[2,32,128]{2,1,0:T(8,128)S(1)}, u32[]{:S(2)}, u32[]{:S(2)}) collective-permute-start(f32[2,32,128]{2,1,0:T(8,128)S(1)} %get-tuple-element.53), channel_id=1, source_target_pairs={{0,16},{16,0},{32,48},{48,32},{64,80},{80,64},{96,112},{112,96},{1... | collective-permute-start | bytes 98312 | tf_op jit(solution)/shard_map/ppermute | solution.py:614
  57.4 6.0 %collective-permute-start.7 = (f32[24,128]{1,0:T(8,128)S(1)}, f32[24,128]{1,0:T(8,128)S(1)}, u32[]{:S(2)}, u32[]{:S(2)}) collective-permute-start(f32[24,128]{1,0:T(8,128)S(1)} %get-tuple-element.48.own_right_ref), channel_id=1, source_target_pairs={{0,1},{1,2},{2,3},{3,4},{4,5},{5,6},{6,7},{7,8},{8,9},{9,10},{10,1... | collective-permute-start | bytes 36872 | tf_op jit(solution)/shard_map/ppermute | solution.py:601
  58.6 4.8 %collective-permute-start.8 = (f32[24,128]{1,0:T(8,128)S(1)}, f32[24,128]{1,0:T(8,128)S(1)}, u32[]{:S(2)}, u32[]{:S(2)}) collective-permute-start(f32[24,128]{1,0:T(8,128)S(1)} %get-tuple-element.47.own_left_ref), channel_id=1, source_target_pairs={{0,15},{1,0},{2,1},{3,2},{4,3},{5,4},{6,5},{7,6},{8,7},{9,8},{10,9... | collective-permute-start | bytes 36872 | tf_op jit(solution)/shard_map/ppermute | solution.py:601
  63.4 10.0 %copy-start.3 = (f32[4,64,128]{2,1,0:T(8,128)S(1)}, f32[4,64,128]{2,1,0:T(8,128)}, u32[]{:S(2)}) copy-start(f32[4,64,128]{2,1,0:T(8,128)} %seed_ref.3) | copy-start | bytes 393220
  64.8 8.6 %collective-permute-start.10 = (f32[2,32,128]{2,1,0:T(8,128)S(1)}, f32[2,32,128]{2,1,0:T(8,128)S(1)}, u32[]{:S(2)}, u32[]{:S(2)}) collective-permute-start(f32[2,32,128]{2,1,0:T(8,128)S(1)} %get-tuple-element.56), channel_id=1, source_target_pairs={{0,16},{16,0},{32,48},{48,32},{64,80},{80,64},{96,112},{112,96},{1... | collective-permute-start | bytes 98312 | tf_op jit(solution)/shard_map/ppermute | solution.py:614
  67.0 15.7 %all-to-all-start.2 = ((s16[16,2,16,128]{3,2,1,0:T(8,128)(2,1)}), s16[16,2,16,128]{3,2,1,0:T(8,128)(2,1)S(1)}, u32[]{:S(2)}, u32[]{:S(2)}) async-start(s16[16,2,16,128]{3,2,1,0:T(8,128)(2,1)} %get-tuple-element.63), calls=%async_computation.2 | async-start | bytes 262144 | tf_op jit(solution)/shard_map/all_to_all | solution.py:683
  73.4 9.3 %copy-start.5 = (f32[17]{0:T(128)S(1)}, f32[17]{0:T(128)}, u32[]{:S(2)}) copy-start(f32[17]{0:T(128)} %weight_ref.1) | copy-start | bytes 208
  74.5 7.9 %collective-permute-start.11 = (f32[64,128]{1,0:T(8,128)S(1)}, f32[64,128]{1,0:T(8,128)S(1)}, u32[]{:S(2)}, u32[]{:S(2)}) collective-permute-start(f32[64,128]{1,0:T(8,128)S(1)} %get-tuple-element.59), channel_id=1, source_target_pairs={{0,16},{16,0},{32,48},{48,32},{64,80},{80,64},{96,112},{112,96},{1... | collective-permute-start | bytes 98312 | tf_op jit(solution)/shard_map/ppermute | solution.py:614
  74.7 7.7 %collective-permute-start.12 = (f32[64,128]{1,0:T(8,128)S(1)}, f32[64,128]{1,0:T(8,128)S(1)}, u32[]{:S(2)}, u32[]{:S(2)}) collective-permute-start(f32[64,128]{1,0:T(8,128)S(1)} %get-tuple-element.60), channel_id=1, source_target_pairs={{0,240},{16,32},{32,16},{48,64},{64,48},{80,96},{96,80},{112,128},... | collective-permute-start | bytes 98312 | tf_op jit(solution)/shard_map/ppermute | solution.py:619
  76.3 6.0 %collective-permute-start.13 = (f32[8,128]{1,0:T(8,128)S(1)}, f32[8,128]{1,0:T(8,128)S(1)}, u32[]{:S(2)}, u32[]{:S(2)}) collective-permute-start(f32[8,128]{1,0:T(8,128)S(1)} %get-tuple-element.61), channel_id=1, source_target_pairs={{0,1},{1,2},{2,3},{3,4},{4,5},{5,6},{6,7},{7,8},{8,9},{9,10},{10,1... | collective-permute-start | bytes 12296 | tf_op jit(solution)/shard_map/ppermute | solution.py:601
  76.3 6.0 %collective-permute-start.14 = (f32[8,128]{1,0:T(8,128)S(1)}, f32[8,128]{1,0:T(8,128)S(1)}, u32[]{:S(2)}, u32[]{:S(2)}) collective-permute-start(f32[8,128]{1,0:T(8,128)S(1)} %get-tuple-element.62), channel_id=1, source_target_pairs={{0,15},{1,0},{2,1},{3,2},{4,3},{5,4},{6,5},{7,6},{8,7},{9,8},{10,9... | collective-permute-start | bytes 12296 | tf_op jit(solution)/shard_map/ppermute | solution.py:601
  (1 other events, 3.5 us)

commit v6 on v5

--- a/solution.py
+++ b/solution.py
@@ -11,8 +11,6 @@
 RATE_SCALE = 10500.0
 COEF_SCALE = 1374.0
 COEF_BASE = 23.0
-SEED_SCALE = 1023.0
-SEED_BASE = 31.0
 SUM_SCALE = 728.0
 SUM_BASE = 36.0
 ENCODE_VMEM = 60 * 1024 * 1024
@@ -36,18 +34,11 @@
     return jnp.where(code > 0.0, size, jnp.where(code < 0.0, -size, 0.0))
 
 
-def encode_body(
-    stored_ref, seed_ref, length_ref, out_ref, pieces, seed, length, codes, in_sems, more_sems,
-    out_sems,
-):
+def encode_body(stored_ref, out_ref, pieces, codes, in_sems, out_sems):
     steps, slots = stored_ref.shape[:2]
-    owners = out_ref.shape[0]
-    cap = slots // owners
+    cap = slots // out_ref.shape[0]
     rows = 8 * ROWS
-    first = [
-        pltpu.make_async_copy(seed_ref, seed, more_sems.at[0]),
-        pltpu.make_async_copy(length_ref, length, more_sems.at[1]),
-    ]
+    per = 2 * cap
     half_way = steps // 2
     cuts = [*range(half_way), half_way, steps]
     arrivals = {
@@ -58,24 +49,12 @@
         )
         for start, end in zip(cuts[:-1], cuts[1:])
     }
-    for copy in [*first, *arrivals.values()]:
+    for copy in arrivals.values():
         copy.start()
     row = lax.broadcasted_iota(jnp.int32, (rows, rows), 0)
     column = lax.broadcasted_iota(jnp.int32, (rows, rows), 1)
     picked = (row % ROWS) * 8 + row // ROWS == column
     order = jnp.where(picked, 1.0, 0.0).astype(jnp.bfloat16)
-    for copy in first:
-        copy.wait()
-    decay, _, _ = powers(length[...])
-    field = [seed[layer] for layer in range(seed.shape[0])]
-    _, total = chain(field, decay, jnp.zeros_like(decay))
-    total = squeezed(total, SEED_BASE, SEED_SCALE).astype(jnp.int16)
-    per = 2 * cap
-    half = total.shape[0] // 2
-    for owner in range(owners):
-        for block in range(half // ROWS):
-            top = half * (owner % 2) + ROWS * block
-            codes[owner, steps * per + block] = total[top : top + ROWS, :]
 
     def mixed(step, slot):
         cells = pieces[step, slot].astype(jnp.float32)
@@ -125,26 +104,23 @@
         copy.wait()
 
 
-def encode(stored, seed, length):
+def encode(stored):
     steps, _, _, owners, cap, comps, cells = stored.shape
     flat = stored.reshape(steps, owners * cap, comps, cells)
-    shape = (owners, steps * cap * 2 + seed.shape[1] // (2 * ROWS), ROWS, LANES)
+    shape = (owners, steps * cap * 2, ROWS, LANES)
     return pl.pallas_call(
         encode_body,
-        in_specs=[pl.BlockSpec(memory_space=pl.ANY)] * 3,
+        in_specs=[pl.BlockSpec(memory_space=pl.ANY)],
         out_specs=pl.BlockSpec(memory_space=pl.ANY),
         out_shape=jax.ShapeDtypeStruct(shape, jnp.int16),
         scratch_shapes=[
             pltpu.VMEM(flat.shape, jnp.bfloat16),
-            pltpu.VMEM(seed.shape, jnp.float32),
-            pltpu.VMEM(length.shape, jnp.float32),
             pltpu.VMEM(shape, jnp.int16),
             pltpu.SemaphoreType.DMA((steps,)),
             pltpu.SemaphoreType.DMA((2,)),
-            pltpu.SemaphoreType.DMA((steps + 1,)),
         ],
         compiler_params=pltpu.CompilerParams(vmem_limit_bytes=ENCODE_VMEM),
-    )(flat, seed, length)
+    )(flat)
 
 
 def decoded(info_ref, rec_ref, step, layer, field):
@@ -242,7 +218,7 @@
 
 def cores(info_ref, keep_ref, got_ref):
     upper_here = info_ref[64] % 2 == 1
-    own = [keep_ref[index] for index in range(keep_ref.shape[0])]
+    own = [keep_ref[index] for index in range(min(4, keep_ref.shape[0]))]
     other = [got_ref[index] for index in range(len(own))]
     upper = [jnp.where(upper_here, a, b) for a, b in zip(own, other)]
     lower = [jnp.where(upper_here, b, a) for a, b in zip(own, other)]
@@ -260,6 +236,7 @@
     out = [sums + fall * value for value, sums in zip(carry, here)]
     if len(carry) > 1:
         out[1] = out[1] + cross * carry[0]
+        out[2] = out[2] + cross * carry[1] + here[3] * carry[0]
     return tuple(out)
 
 
@@ -274,96 +251,100 @@
     return jnp.concatenate([spread_out(part, SUM_BASE, SUM_SCALE) for part in code], axis=0)
 
 
-def climbed(info_ref, sums_ref, fall, cross):
-    chips, blocks = sums_ref.shape[:2]
-    per = fall.shape[0] // ROWS
-    count = blocks // per
-    total = (jnp.zeros_like(fall),) * count
-    for chip in reversed(range(1, chips)):
-        here = [got_sum(sums_ref, chip, per * index, per) for index in range(count)]
-        new = applied(total, here, fall * fall, 2.0 * fall * cross)
-        inside = chip > info_ref[64] // 2
-        total = tuple(jnp.where(inside, a, b) for a, b in zip(new, total))
-    return total
-
-
 def answered(gain, share, decay):
     climbs, _ = chain(share, decay, jnp.zeros_like(decay))
     return [g * s + c for g, s, c in zip(gain, share, climbs)]
 
 
-def seed_carry_body(info_ref, rec_ref, length_ref, mine_ref, other_ref):
-    _, fall, _ = half_powers(info_ref, length_ref)
-    peers, blocks = rec_ref.shape[:2]
-    count = fall.shape[0] // ROWS
-
-    def total_of(peer):
-        code = [rec_ref[peer, blocks - count + block] for block in range(count)]
-        return jnp.concatenate(
-            [spread_out(part, SEED_BASE, SEED_SCALE) for part in code], axis=0
-        )
-
-    upper = info_ref[64] // 2 * 2 + 1
-    above = jnp.zeros_like(fall)
-    for peer in reversed(range(2, peers)):
-        above = jnp.where(peer > upper, fall * above + total_of(peer), above)
-    below = fall * above + total_of(upper)
-    share_out(info_ref, (above,), (below,), mine_ref, other_ref)
+def shares(decay, layers):
+    out = [None] * layers
+    power = jnp.ones_like(decay)
+    for layer in reversed(range(layers)):
+        out[layer] = power
+        power = decay * power
+    return out
 
 
 def first_body(
     info_ref, rec_ref, lt_ref, lr_ref, low_ref, high_ref, left_ref, right_ref, length_ref,
-    mine_ref, got_ref, new_lt_ref, new_lr_ref, source_ref, far_ref, keep_ref, give_ref,
-    carried, scratch,
+    new_lt_ref, new_lr_ref, source_ref, far_ref, keep_ref, give_ref, scratch,
 ):
     layers = lt_ref.shape[0]
     decay, _, _ = powers(length_ref[...])
-    (zero,) = restored(info_ref, mine_ref, got_ref, carried)
+    nothing = jnp.zeros_like(decay)
     lt = [lt_ref[layer] for layer in range(layers)]
     lr = [lr_ref[layer] for layer in range(layers)]
-    spread = laplace(lt, *halos(info_ref, low_ref, high_ref, left_ref, right_ref))
+    low = jnp.where(info_ref[64] == 0, 0.0, low_ref[...])
+    high = jnp.where(info_ref[64] == info_ref[65] - 1, 0.0, high_ref[0])
+    spread = laplace(lt, low, high, left_ref[0:layers, :], right_ref[0:layers, :])
     new_lt = [
         lt[l] + 0.15 * spread[l] + decoded(info_ref, rec_ref, 3, l, 1) * lr[l]
         for l in range(layers)
     ]
-    climbs, _ = chain(lr, decay, zero)
-    lr = [
-        -0.3 * lt[l] + (1.0 + 0.2 * decoded(info_ref, rec_ref, 3, l, 0)) * lr[l] + climbs[l]
+    climbs, begin = chain(lr, decay, nothing)
+    base = [
+        -0.3 * lt[l] + (1.0 + 0.2 * decoded(info_ref, rec_ref, 3, l, 0)) * lr[l]
         for l in range(layers)
     ]
-    source = [decoded(info_ref, rec_ref, 2, l, 1) * lr[l] for l in range(layers)]
+    lr = [base[l] + climbs[l] for l in range(layers)]
+    gate = [decoded(info_ref, rec_ref, 2, l, 1) for l in range(layers)]
     half = decay.shape[0] // 2
-    up, down = (new_lt[-2], new_lt[-1], source[-1]), (new_lt[0], new_lt[1], source[0])
-    upper_here = info_ref[64] % 2 == 1
-    for index in range(3):
+    up = (new_lt[-2], new_lt[-1], gate[-1] * base[-1], gate[-1])
+    down = (new_lt[0], new_lt[1], gate[0] * base[0], gate[0])
+    upper_here = info_ref[64] % 2 == 1
+    for index in range(4):
         far_ref[index] = jnp.where(upper_here, up[index], down[index])
         near = jnp.where(upper_here, down[index], up[index])
-        give_ref[2 + 2 * index] = near[:half]
-        give_ref[3 + 2 * index] = near[half:]
+        give_ref[4 + 2 * index] = near[:half]
+        give_ref[5 + 2 * index] = near[half:]
     for l in range(layers):
-        give_ref[8, l : l + 1, :] = new_lt[l][0:1, :]
-        give_ref[8, layers + l : layers + l + 1, :] = new_lt[l][2 * half - 1 : 2 * half, :]
-    nothing = jnp.zeros_like(decay)
+        give_ref[12, l : l + 1, :] = new_lt[l][0:1, :]
+        give_ref[12, layers + l : layers + l + 1, :] = new_lt[l][2 * half - 1 : 2 * half, :]
+    beyond_sums = []
+    for ref in (left_ref, right_ref):
+        side_decay, _, _ = powers(ref[2 * layers : 2 * layers + 1, :])
+        side = [ref[layers + l : layers + l + 1, :] for l in range(layers)]
+        beyond_sums.append(chain(side, side_decay, jnp.zeros_like(side_decay))[1])
+    keep_ref[4] = jnp.zeros_like(keep_ref[4])
+    give_ref[12, 8:, :] = jnp.zeros_like(give_ref[12, 8:, :])
+    keep_ref[4, 0:1, :] = jnp.where(upper_here, beyond_sums[1], beyond_sums[0])
+    give_ref[12, 8:9, :] = jnp.where(upper_here, beyond_sums[0], beyond_sums[1])
     _, now = chain(lr, decay, nothing)
     gain = [1.0 + 0.2 * decoded(info_ref, rec_ref, 2, l, 0) for l in range(layers)]
     after = [a - 0.3 * new_lt[l] for l, a in enumerate(answered(gain, lr, decay))]
     _, later = chain(after, decay, nothing)
-    halves(info_ref, (now, later), scratch, keep_ref, give_ref)
+    _, weight = chain(answered(gain, shares(decay, layers), decay), decay, nothing)
+    halves(info_ref, (begin, now, later, weight), scratch, keep_ref, give_ref)
     for l in range(layers):
         new_lt_ref[l] = new_lt[l]
         new_lr_ref[l] = lr[l]
-        source_ref[l] = source[l]
-
-
-def pair_chip_body(info_ref, keep_ref, got_ref, length_ref, out_ref):
+        source_ref[l] = gate[l] * lr[l]
+
+
+def side_powers(info_ref, early_left_ref, early_right_ref):
+    upper_here = info_ref[64] % 2 == 1
+    length = jnp.where(upper_here, early_right_ref[8:9, :], early_left_ref[8:9, :])
+    return powers(length)
+
+
+def pair_chip_body(
+    info_ref, keep_ref, got_ref, early_left_ref, early_right_ref, length_ref, out_ref,
+):
     _, fall, cross = half_powers(info_ref, length_ref)
+    _, side_fall, _ = side_powers(info_ref, early_left_ref, early_right_ref)
     upper, lower = cores(info_ref, keep_ref, got_ref)
-    total = applied(upper, lower, fall, cross)
-    total = [squeezed(value, SUM_BASE, SUM_SCALE) for value in total]
-    per = fall.shape[0] // ROWS
-    for chip in range(out_ref.shape[0]):
-        for index, value in enumerate(total):
-            put_sum(out_ref, chip, per * index, value)
+    total = list(applied(upper[:3], lower, fall, cross))
+    total.append(fall * (lower[3] + upper[3]) + cross * cross)
+    upper_here = info_ref[64] % 2 == 1
+    own, other = keep_ref[4, 0:1, :], got_ref[12, 8:9, :]
+    side = jnp.where(upper_here, other, own) + side_fall * jnp.where(upper_here, own, other)
+    total.append(jnp.broadcast_to(side, (ROWS, side.shape[1])))
+    start = 0
+    for value in total:
+        code = squeezed(value, SUM_BASE, SUM_SCALE)
+        for chip in range(out_ref.shape[0]):
+            put_sum(out_ref, chip, start, code)
+        start += value.shape[0] // ROWS
 
 
 def reach_body(
@@ -376,7 +357,7 @@
     upper_here = info_ref[64] % 2 == 1
     low, high = [], []
     for index in range(3):
-        near = jnp.concatenate([near_ref[2 + 2 * index], near_ref[3 + 2 * index]], axis=0)
+        near = jnp.concatenate([near_ref[4 + 2 * index], near_ref[5 + 2 * index]], axis=0)
         far = jnp.where(jnp.logical_or(bottom, top), 0.0, far_ref[index])
         low.append(jnp.where(upper_here, near, far))
         high.append(jnp.where(upper_here, far, near))
@@ -386,6 +367,7 @@
     new_lt = [lt[l] + 0.15 * spread[l] + source[l] for l in range(layers + 2)]
     new_lt[0] = jnp.where(bottom, 0.0, new_lt[0])
     new_lt[-1] = jnp.where(top, 0.0, new_lt[-1])
+    gate = [decoded(info_ref, rec_ref, 2, l, 1) for l in range(layers)]
     sides = ((left_out, 0, 1, 0), (right_out, azimuths - 1, azimuths - 2, layers))
     for out, edge, inside, other in sides:
         for l in range(layers + 2):
@@ -394,8 +376,8 @@
         for l in range(layers):
             out[8 + l : 9 + l, :] = lt[l + 1][inside : inside + 1, :]
             out[12 + l : 13 + l, :] = source[l + 1][edge : edge + 1, :]
-        out[16:20, :] = near_ref[8, other : other + layers, :]
-        out[20:24, :] = jnp.zeros_like(out[20:24, :])
+            out[20 + l : 21 + l, :] = gate[l][edge : edge + 1, :]
+        out[16:20, :] = near_ref[12, other : other + layers, :]
     for l in range(layers + 2):
         new_lt_ref[l] = new_lt[l]
     new_lt = new_lt[1:-1]
@@ -407,13 +389,12 @@
     lr = [a - 0.3 * lt_ref[l] for l, a in enumerate(answered(one, lr, decay))]
     lr = [a - 0.3 * new_lt[l] for l, a in enumerate(answered(two, lr, decay))]
     _, later = chain(lr, decay, nothing)
-    share = [None] * layers
-    power = jnp.ones_like(decay)
-    for layer in reversed(range(layers)):
-        share[layer] = power
-        power = decay * power
-    _, weight = chain(answered(two, share, decay), decay, nothing)
-    halves(info_ref, (later, weight), scratch, keep_ref, give_ref)
+    share = shares(decay, layers)
+    by_zero = answered(two, answered(one, share, decay), decay)
+    by_zero = [by_zero[l] - 0.3 * gate[l] * share[l] for l in range(layers)]
+    _, one_weight = chain(answered(two, share, decay), decay, nothing)
+    _, zero_weight = chain(by_zero, decay, nothing)
+    halves(info_ref, (later, one_weight, zero_weight), scratch, keep_ref, give_ref)
 
 
 def beyond(there, here):
@@ -424,17 +405,35 @@
 
 def pair_carry_body(
     info_ref, keep_ref, got_ref, more_ref, more_got_ref, sums_ref, left_ref, right_ref,
-    length_ref, mine_ref, other_ref, out_ref,
+    early_left_ref, early_right_ref, length_ref, mine_ref, other_ref, out_ref,
 ):
     _, fall, cross = half_powers(info_ref, length_ref)
-    above = climbed(info_ref, sums_ref, fall, cross)
+    _, side_fall, _ = side_powers(info_ref, early_left_ref, early_right_ref)
+    chips = sums_ref.shape[0]
+    per = fall.shape[0] // ROWS
+    above = (jnp.zeros_like(fall),) * 3
+    side = jnp.zeros_like(side_fall)
+    for chip in reversed(range(1, chips)):
+        inside = chip > info_ref[64] // 2
+        here = [got_sum(sums_ref, chip, per * index, per) for index in range(4)]
+        new = applied(above, here, fall * fall, 2.0 * fall * cross)
+        above = tuple(jnp.where(inside, a, b) for a, b in zip(new, above))
+        new = got_sum(sums_ref, chip, 4 * per, 1)[0:1, :] + side_fall * side_fall * side
+        side = jnp.where(inside, new, side)
     upper, _ = cores(info_ref, keep_ref, got_ref)
     below = applied(above, upper, fall, cross)
     share_out(info_ref, above, below, mine_ref, other_ref)
+    upper_here = info_ref[64] % 2 == 1
+    below_side = side_fall * side + jnp.where(
+        upper_here, keep_ref[4, 0:1, :], got_ref[12, 8:9, :]
+    )
+    mine_ref[3] = jnp.zeros_like(fall)
+    other_ref[3] = jnp.zeros_like(fall)
+    mine_ref[3, 0:1, :] = jnp.where(upper_here, side, below_side)
+    other_ref[3, 0:1, :] = jnp.where(upper_here, below_side, side)
     upper, lower = cores(info_ref, more_ref, more_got_ref)
-    upper = upper[0] + upper[1] * above[0] + cross * above[1]
-    lower = lower[0] + lower[1] * below[0] + cross * below[1]
-    upper_here = info_ref[64] % 2 == 1
+    upper = upper[0] + upper[1] * above[1] + upper[2] * above[0] + cross * above[2]
+    lower = lower[0] + lower[1] * below[1] + lower[2] * below[0] + cross * below[2]
     end = length_ref.shape[0] - 1
     beside = jnp.where(upper_here, right_ref[...], left_ref[...])
     decay, _, _ = powers(jnp.where(upper_here, length_ref[end:, :], length_ref[0:1, :]))
@@ -455,14 +454,36 @@
 
 
 def third_body(
-    info_ref, rec_ref, seed_ref, one_ref, lt_ref, lr_ref, own_left_ref, own_right_ref,
-    left_ref, right_ref, length_ref, face_ref,
+    info_ref, rec_ref, seed_ref, seed_lr_ref, one_ref, lt_ref, lr_ref, own_left_ref,
+    own_right_ref, left_ref, right_ref, near_ref, beyond_ref, high_ref, early_left_ref,
+    early_right_ref, length_ref, face_ref,
     mine_ref, got_ref, new_lt_ref, new_lr_ref, flux_ref, near_out, far_out, left_out, right_out,
     scratch,
 ):
     layers, azimuths, radials = lr_ref.shape
     decay, _, _ = powers(length_ref[...])
-    one, two = restored(info_ref, mine_ref, got_ref, scratch)
+    zero, one, two = restored(info_ref, mine_ref, got_ref, scratch)
+    upper_here = info_ref[64] % 2 == 1
+    share = shares(decay, layers)
+    lift = [share[l] * zero for l in range(layers)]
+    seed_lr = [seed_lr_ref[layer] for layer in range(layers)]
+    _, under = chain(seed_lr, decay, zero)
+    over = (zero - (1.0 - decay) * high_ref[1]) / decay
+    near = jnp.concatenate([near_ref[10], near_ref[11]], axis=0)
+    gate_low = jnp.where(upper_here, near, beyond_ref[3])
+    gate_high = jnp.where(upper_here, beyond_ref[3], near)
+    lifts = [
+        jnp.where(info_ref[64] == 0, 0.0, gate_low * under),
+        *[decoded(info_ref, rec_ref, 2, l, 1) * lift[l] for l in range(layers)],
+        jnp.where(info_ref[64] == info_ref[65] - 1, 0.0, gate_high * over),
+    ]
+    mine_side, got_side = mine_ref[3, 0:1, :], got_ref[3, 0:1, :]
+
+    def lifted(there, early_ref, side):
+        side_decay, _, _ = powers(early_ref[8:9, :])
+        side_share = jnp.concatenate(shares(side_decay, layers), axis=0)
+        return there[20:24] * side_share * side
+
     before = [one_ref[layer] for layer in range(layers)]
     left, right = left_ref[...], right_ref[...]
     row = lax.broadcasted_iota(jnp.int32, (azimuths, radials), 0)
@@ -473,9 +494,9 @@
             left[l : l + 1, :],
             jnp.where(row == azimuths - 1, right[l : l + 1, :], 0.0),
         )
-        full.append(lt_ref[l] + 0.15 * missing)
+        full.append(lt_ref[l] + 0.15 * missing + lifts[l])
     lt = full[1:-1]
-    lr = [lr_ref[layer] for layer in range(layers)]
+    lr = [lr_ref[layer] + lift[layer] for layer in range(layers)]
     climbs, _ = chain(lr, decay, one)
     lr = [
         -0.3 * before[l]
@@ -487,8 +508,10 @@
         lt,
         full[0],
         full[-1],
-        beyond(left, own_left_ref[...]),
-        beyond(right, own_right_ref[...]),
+        beyond(left, own_left_ref[...])
+        + lifted(left, early_left_ref, jnp.where(upper_here, got_side, mine_side)),
+        beyond(right, own_right_ref[...])
+        + lifted(right, early_right_ref, jnp.where(upper_here, mine_side, got_side)),
     )
     new_lt = [
         lt[l] + 0.15 * spread[l] + decoded(info_ref, rec_ref, 1, l, 1) * lr[l]
@@ -643,32 +666,39 @@
     def copies(peers, count):
         return (peers, count * azimuths // (2 * ROWS), ROWS, radials)
 
-    codes = encode(stored, seed_disloc, decay_length)
-    pieces = lax.all_to_all(codes, "axial", 0, 0, tiled=True)
-    halo = exchanged(
-        seed_temp[0], seed_temp[layers - 1], seed_temp[:, 0], seed_temp[:, azimuths - 1]
-    )
-    pieces, *halo = lax.optimization_barrier((pieces, *halo))
-    mine, other = run(seed_carry_body, (info,), (pieces, decay_length), [half(1)] * 2)
+    pieces = lax.all_to_all(encode(stored), "axial", 0, 0, tiled=True)
+
+    def column(at):
+        rows = [seed_temp[:, at], seed_disloc[:, at], decay_length[at : at + 1]]
+        return jnp.pad(jnp.concatenate(rows, axis=0), ((0, 16 - 2 * layers - 1), (0, 0)))
+
+    low = turned(seed_temp[layers - 1], "axial", 1)
+    high = turned(jnp.stack([seed_temp[0], seed_disloc[0]]), "axial", -1)
+    early = (turned(column(azimuths - 1), "azim", 1), turned(column(0), "azim", -1))
+    pieces, low, high, *early = lax.optimization_barrier((pieces, low, high, *early))
     lt1, lr1, source, far, keep, give = run(
         first_body,
         (info,),
-        (pieces, seed_temp, seed_disloc, *halo, decay_length, mine, swapped(other)),
-        [block, block, block, (3, *plane), half(2), half(9)],
-        [(1, *plane), (2, *plane)],
+        (pieces, seed_temp, seed_disloc, low, high, *early, decay_length),
+        [block, block, block, (4, *plane), half(5), half(13)],
+        [(4, *plane)],
     )
     got = swapped(give)
     far = crossed(far)
     (total,) = run(
-        pair_chip_body, (info,), (keep, got, decay_length), [copies(axial // 2, 2)], span=CHIP_SPAN
+        pair_chip_body,
+        (info,),
+        (keep, got, *early, decay_length),
+        [(axial // 2, azimuths // ROWS * 2 + 1, ROWS, radials)],
+        span=CHIP_SPAN,
     )
     sums = between_chips(total)
     lt2, left, right, more, give = run(
         reach_body,
         (info,),
         (pieces, lt1, lr1, source, got, far, decay_length),
-        [(layers + 2, *plane), (24, radials), (24, radials), half(2), half(2)],
-        [(2, *plane)],
+        [(layers + 2, *plane), (24, radials), (24, radials), half(3), half(3)],
+        [(3, *plane)],
         span=REACH_SPAN,
     )
     more_got = swapped(give)
@@ -677,19 +707,19 @@
     mine, other, total = run(
         pair_carry_body,
         (info,),
-        (keep, got, more, more_got, sums, *sides, decay_length),
-        [half(2), half(2), copies(axial, 1)],
+        (keep, got, more, more_got, sums, *sides, *early, decay_length),
+        [half(4), half(4), copies(axial, 1)],
     )
     sums = lax.all_to_all(total, "axial", 0, 0, tiled=True)
     lt3, lr3, flux, near, far, left, right = run(
         third_body,
         (info,),
         (
-            pieces, seed_temp, lt1, lt2, lr1, left, right, *sides, decay_length,
-            face_radius[:, :, None], mine, swapped(other),
+            pieces, seed_temp, seed_disloc, lt1, lt2, lr1, left, right, *sides, got, far,
+            high, *early, decay_length, face_radius[:, :, None], mine, swapped(other),
         ),
         [block, block, side, plane, plane, wide, wide],
-        [(2, *plane)],
+        [(3, *plane)],
         span=THIRD_SPAN,
     )
     halo = (

time: 85.5 us -> 81 us (0.947)
  waiting for transfers between devices: 28.4 us -> 25.9 us
  starting transfers between devices: 42.5 us -> 40.8 us
    ppermute x8, waiting for transfers between devices: 23.6 us -> 20.7 us  [turned(): lax.ppermute(value, axis, [(i, (i + shift) % count) for i in range(count)])]
    all_to_all x1, starting transfers between devices: 6.37 us -> 3.67 us  [local(): sums = lax.all_to_all(total, 'axial', 0, 0, tiled=True)]
    all_to_all x1, waiting for transfers between devices: 0.01 us -> 1.82 us  [between_chips(): lax.all_to_all(value, 'axial', 0, 0, tiled=True, axis_index_groups=groups)]
    ppermute x5 -> x4, waiting for transfers between devices: 2.38 us -> 1.36 us  [swapped(): lax.ppermute(value, 'axial', [(i, i ^ 1) for i in range(lax.axis_size('ax...]
    ppermute x5 -> x4, starting transfers between devices: 4 us -> 4.74 us  [swapped(): lax.ppermute(value, 'axial', [(i, i ^ 1) for i in range(lax.axis_size('ax...]
    pallas_call x7 -> x6, Pallas kernels: 7.84 us -> 7.63 us  [run(): pl.pallas_call(body, in_specs=[smem] * len(scalars) + [vmem] * len(args),...]
  transfers between devices with their start and end apart: 18 -> 17, of which waited for: 9 -> 8; matrix products, arithmetic and copies ran while one was open for 0% -> 0% of each run, Pallas kernels for 4% -> 5%
where the time goes in v6:
time: 81 us; the launch traced here: 79.7 us
  starting transfers between devices  40.8 us (50%)
  waiting for transfers between devices  25.9 us (32%)
  Pallas kernels  11.7 us (14%)
  between operations  0.88 us (1%)
    ppermute x8, waiting for transfers between devices, turned(): lax.ppermute(value, axis, [(i, (i + shift) % count) for i in range(count)])  20.7 us
    ppermute x8, starting transfers between devices, turned(): lax.ppermute(value, axis, [(i, (i + shift) % count) for i in range(count)])  17.2 us
    all_to_all x1, starting transfers between devices, local(): pieces = lax.all_to_all(encode(stored), 'axial', 0, 0, tiled=True)  10 us
    pallas_call x6, Pallas kernels, run(): pl.pallas_call(body, in_specs=[smem] * len(scalars) + [vmem] * len(args),...  7.63 us
    ppermute x4, starting transfers between devices, swapped(): lax.ppermute(value, 'axial', [(i, i ^ 1) for i in range(lax.axis_size('ax...  4.74 us
    pallas_call x1, Pallas kernels, encode(): pl.pallas_call(encode_body, in_specs=[pl.BlockSpec(memory_space=pl.ANY)],...  4.11 us
    all_to_all x1, starting transfers between devices, local(): sums = lax.all_to_all(total, 'axial', 0, 0, tiled=True)  3.67 us
    all_to_all x1, starting transfers between devices, between_chips(): lax.all_to_all(value, 'axial', 0, 0, tiled=True, axis_index_groups=groups)  3.42 us
  transfers between devices with their start and end apart: 17, of which 8 were waited for; matrix products, arithmetic and copies ran while one was open for 0% of the time, Pallas kernels for 5%

profile of v6, /device:TPU:1, one launch (start us, length us, event | category | flops | bytes accessed | tf_op | source)
XLA Modules:
  0.0 79.7 jit_solution(8565982771145845712)
XLA Ops:
  0.7 4.1 %shard_map.94 = s16[16,16,16,128]{3,2,1,0:T(8,128)(2,1)} custom-call(bf16[4,32,8,2048]{3,2,1,0:T(8,128)(2,1)} %bitcast.17), custom_call_target="tpu_custom_call" | custom-call | tf_op jit(solution)/shard_map/pallas_call | solution.py:111
  4.8 10.0 %all-to-all-start = ((s16[16,16,16,128]{3,2,1,0:T(8,128)(2,1)}), s16[16,16,16,128]{3,2,1,0:T(8,128)(2,1)S(1)}, u32[]{:S(2)}, u32[]{:S(2)}) async-start(s16[16,16,16,128]{3,2,1,0:T(8,128)(2,1)} %shard_map.94), calls=%async_computation | async-start | bytes 2097152 | tf_op jit(solution)/shard_map/all_to_all | solution.py:669
  14.9 1.3 %collective-permute-start.2 = (f32[16,128]{1,0:T(8,128)S(1)}, f32[16,128]{1,0:T(8,128)S(1)}, u32[]{:S(2)}, u32[]{:S(2)}) collective-permute-start(f32[16,128]{1,0:T(8,128)S(1)} %select_maximum_fusion.2), channel_id=1, source_target_pairs={{0,1},{1,2},{2,3},{3,4},{4,5},{5,6},{6,7},{7,8},{8,9},{9,10},{10,1... | collective-permute-start | bytes 24584 | tf_op jit(solution)/shard_map/ppermute | solution.py:624
  16.2 3.8 %collective-permute-start.3 = (f32[16,128]{1,0:T(8,128)S(1)}, f32[16,128]{1,0:T(8,128)S(1)}, u32[]{:S(2)}, u32[]{:S(2)}) collective-permute-start(f32[16,128]{1,0:T(8,128)S(1)} %select_maximum_fusion), channel_id=1, source_target_pairs={{0,15},{1,0},{2,1},{3,2},{4,3},{5,4},{6,5},{7,6},{8,7},{9,8},{10,9... | collective-permute-start | bytes 24584 | tf_op jit(solution)/shard_map/ppermute | solution.py:624
  20.5 1.6 %collective-permute-start = (f32[64,128]{1,0:T(8,128)S(1)}, f32[64,128]{1,0:T(8,128)S(1)}, u32[]{:S(2)}, u32[]{:S(2)}) collective-permute-start(f32[64,128]{1,0:T(8,128)S(1)} %get-tuple-element.66), channel_id=1, source_target_pairs={{0,16},{16,32},{32,48},{48,64},{64,80},{80,96},{96,112},{112,128},... | collective-permute-start | bytes 98312 | tf_op jit(solution)/shard_map/ppermute | solution.py:624
  22.3 15.7 %collective-permute-done.low_ref = f32[64,128]{1,0:T(8,128)S(1)} collective-permute-done((f32[64,128]{1,0:T(8,128)S(1)}, f32[64,128]{1,0:T(8,128)S(1)}, u32[]{:S(2)}, u32[]{:S(2)}) %collective-permute-start) | collective-permute-done | bytes 32800 | tf_op jit(solution)/shard_map/ppermute | solution.py:624
  38.0 2.8 %collective-permute-done.1.high_ref = f32[2,64,128]{2,1,0:T(8,128)S(1)} collective-permute-done((f32[2,64,128]{2,1,0:T(8,128)S(1)}, f32[2,64,128]{2,1,0:T(8,128)S(1)}, u32[]{:S(2)}, u32[]{:S(2)}) %collective-permute-start.1) | collective-permute-done | bytes 65568 | tf_op jit(solution)/shard_map/ppermute | solution.py:624
  40.9 1.9 %all-to-all-done.rec_ref = s16[16,16,16,128]{3,2,1,0:T(8,128)(2,1)S(1)} async-done(((s16[16,16,16,128]{3,2,1,0:T(8,128)(2,1)}), s16[16,16,16,128]{3,2,1,0:T(8,128)(2,1)S(1)}, u32[]{:S(2)}, u32[]{:S(2)}) %all-to-all-start) | async-done | bytes 1048608 | tf_op jit(solution)/shard_map/all_to_all | solution.py:669
  43.9 1.4 %collective-permute-done.4.near_ref.got_ref = f32[13,32,128]{2,1,0:T(8,128)S(1)} collective-permute-done((f32[13,32,128]{2,1,0:T(8,128)S(1)}, f32[13,32,128]{2,1,0:T(8,128)S(1)}, u32[]{:S(2)}, u32[]{:S(2)}) %collective-permute-start.4) | collective-permute-done | bytes 213024 | tf_op jit(solution)/shard_map/ppermute | solution.py:637
  45.2 1.3 %shard_map.97 = s16[8,9,16,128]{3,2,1,0:T(8,128)(2,1)} custom-call(s32[66]{0:T(128)S(1)} %pad_add_fusion.info_ref, f32[5,32,128]{2,1,0:T(8,128)S(1)} %get-tuple-element.45.keep_ref, f32[13,32,128]{2,1,0:T(8,128)S(1)} %collective-permute-done.4.near_ref.got_ref, f32[16,128]{1,0:T(8,128)S(1)} %collective-permute-done.2.left_ref.early_left_ref, ...), custom_call_target="tpu_custom_call" | custom-call | flops 49999998976 | bytes 150000000 | tf_op jit(solution)/shard_map/pallas_call | solution.py:606
  46.6 3.4 %all-to-all-start.1 = ((s16[8,9,16,128]{3,2,1,0:T(8,128)(2,1)}), s16[8,9,16,128]{3,2,1,0:T(8,128)(2,1)S(1)}, u32[]{:S(2)}, u32[]{:S(2)}) async-start(s16[8,9,16,128]{3,2,1,0:T(8,128)(2,1)} %shard_map.97), calls=%async_computation.1 | async-start | bytes 589824 | tf_op jit(solution)/shard_map/all_to_all | solution.py:650
  51.0 1.6 %collective-permute-start.8 = (f32[3,32,128]{2,1,0:T(8,128)S(1)}, f32[3,32,128]{2,1,0:T(8,128)S(1)}, u32[]{:S(2)}, u32[]{:S(2)}) collective-permute-start(f32[3,32,128]{2,1,0:T(8,128)S(1)} %get-tuple-element.49), channel_id=1, source_target_pairs={{0,16},{16,0},{32,48},{48,32},{64,80},{80,64},{96,112},{112,96},{1... | collective-permute-start | bytes 147464 | tf_op jit(solution)/shard_map/ppermute | solution.py:637
  52.7 1.2 %collective-permute-start.6 = (f32[24,128]{1,0:T(8,128)S(1)}, f32[24,128]{1,0:T(8,128)S(1)}, u32[]{:S(2)}, u32[]{:S(2)}) collective-permute-start(f32[24,128]{1,0:T(8,128)S(1)} %get-tuple-element.44.own_right_ref), channel_id=1, source_target_pairs={{0,1},{1,2},{2,3},{3,4},{4,5},{5,6},{6,7},{7,8},{8,9},{9,10},{10,1... | collective-permute-start | bytes 36872 | tf_op jit(solution)/shard_map/ppermute | solution.py:624
  53.9 3.7 %collective-permute-start.7 = (f32[24,128]{1,0:T(8,128)S(1)}, f32[24,128]{1,0:T(8,128)S(1)}, u32[]{:S(2)}, u32[]{:S(2)}) collective-permute-start(f32[24,128]{1,0:T(8,128)S(1)} %get-tuple-element.43.own_left_ref), channel_id=1, source_target_pairs={{0,15},{1,0},{2,1},{3,2},{4,3},{5,4},{6,5},{7,6},{8,7},{9,8},{10,9... | collective-permute-start | bytes 36872 | tf_op jit(solution)/shard_map/ppermute | solution.py:624
  57.6 1.1 %collective-permute-done.6.left_ref = f32[24,128]{1,0:T(8,128)S(1)} collective-permute-done((f32[24,128]{1,0:T(8,128)S(1)}, f32[24,128]{1,0:T(8,128)S(1)}, u32[]{:S(2)}, u32[]{:S(2)}) %collective-permute-start.6) | collective-permute-done | bytes 12320 | tf_op jit(solution)/shard_map/ppermute | solution.py:624
  58.7 1.8 %all-to-all-done.1.sums_ref = s16[8,9,16,128]{3,2,1,0:T(8,128)(2,1)S(1)} async-done(((s16[8,9,16,128]{3,2,1,0:T(8,128)(2,1)}), s16[8,9,16,128]{3,2,1,0:T(8,128)(2,1)S(1)}, u32[]{:S(2)}, u32[]{:S(2)}) %all-to-all-start.1) | async-done | bytes 294944 | tf_op jit(solution)/shard_map/all_to_all | solution.py:650
  60.5 1.5 %shard_map.98 = (f32[4,32,128]{2,1,0:T(8,128)S(1)}, f32[4,32,128]{2,1,0:T(8,128)S(1)}, s16[16,2,16,128]{3,2,1,0:T(8,128)(2,1)}) custom-call(s32[66]{0:T(128)S(1)} %pad_add_fusion.info_ref, f32[5,32,128]{2,1,0:T(8,128)S(1)} %get-tuple-element.45.keep_ref, f32[13,32,128]{2,1,0:T(8,128)S(1)} %collective-permute-done.4.near_ref.got_ref, ...), custom_call_target="tpu_custom_call" | custom-call | flops 1000000000 | bytes 3000000 | tf_op jit(solution)/shard_map/pallas_call | solution.py:606
  62.0 2.9 %collective-permute-start.9 = (f32[4,32,128]{2,1,0:T(8,128)S(1)}, f32[4,32,128]{2,1,0:T(8,128)S(1)}, u32[]{:S(2)}, u32[]{:S(2)}) collective-permute-start(f32[4,32,128]{2,1,0:T(8,128)S(1)} %get-tuple-element.52), channel_id=1, source_target_pairs={{0,16},{16,0},{32,48},{48,32},{64,80},{80,64},{96,112},{112,96},{1... | collective-permute-start | bytes 196616 | tf_op jit(solution)/shard_map/ppermute | solution.py:637
  65.1 3.7 %all-to-all-start.2 = ((s16[16,2,16,128]{3,2,1,0:T(8,128)(2,1)}), s16[16,2,16,128]{3,2,1,0:T(8,128)(2,1)S(1)}, u32[]{:S(2)}, u32[]{:S(2)}) async-start(s16[16,2,16,128]{3,2,1,0:T(8,128)(2,1)} %get-tuple-element.59), calls=%async_computation.2 | async-start | bytes 262144 | tf_op jit(solution)/shard_map/all_to_all | solution.py:713
  68.8 1.3 %shard_map.99 = (f32[4,64,128]{2,1,0:T(8,128)S(1)}, f32[4,64,128]{2,1,0:T(8,128)S(1)}, f32[4,128]{1,0:T(4,128)S(1)}, f32[64,128]{1,0:T(8,128)S(1)}, f32[64,128]{...) custom-call(s32[66]{0:T(128)S(1)} %pad_add_fusion.info_ref, ...), custom_call_target="tpu_custom_call" | custom-call | flops 99999997952 | bytes 300000000 | tf_op jit(solution)/shard_map/pallas_call | solution.py:606
  70.2 1.7 %collective-permute-start.11 = (f32[64,128]{1,0:T(8,128)S(1)}, f32[64,128]{1,0:T(8,128)S(1)}, u32[]{:S(2)}, u32[]{:S(2)}) collective-permute-start(f32[64,128]{1,0:T(8,128)S(1)} %get-tuple-element.56), channel_id=1, source_target_pairs={{0,240},{16,32},{32,16},{48,64},{64,48},{80,96},{96,80},{112,128},... | collective-permute-start | bytes 98312 | tf_op jit(solution)/shard_map/ppermute | solution.py:642
  72.7 4.2 %collective-permute-start.13 = (f32[8,128]{1,0:T(8,128)S(1)}, f32[8,128]{1,0:T(8,128)S(1)}, u32[]{:S(2)}, u32[]{:S(2)}) collective-permute-start(f32[8,128]{1,0:T(8,128)S(1)} %get-tuple-element.58), channel_id=1, source_target_pairs={{0,15},{1,0},{2,1},{3,2},{4,3},{5,4},{6,5},{7,6},{8,7},{9,8},{10,9... | collective-permute-start | bytes 12296 | tf_op jit(solution)/shard_map/ppermute | solution.py:624
  76.9 1.0 %collective-permute-done.12.left_ref = f32[8,128]{1,0:T(8,128)S(1)} collective-permute-done((f32[8,128]{1,0:T(8,128)S(1)}, f32[8,128]{1,0:T(8,128)S(1)}, u32[]{:S(2)}, u32[]{:S(2)}) %collective-permute-start.12) | collective-permute-done | bytes 4128 | tf_op jit(solution)/shard_map/ppermute | solution.py:624
  78.1 1.6 %shard_map.100 = (f32[4,64,128]{2,1,0:T(8,128)}, f32[4,64,128]{2,1,0:T(8,128)}, f32[4,64]{1,0:T(4,128)}) custom-call(s32[66]{0:T(128)S(1)} %pad_add_fusion.info_ref, f32[17]{0:T(128)S(1)} %copy-done.8, s16[16,16,16,128]{3,2,1,0:T(8,128)(2,1)S(1)} %all-to-all-done.rec_ref, f32[4,64,128]{2,1,0:T(8,128)S(1)} %get-tuple-element.53.lt_ref, ...), custom_call_target="tpu_custom_call" | custom-call | flops 1000000000 | bytes 3000000 | tf_op jit(solution)/shard_map/pallas_call | solution.py:606
  (50 shorter events, 4.2 us)
Async XLA Ops:
  0.6 21.5 %copy-start = (s32[4,16,16]{2,1,0:T(8,128)S(1)}, s32[4,16,16]{2,1,0:T(8,128)}, u32[]{:S(2)}) copy-start(s32[4,16,16]{2,1,0:T(8,128)} %param.8) | copy-start | bytes 12292
  0.7 14.2 %copy-start.3 = (f32[4,64,128]{2,1,0:T(8,128)S(1)}, f32[4,64,128]{2,1,0:T(8,128)}, u32[]{:S(2)}) copy-start(f32[4,64,128]{2,1,0:T(8,128)} %seed_lr_ref.1) | copy-start | bytes 393220
  0.7 19.3 %slice-start = ((f32[4,64,128]{2,1,0:T(8,128)}), f32[1,64,128]{2,1,0:T(8,128)S(1)}, s32[]{:S(2)}) async-start(f32[4,64,128]{2,1,0:T(8,128)} %seed_lr_ref.1), calls=%async_computation.3 | async-start | bytes 65536 | tf_op jit(solution)/shard_map/slice | solution.py:676
  4.8 37.9 %all-to-all-start = ((s16[16,16,16,128]{3,2,1,0:T(8,128)(2,1)}), s16[16,16,16,128]{3,2,1,0:T(8,128)(2,1)S(1)}, u32[]{:S(2)}, u32[]{:S(2)}) async-start(s16[16,16,16,128]{3,2,1,0:T(8,128)(2,1)} %shard_map.94), calls=%async_computation | async-start | bytes 2097152 | tf_op jit(solution)/shard_map/all_to_all | solution.py:669
  14.9 7.4 %collective-permute-start.2 = (f32[16,128]{1,0:T(8,128)S(1)}, f32[16,128]{1,0:T(8,128)S(1)}, u32[]{:S(2)}, u32[]{:S(2)}) collective-permute-start(f32[16,128]{1,0:T(8,128)S(1)} %select_maximum_fusion.2), channel_id=1, source_target_pairs={{0,1},{1,2},{2,3},{3,4},{4,5},{5,6},{6,7},{7,8},{8,9},{9,10},{10,1... | collective-permute-start | bytes 24584 | tf_op jit(solution)/shard_map/ppermute | solution.py:624
  16.2 6.1 %collective-permute-start.3 = (f32[16,128]{1,0:T(8,128)S(1)}, f32[16,128]{1,0:T(8,128)S(1)}, u32[]{:S(2)}, u32[]{:S(2)}) collective-permute-start(f32[16,128]{1,0:T(8,128)S(1)} %select_maximum_fusion), channel_id=1, source_target_pairs={{0,15},{1,0},{2,1},{3,2},{4,3},{5,4},{6,5},{7,6},{8,7},{9,8},{10,9... | collective-permute-start | bytes 24584 | tf_op jit(solution)/shard_map/ppermute | solution.py:624
  20.0 20.8 %collective-permute-start.1 = (f32[2,64,128]{2,1,0:T(8,128)S(1)}, f32[2,64,128]{2,1,0:T(8,128)S(1)}, u32[]{:S(2)}, u32[]{:S(2)}) collective-permute-start(f32[2,64,128]{2,1,0:T(8,128)S(1)} %pad_maximum_fusion), channel_id=1, source_target_pairs={{0,240},{16,0},{32,16},{48,32},{64,48},{80,64},{96,80},{112,96},{1... | collective-permute-start | bytes 196616 | tf_op jit(solution)/shard_map/ppermute | solution.py:624
  20.5 17.5 %collective-permute-start = (f32[64,128]{1,0:T(8,128)S(1)}, f32[64,128]{1,0:T(8,128)S(1)}, u32[]{:S(2)}, u32[]{:S(2)}) collective-permute-start(f32[64,128]{1,0:T(8,128)S(1)} %get-tuple-element.66), channel_id=1, source_target_pairs={{0,16},{16,32},{32,48},{48,64},{64,80},{80,96},{96,112},{112,128},... | collective-permute-start | bytes 98312 | tf_op jit(solution)/shard_map/ppermute | solution.py:624
  43.7 1.6 %collective-permute-start.4 = (f32[13,32,128]{2,1,0:T(8,128)S(1)}, f32[13,32,128]{2,1,0:T(8,128)S(1)}, u32[]{:S(2)}, u32[]{:S(2)}) collective-permute-start(f32[13,32,128]{2,1,0:T(8,128)S(1)} %get-tuple-element.40), channel_id=1, source_target_pairs={{0,16},{16,0},{32,48},{48,32},{64,80},{80,64},{96,112},{112,96},{1... | collective-permute-start | bytes 638984 | tf_op jit(solution)/shard_map/ppermute | solution.py:637
  43.8 6.2 %collective-permute-start.5 = (f32[4,64,128]{2,1,0:T(8,128)S(1)}, f32[4,64,128]{2,1,0:T(8,128)S(1)}, u32[]{:S(2)}, u32[]{:S(2)}) collective-permute-start(f32[4,64,128]{2,1,0:T(8,128)S(1)} %get-tuple-element.41), channel_id=1, source_target_pairs={{0,240},{16,32},{32,16},{48,64},{64,48},{80,96},{96,80},{112,128},... | collective-permute-start | bytes 393224 | tf_op jit(solution)/shard_map/ppermute | solution.py:642
  46.6 14.0 %all-to-all-start.1 = ((s16[8,9,16,128]{3,2,1,0:T(8,128)(2,1)}), s16[8,9,16,128]{3,2,1,0:T(8,128)(2,1)S(1)}, u32[]{:S(2)}, u32[]{:S(2)}) async-start(s16[8,9,16,128]{3,2,1,0:T(8,128)(2,1)} %shard_map.97), calls=%async_computation.1 | async-start | bytes 589824 | tf_op jit(solution)/shard_map/all_to_all | solution.py:650
  50.0 14.9 %copy-start.9 = (s32[4,64]{1,0:T(4,128)S(1)}, s32[4,64]{1,0:T(4,128)}, u32[]{:S(2)}) copy-start(s32[4,64]{1,0:T(4,128)} %param.12) | copy-start | bytes 3076
  50.0 18.7 %copy-start.2 = (f32[4,64,128]{2,1,0:T(8,128)S(1)}, f32[4,64,128]{2,1,0:T(8,128)}, u32[]{:S(2)}) copy-start(f32[4,64,128]{2,1,0:T(8,128)} %seed_ref.1) | copy-start | bytes 393220
  50.0 18.7 %copy-start.4 = (f32[4,64,128]{2,1,0:T(8,128)S(1)}, f32[4,64,128]{2,1,0:T(8,128)}, u32[]{:S(2)}) copy-start(f32[4,64,128]{2,1,0:T(8,128)} %seed_lr_ref.1) | copy-start | bytes 393220
  50.0 18.7 %copy-start.7 = (f32[2,64,128]{2,1,0:T(8,128)S(1)}, f32[2,64,128]{2,1,0:T(8,128)}, u32[]{:S(2)}) copy-start(f32[2,64,128]{2,1,0:T(8,128)} %copy-done.6) | copy-start | bytes 196612
  51.0 9.5 %collective-permute-start.8 = (f32[3,32,128]{2,1,0:T(8,128)S(1)}, f32[3,32,128]{2,1,0:T(8,128)S(1)}, u32[]{:S(2)}, u32[]{:S(2)}) collective-permute-start(f32[3,32,128]{2,1,0:T(8,128)S(1)} %get-tuple-element.49), channel_id=1, source_target_pairs={{0,16},{16,0},{32,48},{48,32},{64,80},{80,64},{96,112},{112,96},{1... | collective-permute-start | bytes 147464 | tf_op jit(solution)/shard_map/ppermute | solution.py:637
  52.7 6.0 %collective-permute-start.6 = (f32[24,128]{1,0:T(8,128)S(1)}, f32[24,128]{1,0:T(8,128)S(1)}, u32[]{:S(2)}, u32[]{:S(2)}) collective-permute-start(f32[24,128]{1,0:T(8,128)S(1)} %get-tuple-element.44.own_right_ref), channel_id=1, source_target_pairs={{0,1},{1,2},{2,3},{3,4},{4,5},{5,6},{6,7},{7,8},{8,9},{9,10},{10,1... | collective-permute-start | bytes 36872 | tf_op jit(solution)/shard_map/ppermute | solution.py:624
  53.9 4.8 %collective-permute-start.7 = (f32[24,128]{1,0:T(8,128)S(1)}, f32[24,128]{1,0:T(8,128)S(1)}, u32[]{:S(2)}, u32[]{:S(2)}) collective-permute-start(f32[24,128]{1,0:T(8,128)S(1)} %get-tuple-element.43.own_left_ref), channel_id=1, source_target_pairs={{0,15},{1,0},{2,1},{3,2},{4,3},{5,4},{6,5},{7,6},{8,7},{9,8},{10,9... | collective-permute-start | bytes 36872 | tf_op jit(solution)/shard_map/ppermute | solution.py:624
  62.0 6.7 %collective-permute-start.9 = (f32[4,32,128]{2,1,0:T(8,128)S(1)}, f32[4,32,128]{2,1,0:T(8,128)S(1)}, u32[]{:S(2)}, u32[]{:S(2)}) collective-permute-start(f32[4,32,128]{2,1,0:T(8,128)S(1)} %get-tuple-element.52), channel_id=1, source_target_pairs={{0,16},{16,0},{32,48},{48,32},{64,80},{80,64},{96,112},{112,96},{1... | collective-permute-start | bytes 196616 | tf_op jit(solution)/shard_map/ppermute | solution.py:637
  65.1 13.0 %all-to-all-start.2 = ((s16[16,2,16,128]{3,2,1,0:T(8,128)(2,1)}), s16[16,2,16,128]{3,2,1,0:T(8,128)(2,1)S(1)}, u32[]{:S(2)}, u32[]{:S(2)}) async-start(s16[16,2,16,128]{3,2,1,0:T(8,128)(2,1)} %get-tuple-element.59), calls=%async_computation.2 | async-start | bytes 262144 | tf_op jit(solution)/shard_map/all_to_all | solution.py:713
  70.1 7.9 %collective-permute-start.10 = (f32[64,128]{1,0:T(8,128)S(1)}, f32[64,128]{1,0:T(8,128)S(1)}, u32[]{:S(2)}, u32[]{:S(2)}) collective-permute-start(f32[64,128]{1,0:T(8,128)S(1)} %get-tuple-element.55), channel_id=1, source_target_pairs={{0,16},{16,0},{32,48},{48,32},{64,80},{80,64},{96,112},{112,96},{1... | collective-permute-start | bytes 98312 | tf_op jit(solution)/shard_map/ppermute | solution.py:637
  70.2 7.7 %collective-permute-start.11 = (f32[64,128]{1,0:T(8,128)S(1)}, f32[64,128]{1,0:T(8,128)S(1)}, u32[]{:S(2)}, u32[]{:S(2)}) collective-permute-start(f32[64,128]{1,0:T(8,128)S(1)} %get-tuple-element.56), channel_id=1, source_target_pairs={{0,240},{16,32},{32,16},{48,64},{64,48},{80,96},{96,80},{112,128},... | collective-permute-start | bytes 98312 | tf_op jit(solution)/shard_map/ppermute | solution.py:642
  71.9 6.1 %collective-permute-start.12 = (f32[8,128]{1,0:T(8,128)S(1)}, f32[8,128]{1,0:T(8,128)S(1)}, u32[]{:S(2)}, u32[]{:S(2)}) collective-permute-start(f32[8,128]{1,0:T(8,128)S(1)} %get-tuple-element.57), channel_id=1, source_target_pairs={{0,1},{1,2},{2,3},{3,4},{4,5},{5,6},{6,7},{7,8},{8,9},{9,10},{10,1... | collective-permute-start | bytes 12296 | tf_op jit(solution)/shard_map/ppermute | solution.py:624
  72.7 5.2 %collective-permute-start.13 = (f32[8,128]{1,0:T(8,128)S(1)}, f32[8,128]{1,0:T(8,128)S(1)}, u32[]{:S(2)}, u32[]{:S(2)}) collective-permute-start(f32[8,128]{1,0:T(8,128)S(1)} %get-tuple-element.58), channel_id=1, source_target_pairs={{0,15},{1,0},{2,1},{3,2},{4,3},{5,4},{6,5},{7,6},{8,7},{9,8},{10,9... | collective-permute-start | bytes 12296 | tf_op jit(solution)/shard_map/ppermute | solution.py:624
  (4 other events, 43.4 us)

commit v7 on v6

--- a/solution.py
+++ b/solution.py
@@ -11,8 +11,9 @@
 RATE_SCALE = 10500.0
 COEF_SCALE = 1374.0
 COEF_BASE = 23.0
-SUM_SCALE = 728.0
-SUM_BASE = 36.0
+SUM_SCALE = 862.0
+SUM_BASE = 29.0
+PLANE_TOP = 32000.0
 ENCODE_VMEM = 60 * 1024 * 1024
 STEP_VMEM = 16 * 1024 * 1024
 SPAN_FLOPS = 1_000_000_000
@@ -136,12 +137,6 @@
     return jnp.concatenate(pieces, axis=0)
 
 
-def halos(info_ref, low_ref, high_ref, left_ref, right_ref):
-    low = jnp.where(info_ref[64] == 0, 0.0, low_ref[...])
-    high = jnp.where(info_ref[64] == info_ref[65] - 1, 0.0, high_ref[...])
-    return low, high, left_ref[...], right_ref[...]
-
-
 def radial(x):
     lane = lax.broadcasted_iota(jnp.int32, x.shape, 1)
     inner = jnp.where(lane == 0, 0.0, pltpu.roll(x, 1, axis=1))
@@ -175,16 +170,6 @@
     return out, carry
 
 
-def put_edges(field, low_ref, high_ref, left_ref, right_ref):
-    layers = len(field)
-    azimuths = field[0].shape[0]
-    low_ref[...] = field[0]
-    high_ref[...] = field[-1]
-    for layer in range(layers):
-        left_ref[layer : layer + 1, :] = field[layer][0:1, :]
-        right_ref[layer : layer + 1, :] = field[layer][azimuths - 1 : azimuths, :]
-
-
 def powers(length):
     decay = jnp.exp(-1.0 / length)
     cube = decay * decay * decay
@@ -238,6 +223,17 @@
         out[1] = out[1] + cross * carry[0]
         out[2] = out[2] + cross * carry[1] + here[3] * carry[0]
     return tuple(out)
+
+
+def scaled(value):
+    top = jnp.max(jnp.max(jnp.abs(value), axis=1, keepdims=True), axis=0, keepdims=True)
+    size = jnp.ceil(jnp.log2(jnp.maximum(top, 2.0**-100)))
+    code = jnp.round(value * jnp.exp2(-size) * PLANE_TOP)
+    return code.astype(jnp.int32), jnp.broadcast_to(size, (1, value.shape[1])).astype(jnp.int32)
+
+
+def unscaled(code, size):
+    return code.astype(jnp.int32).astype(jnp.float32) * (jnp.exp2(size) * (1.0 / PLANE_TOP))
 
 
 def put_sum(out_ref, at, start, code):
@@ -338,13 +334,14 @@
     upper_here = info_ref[64] % 2 == 1
     own, other = keep_ref[4, 0:1, :], got_ref[12, 8:9, :]
     side = jnp.where(upper_here, other, own) + side_fall * jnp.where(upper_here, own, other)
-    total.append(jnp.broadcast_to(side, (ROWS, side.shape[1])))
-    start = 0
-    for value in total:
-        code = squeezed(value, SUM_BASE, SUM_SCALE)
-        for chip in range(out_ref.shape[0]):
+    codes, sizes = zip(*[scaled(value) for value in [*total, side]])
+    filler = jnp.zeros((ROWS - 1 - len(sizes), side.shape[1]), jnp.int32)
+    last = jnp.concatenate([codes[-1], *sizes, filler], axis=0)
+    for chip in range(out_ref.shape[0]):
+        start = 0
+        for code in (*codes[:-1], last):
             put_sum(out_ref, chip, start, code)
-        start += value.shape[0] // ROWS
+            start += code.shape[0] // ROWS
 
 
 def reach_body(
@@ -415,10 +412,20 @@
     side = jnp.zeros_like(side_fall)
     for chip in reversed(range(1, chips)):
         inside = chip > info_ref[64] // 2
-        here = [got_sum(sums_ref, chip, per * index, per) for index in range(4)]
+        tail = sums_ref[chip, 4 * per].astype(jnp.int32).astype(jnp.float32)
+        here = [
+            jnp.concatenate(
+                [
+                    unscaled(sums_ref[chip, per * index + block], tail[1 + index : 2 + index])
+                    for block in range(per)
+                ],
+                axis=0,
+            )
+            for index in range(4)
+        ]
         new = applied(above, here, fall * fall, 2.0 * fall * cross)
         above = tuple(jnp.where(inside, a, b) for a, b in zip(new, above))
-        new = got_sum(sums_ref, chip, 4 * per, 1)[0:1, :] + side_fall * side_fall * side
+        new = tail[0:1] * (jnp.exp2(tail[5:6]) * (1.0 / PLANE_TOP)) + side_fall * side_fall * side
         side = jnp.where(inside, new, side)
     upper, _ = cores(info_ref, keep_ref, got_ref)
     below = applied(above, upper, fall, cross)
@@ -624,15 +631,6 @@
     return lax.ppermute(value, axis, [(i, (i + shift) % count) for i in range(count)])
 
 
-def exchanged(low, high, left, right):
-    return (
-        turned(high, "axial", 1),
-        turned(low, "axial", -1),
-        turned(right, "azim", 1),
-        turned(left, "azim", -1),
-    )
-
-
 def swapped(value):
     return lax.ppermute(value, "axial", [(i, i ^ 1) for i in range(lax.axis_size("axial"))])
 
@@ -675,7 +673,10 @@
     low = turned(seed_temp[layers - 1], "axial", 1)
     high = turned(jnp.stack([seed_temp[0], seed_disloc[0]]), "axial", -1)
     early = (turned(column(azimuths - 1), "azim", 1), turned(column(0), "azim", -1))
-    pieces, low, high, *early = lax.optimization_barrier((pieces, low, high, *early))
+    face = face_radius[:, :, None]
+    pieces, low, high, face, *early = lax.optimization_barrier(
+        (pieces, low, high, face, *early)
+    )
     lt1, lr1, source, far, keep, give = run(
         first_body,
         (info,),
@@ -716,7 +717,7 @@
         (info,),
         (
             pieces, seed_temp, seed_disloc, lt1, lt2, lr1, left, right, *sides, got, far,
-            high, *early, decay_length, face_radius[:, :, None], mine, swapped(other),
+            high, *early, decay_length, face, mine, swapped(other),
         ),
         [block, block, side, plane, plane, wide, wide],
         [(3, *plane)],

time: 81 us -> 80.9 us (level)
  no operation moved by 1% of the time
where the time goes in v7:
time: 80.9 us; the launch traced here: 79.7 us
  starting transfers between devices  40.8 us (50%)
  waiting for transfers between devices  25.9 us (32%)
  Pallas kernels  11.7 us (14%)
  between operations  0.88 us (1%)
    ppermute x8, waiting for transfers between devices, turned(): lax.ppermute(value, axis, [(i, (i + shift) % count) for i in range(count)])  20.7 us
    ppermute x8, starting transfers between devices, turned(): lax.ppermute(value, axis, [(i, (i + shift) % count) for i in range(count)])  17.2 us
    all_to_all x1, starting transfers between devices, local(): pieces = lax.all_to_all(encode(stored), 'axial', 0, 0, tiled=True)  10 us
    pallas_call x6, Pallas kernels, run(): pl.pallas_call(body, in_specs=[smem] * len(scalars) + [vmem] * len(args),...  7.61 us
    ppermute x4, starting transfers between devices, swapped(): lax.ppermute(value, 'axial', [(i, i ^ 1) for i in range(lax.axis_size('ax...  4.74 us
    pallas_call x1, Pallas kernels, encode(): pl.pallas_call(encode_body, in_specs=[pl.BlockSpec(memory_space=pl.ANY)],...  4.11 us
    all_to_all x1, starting transfers between devices, local(): sums = lax.all_to_all(total, 'axial', 0, 0, tiled=True)  3.67 us
    all_to_all x1, starting transfers between devices, between_chips(): lax.all_to_all(value, 'axial', 0, 0, tiled=True, axis_index_groups=groups)  3.42 us
  transfers between devices with their start and end apart: 17, of which 8 were waited for; matrix products, arithmetic and copies ran while one was open for 0% of the time, Pallas kernels for 5%

profile of v7, /device:TPU:1, one launch (start us, length us, event | category | flops | bytes accessed | tf_op | source)
XLA Modules:
  0.0 79.7 jit_solution(3825996780502698534)
XLA Ops:
  0.7 4.1 %shard_map.94 = s16[16,16,16,128]{3,2,1,0:T(8,128)(2,1)} custom-call(bf16[4,32,8,2048]{3,2,1,0:T(8,128)(2,1)} %bitcast.17), custom_call_target="tpu_custom_call" | custom-call | tf_op jit(solution)/shard_map/pallas_call | solution.py:112
  4.8 10.0 %all-to-all-start = ((s16[16,16,16,128]{3,2,1,0:T(8,128)(2,1)}), s16[16,16,16,128]{3,2,1,0:T(8,128)(2,1)S(1)}, u32[]{:S(2)}, u32[]{:S(2)}) async-start(s16[16,16,16,128]{3,2,1,0:T(8,128)(2,1)} %shard_map.94), calls=%async_computation | async-start | bytes 2097152 | tf_op jit(solution)/shard_map/all_to_all | solution.py:667
  14.9 1.3 %collective-permute-start.2 = (f32[16,128]{1,0:T(8,128)S(1)}, f32[16,128]{1,0:T(8,128)S(1)}, u32[]{:S(2)}, u32[]{:S(2)}) collective-permute-start(f32[16,128]{1,0:T(8,128)S(1)} %select_maximum_fusion.2), channel_id=1, source_target_pairs={{0,1},{1,2},{2,3},{3,4},{4,5},{5,6},{6,7},{7,8},{8,9},{9,10},{10,1... | collective-permute-start | bytes 24584 | tf_op jit(solution)/shard_map/ppermute | solution.py:631
  16.2 3.8 %collective-permute-start.3 = (f32[16,128]{1,0:T(8,128)S(1)}, f32[16,128]{1,0:T(8,128)S(1)}, u32[]{:S(2)}, u32[]{:S(2)}) collective-permute-start(f32[16,128]{1,0:T(8,128)S(1)} %select_maximum_fusion), channel_id=1, source_target_pairs={{0,15},{1,0},{2,1},{3,2},{4,3},{5,4},{6,5},{7,6},{8,7},{9,8},{10,9... | collective-permute-start | bytes 24584 | tf_op jit(solution)/shard_map/ppermute | solution.py:631
  20.5 1.6 %collective-permute-start = (f32[64,128]{1,0:T(8,128)S(1)}, f32[64,128]{1,0:T(8,128)S(1)}, u32[]{:S(2)}, u32[]{:S(2)}) collective-permute-start(f32[64,128]{1,0:T(8,128)S(1)} %get-tuple-element.68), channel_id=1, source_target_pairs={{0,16},{16,32},{32,48},{48,64},{64,80},{80,96},{96,112},{112,128},... | collective-permute-start | bytes 98312 | tf_op jit(solution)/shard_map/ppermute | solution.py:631
  22.3 15.7 %collective-permute-done.low_ref = f32[64,128]{1,0:T(8,128)S(1)} collective-permute-done((f32[64,128]{1,0:T(8,128)S(1)}, f32[64,128]{1,0:T(8,128)S(1)}, u32[]{:S(2)}, u32[]{:S(2)}) %collective-permute-start) | collective-permute-done | bytes 32800 | tf_op jit(solution)/shard_map/ppermute | solution.py:631
  38.0 2.8 %collective-permute-done.1.high_ref = f32[2,64,128]{2,1,0:T(8,128)S(1)} collective-permute-done((f32[2,64,128]{2,1,0:T(8,128)S(1)}, f32[2,64,128]{2,1,0:T(8,128)S(1)}, u32[]{:S(2)}, u32[]{:S(2)}) %collective-permute-start.1) | collective-permute-done | bytes 65568 | tf_op jit(solution)/shard_map/ppermute | solution.py:631
  40.9 1.9 %all-to-all-done.rec_ref = s16[16,16,16,128]{3,2,1,0:T(8,128)(2,1)S(1)} async-done(((s16[16,16,16,128]{3,2,1,0:T(8,128)(2,1)}), s16[16,16,16,128]{3,2,1,0:T(8,128)(2,1)S(1)}, u32[]{:S(2)}, u32[]{:S(2)}) %all-to-all-start) | async-done | bytes 1048608 | tf_op jit(solution)/shard_map/all_to_all | solution.py:667
  43.9 1.4 %collective-permute-done.4.near_ref.got_ref = f32[13,32,128]{2,1,0:T(8,128)S(1)} collective-permute-done((f32[13,32,128]{2,1,0:T(8,128)S(1)}, f32[13,32,128]{2,1,0:T(8,128)S(1)}, u32[]{:S(2)}, u32[]{:S(2)}) %collective-permute-start.4) | collective-permute-done | bytes 213024 | tf_op jit(solution)/shard_map/ppermute | solution.py:635
  45.2 1.4 %shard_map.97 = s16[8,9,16,128]{3,2,1,0:T(8,128)(2,1)} custom-call(s32[66]{0:T(128)S(1)} %pad_add_fusion.info_ref, f32[5,32,128]{2,1,0:T(8,128)S(1)} %get-tuple-element.46.keep_ref, f32[13,32,128]{2,1,0:T(8,128)S(1)} %collective-permute-done.4.near_ref.got_ref, f32[16,128]{1,0:T(8,128)S(1)} %collective-permute-done.2.left_ref.early_left_ref, ...), custom_call_target="tpu_custom_call" | custom-call | flops 49999998976 | bytes 150000000 | tf_op jit(solution)/shard_map/pallas_call | solution.py:613
  46.7 3.4 %all-to-all-start.1 = ((s16[8,9,16,128]{3,2,1,0:T(8,128)(2,1)}), s16[8,9,16,128]{3,2,1,0:T(8,128)(2,1)S(1)}, u32[]{:S(2)}, u32[]{:S(2)}) async-start(s16[8,9,16,128]{3,2,1,0:T(8,128)(2,1)} %shard_map.97), calls=%async_computation.1 | async-start | bytes 589824 | tf_op jit(solution)/shard_map/all_to_all | solution.py:648
  51.1 1.6 %collective-permute-start.8 = (f32[3,32,128]{2,1,0:T(8,128)S(1)}, f32[3,32,128]{2,1,0:T(8,128)S(1)}, u32[]{:S(2)}, u32[]{:S(2)}) collective-permute-start(f32[3,32,128]{2,1,0:T(8,128)S(1)} %get-tuple-element.51), channel_id=1, source_target_pairs={{0,16},{16,0},{32,48},{48,32},{64,80},{80,64},{96,112},{112,96},{1... | collective-permute-start | bytes 147464 | tf_op jit(solution)/shard_map/ppermute | solution.py:635
  52.7 1.2 %collective-permute-start.6 = (f32[24,128]{1,0:T(8,128)S(1)}, f32[24,128]{1,0:T(8,128)S(1)}, u32[]{:S(2)}, u32[]{:S(2)}) collective-permute-start(f32[24,128]{1,0:T(8,128)S(1)} %get-tuple-element.45.own_right_ref), channel_id=1, source_target_pairs={{0,1},{1,2},{2,3},{3,4},{4,5},{5,6},{6,7},{7,8},{8,9},{9,10},{10,1... | collective-permute-start | bytes 36872 | tf_op jit(solution)/shard_map/ppermute | solution.py:631
  54.0 3.7 %collective-permute-start.7 = (f32[24,128]{1,0:T(8,128)S(1)}, f32[24,128]{1,0:T(8,128)S(1)}, u32[]{:S(2)}, u32[]{:S(2)}) collective-permute-start(f32[24,128]{1,0:T(8,128)S(1)} %get-tuple-element.44.own_left_ref), channel_id=1, source_target_pairs={{0,15},{1,0},{2,1},{3,2},{4,3},{5,4},{6,5},{7,6},{8,7},{9,8},{10,9... | collective-permute-start | bytes 36872 | tf_op jit(solution)/shard_map/ppermute | solution.py:631
  57.7 1.1 %collective-permute-done.6.left_ref = f32[24,128]{1,0:T(8,128)S(1)} collective-permute-done((f32[24,128]{1,0:T(8,128)S(1)}, f32[24,128]{1,0:T(8,128)S(1)}, u32[]{:S(2)}, u32[]{:S(2)}) %collective-permute-start.6) | collective-permute-done | bytes 12320 | tf_op jit(solution)/shard_map/ppermute | solution.py:631
  58.8 1.8 %all-to-all-done.1.sums_ref = s16[8,9,16,128]{3,2,1,0:T(8,128)(2,1)S(1)} async-done(((s16[8,9,16,128]{3,2,1,0:T(8,128)(2,1)}), s16[8,9,16,128]{3,2,1,0:T(8,128)(2,1)S(1)}, u32[]{:S(2)}, u32[]{:S(2)}) %all-to-all-start.1) | async-done | bytes 294944 | tf_op jit(solution)/shard_map/all_to_all | solution.py:648
  60.6 1.4 %shard_map.98 = (f32[4,32,128]{2,1,0:T(8,128)S(1)}, f32[4,32,128]{2,1,0:T(8,128)S(1)}, s16[16,2,16,128]{3,2,1,0:T(8,128)(2,1)}) custom-call(s32[66]{0:T(128)S(1)} %pad_add_fusion.info_ref, f32[5,32,128]{2,1,0:T(8,128)S(1)} %get-tuple-element.46.keep_ref, f32[13,32,128]{2,1,0:T(8,128)S(1)} %collective-permute-done.4.near_ref.got_ref, ...), custom_call_target="tpu_custom_call" | custom-call | flops 1000000000 | bytes 3000000 | tf_op jit(solution)/shard_map/pallas_call | solution.py:613
  62.0 2.9 %collective-permute-start.9 = (f32[4,32,128]{2,1,0:T(8,128)S(1)}, f32[4,32,128]{2,1,0:T(8,128)S(1)}, u32[]{:S(2)}, u32[]{:S(2)}) collective-permute-start(f32[4,32,128]{2,1,0:T(8,128)S(1)} %get-tuple-element.54), channel_id=1, source_target_pairs={{0,16},{16,0},{32,48},{48,32},{64,80},{80,64},{96,112},{112,96},{1... | collective-permute-start | bytes 196616 | tf_op jit(solution)/shard_map/ppermute | solution.py:635
  65.0 3.7 %all-to-all-start.2 = ((s16[16,2,16,128]{3,2,1,0:T(8,128)(2,1)}), s16[16,2,16,128]{3,2,1,0:T(8,128)(2,1)S(1)}, u32[]{:S(2)}, u32[]{:S(2)}) async-start(s16[16,2,16,128]{3,2,1,0:T(8,128)(2,1)} %get-tuple-element.61), calls=%async_computation.2 | async-start | bytes 262144 | tf_op jit(solution)/shard_map/all_to_all | solution.py:714
  68.8 1.3 %shard_map.99 = (f32[4,64,128]{2,1,0:T(8,128)S(1)}, f32[4,64,128]{2,1,0:T(8,128)S(1)}, f32[4,128]{1,0:T(4,128)S(1)}, f32[64,128]{1,0:T(8,128)S(1)}, f32[64,128]{...) custom-call(s32[66]{0:T(128)S(1)} %pad_add_fusion.info_ref, ...), custom_call_target="tpu_custom_call" | custom-call | flops 99999997952 | bytes 300000000 | tf_op jit(solution)/shard_map/pallas_call | solution.py:613
  70.2 1.7 %collective-permute-start.11 = (f32[64,128]{1,0:T(8,128)S(1)}, f32[64,128]{1,0:T(8,128)S(1)}, u32[]{:S(2)}, u32[]{:S(2)}) collective-permute-start(f32[64,128]{1,0:T(8,128)S(1)} %get-tuple-element.58), channel_id=1, source_target_pairs={{0,240},{16,32},{32,16},{48,64},{64,48},{80,96},{96,80},{112,128},... | collective-permute-start | bytes 98312 | tf_op jit(solution)/shard_map/ppermute | solution.py:640
  72.7 4.2 %collective-permute-start.13 = (f32[8,128]{1,0:T(8,128)S(1)}, f32[8,128]{1,0:T(8,128)S(1)}, u32[]{:S(2)}, u32[]{:S(2)}) collective-permute-start(f32[8,128]{1,0:T(8,128)S(1)} %get-tuple-element.60), channel_id=1, source_target_pairs={{0,15},{1,0},{2,1},{3,2},{4,3},{5,4},{6,5},{7,6},{8,7},{9,8},{10,9... | collective-permute-start | bytes 12296 | tf_op jit(solution)/shard_map/ppermute | solution.py:631
  76.9 1.0 %collective-permute-done.12.left_ref = f32[8,128]{1,0:T(8,128)S(1)} collective-permute-done((f32[8,128]{1,0:T(8,128)S(1)}, f32[8,128]{1,0:T(8,128)S(1)}, u32[]{:S(2)}, u32[]{:S(2)}) %collective-permute-start.12) | collective-permute-done | bytes 4128 | tf_op jit(solution)/shard_map/ppermute | solution.py:631
  78.1 1.6 %shard_map.100 = (f32[4,64,128]{2,1,0:T(8,128)}, f32[4,64,128]{2,1,0:T(8,128)}, f32[4,64]{1,0:T(4,128)}) custom-call(s32[66]{0:T(128)S(1)} %pad_add_fusion.info_ref, f32[17]{0:T(128)S(1)} %copy-done.8, s16[16,16,16,128]{3,2,1,0:T(8,128)(2,1)S(1)} %all-to-all-done.rec_ref, f32[4,64,128]{2,1,0:T(8,128)S(1)} %get-tuple-element.55.lt_ref, ...), custom_call_target="tpu_custom_call" | custom-call | flops 1000000000 | bytes 3000000 | tf_op jit(solution)/shard_map/pallas_call | solution.py:613
  (50 shorter events, 4.2 us)
Async XLA Ops:
  0.6 21.5 %copy-start = (s32[4,16,16]{2,1,0:T(8,128)S(1)}, s32[4,16,16]{2,1,0:T(8,128)}, u32[]{:S(2)}) copy-start(s32[4,16,16]{2,1,0:T(8,128)} %param.8) | copy-start | bytes 12292
  0.7 14.2 %copy-start.3 = (f32[4,64,128]{2,1,0:T(8,128)S(1)}, f32[4,64,128]{2,1,0:T(8,128)}, u32[]{:S(2)}) copy-start(f32[4,64,128]{2,1,0:T(8,128)} %seed_lr_ref.1) | copy-start | bytes 393220
  0.7 19.3 %slice-start = ((f32[4,64,128]{2,1,0:T(8,128)}), f32[1,64,128]{2,1,0:T(8,128)S(1)}, s32[]{:S(2)}) async-start(f32[4,64,128]{2,1,0:T(8,128)} %seed_lr_ref.1), calls=%async_computation.3 | async-start | bytes 65536 | tf_op jit(solution)/shard_map/slice | solution.py:674
  4.8 37.9 %all-to-all-start = ((s16[16,16,16,128]{3,2,1,0:T(8,128)(2,1)}), s16[16,16,16,128]{3,2,1,0:T(8,128)(2,1)S(1)}, u32[]{:S(2)}, u32[]{:S(2)}) async-start(s16[16,16,16,128]{3,2,1,0:T(8,128)(2,1)} %shard_map.94), calls=%async_computation | async-start | bytes 2097152 | tf_op jit(solution)/shard_map/all_to_all | solution.py:667
  14.9 7.4 %collective-permute-start.2 = (f32[16,128]{1,0:T(8,128)S(1)}, f32[16,128]{1,0:T(8,128)S(1)}, u32[]{:S(2)}, u32[]{:S(2)}) collective-permute-start(f32[16,128]{1,0:T(8,128)S(1)} %select_maximum_fusion.2), channel_id=1, source_target_pairs={{0,1},{1,2},{2,3},{3,4},{4,5},{5,6},{6,7},{7,8},{8,9},{9,10},{10,1... | collective-permute-start | bytes 24584 | tf_op jit(solution)/shard_map/ppermute | solution.py:631
  16.2 6.1 %collective-permute-start.3 = (f32[16,128]{1,0:T(8,128)S(1)}, f32[16,128]{1,0:T(8,128)S(1)}, u32[]{:S(2)}, u32[]{:S(2)}) collective-permute-start(f32[16,128]{1,0:T(8,128)S(1)} %select_maximum_fusion), channel_id=1, source_target_pairs={{0,15},{1,0},{2,1},{3,2},{4,3},{5,4},{6,5},{7,6},{8,7},{9,8},{10,9... | collective-permute-start | bytes 24584 | tf_op jit(solution)/shard_map/ppermute | solution.py:631
  20.0 20.8 %collective-permute-start.1 = (f32[2,64,128]{2,1,0:T(8,128)S(1)}, f32[2,64,128]{2,1,0:T(8,128)S(1)}, u32[]{:S(2)}, u32[]{:S(2)}) collective-permute-start(f32[2,64,128]{2,1,0:T(8,128)S(1)} %pad_maximum_fusion), channel_id=1, source_target_pairs={{0,240},{16,0},{32,16},{48,32},{64,48},{80,64},{96,80},{112,96},{1... | collective-permute-start | bytes 196616 | tf_op jit(solution)/shard_map/ppermute | solution.py:631
  20.5 17.5 %collective-permute-start = (f32[64,128]{1,0:T(8,128)S(1)}, f32[64,128]{1,0:T(8,128)S(1)}, u32[]{:S(2)}, u32[]{:S(2)}) collective-permute-start(f32[64,128]{1,0:T(8,128)S(1)} %get-tuple-element.68), channel_id=1, source_target_pairs={{0,16},{16,32},{32,48},{48,64},{64,80},{80,96},{96,112},{112,128},... | collective-permute-start | bytes 98312 | tf_op jit(solution)/shard_map/ppermute | solution.py:631
  43.7 1.6 %collective-permute-start.4 = (f32[13,32,128]{2,1,0:T(8,128)S(1)}, f32[13,32,128]{2,1,0:T(8,128)S(1)}, u32[]{:S(2)}, u32[]{:S(2)}) collective-permute-start(f32[13,32,128]{2,1,0:T(8,128)S(1)} %get-tuple-element.41), channel_id=1, source_target_pairs={{0,16},{16,0},{32,48},{48,32},{64,80},{80,64},{96,112},{112,96},{1... | collective-permute-start | bytes 638984 | tf_op jit(solution)/shard_map/ppermute | solution.py:635
  43.8 6.3 %collective-permute-start.5 = (f32[4,64,128]{2,1,0:T(8,128)S(1)}, f32[4,64,128]{2,1,0:T(8,128)S(1)}, u32[]{:S(2)}, u32[]{:S(2)}) collective-permute-start(f32[4,64,128]{2,1,0:T(8,128)S(1)} %get-tuple-element.42), channel_id=1, source_target_pairs={{0,240},{16,32},{32,16},{48,64},{64,48},{80,96},{96,80},{112,128},... | collective-permute-start | bytes 393224 | tf_op jit(solution)/shard_map/ppermute | solution.py:640
  46.7 14.0 %all-to-all-start.1 = ((s16[8,9,16,128]{3,2,1,0:T(8,128)(2,1)}), s16[8,9,16,128]{3,2,1,0:T(8,128)(2,1)S(1)}, u32[]{:S(2)}, u32[]{:S(2)}) async-start(s16[8,9,16,128]{3,2,1,0:T(8,128)(2,1)} %shard_map.97), calls=%async_computation.1 | async-start | bytes 589824 | tf_op jit(solution)/shard_map/all_to_all | solution.py:648
  50.1 14.8 %copy-start.9 = (s32[4,64]{1,0:T(4,128)S(1)}, s32[4,64]{1,0:T(4,128)}, u32[]{:S(2)}) copy-start(s32[4,64]{1,0:T(4,128)} %param.12) | copy-start | bytes 3076
  50.1 18.6 %copy-start.2 = (f32[4,64,128]{2,1,0:T(8,128)S(1)}, f32[4,64,128]{2,1,0:T(8,128)}, u32[]{:S(2)}) copy-start(f32[4,64,128]{2,1,0:T(8,128)} %seed_ref.1) | copy-start | bytes 393220
  50.1 18.6 %copy-start.4 = (f32[4,64,128]{2,1,0:T(8,128)S(1)}, f32[4,64,128]{2,1,0:T(8,128)}, u32[]{:S(2)}) copy-start(f32[4,64,128]{2,1,0:T(8,128)} %seed_lr_ref.1) | copy-start | bytes 393220
  50.1 18.6 %copy-start.7 = (f32[2,64,128]{2,1,0:T(8,128)S(1)}, f32[2,64,128]{2,1,0:T(8,128)}, u32[]{:S(2)}) copy-start(f32[2,64,128]{2,1,0:T(8,128)} %copy-done.6) | copy-start | bytes 196612
  51.1 9.5 %collective-permute-start.8 = (f32[3,32,128]{2,1,0:T(8,128)S(1)}, f32[3,32,128]{2,1,0:T(8,128)S(1)}, u32[]{:S(2)}, u32[]{:S(2)}) collective-permute-start(f32[3,32,128]{2,1,0:T(8,128)S(1)} %get-tuple-element.51), channel_id=1, source_target_pairs={{0,16},{16,0},{32,48},{48,32},{64,80},{80,64},{96,112},{112,96},{1... | collective-permute-start | bytes 147464 | tf_op jit(solution)/shard_map/ppermute | solution.py:635
  52.7 6.0 %collective-permute-start.6 = (f32[24,128]{1,0:T(8,128)S(1)}, f32[24,128]{1,0:T(8,128)S(1)}, u32[]{:S(2)}, u32[]{:S(2)}) collective-permute-start(f32[24,128]{1,0:T(8,128)S(1)} %get-tuple-element.45.own_right_ref), channel_id=1, source_target_pairs={{0,1},{1,2},{2,3},{3,4},{4,5},{5,6},{6,7},{7,8},{8,9},{9,10},{10,1... | collective-permute-start | bytes 36872 | tf_op jit(solution)/shard_map/ppermute | solution.py:631
  54.0 4.8 %collective-permute-start.7 = (f32[24,128]{1,0:T(8,128)S(1)}, f32[24,128]{1,0:T(8,128)S(1)}, u32[]{:S(2)}, u32[]{:S(2)}) collective-permute-start(f32[24,128]{1,0:T(8,128)S(1)} %get-tuple-element.44.own_left_ref), channel_id=1, source_target_pairs={{0,15},{1,0},{2,1},{3,2},{4,3},{5,4},{6,5},{7,6},{8,7},{9,8},{10,9... | collective-permute-start | bytes 36872 | tf_op jit(solution)/shard_map/ppermute | solution.py:631
  62.0 6.7 %collective-permute-start.9 = (f32[4,32,128]{2,1,0:T(8,128)S(1)}, f32[4,32,128]{2,1,0:T(8,128)S(1)}, u32[]{:S(2)}, u32[]{:S(2)}) collective-permute-start(f32[4,32,128]{2,1,0:T(8,128)S(1)} %get-tuple-element.54), channel_id=1, source_target_pairs={{0,16},{16,0},{32,48},{48,32},{64,80},{80,64},{96,112},{112,96},{1... | collective-permute-start | bytes 196616 | tf_op jit(solution)/shard_map/ppermute | solution.py:635
  65.0 13.0 %all-to-all-start.2 = ((s16[16,2,16,128]{3,2,1,0:T(8,128)(2,1)}), s16[16,2,16,128]{3,2,1,0:T(8,128)(2,1)S(1)}, u32[]{:S(2)}, u32[]{:S(2)}) async-start(s16[16,2,16,128]{3,2,1,0:T(8,128)(2,1)} %get-tuple-element.61), calls=%async_computation.2 | async-start | bytes 262144 | tf_op jit(solution)/shard_map/all_to_all | solution.py:714
  70.1 7.9 %collective-permute-start.10 = (f32[64,128]{1,0:T(8,128)S(1)}, f32[64,128]{1,0:T(8,128)S(1)}, u32[]{:S(2)}, u32[]{:S(2)}) collective-permute-start(f32[64,128]{1,0:T(8,128)S(1)} %get-tuple-element.57), channel_id=1, source_target_pairs={{0,16},{16,0},{32,48},{48,32},{64,80},{80,64},{96,112},{112,96},{1... | collective-permute-start | bytes 98312 | tf_op jit(solution)/shard_map/ppermute | solution.py:635
  70.2 7.7 %collective-permute-start.11 = (f32[64,128]{1,0:T(8,128)S(1)}, f32[64,128]{1,0:T(8,128)S(1)}, u32[]{:S(2)}, u32[]{:S(2)}) collective-permute-start(f32[64,128]{1,0:T(8,128)S(1)} %get-tuple-element.58), channel_id=1, source_target_pairs={{0,240},{16,32},{32,16},{48,64},{64,48},{80,96},{96,80},{112,128},... | collective-permute-start | bytes 98312 | tf_op jit(solution)/shard_map/ppermute | solution.py:640
  71.9 6.1 %collective-permute-start.12 = (f32[8,128]{1,0:T(8,128)S(1)}, f32[8,128]{1,0:T(8,128)S(1)}, u32[]{:S(2)}, u32[]{:S(2)}) collective-permute-start(f32[8,128]{1,0:T(8,128)S(1)} %get-tuple-element.59), channel_id=1, source_target_pairs={{0,1},{1,2},{2,3},{3,4},{4,5},{5,6},{6,7},{7,8},{8,9},{9,10},{10,1... | collective-permute-start | bytes 12296 | tf_op jit(solution)/shard_map/ppermute | solution.py:631
  72.7 5.2 %collective-permute-start.13 = (f32[8,128]{1,0:T(8,128)S(1)}, f32[8,128]{1,0:T(8,128)S(1)}, u32[]{:S(2)}, u32[]{:S(2)}) collective-permute-start(f32[8,128]{1,0:T(8,128)S(1)} %get-tuple-element.60), channel_id=1, source_target_pairs={{0,15},{1,0},{2,1},{3,2},{4,3},{5,4},{6,5},{7,6},{8,7},{9,8},{10,9... | collective-permute-start | bytes 12296 | tf_op jit(solution)/shard_map/ppermute | solution.py:631
  (4 other events, 43.4 us)

commit v8 on v7

--- a/solution.py
+++ b/solution.py
@@ -174,6 +174,10 @@
     decay = jnp.exp(-1.0 / length)
     cube = decay * decay * decay
     return decay, decay * cube, 4.0 * (1.0 - decay) * cube
+
+
+def place():
+    return {64: lax.axis_index("axial"), 65: lax.axis_size("axial")}
 
 
 def half_powers(info_ref, length_ref):
@@ -324,8 +328,9 @@
 
 
 def pair_chip_body(
-    info_ref, keep_ref, got_ref, early_left_ref, early_right_ref, length_ref, out_ref,
+    keep_ref, got_ref, early_left_ref, early_right_ref, length_ref, out_ref,
 ):
+    info_ref = place()
     _, fall, cross = half_powers(info_ref, length_ref)
     _, side_fall, _ = side_powers(info_ref, early_left_ref, early_right_ref)
     upper, lower = cores(info_ref, keep_ref, got_ref)
@@ -346,7 +351,7 @@
 
 def reach_body(
     info_ref, rec_ref, lt_ref, lr_ref, source_ref, near_ref, far_ref, length_ref,
-    new_lt_ref, left_out, right_out, keep_ref, give_ref, scratch,
+    new_lt_ref, left_out, right_out, keep_ref, give_ref, fields_ref, scratch,
 ):
     layers, azimuths, _ = lt_ref.shape
     bottom = info_ref[64] == 0
@@ -392,6 +397,9 @@
     _, one_weight = chain(answered(two, share, decay), decay, nothing)
     _, zero_weight = chain(by_zero, decay, nothing)
     halves(info_ref, (later, one_weight, zero_weight), scratch, keep_ref, give_ref)
+    for l in range(layers):
+        fields_ref[l] = 1.0 + 0.2 * decoded(info_ref, rec_ref, 0, l, 0)
+        fields_ref[layers + l] = decoded(info_ref, rec_ref, 0, l, 1)
 
 
 def beyond(there, here):
@@ -401,9 +409,10 @@
 
 
 def pair_carry_body(
-    info_ref, keep_ref, got_ref, more_ref, more_got_ref, sums_ref, left_ref, right_ref,
+    keep_ref, got_ref, more_ref, more_got_ref, sums_ref, left_ref, right_ref,
     early_left_ref, early_right_ref, length_ref, mine_ref, other_ref, out_ref,
 ):
+    info_ref = place()
     _, fall, cross = half_powers(info_ref, length_ref)
     _, side_fall, _ = side_powers(info_ref, early_left_ref, early_right_ref)
     chips = sums_ref.shape[0]
@@ -556,9 +565,10 @@
 
 
 def last_body(
-    info_ref, weight_ref, rec_ref, lt_ref, lr_ref, near_ref, far_ref, left_ref, right_ref,
+    weight_ref, fields_ref, lt_ref, lr_ref, near_ref, far_ref, left_ref, right_ref,
     length_ref, sums_ref, flux_ref, new_lt_ref, new_lr_ref, heat_ref,
 ):
+    info_ref = place()
     layers, azimuths, radials = lt_ref.shape
     band = weight_ref.shape[0] // 2
     decay, fall, _ = powers(length_ref[...])
@@ -585,10 +595,10 @@
     spread = laplace(lt, low, high, left_ref[...], right_ref[...])
     climbs, _ = chain(lr, decay, three)
     for l in range(layers):
-        new_lt_ref[l] = lt[l] + 0.15 * spread[l] + decoded(info_ref, rec_ref, 0, l, 1) * lr[l]
+        new_lt_ref[l] = lt[l] + 0.15 * spread[l] + fields_ref[layers + l] * lr[l]
         new_lr_ref[l] = (
             -0.3 * lt[l]
-            + (1.0 + 0.2 * decoded(info_ref, rec_ref, 0, l, 0)) * lr[l]
+            + fields_ref[l] * lr[l]
             + climbs[l]
         )
     lane = lax.broadcasted_iota(jnp.int32, (layers, radials), 1)
@@ -603,7 +613,7 @@
     )
     heat = jnp.zeros_like(ring)
     for offset in range(-band, band + 1):
-        heat = heat + weight_ref[offset + band] * pltpu.roll(ring, (-offset) % radials, axis=1)
+        heat = heat + weight_ref[offset + band : offset + band + 1, :] * pltpu.roll(ring, (-offset) % radials, axis=1)
     heat_ref[...] = heat[:, :azimuths]
 
 
@@ -653,6 +663,7 @@
     axial, me = lax.axis_size("axial"), lax.axis_index("axial")
     wanted = lax.dynamic_index_in_dim(holder, me, 1, keepdims=False).reshape(-1)
     info = jnp.concatenate([wanted, jnp.stack([me, axial]).astype(jnp.int32)])
+    weights = jnp.broadcast_to(kernel[:, None], (kernel.shape[0], radials))
     plane = (azimuths, radials)
     side = (layers, radials)
     wide = (2 * layers, radials)
@@ -688,17 +699,20 @@
     far = crossed(far)
     (total,) = run(
         pair_chip_body,
-        (info,),
+        (),
         (keep, got, *early, decay_length),
         [(axial // 2, azimuths // ROWS * 2 + 1, ROWS, radials)],
         span=CHIP_SPAN,
     )
     sums = between_chips(total)
-    lt2, left, right, more, give = run(
+    lt2, left, right, more, give, fields = run(
         reach_body,
         (info,),
         (pieces, lt1, lr1, source, got, far, decay_length),
-        [(layers + 2, *plane), (24, radials), (24, radials), half(3), half(3)],
+        [
+            (layers + 2, *plane), (24, radials), (24, radials), half(3), half(3),
+            (2 * layers, *plane),
+        ],
         [(3, *plane)],
         span=REACH_SPAN,
     )
@@ -707,7 +721,7 @@
     sums, *sides = lax.optimization_barrier((sums, *sides))
     mine, other, total = run(
         pair_carry_body,
-        (info,),
+        (),
         (keep, got, more, more_got, sums, *sides, *early, decay_length),
         [half(4), half(4), copies(axial, 1)],
     )
@@ -732,8 +746,8 @@
     return tuple(
         run(
             last_body,
-            (info, kernel),
-            (pieces, lt3, lr3, *halo, decay_length, sums, flux),
+            (),
+            (weights, fields, lt3, lr3, *halo, decay_length, sums, flux),
             [block, block, (layers, azimuths)],
         )
     )

time: 80.9 us -> 79.4 us (0.981)
  Pallas kernels: 11.7 us -> 10.1 us
    pallas_call x6, Pallas kernels: 7.61 us -> 6.02 us  [run(): pl.pallas_call(body, in_specs=[smem] * len(scalars) + [vmem] * len(args),...]
  transfers between devices with their start and end apart: 17 -> 17, of which waited for: 8 -> 8; matrix products, arithmetic and copies ran while one was open for 0% -> 0% of each run, Pallas kernels for 5% -> 4%
where the time goes in v8:
time: 79.4 us; the launch traced here: 78.1 us
  starting transfers between devices  40.9 us (52%)
  waiting for transfers between devices  25.8 us (32%)
  Pallas kernels  10.1 us (13%)
  between operations  0.88 us (1%)
    ppermute x8, waiting for transfers between devices, turned(): lax.ppermute(value, axis, [(i, (i + shift) % count) for i in range(count)])  20.6 us
    ppermute x8, starting transfers between devices, turned(): lax.ppermute(value, axis, [(i, (i + shift) % count) for i in range(count)])  17.2 us
    all_to_all x1, starting transfers between devices, local(): pieces = lax.all_to_all(encode(stored), 'axial', 0, 0, tiled=True)  10 us
    pallas_call x6, Pallas kernels, run(): pl.pallas_call(body, in_specs=[smem] * len(scalars) + [vmem] * len(args),...  6.02 us
    ppermute x4, starting transfers between devices, swapped(): lax.ppermute(value, 'axial', [(i, i ^ 1) for i in range(lax.axis_size('ax...  4.74 us
    pallas_call x1, Pallas kernels, encode(): pl.pallas_call(encode_body, in_specs=[pl.BlockSpec(memory_space=pl.ANY)],...  4.11 us
    all_to_all x1, starting transfers between devices, local(): sums = lax.all_to_all(total, 'axial', 0, 0, tiled=True)  3.77 us
    all_to_all x1, starting transfers between devices, between_chips(): lax.all_to_all(value, 'axial', 0, 0, tiled=True, axis_index_groups=groups)  3.42 us
  transfers between devices with their start and end apart: 17, of which 8 were waited for; matrix products, arithmetic and copies ran while one was open for 0% of the time, Pallas kernels for 4%

profile of v8, /device:TPU:1, one launch (start us, length us, event | category | flops | bytes accessed | tf_op | source)
XLA Modules:
  0.0 78.1 jit_solution(16584483637805351335)
XLA Ops:
  0.7 4.1 %shard_map.94 = s16[16,16,16,128]{3,2,1,0:T(8,128)(2,1)} custom-call(bf16[4,32,8,2048]{3,2,1,0:T(8,128)(2,1)} %bitcast.17), custom_call_target="tpu_custom_call" | custom-call | tf_op jit(solution)/shard_map/pallas_call | solution.py:112
  4.8 10.0 %all-to-all-start = ((s16[16,16,16,128]{3,2,1,0:T(8,128)(2,1)}), s16[16,16,16,128]{3,2,1,0:T(8,128)(2,1)S(1)}, u32[]{:S(2)}, u32[]{:S(2)}) async-start(s16[16,16,16,128]{3,2,1,0:T(8,128)(2,1)} %shard_map.94), calls=%async_computation | async-start | bytes 2097152 | tf_op jit(solution)/shard_map/all_to_all | solution.py:678
  14.9 1.3 %collective-permute-start.2 = (f32[16,128]{1,0:T(8,128)S(1)}, f32[16,128]{1,0:T(8,128)S(1)}, u32[]{:S(2)}, u32[]{:S(2)}) collective-permute-start(f32[16,128]{1,0:T(8,128)S(1)} %select_maximum_fusion.2), channel_id=1, source_target_pairs={{0,1},{1,2},{2,3},{3,4},{4,5},{5,6},{6,7},{7,8},{8,9},{9,10},{10,1... | collective-permute-start | bytes 24584 | tf_op jit(solution)/shard_map/ppermute | solution.py:641
  16.2 3.8 %collective-permute-start.3 = (f32[16,128]{1,0:T(8,128)S(1)}, f32[16,128]{1,0:T(8,128)S(1)}, u32[]{:S(2)}, u32[]{:S(2)}) collective-permute-start(f32[16,128]{1,0:T(8,128)S(1)} %select_maximum_fusion), channel_id=1, source_target_pairs={{0,15},{1,0},{2,1},{3,2},{4,3},{5,4},{6,5},{7,6},{8,7},{9,8},{10,9... | collective-permute-start | bytes 24584 | tf_op jit(solution)/shard_map/ppermute | solution.py:641
  20.5 1.6 %collective-permute-start = (f32[64,128]{1,0:T(8,128)S(1)}, f32[64,128]{1,0:T(8,128)S(1)}, u32[]{:S(2)}, u32[]{:S(2)}) collective-permute-start(f32[64,128]{1,0:T(8,128)S(1)} %get-tuple-element.70), channel_id=1, source_target_pairs={{0,16},{16,32},{32,48},{48,64},{64,80},{80,96},{96,112},{112,128},... | collective-permute-start | bytes 98312 | tf_op jit(solution)/shard_map/ppermute | solution.py:641
  22.3 15.7 %collective-permute-done.low_ref = f32[64,128]{1,0:T(8,128)S(1)} collective-permute-done((f32[64,128]{1,0:T(8,128)S(1)}, f32[64,128]{1,0:T(8,128)S(1)}, u32[]{:S(2)}, u32[]{:S(2)}) %collective-permute-start) | collective-permute-done | bytes 32800 | tf_op jit(solution)/shard_map/ppermute | solution.py:641
  38.0 2.8 %collective-permute-done.1.high_ref = f32[2,64,128]{2,1,0:T(8,128)S(1)} collective-permute-done((f32[2,64,128]{2,1,0:T(8,128)S(1)}, f32[2,64,128]{2,1,0:T(8,128)S(1)}, u32[]{:S(2)}, u32[]{:S(2)}) %collective-permute-start.1) | collective-permute-done | bytes 65568 | tf_op jit(solution)/shard_map/ppermute | solution.py:641
  40.9 1.9 %all-to-all-done.rec_ref = s16[16,16,16,128]{3,2,1,0:T(8,128)(2,1)S(1)} async-done(((s16[16,16,16,128]{3,2,1,0:T(8,128)(2,1)}), s16[16,16,16,128]{3,2,1,0:T(8,128)(2,1)S(1)}, u32[]{:S(2)}, u32[]{:S(2)}) %all-to-all-start) | async-done | bytes 1048608 | tf_op jit(solution)/shard_map/all_to_all | solution.py:678
  42.7 0.9 %shard_map.95 = (f32[4,64,128]{2,1,0:T(8,128)S(1)}, f32[4,64,128]{2,1,0:T(8,128)S(1)}, f32[4,64,128]{2,1,0:T(8,128)S(1)}, f32[4,64,128]{2,1,0:T(8,128)S(1)}, f32...) custom-call(s32[66]{0:T(128)S(1)} %pad_add_fusion.info_ref, s16[16,16,16,128]{3,2,1,0:T(8,128)(2,1)S(1)} %all-to-all-done.rec_ref, ...), custom_call_target="tpu_custom_call" | custom-call | flops 1000000000 | bytes 3000000 | tf_op jit(solution)/shard_map/pallas_call | solution.py:623
  43.9 1.4 %collective-permute-done.4.near_ref.got_ref = f32[13,32,128]{2,1,0:T(8,128)S(1)} collective-permute-done((f32[13,32,128]{2,1,0:T(8,128)S(1)}, f32[13,32,128]{2,1,0:T(8,128)S(1)}, u32[]{:S(2)}, u32[]{:S(2)}) %collective-permute-start.4) | collective-permute-done | bytes 213024 | tf_op jit(solution)/shard_map/ppermute | solution.py:645
  46.1 3.4 %all-to-all-start.1 = ((s16[8,9,16,128]{3,2,1,0:T(8,128)(2,1)}), s16[8,9,16,128]{3,2,1,0:T(8,128)(2,1)S(1)}, u32[]{:S(2)}, u32[]{:S(2)}) async-start(s16[8,9,16,128]{3,2,1,0:T(8,128)(2,1)} %shard_map.97), calls=%async_computation.1 | async-start | bytes 589824 | tf_op jit(solution)/shard_map/all_to_all | solution.py:658
  49.6 1.1 %shard_map.96 = (f32[6,64,128]{2,1,0:T(8,128)S(1)}, f32[24,128]{1,0:T(8,128)S(1)}, f32[24,128]{1,0:T(8,128)S(1)}, f32[3,32,128]{2,1,0:T(8,128)S(1)}, f32[3,32,12...) custom-call(s32[66]{0:T(128)S(1)} %pad_add_fusion.info_ref, s16[16,16,16,128]{3,2,1,0:T(8,128)(2,1)S(1)} %all-to-all-done.rec_ref, ...), custom_call_target="tpu_custom_call" | custom-call | flops 99999997952 | bytes 300000000 | tf_op jit(solution)/shard_map/pallas_call | solution.py:623
  50.7 1.6 %collective-permute-start.8 = (f32[3,32,128]{2,1,0:T(8,128)S(1)}, f32[3,32,128]{2,1,0:T(8,128)S(1)}, u32[]{:S(2)}, u32[]{:S(2)}) collective-permute-start(f32[3,32,128]{2,1,0:T(8,128)S(1)} %get-tuple-element.53), channel_id=1, source_target_pairs={{0,16},{16,0},{32,48},{48,32},{64,80},{80,64},{96,112},{112,96},{1... | collective-permute-start | bytes 147464 | tf_op jit(solution)/shard_map/ppermute | solution.py:645
  52.3 1.2 %collective-permute-start.6 = (f32[24,128]{1,0:T(8,128)S(1)}, f32[24,128]{1,0:T(8,128)S(1)}, u32[]{:S(2)}, u32[]{:S(2)}) collective-permute-start(f32[24,128]{1,0:T(8,128)S(1)} %get-tuple-element.47.own_right_ref), channel_id=1, source_target_pairs={{0,1},{1,2},{2,3},{3,4},{4,5},{5,6},{6,7},{7,8},{8,9},{9,10},{10,1... | collective-permute-start | bytes 36872 | tf_op jit(solution)/shard_map/ppermute | solution.py:641
  53.5 3.7 %collective-permute-start.7 = (f32[24,128]{1,0:T(8,128)S(1)}, f32[24,128]{1,0:T(8,128)S(1)}, u32[]{:S(2)}, u32[]{:S(2)}) collective-permute-start(f32[24,128]{1,0:T(8,128)S(1)} %get-tuple-element.46.own_left_ref), channel_id=1, source_target_pairs={{0,15},{1,0},{2,1},{3,2},{4,3},{5,4},{6,5},{7,6},{8,7},{9,8},{10,9... | collective-permute-start | bytes 36872 | tf_op jit(solution)/shard_map/ppermute | solution.py:641
  57.2 1.1 %collective-permute-done.6.left_ref = f32[24,128]{1,0:T(8,128)S(1)} collective-permute-done((f32[24,128]{1,0:T(8,128)S(1)}, f32[24,128]{1,0:T(8,128)S(1)}, u32[]{:S(2)}, u32[]{:S(2)}) %collective-permute-start.6) | collective-permute-done | bytes 12320 | tf_op jit(solution)/shard_map/ppermute | solution.py:641
  58.3 1.7 %all-to-all-done.1.sums_ref = s16[8,9,16,128]{3,2,1,0:T(8,128)(2,1)S(1)} async-done(((s16[8,9,16,128]{3,2,1,0:T(8,128)(2,1)}), s16[8,9,16,128]{3,2,1,0:T(8,128)(2,1)S(1)}, u32[]{:S(2)}, u32[]{:S(2)}) %all-to-all-start.1) | async-done | bytes 294944 | tf_op jit(solution)/shard_map/all_to_all | solution.py:658
  60.9 2.9 %collective-permute-start.9 = (f32[4,32,128]{2,1,0:T(8,128)S(1)}, f32[4,32,128]{2,1,0:T(8,128)S(1)}, u32[]{:S(2)}, u32[]{:S(2)}) collective-permute-start(f32[4,32,128]{2,1,0:T(8,128)S(1)} %get-tuple-element.56), channel_id=1, source_target_pairs={{0,16},{16,0},{32,48},{48,32},{64,80},{80,64},{96,112},{112,96},{1... | collective-permute-start | bytes 196616 | tf_op jit(solution)/shard_map/ppermute | solution.py:645
  64.0 3.8 %all-to-all-start.2 = ((s16[16,2,16,128]{3,2,1,0:T(8,128)(2,1)}), s16[16,2,16,128]{3,2,1,0:T(8,128)(2,1)S(1)}, u32[]{:S(2)}, u32[]{:S(2)}) async-start(s16[16,2,16,128]{3,2,1,0:T(8,128)(2,1)} %get-tuple-element.63), calls=%async_computation.2 | async-start | bytes 262144 | tf_op jit(solution)/shard_map/all_to_all | solution.py:728
  67.8 1.3 %shard_map.99 = (f32[4,64,128]{2,1,0:T(8,128)S(1)}, f32[4,64,128]{2,1,0:T(8,128)S(1)}, f32[4,128]{1,0:T(4,128)S(1)}, f32[64,128]{1,0:T(8,128)S(1)}, f32[64,128]{...) custom-call(s32[66]{0:T(128)S(1)} %pad_add_fusion.info_ref, ...), custom_call_target="tpu_custom_call" | custom-call | flops 99999997952 | bytes 300000000 | tf_op jit(solution)/shard_map/pallas_call | solution.py:623
  69.2 1.7 %collective-permute-start.11 = (f32[64,128]{1,0:T(8,128)S(1)}, f32[64,128]{1,0:T(8,128)S(1)}, u32[]{:S(2)}, u32[]{:S(2)}) collective-permute-start(f32[64,128]{1,0:T(8,128)S(1)} %get-tuple-element.60), channel_id=1, source_target_pairs={{0,240},{16,32},{32,16},{48,64},{64,48},{80,96},{96,80},{112,128},... | collective-permute-start | bytes 98312 | tf_op jit(solution)/shard_map/ppermute | solution.py:650
  71.6 4.3 %collective-permute-start.13 = (f32[8,128]{1,0:T(8,128)S(1)}, f32[8,128]{1,0:T(8,128)S(1)}, u32[]{:S(2)}, u32[]{:S(2)}) collective-permute-start(f32[8,128]{1,0:T(8,128)S(1)} %get-tuple-element.62), channel_id=1, source_target_pairs={{0,15},{1,0},{2,1},{3,2},{4,3},{5,4},{6,5},{7,6},{8,7},{9,8},{10,9... | collective-permute-start | bytes 12296 | tf_op jit(solution)/shard_map/ppermute | solution.py:641
  75.9 1.0 %collective-permute-done.12.left_ref = f32[8,128]{1,0:T(8,128)S(1)} collective-permute-done((f32[8,128]{1,0:T(8,128)S(1)}, f32[8,128]{1,0:T(8,128)S(1)}, u32[]{:S(2)}, u32[]{:S(2)}) %collective-permute-start.12) | collective-permute-done | bytes 4128 | tf_op jit(solution)/shard_map/ppermute | solution.py:641
  77.2 1.0 %shard_map.100 = (f32[4,64,128]{2,1,0:T(8,128)}, f32[4,64,128]{2,1,0:T(8,128)}, f32[4,64]{1,0:T(4,128)}) custom-call(f32[17,128]{1,0:T(8,128)S(1)} %broadcast_in_dim.4.weight_ref, f32[8,64,128]{2,1,0:T(8,128)S(1)} %get-tuple-element.44.fields_ref, f32[4,64,128]{2,1,0:T(8,128)S(1)} %get-tuple-element.57.lt_ref, f32[4,64,128]{2,1,0:T(8,128)S(1)} %get-tuple-element.58.lr_ref, ...), custom_call_target="tpu_custom_call" | custom-call | flops 1000000000 | bytes 3000000 | tf_op jit(solution)/shard_map/pallas_call | solution.py:623
  (51 shorter events, 4.0 us)
Async XLA Ops:
  0.6 21.5 %copy-start = (s32[4,16,16]{2,1,0:T(8,128)S(1)}, s32[4,16,16]{2,1,0:T(8,128)}, u32[]{:S(2)}) copy-start(s32[4,16,16]{2,1,0:T(8,128)} %param.8) | copy-start | bytes 12292
  0.7 14.2 %copy-start.3 = (f32[4,64,128]{2,1,0:T(8,128)S(1)}, f32[4,64,128]{2,1,0:T(8,128)}, u32[]{:S(2)}) copy-start(f32[4,64,128]{2,1,0:T(8,128)} %seed_lr_ref.1) | copy-start | bytes 393220
  0.7 19.3 %slice-start = ((f32[4,64,128]{2,1,0:T(8,128)}), f32[1,64,128]{2,1,0:T(8,128)S(1)}, s32[]{:S(2)}) async-start(f32[4,64,128]{2,1,0:T(8,128)} %seed_lr_ref.1), calls=%async_computation.3 | async-start | bytes 65536 | tf_op jit(solution)/shard_map/slice | solution.py:685
  4.8 37.9 %all-to-all-start = ((s16[16,16,16,128]{3,2,1,0:T(8,128)(2,1)}), s16[16,16,16,128]{3,2,1,0:T(8,128)(2,1)S(1)}, u32[]{:S(2)}, u32[]{:S(2)}) async-start(s16[16,16,16,128]{3,2,1,0:T(8,128)(2,1)} %shard_map.94), calls=%async_computation | async-start | bytes 2097152 | tf_op jit(solution)/shard_map/all_to_all | solution.py:678
  14.9 7.4 %collective-permute-start.2 = (f32[16,128]{1,0:T(8,128)S(1)}, f32[16,128]{1,0:T(8,128)S(1)}, u32[]{:S(2)}, u32[]{:S(2)}) collective-permute-start(f32[16,128]{1,0:T(8,128)S(1)} %select_maximum_fusion.2), channel_id=1, source_target_pairs={{0,1},{1,2},{2,3},{3,4},{4,5},{5,6},{6,7},{7,8},{8,9},{9,10},{10,1... | collective-permute-start | bytes 24584 | tf_op jit(solution)/shard_map/ppermute | solution.py:641
  16.2 6.1 %collective-permute-start.3 = (f32[16,128]{1,0:T(8,128)S(1)}, f32[16,128]{1,0:T(8,128)S(1)}, u32[]{:S(2)}, u32[]{:S(2)}) collective-permute-start(f32[16,128]{1,0:T(8,128)S(1)} %select_maximum_fusion), channel_id=1, source_target_pairs={{0,15},{1,0},{2,1},{3,2},{4,3},{5,4},{6,5},{7,6},{8,7},{9,8},{10,9... | collective-permute-start | bytes 24584 | tf_op jit(solution)/shard_map/ppermute | solution.py:641
  20.0 20.8 %collective-permute-start.1 = (f32[2,64,128]{2,1,0:T(8,128)S(1)}, f32[2,64,128]{2,1,0:T(8,128)S(1)}, u32[]{:S(2)}, u32[]{:S(2)}) collective-permute-start(f32[2,64,128]{2,1,0:T(8,128)S(1)} %pad_maximum_fusion), channel_id=1, source_target_pairs={{0,240},{16,0},{32,16},{48,32},{64,48},{80,64},{96,80},{112,96},{1... | collective-permute-start | bytes 196616 | tf_op jit(solution)/shard_map/ppermute | solution.py:641
  20.5 17.5 %collective-permute-start = (f32[64,128]{1,0:T(8,128)S(1)}, f32[64,128]{1,0:T(8,128)S(1)}, u32[]{:S(2)}, u32[]{:S(2)}) collective-permute-start(f32[64,128]{1,0:T(8,128)S(1)} %get-tuple-element.70), channel_id=1, source_target_pairs={{0,16},{16,32},{32,48},{48,64},{64,80},{80,96},{96,112},{112,128},... | collective-permute-start | bytes 98312 | tf_op jit(solution)/shard_map/ppermute | solution.py:641
  43.7 1.6 %collective-permute-start.4 = (f32[13,32,128]{2,1,0:T(8,128)S(1)}, f32[13,32,128]{2,1,0:T(8,128)S(1)}, u32[]{:S(2)}, u32[]{:S(2)}) collective-permute-start(f32[13,32,128]{2,1,0:T(8,128)S(1)} %get-tuple-element.42), channel_id=1, source_target_pairs={{0,16},{16,0},{32,48},{48,32},{64,80},{80,64},{96,112},{112,96},{1... | collective-permute-start | bytes 638984 | tf_op jit(solution)/shard_map/ppermute | solution.py:645
  43.8 5.8 %collective-permute-start.5 = (f32[4,64,128]{2,1,0:T(8,128)S(1)}, f32[4,64,128]{2,1,0:T(8,128)S(1)}, u32[]{:S(2)}, u32[]{:S(2)}) collective-permute-start(f32[4,64,128]{2,1,0:T(8,128)S(1)} %get-tuple-element.43), channel_id=1, source_target_pairs={{0,240},{16,32},{32,16},{48,64},{64,48},{80,96},{96,80},{112,128},... | collective-permute-start | bytes 393224 | tf_op jit(solution)/shard_map/ppermute | solution.py:650
  46.1 14.0 %all-to-all-start.1 = ((s16[8,9,16,128]{3,2,1,0:T(8,128)(2,1)}), s16[8,9,16,128]{3,2,1,0:T(8,128)(2,1)S(1)}, u32[]{:S(2)}, u32[]{:S(2)}) async-start(s16[8,9,16,128]{3,2,1,0:T(8,128)(2,1)} %shard_map.97), calls=%async_computation.1 | async-start | bytes 589824 | tf_op jit(solution)/shard_map/all_to_all | solution.py:658
  49.5 14.3 %copy-start.8 = (s32[4,64]{1,0:T(4,128)S(1)}, s32[4,64]{1,0:T(4,128)}, u32[]{:S(2)}) copy-start(s32[4,64]{1,0:T(4,128)} %param.12) | copy-start | bytes 3076
  49.6 18.2 %copy-start.2 = (f32[4,64,128]{2,1,0:T(8,128)S(1)}, f32[4,64,128]{2,1,0:T(8,128)}, u32[]{:S(2)}) copy-start(f32[4,64,128]{2,1,0:T(8,128)} %seed_ref.1) | copy-start | bytes 393220
  49.6 18.2 %copy-start.4 = (f32[4,64,128]{2,1,0:T(8,128)S(1)}, f32[4,64,128]{2,1,0:T(8,128)}, u32[]{:S(2)}) copy-start(f32[4,64,128]{2,1,0:T(8,128)} %seed_lr_ref.1) | copy-start | bytes 393220
  49.6 18.2 %copy-start.7 = (f32[2,64,128]{2,1,0:T(8,128)S(1)}, f32[2,64,128]{2,1,0:T(8,128)}, u32[]{:S(2)}) copy-start(f32[2,64,128]{2,1,0:T(8,128)} %copy-done.6) | copy-start | bytes 196612
  50.7 9.4 %collective-permute-start.8 = (f32[3,32,128]{2,1,0:T(8,128)S(1)}, f32[3,32,128]{2,1,0:T(8,128)S(1)}, u32[]{:S(2)}, u32[]{:S(2)}) collective-permute-start(f32[3,32,128]{2,1,0:T(8,128)S(1)} %get-tuple-element.53), channel_id=1, source_target_pairs={{0,16},{16,0},{32,48},{48,32},{64,80},{80,64},{96,112},{112,96},{1... | collective-permute-start | bytes 147464 | tf_op jit(solution)/shard_map/ppermute | solution.py:645
  52.3 6.0 %collective-permute-start.6 = (f32[24,128]{1,0:T(8,128)S(1)}, f32[24,128]{1,0:T(8,128)S(1)}, u32[]{:S(2)}, u32[]{:S(2)}) collective-permute-start(f32[24,128]{1,0:T(8,128)S(1)} %get-tuple-element.47.own_right_ref), channel_id=1, source_target_pairs={{0,1},{1,2},{2,3},{3,4},{4,5},{5,6},{6,7},{7,8},{8,9},{9,10},{10,1... | collective-permute-start | bytes 36872 | tf_op jit(solution)/shard_map/ppermute | solution.py:641
  53.5 4.8 %collective-permute-start.7 = (f32[24,128]{1,0:T(8,128)S(1)}, f32[24,128]{1,0:T(8,128)S(1)}, u32[]{:S(2)}, u32[]{:S(2)}) collective-permute-start(f32[24,128]{1,0:T(8,128)S(1)} %get-tuple-element.46.own_left_ref), channel_id=1, source_target_pairs={{0,15},{1,0},{2,1},{3,2},{4,3},{5,4},{6,5},{7,6},{8,7},{9,8},{10,9... | collective-permute-start | bytes 36872 | tf_op jit(solution)/shard_map/ppermute | solution.py:641
  60.9 6.8 %collective-permute-start.9 = (f32[4,32,128]{2,1,0:T(8,128)S(1)}, f32[4,32,128]{2,1,0:T(8,128)S(1)}, u32[]{:S(2)}, u32[]{:S(2)}) collective-permute-start(f32[4,32,128]{2,1,0:T(8,128)S(1)} %get-tuple-element.56), channel_id=1, source_target_pairs={{0,16},{16,0},{32,48},{48,32},{64,80},{80,64},{96,112},{112,96},{1... | collective-permute-start | bytes 196616 | tf_op jit(solution)/shard_map/ppermute | solution.py:645
  64.0 13.1 %all-to-all-start.2 = ((s16[16,2,16,128]{3,2,1,0:T(8,128)(2,1)}), s16[16,2,16,128]{3,2,1,0:T(8,128)(2,1)S(1)}, u32[]{:S(2)}, u32[]{:S(2)}) async-start(s16[16,2,16,128]{3,2,1,0:T(8,128)(2,1)} %get-tuple-element.63), calls=%async_computation.2 | async-start | bytes 262144 | tf_op jit(solution)/shard_map/all_to_all | solution.py:728
  69.1 7.9 %collective-permute-start.10 = (f32[64,128]{1,0:T(8,128)S(1)}, f32[64,128]{1,0:T(8,128)S(1)}, u32[]{:S(2)}, u32[]{:S(2)}) collective-permute-start(f32[64,128]{1,0:T(8,128)S(1)} %get-tuple-element.59), channel_id=1, source_target_pairs={{0,16},{16,0},{32,48},{48,32},{64,80},{80,64},{96,112},{112,96},{1... | collective-permute-start | bytes 98312 | tf_op jit(solution)/shard_map/ppermute | solution.py:645
  69.2 7.7 %collective-permute-start.11 = (f32[64,128]{1,0:T(8,128)S(1)}, f32[64,128]{1,0:T(8,128)S(1)}, u32[]{:S(2)}, u32[]{:S(2)}) collective-permute-start(f32[64,128]{1,0:T(8,128)S(1)} %get-tuple-element.60), channel_id=1, source_target_pairs={{0,240},{16,32},{32,16},{48,64},{64,48},{80,96},{96,80},{112,128},... | collective-permute-start | bytes 98312 | tf_op jit(solution)/shard_map/ppermute | solution.py:650
  70.9 6.1 %collective-permute-start.12 = (f32[8,128]{1,0:T(8,128)S(1)}, f32[8,128]{1,0:T(8,128)S(1)}, u32[]{:S(2)}, u32[]{:S(2)}) collective-permute-start(f32[8,128]{1,0:T(8,128)S(1)} %get-tuple-element.61), channel_id=1, source_target_pairs={{0,1},{1,2},{2,3},{3,4},{4,5},{5,6},{6,7},{7,8},{8,9},{9,10},{10,1... | collective-permute-start | bytes 12296 | tf_op jit(solution)/shard_map/ppermute | solution.py:641
  71.6 5.3 %collective-permute-start.13 = (f32[8,128]{1,0:T(8,128)S(1)}, f32[8,128]{1,0:T(8,128)S(1)}, u32[]{:S(2)}, u32[]{:S(2)}) collective-permute-start(f32[8,128]{1,0:T(8,128)S(1)} %get-tuple-element.62), channel_id=1, source_target_pairs={{0,15},{1,0},{2,1},{3,2},{4,3},{5,4},{6,5},{7,6},{8,7},{9,8},{10,9... | collective-permute-start | bytes 12296 | tf_op jit(solution)/shard_map/ppermute | solution.py:641
  (4 other events, 42.9 us)

commit v9 on v8

--- a/solution.py
+++ b/solution.py
@@ -124,17 +124,28 @@
     )(flat)
 
 
+def taken(info_ref, rec_ref, step, piece, field):
+    held = info_ref[16 * step + piece]
+    return rec_ref[held // 2, 4 * step + 2 * (held % 2) + field]
+
+
+def joined(codes, field):
+    if field == 1:
+        codes = [spread_out(code, COEF_BASE, COEF_SCALE) for code in codes]
+    else:
+        codes = [code.astype(jnp.int32).astype(jnp.float32) for code in codes]
+        codes = [code * (1.0 / RATE_SCALE) + RATE_MID for code in codes]
+    return jnp.concatenate(codes, axis=0)
+
+
 def decoded(info_ref, rec_ref, step, layer, field):
-    pieces = []
-    for quarter in range(4):
-        held = info_ref[16 * step + 4 * layer + quarter]
-        code = rec_ref[held // 2, 4 * step + 2 * (held % 2) + field]
-        if field == 0:
-            code = code.astype(jnp.int32).astype(jnp.float32)
-            pieces.append(code * (1.0 / RATE_SCALE) + RATE_MID)
-        else:
-            pieces.append(spread_out(code, COEF_BASE, COEF_SCALE))
-    return jnp.concatenate(pieces, axis=0)
+    codes = [taken(info_ref, rec_ref, step, 4 * layer + q, field) for q in range(4)]
+    return joined(codes, field)
+
+
+def sorted_field(codes_ref, step, layer, field):
+    codes = [codes_ref[2 * step + field, 4 * layer + q] for q in range(4)]
+    return joined(codes, field)
 
 
 def radial(x):
@@ -397,9 +408,12 @@
     _, one_weight = chain(answered(two, share, decay), decay, nothing)
     _, zero_weight = chain(by_zero, decay, nothing)
     halves(info_ref, (later, one_weight, zero_weight), scratch, keep_ref, give_ref)
-    for l in range(layers):
-        fields_ref[l] = 1.0 + 0.2 * decoded(info_ref, rec_ref, 0, l, 0)
-        fields_ref[layers + l] = decoded(info_ref, rec_ref, 0, l, 1)
+    for step in range(3):
+        for field in range(2):
+            for piece in range(16):
+                fields_ref[2 * step + field, piece] = taken(
+                    info_ref, rec_ref, step, piece, field
+                )
 
 
 def beyond(there, here):
@@ -470,12 +484,13 @@
 
 
 def third_body(
-    info_ref, rec_ref, seed_ref, seed_lr_ref, one_ref, lt_ref, lr_ref, own_left_ref,
+    fields_ref, seed_ref, seed_lr_ref, one_ref, lt_ref, lr_ref, own_left_ref,
     own_right_ref, left_ref, right_ref, near_ref, beyond_ref, high_ref, early_left_ref,
     early_right_ref, length_ref, face_ref,
     mine_ref, got_ref, new_lt_ref, new_lr_ref, flux_ref, near_out, far_out, left_out, right_out,
     scratch,
 ):
+    info_ref = place()
     layers, azimuths, radials = lr_ref.shape
     decay, _, _ = powers(length_ref[...])
     zero, one, two = restored(info_ref, mine_ref, got_ref, scratch)
@@ -490,7 +505,7 @@
     gate_high = jnp.where(upper_here, beyond_ref[3], near)
     lifts = [
         jnp.where(info_ref[64] == 0, 0.0, gate_low * under),
-        *[decoded(info_ref, rec_ref, 2, l, 1) * lift[l] for l in range(layers)],
+        *[sorted_field(fields_ref, 2, l, 1) * lift[l] for l in range(layers)],
         jnp.where(info_ref[64] == info_ref[65] - 1, 0.0, gate_high * over),
     ]
     mine_side, got_side = mine_ref[3, 0:1, :], got_ref[3, 0:1, :]
@@ -516,7 +531,7 @@
     climbs, _ = chain(lr, decay, one)
     lr = [
         -0.3 * before[l]
-        + (1.0 + 0.2 * decoded(info_ref, rec_ref, 2, l, 0)) * lr[l]
+        + (1.0 + 0.2 * sorted_field(fields_ref, 2, l, 0)) * lr[l]
         + climbs[l]
         for l in range(layers)
     ]
@@ -530,7 +545,7 @@
         + lifted(right, early_right_ref, jnp.where(upper_here, mine_side, got_side)),
     )
     new_lt = [
-        lt[l] + 0.15 * spread[l] + decoded(info_ref, rec_ref, 1, l, 1) * lr[l]
+        lt[l] + 0.15 * spread[l] + sorted_field(fields_ref, 1, l, 1) * lr[l]
         for l in range(layers)
     ]
     upper_here = info_ref[64] % 2 == 1
@@ -543,7 +558,7 @@
     for l in range(layers):
         new_lt_ref[l] = new_lt[l]
         new_lr_ref[l] = (
-            -0.3 * lt[l] + (1.0 + 0.2 * decoded(info_ref, rec_ref, 1, l, 0)) * lr[l] + climbs[l]
+            -0.3 * lt[l] + (1.0 + 0.2 * sorted_field(fields_ref, 1, l, 0)) * lr[l] + climbs[l]
         )
     lane = lax.broadcasted_iota(jnp.int32, (azimuths, radials), 1)
     ones = jnp.ones((8, radials), jnp.float32)
@@ -595,10 +610,10 @@
     spread = laplace(lt, low, high, left_ref[...], right_ref[...])
     climbs, _ = chain(lr, decay, three)
     for l in range(layers):
-        new_lt_ref[l] = lt[l] + 0.15 * spread[l] + fields_ref[layers + l] * lr[l]
+        new_lt_ref[l] = lt[l] + 0.15 * spread[l] + sorted_field(fields_ref, 0, l, 1) * lr[l]
         new_lr_ref[l] = (
             -0.3 * lt[l]
-            + fields_ref[l] * lr[l]
+            + (1.0 + 0.2 * sorted_field(fields_ref, 0, l, 0)) * lr[l]
             + climbs[l]
         )
     lane = lax.broadcasted_iota(jnp.int32, (layers, radials), 1)
@@ -711,7 +726,7 @@
         (pieces, lt1, lr1, source, got, far, decay_length),
         [
             (layers + 2, *plane), (24, radials), (24, radials), half(3), half(3),
-            (2 * layers, *plane),
+            (6, 4 * layers, ROWS, radials),
         ],
         [(3, *plane)],
         span=REACH_SPAN,
@@ -728,9 +743,9 @@
     sums = lax.all_to_all(total, "axial", 0, 0, tiled=True)
     lt3, lr3, flux, near, far, left, right = run(
         third_body,
-        (info,),
+        (),
         (
-            pieces, seed_temp, seed_disloc, lt1, lt2, lr1, left, right, *sides, got, far,
+            fields, seed_temp, seed_disloc, lt1, lt2, lr1, left, right, *sides, got, far,
             high, *early, decay_length, face, mine, swapped(other),
         ),
         [block, block, side, plane, plane, wide, wide],

time: 79.4 us -> 79.1 us (level)
  waiting for transfers between devices: 25.8 us -> 26.6 us
  transfers between devices with their start and end apart: 17 -> 17, of which waited for: 8 -> 9; matrix products, arithmetic and copies ran while one was open for 0% -> 0% of each run, Pallas kernels for 4% -> 4%
where the time goes in v9:
time: 79.1 us; the launch traced here: 78.4 us
  starting transfers between devices  40.7 us (51%)
  waiting for transfers between devices  26.6 us (34%)
  Pallas kernels  9.81 us (12%)
  between operations  0.9 us (1%)
    ppermute x8, waiting for transfers between devices, turned(): lax.ppermute(value, axis, [(i, (i + shift) % count) for i in range(count)])  21 us
    ppermute x8, starting transfers between devices, turned(): lax.ppermute(value, axis, [(i, (i + shift) % count) for i in range(count)])  16.8 us
    all_to_all x1, starting transfers between devices, local(): pieces = lax.all_to_all(encode(stored), 'axial', 0, 0, tiled=True)  9.99 us
    pallas_call x6, Pallas kernels, run(): pl.pallas_call(body, in_specs=[smem] * len(scalars) + [vmem] * len(args),...  5.71 us
    ppermute x4, starting transfers between devices, swapped(): lax.ppermute(value, 'axial', [(i, i ^ 1) for i in range(lax.axis_size('ax...  4.74 us
    pallas_call x1, Pallas kernels, encode(): pl.pallas_call(encode_body, in_specs=[pl.BlockSpec(memory_space=pl.ANY)],...  4.1 us
    all_to_all x1, starting transfers between devices, local(): sums = lax.all_to_all(total, 'axial', 0, 0, tiled=True)  3.97 us
    all_to_all x1, starting transfers between devices, between_chips(): lax.all_to_all(value, 'axial', 0, 0, tiled=True, axis_index_groups=groups)  3.42 us
  transfers between devices with their start and end apart: 17, of which 9 were waited for; matrix products, arithmetic and copies ran while one was open for 0% of the time, Pallas kernels for 4%

profile of v9, /device:TPU:1, one launch (start us, length us, event | category | flops | bytes accessed | tf_op | source)
XLA Modules:
  0.0 78.4 jit_solution(14244402741810429438)
XLA Ops:
  0.7 4.1 %shard_map.94 = s16[16,16,16,128]{3,2,1,0:T(8,128)(2,1)} custom-call(bf16[4,32,8,2048]{3,2,1,0:T(8,128)(2,1)} %bitcast.17), custom_call_target="tpu_custom_call" | custom-call | tf_op jit(solution)/shard_map/pallas_call | solution.py:112
  4.8 10.0 %all-to-all-start = ((s16[16,16,16,128]{3,2,1,0:T(8,128)(2,1)}), s16[16,16,16,128]{3,2,1,0:T(8,128)(2,1)S(1)}, u32[]{:S(2)}, u32[]{:S(2)}) async-start(s16[16,16,16,128]{3,2,1,0:T(8,128)(2,1)} %shard_map.94), calls=%async_computation | async-start | bytes 2097152 | tf_op jit(solution)/shard_map/all_to_all | solution.py:693
  14.8 1.6 %collective-permute-start = (f32[64,128]{1,0:T(8,128)S(1)}, f32[64,128]{1,0:T(8,128)S(1)}, u32[]{:S(2)}, u32[]{:S(2)}) collective-permute-start(f32[64,128]{1,0:T(8,128)S(1)} %get-tuple-element.70), channel_id=1, source_target_pairs={{0,16},{16,32},{32,48},{48,64},{64,80},{80,96},{96,112},{112,128},... | collective-permute-start | bytes 98312 | tf_op jit(solution)/shard_map/ppermute | solution.py:656
  16.6 1.3 %collective-permute-start.2 = (f32[16,128]{1,0:T(8,128)S(1)}, f32[16,128]{1,0:T(8,128)S(1)}, u32[]{:S(2)}, u32[]{:S(2)}) collective-permute-start(f32[16,128]{1,0:T(8,128)S(1)} %select_maximum_fusion.2), channel_id=1, source_target_pairs={{0,1},{1,2},{2,3},{3,4},{4,5},{5,6},{6,7},{7,8},{8,9},{9,10},{10,1... | collective-permute-start | bytes 24584 | tf_op jit(solution)/shard_map/ppermute | solution.py:656
  17.9 3.8 %collective-permute-start.3 = (f32[16,128]{1,0:T(8,128)S(1)}, f32[16,128]{1,0:T(8,128)S(1)}, u32[]{:S(2)}, u32[]{:S(2)}) collective-permute-start(f32[16,128]{1,0:T(8,128)S(1)} %select_maximum_fusion), channel_id=1, source_target_pairs={{0,15},{1,0},{2,1},{3,2},{4,3},{5,4},{6,5},{7,6},{8,7},{9,8},{10,9... | collective-permute-start | bytes 24584 | tf_op jit(solution)/shard_map/ppermute | solution.py:656
  22.6 15.4 %collective-permute-done.low_ref = f32[64,128]{1,0:T(8,128)S(1)} collective-permute-done((f32[64,128]{1,0:T(8,128)S(1)}, f32[64,128]{1,0:T(8,128)S(1)}, u32[]{:S(2)}, u32[]{:S(2)}) %collective-permute-start) | collective-permute-done | bytes 32800 | tf_op jit(solution)/shard_map/ppermute | solution.py:656
  38.0 2.8 %collective-permute-done.1.high_ref = f32[2,64,128]{2,1,0:T(8,128)S(1)} collective-permute-done((f32[2,64,128]{2,1,0:T(8,128)S(1)}, f32[2,64,128]{2,1,0:T(8,128)S(1)}, u32[]{:S(2)}, u32[]{:S(2)}) %collective-permute-start.1) | collective-permute-done | bytes 65568 | tf_op jit(solution)/shard_map/ppermute | solution.py:656
  40.8 1.9 %all-to-all-done.rec_ref = s16[16,16,16,128]{3,2,1,0:T(8,128)(2,1)S(1)} async-done(((s16[16,16,16,128]{3,2,1,0:T(8,128)(2,1)}), s16[16,16,16,128]{3,2,1,0:T(8,128)(2,1)S(1)}, u32[]{:S(2)}, u32[]{:S(2)}) %all-to-all-start) | async-done | bytes 1048608 | tf_op jit(solution)/shard_map/all_to_all | solution.py:693
  42.7 0.9 %shard_map.95 = (f32[4,64,128]{2,1,0:T(8,128)S(1)}, f32[4,64,128]{2,1,0:T(8,128)S(1)}, f32[4,64,128]{2,1,0:T(8,128)S(1)}, f32[4,64,128]{2,1,0:T(8,128)S(1)}, f32...) custom-call(s32[66]{0:T(128)S(1)} %pad_add_fusion.info_ref, s16[16,16,16,128]{3,2,1,0:T(8,128)(2,1)S(1)} %all-to-all-done.rec_ref, ...), custom_call_target="tpu_custom_call" | custom-call | flops 1000000000 | bytes 3000000 | tf_op jit(solution)/shard_map/pallas_call | solution.py:638
  43.9 1.4 %collective-permute-done.4.near_ref.got_ref = f32[13,32,128]{2,1,0:T(8,128)S(1)} collective-permute-done((f32[13,32,128]{2,1,0:T(8,128)S(1)}, f32[13,32,128]{2,1,0:T(8,128)S(1)}, u32[]{:S(2)}, u32[]{:S(2)}) %collective-permute-start.4) | collective-permute-done | bytes 213024 | tf_op jit(solution)/shard_map/ppermute | solution.py:660
  45.2 0.9 %shard_map.97 = s16[8,9,16,128]{3,2,1,0:T(8,128)(2,1)} custom-call(f32[5,32,128]{2,1,0:T(8,128)S(1)} %get-tuple-element.48.keep_ref, f32[13,32,128]{2,1,0:T(8,128)S(1)} %collective-permute-done.4.near_ref.got_ref, f32[16,128]{1,0:T(8,128)S(1)} %collective-permute-done.2.left_ref.early_left_ref, ...), custom_call_target="tpu_custom_call" | custom-call | flops 49999998976 | bytes 150000000 | tf_op jit(solution)/shard_map/pallas_call | solution.py:638
  46.1 3.4 %all-to-all-start.1 = ((s16[8,9,16,128]{3,2,1,0:T(8,128)(2,1)}), s16[8,9,16,128]{3,2,1,0:T(8,128)(2,1)S(1)}, u32[]{:S(2)}, u32[]{:S(2)}) async-start(s16[8,9,16,128]{3,2,1,0:T(8,128)(2,1)} %shard_map.97), calls=%async_computation.1 | async-start | bytes 589824 | tf_op jit(solution)/shard_map/all_to_all | solution.py:673
  49.6 1.3 %shard_map.96 = (f32[6,64,128]{2,1,0:T(8,128)S(1)}, f32[24,128]{1,0:T(8,128)S(1)}, f32[24,128]{1,0:T(8,128)S(1)}, f32[3,32,128]{2,1,0:T(8,128)S(1)}, f32[3,32,12...) custom-call(s32[66]{0:T(128)S(1)} %pad_add_fusion.info_ref, s16[16,16,16,128]{3,2,1,0:T(8,128)(2,1)S(1)} %all-to-all-done.rec_ref, ...), custom_call_target="tpu_custom_call" | custom-call | flops 99999997952 | bytes 300000000 | tf_op jit(solution)/shard_map/pallas_call | solution.py:638
  50.9 1.6 %collective-permute-start.8 = (f32[3,32,128]{2,1,0:T(8,128)S(1)}, f32[3,32,128]{2,1,0:T(8,128)S(1)}, u32[]{:S(2)}, u32[]{:S(2)}) collective-permute-start(f32[3,32,128]{2,1,0:T(8,128)S(1)} %get-tuple-element.53), channel_id=1, source_target_pairs={{0,16},{16,0},{32,48},{48,32},{64,80},{80,64},{96,112},{112,96},{1... | collective-permute-start | bytes 147464 | tf_op jit(solution)/shard_map/ppermute | solution.py:660
  52.5 1.2 %collective-permute-start.6 = (f32[24,128]{1,0:T(8,128)S(1)}, f32[24,128]{1,0:T(8,128)S(1)}, u32[]{:S(2)}, u32[]{:S(2)}) collective-permute-start(f32[24,128]{1,0:T(8,128)S(1)} %get-tuple-element.47.own_right_ref), channel_id=1, source_target_pairs={{0,1},{1,2},{2,3},{3,4},{4,5},{5,6},{6,7},{7,8},{8,9},{9,10},{10,1... | collective-permute-start | bytes 36872 | tf_op jit(solution)/shard_map/ppermute | solution.py:656
  53.7 3.7 %collective-permute-start.7 = (f32[24,128]{1,0:T(8,128)S(1)}, f32[24,128]{1,0:T(8,128)S(1)}, u32[]{:S(2)}, u32[]{:S(2)}) collective-permute-start(f32[24,128]{1,0:T(8,128)S(1)} %get-tuple-element.46.own_left_ref), channel_id=1, source_target_pairs={{0,15},{1,0},{2,1},{3,2},{4,3},{5,4},{6,5},{7,6},{8,7},{9,8},{10,9... | collective-permute-start | bytes 36872 | tf_op jit(solution)/shard_map/ppermute | solution.py:656
  57.4 1.1 %collective-permute-done.6.left_ref = f32[24,128]{1,0:T(8,128)S(1)} collective-permute-done((f32[24,128]{1,0:T(8,128)S(1)}, f32[24,128]{1,0:T(8,128)S(1)}, u32[]{:S(2)}, u32[]{:S(2)}) %collective-permute-start.6) | collective-permute-done | bytes 12320 | tf_op jit(solution)/shard_map/ppermute | solution.py:656
  58.5 1.6 %all-to-all-done.1.sums_ref = s16[8,9,16,128]{3,2,1,0:T(8,128)(2,1)S(1)} async-done(((s16[8,9,16,128]{3,2,1,0:T(8,128)(2,1)}), s16[8,9,16,128]{3,2,1,0:T(8,128)(2,1)S(1)}, u32[]{:S(2)}, u32[]{:S(2)}) %all-to-all-start.1) | async-done | bytes 294944 | tf_op jit(solution)/shard_map/all_to_all | solution.py:673
  60.9 2.9 %collective-permute-start.9 = (f32[4,32,128]{2,1,0:T(8,128)S(1)}, f32[4,32,128]{2,1,0:T(8,128)S(1)}, u32[]{:S(2)}, u32[]{:S(2)}) collective-permute-start(f32[4,32,128]{2,1,0:T(8,128)S(1)} %get-tuple-element.56), channel_id=1, source_target_pairs={{0,16},{16,0},{32,48},{48,32},{64,80},{80,64},{96,112},{112,96},{1... | collective-permute-start | bytes 196616 | tf_op jit(solution)/shard_map/ppermute | solution.py:660
  64.0 4.0 %all-to-all-start.2 = ((s16[16,2,16,128]{3,2,1,0:T(8,128)(2,1)}), s16[16,2,16,128]{3,2,1,0:T(8,128)(2,1)S(1)}, u32[]{:S(2)}, u32[]{:S(2)}) async-start(s16[16,2,16,128]{3,2,1,0:T(8,128)(2,1)} %get-tuple-element.63), calls=%async_computation.2 | async-start | bytes 262144 | tf_op jit(solution)/shard_map/all_to_all | solution.py:743
  68.8 1.7 %collective-permute-start.11 = (f32[64,128]{1,0:T(8,128)S(1)}, f32[64,128]{1,0:T(8,128)S(1)}, u32[]{:S(2)}, u32[]{:S(2)}) collective-permute-start(f32[64,128]{1,0:T(8,128)S(1)} %get-tuple-element.60), channel_id=1, source_target_pairs={{0,240},{16,32},{32,16},{48,64},{64,48},{80,96},{96,80},{112,128},... | collective-permute-start | bytes 98312 | tf_op jit(solution)/shard_map/ppermute | solution.py:665
  71.1 4.5 %collective-permute-start.13 = (f32[8,128]{1,0:T(8,128)S(1)}, f32[8,128]{1,0:T(8,128)S(1)}, u32[]{:S(2)}, u32[]{:S(2)}) collective-permute-start(f32[8,128]{1,0:T(8,128)S(1)} %get-tuple-element.62), channel_id=1, source_target_pairs={{0,15},{1,0},{2,1},{3,2},{4,3},{5,4},{6,5},{7,6},{8,7},{9,8},{10,9... | collective-permute-start | bytes 12296 | tf_op jit(solution)/shard_map/ppermute | solution.py:656
  75.6 1.0 %collective-permute-done.12.left_ref = f32[8,128]{1,0:T(8,128)S(1)} collective-permute-done((f32[8,128]{1,0:T(8,128)S(1)}, f32[8,128]{1,0:T(8,128)S(1)}, u32[]{:S(2)}, u32[]{:S(2)}) %collective-permute-start.12) | collective-permute-done | bytes 4128 | tf_op jit(solution)/shard_map/ppermute | solution.py:656
  77.4 1.0 %shard_map.100 = (f32[4,64,128]{2,1,0:T(8,128)}, f32[4,64,128]{2,1,0:T(8,128)}, f32[4,64]{1,0:T(4,128)}) custom-call(f32[17,128]{1,0:T(8,128)S(1)} %broadcast_in_dim.4.weight_ref, s16[6,16,16,128]{3,2,1,0:T(8,128)(2,1)S(1)} %get-tuple-element.44.fields_ref, f32[4,64,128]{2,1,0:T(8,128)S(1)} %get-tuple-element.57.lt_ref, ...), custom_call_target="tpu_custom_call" | custom-call | flops 1000000000 | bytes 3000000 | tf_op jit(solution)/shard_map/pallas_call | solution.py:638
  (51 shorter events, 4.4 us)
Async XLA Ops:
  0.6 21.1 %copy-start = (s32[4,16,16]{2,1,0:T(8,128)S(1)}, s32[4,16,16]{2,1,0:T(8,128)}, u32[]{:S(2)}) copy-start(s32[4,16,16]{2,1,0:T(8,128)} %param.8) | copy-start | bytes 12292
  0.7 15.8 %slice-start = ((f32[4,64,128]{2,1,0:T(8,128)}), f32[1,64,128]{2,1,0:T(8,128)S(1)}, s32[]{:S(2)}) async-start(f32[4,64,128]{2,1,0:T(8,128)} %seed_lr_ref.1), calls=%async_computation.3 | async-start | bytes 65536 | tf_op jit(solution)/shard_map/slice | solution.py:700
  0.7 15.9 %copy-start.3 = (f32[4,64,128]{2,1,0:T(8,128)S(1)}, f32[4,64,128]{2,1,0:T(8,128)}, u32[]{:S(2)}) copy-start(f32[4,64,128]{2,1,0:T(8,128)} %seed_lr_ref.1) | copy-start | bytes 393220
  0.7 15.8 %copy-start.5 = (f32[64,128]{1,0:T(8,128)S(1)}, f32[64,128]{1,0:T(8,128)}, u32[]{:S(2)}) copy-start(f32[64,128]{1,0:T(8,128)} %length_ref.11) | copy-start | bytes 98308
  4.8 37.9 %all-to-all-start = ((s16[16,16,16,128]{3,2,1,0:T(8,128)(2,1)}), s16[16,16,16,128]{3,2,1,0:T(8,128)(2,1)S(1)}, u32[]{:S(2)}, u32[]{:S(2)}) async-start(s16[16,16,16,128]{3,2,1,0:T(8,128)(2,1)} %shard_map.94), calls=%async_computation | async-start | bytes 2097152 | tf_op jit(solution)/shard_map/all_to_all | solution.py:693
  14.8 23.2 %collective-permute-start = (f32[64,128]{1,0:T(8,128)S(1)}, f32[64,128]{1,0:T(8,128)S(1)}, u32[]{:S(2)}, u32[]{:S(2)}) collective-permute-start(f32[64,128]{1,0:T(8,128)S(1)} %get-tuple-element.70), channel_id=1, source_target_pairs={{0,16},{16,32},{32,48},{48,64},{64,80},{80,96},{96,112},{112,128},... | collective-permute-start | bytes 98312 | tf_op jit(solution)/shard_map/ppermute | solution.py:656
  16.5 24.4 %collective-permute-start.1 = (f32[2,64,128]{2,1,0:T(8,128)S(1)}, f32[2,64,128]{2,1,0:T(8,128)S(1)}, u32[]{:S(2)}, u32[]{:S(2)}) collective-permute-start(f32[2,64,128]{2,1,0:T(8,128)S(1)} %pad_maximum_fusion), channel_id=1, source_target_pairs={{0,240},{16,0},{32,16},{48,32},{64,48},{80,64},{96,80},{112,96},{1... | collective-permute-start | bytes 196616 | tf_op jit(solution)/shard_map/ppermute | solution.py:656
  16.6 6.0 %collective-permute-start.2 = (f32[16,128]{1,0:T(8,128)S(1)}, f32[16,128]{1,0:T(8,128)S(1)}, u32[]{:S(2)}, u32[]{:S(2)}) collective-permute-start(f32[16,128]{1,0:T(8,128)S(1)} %select_maximum_fusion.2), channel_id=1, source_target_pairs={{0,1},{1,2},{2,3},{3,4},{4,5},{5,6},{6,7},{7,8},{8,9},{9,10},{10,1... | collective-permute-start | bytes 24584 | tf_op jit(solution)/shard_map/ppermute | solution.py:656
  17.9 4.8 %collective-permute-start.3 = (f32[16,128]{1,0:T(8,128)S(1)}, f32[16,128]{1,0:T(8,128)S(1)}, u32[]{:S(2)}, u32[]{:S(2)}) collective-permute-start(f32[16,128]{1,0:T(8,128)S(1)} %select_maximum_fusion), channel_id=1, source_target_pairs={{0,15},{1,0},{2,1},{3,2},{4,3},{5,4},{6,5},{7,6},{8,7},{9,8},{10,9... | collective-permute-start | bytes 24584 | tf_op jit(solution)/shard_map/ppermute | solution.py:656
  43.7 1.6 %collective-permute-start.4 = (f32[13,32,128]{2,1,0:T(8,128)S(1)}, f32[13,32,128]{2,1,0:T(8,128)S(1)}, u32[]{:S(2)}, u32[]{:S(2)}) collective-permute-start(f32[13,32,128]{2,1,0:T(8,128)S(1)} %get-tuple-element.42), channel_id=1, source_target_pairs={{0,16},{16,0},{32,48},{48,32},{64,80},{80,64},{96,112},{112,96},{1... | collective-permute-start | bytes 638984 | tf_op jit(solution)/shard_map/ppermute | solution.py:660
  43.8 5.8 %collective-permute-start.5 = (f32[4,64,128]{2,1,0:T(8,128)S(1)}, f32[4,64,128]{2,1,0:T(8,128)S(1)}, u32[]{:S(2)}, u32[]{:S(2)}) collective-permute-start(f32[4,64,128]{2,1,0:T(8,128)S(1)} %get-tuple-element.43), channel_id=1, source_target_pairs={{0,240},{16,32},{32,16},{48,64},{64,48},{80,96},{96,80},{112,128},... | collective-permute-start | bytes 393224 | tf_op jit(solution)/shard_map/ppermute | solution.py:665
  46.1 14.0 %all-to-all-start.1 = ((s16[8,9,16,128]{3,2,1,0:T(8,128)(2,1)}), s16[8,9,16,128]{3,2,1,0:T(8,128)(2,1)S(1)}, u32[]{:S(2)}, u32[]{:S(2)}) async-start(s16[8,9,16,128]{3,2,1,0:T(8,128)(2,1)} %shard_map.97), calls=%async_computation.1 | async-start | bytes 589824 | tf_op jit(solution)/shard_map/all_to_all | solution.py:673
  49.6 18.4 %copy-start.2 = (f32[4,64,128]{2,1,0:T(8,128)S(1)}, f32[4,64,128]{2,1,0:T(8,128)}, u32[]{:S(2)}) copy-start(f32[4,64,128]{2,1,0:T(8,128)} %seed_ref.1) | copy-start | bytes 393220
  49.6 18.4 %copy-start.4 = (f32[4,64,128]{2,1,0:T(8,128)S(1)}, f32[4,64,128]{2,1,0:T(8,128)}, u32[]{:S(2)}) copy-start(f32[4,64,128]{2,1,0:T(8,128)} %seed_lr_ref.1) | copy-start | bytes 393220
  49.6 18.4 %copy-start.7 = (f32[2,64,128]{2,1,0:T(8,128)S(1)}, f32[2,64,128]{2,1,0:T(8,128)}, u32[]{:S(2)}) copy-start(f32[2,64,128]{2,1,0:T(8,128)} %copy-done.6) | copy-start | bytes 196612
  50.9 9.2 %collective-permute-start.8 = (f32[3,32,128]{2,1,0:T(8,128)S(1)}, f32[3,32,128]{2,1,0:T(8,128)S(1)}, u32[]{:S(2)}, u32[]{:S(2)}) collective-permute-start(f32[3,32,128]{2,1,0:T(8,128)S(1)} %get-tuple-element.53), channel_id=1, source_target_pairs={{0,16},{16,0},{32,48},{48,32},{64,80},{80,64},{96,112},{112,96},{1... | collective-permute-start | bytes 147464 | tf_op jit(solution)/shard_map/ppermute | solution.py:660
  52.5 6.0 %collective-permute-start.6 = (f32[24,128]{1,0:T(8,128)S(1)}, f32[24,128]{1,0:T(8,128)S(1)}, u32[]{:S(2)}, u32[]{:S(2)}) collective-permute-start(f32[24,128]{1,0:T(8,128)S(1)} %get-tuple-element.47.own_right_ref), channel_id=1, source_target_pairs={{0,1},{1,2},{2,3},{3,4},{4,5},{5,6},{6,7},{7,8},{8,9},{9,10},{10,1... | collective-permute-start | bytes 36872 | tf_op jit(solution)/shard_map/ppermute | solution.py:656
  53.7 4.8 %collective-permute-start.7 = (f32[24,128]{1,0:T(8,128)S(1)}, f32[24,128]{1,0:T(8,128)S(1)}, u32[]{:S(2)}, u32[]{:S(2)}) collective-permute-start(f32[24,128]{1,0:T(8,128)S(1)} %get-tuple-element.46.own_left_ref), channel_id=1, source_target_pairs={{0,15},{1,0},{2,1},{3,2},{4,3},{5,4},{6,5},{7,6},{8,7},{9,8},{10,9... | collective-permute-start | bytes 36872 | tf_op jit(solution)/shard_map/ppermute | solution.py:656
  60.9 7.0 %collective-permute-start.9 = (f32[4,32,128]{2,1,0:T(8,128)S(1)}, f32[4,32,128]{2,1,0:T(8,128)S(1)}, u32[]{:S(2)}, u32[]{:S(2)}) collective-permute-start(f32[4,32,128]{2,1,0:T(8,128)S(1)} %get-tuple-element.56), channel_id=1, source_target_pairs={{0,16},{16,0},{32,48},{48,32},{64,80},{80,64},{96,112},{112,96},{1... | collective-permute-start | bytes 196616 | tf_op jit(solution)/shard_map/ppermute | solution.py:660
  64.0 13.3 %all-to-all-start.2 = ((s16[16,2,16,128]{3,2,1,0:T(8,128)(2,1)}), s16[16,2,16,128]{3,2,1,0:T(8,128)(2,1)S(1)}, u32[]{:S(2)}, u32[]{:S(2)}) async-start(s16[16,2,16,128]{3,2,1,0:T(8,128)(2,1)} %get-tuple-element.63), calls=%async_computation.2 | async-start | bytes 262144 | tf_op jit(solution)/shard_map/all_to_all | solution.py:743
  68.7 7.9 %collective-permute-start.10 = (f32[64,128]{1,0:T(8,128)S(1)}, f32[64,128]{1,0:T(8,128)S(1)}, u32[]{:S(2)}, u32[]{:S(2)}) collective-permute-start(f32[64,128]{1,0:T(8,128)S(1)} %get-tuple-element.59), channel_id=1, source_target_pairs={{0,16},{16,0},{32,48},{48,32},{64,80},{80,64},{96,112},{112,96},{1... | collective-permute-start | bytes 98312 | tf_op jit(solution)/shard_map/ppermute | solution.py:660
  68.8 7.7 %collective-permute-start.11 = (f32[64,128]{1,0:T(8,128)S(1)}, f32[64,128]{1,0:T(8,128)S(1)}, u32[]{:S(2)}, u32[]{:S(2)}) collective-permute-start(f32[64,128]{1,0:T(8,128)S(1)} %get-tuple-element.60), channel_id=1, source_target_pairs={{0,240},{16,32},{32,16},{48,64},{64,48},{80,96},{96,80},{112,128},... | collective-permute-start | bytes 98312 | tf_op jit(solution)/shard_map/ppermute | solution.py:665
  70.5 6.1 %collective-permute-start.12 = (f32[8,128]{1,0:T(8,128)S(1)}, f32[8,128]{1,0:T(8,128)S(1)}, u32[]{:S(2)}, u32[]{:S(2)}) collective-permute-start(f32[8,128]{1,0:T(8,128)S(1)} %get-tuple-element.61), channel_id=1, source_target_pairs={{0,1},{1,2},{2,3},{3,4},{4,5},{5,6},{6,7},{7,8},{8,9},{9,10},{10,1... | collective-permute-start | bytes 12296 | tf_op jit(solution)/shard_map/ppermute | solution.py:656
  71.1 5.5 %collective-permute-start.13 = (f32[8,128]{1,0:T(8,128)S(1)}, f32[8,128]{1,0:T(8,128)S(1)}, u32[]{:S(2)}, u32[]{:S(2)}) collective-permute-start(f32[8,128]{1,0:T(8,128)S(1)} %get-tuple-element.62), channel_id=1, source_target_pairs={{0,15},{1,0},{2,1},{3,2},{4,3},{5,4},{6,5},{7,6},{8,7},{9,8},{10,9... | collective-permute-start | bytes 12296 | tf_op jit(solution)/shard_map/ppermute | solution.py:656
  (4 other events, 40.6 us)
